TPU v7x, 128 devices: a whole 4x4x4 slice. The times are simulated.
128 devices in a mesh: row: 4 (over z), col: 32 (over y, x, core).
Axes of the slice: x: 4, y: 4, z: 4, core: 2. Of those that a mesh axis runs over, the one named last changes fastest.
Arguments:
- features: bfloat16 [524288, 128], P(('row', 'col')), may hold values from -6 to 6
- neighbors: int32 [524288, 10], P(('row', 'col')), may hold values from 0 to 10239, as said below
- counts: int32 [524288], P(('row', 'col')), may hold values from 1 to 10
- hub_rows: int32 [16384], P(('row', 'col')), may hold values from 0 to 4095, as said below
- w_self: bfloat16 [128, 256], replicated, may hold values from -0.5 to 0.5
- w_neigh: bfloat16 [128, 256], replicated, may hold values from -0.5 to 0.5
- out_bias: float32 [256], replicated, may hold values from -3 to 3
- cotangent: bfloat16 [524288, 256], P(('row', 'col')), may hold values from -6 to 6
Outputs:
- activations: bfloat16 [524288, 256], P(('row', 'col'))
- grad_features: bfloat16 [524288, 128], P(('row', 'col'))
- grad_w_self: float32 [128, 256], replicated
- grad_w_neigh: float32 [128, 256], replicated
- grad_bias: float32 [256], replicated
Inputs may be any that keep to these rules, and one draw needn't show every extreme that they name: `neighbors`: rows below 1024 are never used by a partition of row 0, rows 5120 to 6143 never by one of the last row; slots at or past a node's count hold valid rows and are ignored. `hub_rows`: the 128 rows of one partition are distinct.
All inputs are finite; a program needn't handle non-finite values.
Results may differ from a plain program's by a relative error of at most 0.0075.
Values may be sent and summed in bfloat16 or wider, within the bound.
No kernel may reach another device: no remote copies, remote signals or barrier semaphores. Data moves between devices by JAX's collectives and lax.ppermute only.
A program may use at most 256 MiB of HBM per device.

v0:
```python
import jax
import jax.numpy as jnp
from jax import lax
from jax.sharding import PartitionSpec as P

FANOUT = 10
HALO = 1024


def padded_2(cells, sides, width):
    for axis, dim in sides:
        count = lax.axis_size(axis)
        ends = count - 1
        head = lax.slice_in_dim(cells, 0, width, axis=dim)
        tail = lax.slice_in_dim(cells, cells.shape[dim] - width, cells.shape[dim], axis=dim)
        cells = jnp.concatenate(
            [
                lax.ppermute(tail, axis, [(i, (i + 1) % count) for i in range(ends)]),
                cells,
                lax.ppermute(head, axis, [((i + 1) % count, i) for i in range(ends)]),
            ],
            axis=dim,
        )
    return cells


def gelu_tanh(value):
    return jax.nn.gelu(value, approximate=True)


def on_device(features, neighbors, counts, hub_rows, w_self, w_neigh, out_bias, cotangent):
    node_count = features.shape[0]
    padded = padded_2(features, (("row", 0),), HALO)
    hub_local = jnp.take(features, hub_rows, axis=0)
    hub_table = lax.all_gather(hub_local, "col", axis=0, tiled=True)
    table = jnp.concatenate([padded, hub_table], axis=0)
    extent = table.shape[0]
    active = jnp.arange(FANOUT)[None, :] < counts[:, None]
    divisor = counts.astype(jnp.float32)[:, None]
    picked = jnp.take(table, neighbors, axis=0).astype(jnp.float32)
    agg = (jnp.sum(jnp.where(active[:, :, None], picked, 0.0), axis=1) / divisor).astype(
        jnp.bfloat16
    )
    pre = (
        jnp.dot(features, w_self, preferred_element_type=jnp.float32)
        + jnp.dot(agg, w_neigh, preferred_element_type=jnp.float32)
        + out_bias
    )
    act, backward = jax.vjp(gelu_tanh, pre)
    activations = act.astype(jnp.bfloat16)
    dz = backward(cotangent.astype(jnp.float32))[0].astype(jnp.bfloat16)
    dims = (((0,), (0,)), ((), ()))
    back_dims = (((1,), (1,)), ((), ()))
    grad_self = lax.dot_general(features, dz, dims, preferred_element_type=jnp.float32)
    grad_b = jnp.sum(dz.astype(jnp.float32), axis=0)
    grad_neigh = lax.dot_general(agg, dz, dims, preferred_element_type=jnp.float32)
    source = lax.dot_general(dz, w_neigh, back_dims, preferred_element_type=jnp.float32) / divisor
    grad_width = source.shape[1]
    values = jnp.where(active[:, :, None], source[:, None, :], 0.0)
    d_table = (
        jnp.zeros((extent, grad_width), jnp.float32)
        .at[neighbors.reshape(-1)]
        .add(values.reshape(-1, grad_width))
    )
    border_grads = jnp.concatenate(
        [d_table[:HALO], d_table[HALO + node_count : 2 * HALO + node_count]], axis=0
    )
    returned = padded_2(border_grads.astype(jnp.bfloat16), (("row", 0),), HALO).astype(
        border_grads.dtype
    )
    from_above = returned[:HALO]
    from_below = returned[returned.shape[0] - HALO :]
    mine = d_table[HALO : HALO + node_count]
    mine = mine.at[:HALO].add(from_above)
    mine = mine.at[node_count - HALO :].add(from_below)
    hub_share = lax.psum_scatter(
        d_table[2 * HALO + node_count :].astype(jnp.bfloat16),
        "col",
        scatter_dimension=0,
        tiled=True,
    ).astype(jnp.float32)
    mine = mine.at[hub_rows].add(hub_share)
    local_grad = lax.dot_general(dz, w_self, back_dims, preferred_element_type=jnp.float32)
    grad_features = (local_grad + mine).astype(jnp.bfloat16)
    grad_self, grad_neigh, grad_b = lax.psum((grad_self, grad_neigh, grad_b), ("row", "col"))
    return (activations, grad_features, grad_self, grad_neigh, grad_b)


def solution(mesh):
    placed = (
        P(("row", "col"), None),
        P(("row", "col"), None),
        P(("row", "col")),
        P(("row", "col")),
        P(),
        P(),
        P(),
        P(("row", "col"), None),
    )
    return jax.shard_map(
        on_device,
        mesh=mesh,
        in_specs=placed,
        out_specs=(P(("row", "col"), None), P(("row", "col"), None), P(), P(), P()),
        check_vma=False,
    )
```

profile of v0, /device:TPU:1, one launch (start us, length us, event | category | flops | bytes accessed | tf_op | source)
XLA Modules:
  0.0 636.1 jit_solution(751575490882594704)
XLA Ops:
  8.6 2.1 gather_fusion
  11.4 1.9 fusion.22
  13.3 5.1 collective-permute-start
  20.4 3.1 iota_compare_fusion
  24.5 1.6 copy.17
  26.1 1.5 copy.15
  27.6 3.8 lt.61
  31.4 2.5 reshape.131
  33.9 1.8 compare_select_fusion
  36.4 1.6 copy.16
  37.9 1.7 reshape.142
  39.7 2.7 fusion.23
  42.5 15.4 %all-gather.2.cloned.1.call-done = bf16[4096,128]{1,0:T(8,128)(2,1)} async-done(((bf16[128,128]{1,0:T(8,128)(2,1)}), bf16[4096,128]{1,0:T(8,128)(2,1)}) %all-gather.2.cloned.1.call-update) | async-done | bytes 1048592 | tf_op jit(solution)/shard_map/all_gather | solution.py:35
  57.8 3.3 pad_maximum_fusion
  61.1 142.3 %gather_fusion.1 = bf16[40960,128]{1,0:T(8,128)(2,1)} fusion(bf16[10240,128]{1,0:T(8,128)(2,1)S(1)} %pad_maximum_fusion, s32[40960]{0:T(1024)S(1)} %broadcast_clamp_fusion), kind=kCustom, calls=%fused_computation.1 | custom fusion | bytes 21135360 | tf_op jit(solution)/shard_map/jit(_take)/gather | solution.py:40
  203.5 19.4 %reshape.141 = bf16[4096,10,128]{2,1,0:T(8,128)(2,1)} reshape(bf16[40960,128]{1,0:T(8,128)(2,1)} %gather_fusion.1) | data formatting | bytes 20971520 | tf_op jit(solution)/shard_map/jit(_take)/gather | solution.py:40
  223.0 24.5 %select_reduce_fusion = f32[4096,128]{1,0:T(8,128)S(1)} fusion(bf16[4096,10,128]{2,1,0:T(8,128)(2,1)} %reshape.141, pred[4096,10]{1,0:T(8,128)(4,1)S(1)} %copy-done.9, pred[4096,10]{1,0:T(8,128)(4,1)S(1)} %copy-done.7), kind=kLoop, calls=%fused_computation.4 | loop fusion | flops 20447232 | bytes 12664832 | tf_op jit(solution)/shard_map/reduce_sum | solution.py:41
  248.2 5.2 convert_reduce_fusion
  253.4 1.3 fusion.24
  254.8 1.4 convolution_bitcast_fusion
  257.2 11.0 %broadcast_in_dim.80 = f32[4096,10,128]{2,1,0:T(8,128)} broadcast(f32[4096,128]{1,0:T(8,128)S(1)} %convolution_divide_fusion), dimensions={0,2} | broadcast | bytes 23068672 | tf_op jit(solution)/shard_map/jit(_where)/broadcast_in_dim | solution.py:59
  268.2 27.6 %broadcast_in_dim.81 = f32[40960,128]{1,0:T(8,128)} reshape(f32[4096,10,128]{2,1,0:T(8,128)} %broadcast_in_dim.80) | data formatting | bytes 41943040 | tf_op jit(solution)/shard_map/jit(_where)/broadcast_in_dim | solution.py:59
  295.8 244.2 %scatter_custom_fusion = f32[10240,128]{1,0:T(8,128)} fusion(s32[40960]{0:T(1024)} %bitcast.15, f32[40960,128]{1,0:T(8,128)} %broadcast_in_dim.81, f32[]{:T(128)} %constant.96.clone.1, pred[40960]{0:T(1024)(128)(4,1)S(1)} %copy-done.11), kind=kCustom, calls=%fused_computation.5 | custom fusion | flops 10485760 | bytes 26256384 | tf_op jit(solution)/shard_map/scatter-add | solution.py:63
  540.0 2.7 convert.7
  542.7 1.5 copy-done.6
  546.3 3.2 collective-permute-start.2
  549.5 1.3 collective-permute-start.3
  550.8 65.7 %psum.23 = f32[256]{0:T(256)} all-reduce(f32[256]{0:T(256)S(1)} %get-tuple-element.41), channel_id=1, replica_groups=mesh['row'=4,'col'=32] {'row','col'}, use_global_device_ids=true, to_apply=%region_7.8 | all-reduce | flops 256 | bytes 2048 | tf_op jit(solution)/shard_map/psum | solution.py:85
  616.5 1.7 copy.18
  619.9 2.0 convolution_add_fusion.1
  622.0 4.3 scatter_custom_fusion.1
  626.3 2.7 convert_element_type.40
  (61 shorter events, 12.2 us)
Async XLA Ops:
  7.2 241.0 %copy-start = (bf16[128,256]{1,0:T(8,128)(2,1)S(1)}, bf16[128,256]{1,0:T(8,128)(2,1)}, u32[]{:S(2)}) copy-start(bf16[128,256]{1,0:T(8,128)(2,1)} %param.17) | copy-start | bytes 196612
  7.2 50.6 %all-gather.2.cloned.1.call-start = ((), (), s32[]{:S(2)}) async-start(), calls=%async_computation.1 | async-start | bytes 1081344 | tf_op jit(solution)/shard_map/all_gather | solution.py:35
  7.9 0.7 copy-start.13
  8.6 27.1 %copy-start.8 = (s32[4096,10]{0,1:T(8,128)S(1)}, s32[4096,10]{0,1:T(8,128)}, u32[]{:S(2)}) copy-start(s32[4096,10]{0,1:T(8,128)} %param.13) | copy-start | bytes 491524
  11.4 605.1 %all-reduce.3.cloned.1.call-start = ((), (), s32[]{:S(2)}) async-start(), calls=%async_computation.3 | async-start | bytes 524288 | tf_op jit(solution)/shard_map/psum | solution.py:85
  13.3 29.2 %collective-permute-start = (bf16[1024,128]{1,0:T(8,128)(2,1)}, bf16[1024,128]{1,0:T(8,128)(2,1)}, u32[]{:S(2)}, u32[]{:S(2)}) collective-permute-start(bf16[1024,128]{1,0:T(8,128)(2,1)} %get-tuple-element.46), channel_id=1, source_target_pairs={{0,32},{32,64},{64,96},{1,33},{33,65},{65,97},{2,34},{34,66},{66,9... | collective-permute-start | bytes 786440 | tf_op jit(solution)/shard_map/ppermute | solution.py:18
  18.4 24.1 %collective-permute-start.1 = (bf16[1024,128]{1,0:T(8,128)(2,1)}, bf16[1024,128]{1,0:T(8,128)(2,1)}, u32[]{:S(2)}, u32[]{:S(2)}) collective-permute-start(bf16[1024,128]{1,0:T(8,128)(2,1)} %get-tuple-element.47), channel_id=1, source_target_pairs={{32,0},{64,32},{96,64},{33,1},{65,33},{97,65},{34,2},{66,34},{98,6... | collective-permute-start | bytes 786440 | tf_op jit(solution)/shard_map/ppermute | solution.py:20
  27.6 12.1 %copy-start.1 = (bf16[4096,128]{1,0:T(8,128)(2,1)S(1)}, bf16[4096,128]{1,0:T(8,128)(2,1)}, u32[]{:S(2)}) copy-start(bf16[4096,128]{1,0:T(8,128)(2,1)} %param.12) | copy-start | bytes 3145732
  27.6 12.1 %copy-start.10 = (bf16[128,256]{1,0:T(8,128)(2,1)S(1)}, bf16[128,256]{1,0:T(8,128)(2,1)}, u32[]{:S(2)}) copy-start(bf16[128,256]{1,0:T(8,128)(2,1)} %param.16) | copy-start | bytes 196612
  203.5 19.4 %copy-start.7 = (pred[4096,10]{1,0:T(8,128)(4,1)S(1)}, pred[4096,10]{1,0:T(8,128)(4,1)}, u32[]{:S(2)}) copy-start(pred[4096,10]{1,0:T(8,128)(4,1)} %iota_compare_fusion) | copy-start | bytes 122884
  203.5 19.4 %copy-start.9 = (pred[4096,10]{1,0:T(8,128)(4,1)S(1)}, pred[4096,10]{1,0:T(8,128)(4,1)}, u32[]{:S(2)}) copy-start(pred[4096,10]{1,0:T(8,128)(4,1)} %copy.15) | copy-start | bytes 122884
  222.9 25.3 %copy-start.5 = (f32[4096,256]{1,0:T(8,128)S(1)}, f32[4096,256]{1,0:T(8,128)}, u32[]{:S(2)}) copy-start(f32[4096,256]{1,0:T(8,128)} %fusion.23) | copy-start | bytes 12582916
  222.9 25.3 %copy-start.14 = (bf16[4096,256]{1,0:T(8,128)(2,1)S(1)}, bf16[4096,256]{1,0:T(8,128)(2,1)}, u32[]{:S(2)}) copy-start(bf16[4096,256]{1,0:T(8,128)(2,1)} %param.19) | copy-start | bytes 6291460
  223.0 25.3 %copy-start.15 = (f32[256]{0:T(256)S(1)}, f32[256]{0:T(256)}, u32[]{:S(2)}) copy-start(f32[256]{0:T(256)} %param.18) | copy-start | bytes 3076
  248.2 6.5 %copy-start.2 = (bf16[4096,128]{1,0:T(8,128)(2,1)S(1)}, bf16[4096,128]{1,0:T(8,128)(2,1)}, u32[]{:S(2)}) copy-start(bf16[4096,128]{1,0:T(8,128)(2,1)} %param.12) | copy-start | bytes 3145732
  253.4 3.8 copy-start.3
  256.2 365.8 %reduce-scatter.2.cloned.1.call-start = ((), (), s32[]{:S(2)}) async-start(), calls=%async_computation.2 | async-start | bytes 1081344 | tf_op jit(solution)/shard_map/reduce_scatter | solution.py:76
  268.2 27.6 %copy-start.11 = (pred[40960]{0:T(1024)(128)(4,1)S(1)}, pred[40960]{0:T(1024)(128)(4,1)}, u32[]{:S(2)}) copy-start(pred[40960]{0:T(1024)(128)(4,1)} %lt.61) | copy-start | bytes 122884
  542.7 1.5 copy-start.6
  544.1 74.0 %slice-start = ((f32[10240,128]{1,0:T(8,128)}), f32[4096,128]{1,0:T(8,128)S(1)}, s32[]{:S(2)}) async-start(f32[10240,128]{1,0:T(8,128)} %scatter_custom_fusion), calls=%async_computation.4 | async-start | bytes 4194304 | tf_op jit(solution)/shard_map/slice | solution.py:73
  546.3 71.9 %collective-permute-start.2 = (bf16[1024,128]{1,0:T(8,128)(2,1)S(1)}, bf16[1024,128]{1,0:T(8,128)(2,1)S(1)}, u32[]{:S(2)}, u32[]{:S(2)}) collective-permute-start(bf16[1024,128]{1,0:T(8,128)(2,1)S(1)} %get-tuple-element.44), channel_id=1, source_target_pairs={{0,32},{32,64},{64,96},{1,33},{33,65},{65,97},{2,34},{34,66},{66,9... | collective-permute-start | bytes 786440 | tf_op jit(solution)/shard_map/ppermute | solution.py:18
  549.5 68.7 %collective-permute-start.3 = (bf16[1024,128]{1,0:T(8,128)(2,1)S(1)}, bf16[1024,128]{1,0:T(8,128)(2,1)S(1)}, u32[]{:S(2)}, u32[]{:S(2)}) collective-permute-start(bf16[1024,128]{1,0:T(8,128)(2,1)S(1)} %get-tuple-element.45), channel_id=1, source_target_pairs={{32,0},{64,32},{96,64},{33,1},{65,33},{97,65},{34,2},{66,34},{98,6... | collective-permute-start | bytes 786440 | tf_op jit(solution)/shard_map/ppermute | solution.py:20
  618.2 1.8 copy-start.4
  622.0 7.0 %copy-start.12 = (f32[128,256]{1,0:T(8,128)S(1)}, f32[128,256]{1,0:T(8,128)}, u32[]{:S(2)}) copy-start(f32[128,256]{1,0:T(8,128)} %get-tuple-element.51) | copy-start | bytes 393220
Sparse Core Ops, SparseCore 0:
  11.5 46.2 all-gather.1
  256.3 140.8 all-reduce.2
  545.3 74.6 reduce-scatter.1
where the time goes:
time: 638 us; the launch traced here: 636 us
  other arithmetic  293 us (46%)
  local copies, waits for them, and re-layouts  223 us (35%)
  blocking collectives  65.7 us (10%)
  waiting for transfers between devices  15.4 us (2%)
  between operations  14 us (2%)
  matrix products  13.6 us (2%)
  starting transfers between devices  11 us (2%)
    scatter-add x1, other arithmetic, on_device(): d_table = jnp.zeros((extent, grad_width), jnp.float32).at[neighbors.resha...  244 us
    gather x2, local copies, waits for them, and re-layouts, on_device(): picked = jnp.take(table, neighbors, axis=0).astype(jnp.float32)  162 us
    psum x1, blocking collectives, on_device(): lax.psum((grad_self, grad_neigh, grad_b), ('row', 'col'))  65.7 us
    broadcast_in_dim x2, local copies, waits for them, and re-layouts, on_device(): values = jnp.where(active[:, :, None], source[:, None, :], 0.0)  38.6 us
    reduce_sum x1, other arithmetic, on_device(): jnp.sum(jnp.where(active[:, :, None], picked, 0.0), axis=1) / divisor  24.5 us
    all_gather x1, waiting for transfers between devices, on_device(): hub_table = lax.all_gather(hub_local, 'col', axis=0, tiled=True)  15.4 us
  transfers between devices with their start and end apart: 7, of which 1 were waited for; matrix products, arithmetic and copies ran while one was open for 50% of the time, Pallas kernels for 0%

commit v1 on v0

v1 whole, which is shorter than its diff:
```python
import functools

import jax
import jax.numpy as jnp
from jax import lax
from jax.experimental import pallas as pl
from jax.experimental.pallas import tpu as pltpu
from jax.sharding import Mesh, PartitionSpec as P

F = 128
H = 256
NODES = 4096
HALO = 1024
HUB = 128
FANOUT = 10
COLS = 32
HUBS = HUB * COLS
OWN = HALO
UPPER = HALO + NODES
HUB_AT = 2 * HALO + NODES
EXTENT = HUB_AT + HUBS
LANES = 128
CHAINS = 8
VMEM_BYTES = 60 * 2**20
AXES = ("z", "y", "x", "core")

smem = pl.BlockSpec(memory_space=pltpu.SMEM)
vmem = pl.BlockSpec(memory_space=pltpu.VMEM)
params = pltpu.CompilerParams(vmem_limit_bytes=VMEM_BYTES)


def group_of(count):
    return 16 if count <= 3 else 8


def hub_kernel(hub_rows, features, out, wide, rows):
    @pl.loop(0, NODES // 512)
    def _(i):
        cut = pl.ds(i * 512, 512)
        wide[cut, :] = features[cut, :].astype(jnp.float32)

    @pl.loop(0, HUB // 16)
    def _(i):
        for u in range(16):
            rows[pl.ds(i * 16 + u, 1), :] = wide[pl.ds(hub_rows[i * 16 + u], 1), :]

    out[...] = rows[...].astype(jnp.bfloat16)


def pick_hubs(hub_rows, features):
    return pl.pallas_call(
        hub_kernel,
        out_shape=jax.ShapeDtypeStruct((HUB, F), jnp.bfloat16),
        in_specs=[smem, vmem],
        out_specs=vmem,
        scratch_shapes=[pltpu.VMEM((NODES, F), jnp.float32), pltpu.VMEM((HUB, F), jnp.float32)],
        compiler_params=params,
        name="pick_hubs",
    )(hub_rows, features)


def order_kernel(counts, perm, ends):
    rows = NODES // LANES
    count = counts[...]
    lane_r = lax.broadcasted_iota(jnp.int32, (LANES, LANES), 0)
    lane_c = lax.broadcasted_iota(jnp.int32, (LANES, LANES), 1)
    before = (lane_r < lane_c).astype(jnp.float32)
    row_r = lax.broadcasted_iota(jnp.int32, (rows, rows), 0)
    row_c = lax.broadcasted_iota(jnp.int32, (rows, rows), 1)
    above = (row_c < row_r).astype(jnp.float32)
    place = jnp.zeros((rows, LANES), jnp.float32)
    start = jnp.zeros((1, 1), jnp.float32)
    lane = lax.broadcasted_iota(jnp.int32, (1, LANES), 1)
    end_row = jnp.zeros((1, LANES), jnp.float32)
    for c in range(1, FANOUT + 1):
        hit = (count == c).astype(jnp.float32)
        in_row = jnp.dot(hit, before, preferred_element_type=jnp.float32)
        per_row = jnp.sum(hit, axis=1, keepdims=True)
        earlier = jnp.dot(
            above, jnp.broadcast_to(per_row, (rows, LANES)), preferred_element_type=jnp.float32
        )
        place = place + hit * (in_row + earlier + start)
        start = start + jnp.sum(per_row, axis=0, keepdims=True)
        end_row = end_row + jnp.where(lane == c, start, 0.0)
    ends[...] = end_row.astype(jnp.int32)
    place = place.astype(jnp.int32)
    high = place >> 7
    low = place - high * LANES
    slot_row = lax.broadcasted_iota(jnp.int32, (rows, LANES), 0)
    slot_lane = lax.broadcasted_iota(jnp.int32, (LANES, LANES), 0)
    own_lane = lax.broadcasted_iota(jnp.int32, (rows, LANES), 1).astype(jnp.float32)
    total = jnp.zeros((rows, LANES), jnp.float32)
    for r in range(rows):
        to_row = (high[r : r + 1, :] == slot_row).astype(jnp.float32)
        to_lane = (low[r : r + 1, :] == slot_lane).astype(jnp.bfloat16)
        both = jnp.concatenate([to_row * own_lane, to_row * float(r)], axis=0)
        found = lax.dot_general(
            both.astype(jnp.bfloat16),
            to_lane,
            (((1,), (1,)), ((), ())),
            preferred_element_type=jnp.float32,
        )
        total = total + found[:rows] + found[rows:] * float(LANES)
    perm[...] = total.astype(jnp.int32)


def order_nodes(counts):
    rows = NODES // LANES
    perm, ends = pl.pallas_call(
        order_kernel,
        out_shape=(
            jax.ShapeDtypeStruct((rows, LANES), jnp.int32),
            jax.ShapeDtypeStruct((1, LANES), jnp.int32),
        ),
        in_specs=[vmem],
        out_specs=(vmem, vmem),
        compiler_params=params,
        name="order_nodes",
    )(counts.reshape(rows, LANES))
    return perm.reshape(NODES), ends.reshape(LANES)


def over_nodes(ends, perm, visit):
    for count in range(1, FANOUT + 1):
        size = group_of(count)
        first = ends[count - 1]
        groups = (ends[count] - first) // size
        rest = first + groups * size

        @pl.loop(0, groups)
        def _(g, count=count, size=size, first=first):
            at = first + g * size
            visit([perm[at + u] for u in range(size)], count)

        @pl.loop(rest, ends[count])
        def _(at, count=count):
            visit([perm[at]], count)


def forward_kernel(
    ends, perm, slots, features, lower, upper, h0, h1, h2, h3, h4, h5,
    counts, w_self, w_neigh, bias, cotangent,
    act, src, base, grads, table, sums,
):
    def widen(source, at, rows):
        step = min(rows, 256)

        @pl.loop(0, rows // step)
        def _(i):
            table[pl.ds(at + i * step, step), :] = source[pl.ds(i * step, step), :].astype(
                jnp.float32
            )

    widen(features, OWN, NODES)
    widen(lower, 0, HALO)
    widen(upper, UPPER, HALO)
    y, x, core = lax.axis_index("y"), lax.axis_index("x"), lax.axis_index("core")
    position = 0
    for piece in (h0, h1, h2, h3, h4, h5):
        for i in range(piece.shape[0] // HUB):
            b = [(position >> k) & 1 for k in range(5)]
            owner_y = y ^ (b[0] * 1) ^ (b[1] * 3)
            owner_x = x ^ (b[2] * 1) ^ (b[3] * 3)
            owner = owner_y * 8 + owner_x * 2 + (core ^ b[4])
            table[pl.ds(HUB_AT + owner * HUB, HUB), :] = piece[
                i * HUB : (i + 1) * HUB, :
            ].astype(jnp.float32)
            position += 1

    def gather(nodes, count):
        for n in nodes:
            total = table[pl.ds(slots[0, n], 1), :]
            for s in range(1, count):
                total = total + table[pl.ds(slots[s, n], 1), :]
            sums[pl.ds(n, 1), :] = total

    over_nodes(ends, perm, gather)

    grads[...] = jnp.zeros_like(grads)
    contract_rows = (((0,), (0,)), ((), ()))
    contract_cols = (((1,), (1,)), ((), ()))
    block = 256

    @pl.loop(0, NODES // block)
    def _(i):
        cut = pl.ds(i * block, block)
        parts = []
        for k in range(block // LANES):
            row = counts[pl.ds(i * (block // LANES) + k, 1), :].astype(jnp.float32)
            parts.append(jnp.broadcast_to(row, (LANES, LANES)).T)
        divisor = jnp.concatenate(parts, axis=0)
        own = features[cut, :]
        agg = (sums[cut, :] / divisor).astype(jnp.bfloat16)
        z = (
            jnp.dot(own, w_self[...], preferred_element_type=jnp.float32)
            + jnp.dot(agg, w_neigh[...], preferred_element_type=jnp.float32)
            + bias[...]
        )
        scale = 0.7978845608028654
        squared = z * z
        t = jnp.tanh(scale * (z + 0.044715 * (squared * z)))
        half = 0.5 * (1.0 + t)
        act[cut, :] = (z * half).astype(jnp.bfloat16)
        slope = half + 0.5 * z * (1.0 - t * t) * (scale * (1.0 + 3 * 0.044715 * squared))
        dz_wide = cotangent[cut, :].astype(jnp.float32) * slope
        dz = dz_wide.astype(jnp.bfloat16)
        grads[0:F, :] += lax.dot_general(
            own, dz, contract_rows, preferred_element_type=jnp.float32
        )
        grads[F : 2 * F, :] += lax.dot_general(
            agg, dz, contract_rows, preferred_element_type=jnp.float32
        )
        partial = jnp.sum(
            dz.astype(jnp.float32).reshape(block // 8, 8, H), axis=0
        )
        grads[2 * F : 2 * F + 8, :] += partial
        src[cut, :] = (
            lax.dot_general(dz, w_neigh[...], contract_cols, preferred_element_type=jnp.float32)
            / divisor
        )
        base[cut, :] = lax.dot_general(
            dz, w_self[...], contract_cols, preferred_element_type=jnp.float32
        )


def forward(ends, perm, slots, features, lower, upper, hubs, counts, w_self, w_neigh, bias, cot):
    return pl.pallas_call(
        forward_kernel,
        out_shape=(
            jax.ShapeDtypeStruct((NODES, H), jnp.bfloat16),
            jax.ShapeDtypeStruct((NODES, F), jnp.float32),
            jax.ShapeDtypeStruct((NODES, F), jnp.float32),
            jax.ShapeDtypeStruct((2 * F + 16, H), jnp.float32),
        ),
        in_specs=[smem] * 3 + [vmem] * (3 + len(hubs) + 5),
        out_specs=(vmem,) * 4,
        scratch_shapes=[
            pltpu.VMEM((EXTENT, F), jnp.float32),
            pltpu.VMEM((NODES, F), jnp.float32),
        ],
        compiler_params=params,
        name="forward",
    )(ends, perm, slots, features, lower, upper, *hubs, counts, w_self, w_neigh, bias, cot)


def scatter_kernel(ends, perm, slots, src, base, lower, upper, hub, own, *chains):
    for k, chain in enumerate(chains):
        if k == 0:
            parts = ((0, HALO), (UPPER, EXTENT - UPPER))
            step = 512

            @pl.loop(0, NODES // step)
            def _(i):
                chains[0][pl.ds(OWN + i * step, step), :] = base[pl.ds(i * step, step), :]
        else:
            parts = ((0, EXTENT),)
        for at, rows in parts:
            step = 512

            @pl.loop(0, rows // step)
            def _(i, chain=chain, at=at):
                chain[pl.ds(at + i * step, step), :] = jnp.zeros((step, F), jnp.float32)

    turn = [0]

    def scatter(nodes, count):
        turn[0] = 0
        for n in nodes:
            row = src[pl.ds(n, 1), :]
            for s in range(count):
                chain = chains[turn[0] % CHAINS]
                turn[0] += 1
                at = pl.ds(slots[s, n], 1)
                chain[at, :] = chain[at, :] + row

    over_nodes(ends, perm, scatter)

    def total(cut):
        out = chains[0][cut, :]
        for chain in chains[1:]:
            out = out + chain[cut, :]
        return out

    @pl.loop(0, HALO // HUB)
    def _(i):
        lower[pl.ds(i * HUB, HUB), :] = total(pl.ds(i * HUB, HUB)).astype(jnp.bfloat16)
        upper[pl.ds(i * HUB, HUB), :] = total(pl.ds(UPPER + i * HUB, HUB)).astype(jnp.bfloat16)

    @pl.loop(0, COLS)
    def _(owner):
        y, x, core = owner // 8, (owner // 2) % 4, owner % 2
        at = (core * 16 + x * 4 + y) * HUB
        hub[pl.ds(at, HUB), :] = total(pl.ds(HUB_AT + owner * HUB, HUB)).astype(jnp.bfloat16)

    @pl.loop(0, NODES // HUB)
    def _(i):
        own[pl.ds(i * HUB, HUB), :] = total(pl.ds(OWN + i * HUB, HUB))


def scatter(ends, perm, slots, src, base):
    return pl.pallas_call(
        scatter_kernel,
        out_shape=(
            jax.ShapeDtypeStruct((HALO, F), jnp.bfloat16),
            jax.ShapeDtypeStruct((HALO, F), jnp.bfloat16),
            jax.ShapeDtypeStruct((HUBS, F), jnp.bfloat16),
            jax.ShapeDtypeStruct((NODES, F), jnp.float32),
        ),
        in_specs=[smem] * 3 + [vmem] * 2,
        out_specs=(vmem,) * 4,
        scratch_shapes=[pltpu.VMEM((EXTENT, F), jnp.float32)] * CHAINS,
        compiler_params=params,
        name="scatter",
    )(ends, perm, slots, src, base)


def finish_kernel(hub_rows, own, from_above, from_below, share, out, total):
    step = 256

    @pl.loop(0, NODES // step)
    def _(i):
        cut = pl.ds(i * step, step)
        total[cut, :] = own[cut, :]

    @pl.loop(0, HALO // step)
    def _(i):
        cut = pl.ds(i * step, step)
        total[cut, :] = total[cut, :] + from_above[cut, :].astype(jnp.float32)

    @pl.loop(0, HALO // step)
    def _(i):
        cut = pl.ds(NODES - HALO + i * step, step)
        total[cut, :] = total[cut, :] + from_below[pl.ds(i * step, step), :].astype(jnp.float32)

    @pl.loop(0, HUB // 8)
    def _(i):
        for u in range(8):
            at = pl.ds(hub_rows[i * 8 + u], 1)
            total[at, :] = total[at, :] + share[pl.ds(i * 8 + u, 1), :]

    @pl.loop(0, NODES // step)
    def _(i):
        cut = pl.ds(i * step, step)
        out[cut, :] = total[cut, :].astype(jnp.bfloat16)


def finish(hub_rows, own, from_above, from_below, share):
    return pl.pallas_call(
        finish_kernel,
        out_shape=jax.ShapeDtypeStruct((NODES, F), jnp.bfloat16),
        in_specs=[smem] + [vmem] * 4,
        out_specs=vmem,
        scratch_shapes=[pltpu.VMEM((NODES, F), jnp.float32)],
        compiler_params=params,
        name="finish",
    )(hub_rows, own, from_above, from_below, share)


def swap(value, axis, flip):
    count = lax.axis_size(axis)
    return lax.ppermute(value, axis, [(i, i ^ flip) for i in range(count)])


def shifted(value, axis, by):
    count = lax.axis_size(axis)
    pairs = [(i, i + by) for i in range(count) if 0 <= i + by < count]
    return lax.ppermute(value, axis, pairs)


def gather_hubs(mine):
    pieces = [mine]
    held = mine
    steps = (("y", 1), ("y", 3), ("x", 1), ("x", 3), ("core", 1))
    for k, (axis, flip) in enumerate(steps):
        other = swap(held, axis, flip)
        pieces.append(other)
        if k < len(steps) - 1:
            held = jnp.concatenate([held, other], axis=0)
    return pieces


def halve(value, axis, flip, bit):
    rows = value.shape[0] // 2
    keep = lax.dynamic_slice_in_dim(value, bit * rows, rows, axis=0)
    give = lax.dynamic_slice_in_dim(value, (1 - bit) * rows, rows, axis=0)
    got = swap(give.astype(jnp.bfloat16), axis, flip)
    return keep.astype(jnp.float32) + got.astype(jnp.float32)


def reduce_hubs(hub):
    x, y, core = lax.axis_index("x"), lax.axis_index("y"), lax.axis_index("core")
    value = halve(hub, "core", 1, core)
    value = halve(value, "x", 3, x // 2)
    value = halve(value, "x", 1, x % 2)
    value = halve(value, "y", 3, y // 2)
    return halve(value, "y", 1, y % 2)


def reduce_everywhere(grads):
    core = lax.axis_index("core")
    rows = grads.shape[0] // 2
    keep = lax.dynamic_slice_in_dim(grads, core * rows, rows, axis=0)
    give = lax.dynamic_slice_in_dim(grads, (1 - core) * rows, rows, axis=0)
    value = keep + swap(give, "core", 1)
    for axis in ("z", "x", "y"):
        for flip in (1, 3):
            value = value + swap(value, axis, flip)
    other = swap(value, "core", 1)
    first = jnp.where(core == 0, value, other)
    second = jnp.where(core == 0, other, value)
    return jnp.concatenate([first, second], axis=0)


def on_device(features, neighbors, counts, hub_rows, w_self, w_neigh, out_bias, cotangent):
    hubs = gather_hubs(pick_hubs(hub_rows, features))
    lower = shifted(features[NODES - HALO :], "z", 1)
    upper = shifted(features[:HALO], "z", -1)
    perm, ends = order_nodes(counts)
    slots = neighbors.T
    act, src, base, grads = forward(
        ends, perm, slots, features, lower, upper, hubs,
        counts.reshape(NODES // LANES, LANES), w_self, w_neigh,
        out_bias.reshape(1, H), cotangent,
    )
    to_above, to_below, hub, own = scatter(ends, perm, slots, src, base)
    from_below = shifted(to_above, "z", -1)
    from_above = shifted(to_below, "z", 1)
    share = reduce_hubs(hub)
    grads = reduce_everywhere(grads)
    grad_features = finish(hub_rows, own, from_above, from_below, share)
    grad_bias = jnp.sum(grads[2 * F :], axis=0)
    return act, grad_features, grads[:F], grads[F : 2 * F], grad_bias


def solution(mesh):
    mesh = Mesh(mesh.devices.reshape(4, 4, 4, 2), AXES)
    rows = P(AXES, None)
    placed = (rows, rows, P(AXES), P(AXES), P(), P(), P(), rows)
    return jax.shard_map(
        on_device,
        mesh=mesh,
        in_specs=placed,
        out_specs=(rows, rows, P(), P(), P()),
        check_vma=False,
    )
```

time: 638 us -> 191 us (0.30)
  other arithmetic: 293 us -> 4.65 us
  local copies, waits for them, and re-layouts: 223 us -> 3.78 us
  Pallas kernels: 0 us -> 106 us
  blocking collectives: 65.7 us -> 0 us
  starting transfers between devices: 11 us -> 42.2 us
  waiting for transfers between devices: 15.4 us -> 33 us
  matrix products: 13.6 us -> 0 us
  between operations: 14 us -> 0.97 us
    scatter-add x4 -> x0, other arithmetic: 250 us -> none  [the longest x1 244 us: on_device(): d_table = jnp.zeros((extent, grad_width), jnp.float32).at[neighbors.resha...]
    gather x3 -> x0, local copies, waits for them, and re-layouts: 164 us -> none  [the longest x2 162 us: on_device(): picked = jnp.take(table, neighbors, axis=0).astype(jnp.float32)]
    pallas_call x0 -> x5, Pallas kernels: none -> 106 us  [the longest x1 53 us: forward(): pl.pallas_call(forward_kernel, out_shape=(jax.ShapeDtypeStruct((NODES, H)...]
    psum x1 -> x0, blocking collectives: 65.7 us -> none  [on_device(): lax.psum((grad_self, grad_neigh, grad_b), ('row', 'col'))]
    broadcast_in_dim x3 -> x0, local copies, waits for them, and re-layouts: 40.3 us -> none  [the longest x2 38.6 us: on_device(): values = jnp.where(active[:, :, None], source[:, None, :], 0.0)]
    ppermute x4 -> x22, waiting for transfers between devices: 0.01 us -> 33 us  [the longest x18 26.9 us: swap(): return lax.ppermute(value, axis, [(i, i ^ flip) for i in range(count)])]
    ppermute x4 -> x22, starting transfers between devices: 10.8 us -> 42.2 us  [the longest x18 33.4 us: swap(): return lax.ppermute(value, axis, [(i, i ^ flip) for i in range(count)])]
    reduce_sum x1, other arithmetic: 24.5 us -> 0.58 us  [on_device(): grad_bias = jnp.sum(grads[2 * F:], axis=0)]
  transfers between devices with their start and end apart: 7 -> 22, of which waited for: 1 -> 12; matrix products, arithmetic and copies ran while one was open for 50% -> 1% of each run, Pallas kernels for 0% -> 3%
where the time goes in v1:
time: 191 us
  Pallas kernels  106 us (55%)
  starting transfers between devices  42.2 us (22%)
  waiting for transfers between devices  33 us (17%)
  other arithmetic  4.65 us (2%)
  local copies, waits for them, and re-layouts  3.78 us (2%)
    pallas_call x1, Pallas kernels, forward(): pl.pallas_call(forward_kernel, out_shape=(jax.ShapeDtypeStruct((NODES, H)...  53 us
    pallas_call x1, Pallas kernels, scatter(): pl.pallas_call(scatter_kernel, out_shape=(jax.ShapeDtypeStruct((HALO, F),...  45.2 us
    ppermute x18, starting transfers between devices, swap(): return lax.ppermute(value, axis, [(i, i ^ flip) for i in range(count)])  33.4 us
    ppermute x18, waiting for transfers between devices, swap(): return lax.ppermute(value, axis, [(i, i ^ flip) for i in range(count)])  26.9 us
    ppermute x4, starting transfers between devices, shifted(): return lax.ppermute(value, axis, pairs)  8.77 us
    ppermute x4, waiting for transfers between devices, shifted(): return lax.ppermute(value, axis, pairs)  6.11 us
  transfers between devices with their start and end apart: 22, of which 12 were waited for; matrix products, arithmetic and copies ran while one was open for 1% of the time, Pallas kernels for 3%

profile of v1, /device:TPU:1, one launch (start us, length us, event | category | flops | bytes accessed | tf_op | source)
XLA Modules:
  0.0 191.0 jit_solution(17156533520208932205)
XLA Ops:
  0.6 2.2 %pick_hubs.1.h0 = bf16[128,128]{1,0:T(8,128)(2,1)} custom-call(s32[128]{0:T(128)} %hub_rows.3, bf16[4096,128]{1,0:T(8,128)(2,1)} %features.3), custom_call_target="tpu_custom_call" | custom-call | tf_op jit(solution)/shard_map/pick_hubs/pallas_call | solution.py:51
  2.9 2.1 %collective-permute-start.2 = (bf16[128,128]{1,0:T(8,128)(2,1)}, bf16[128,128]{1,0:T(8,128)(2,1)S(1)}, u32[]{:S(2)}, u32[]{:S(2)}) collective-permute-start(bf16[128,128]{1,0:T(8,128)(2,1)} %pick_hubs.1.h0), channel_id=1, source_target_pairs={{0,8},{8,0},{16,24},{24,16},{1,9},{9,1},{17,25},{25,17},{2,10},{10... | collective-permute-start | bytes 98312 | tf_op jit(solution)/shard_map/ppermute | solution.py:361
  5.0 1.5 collective-permute-done.2.h1
  7.3 2.9 %collective-permute-start.3 = (bf16[256,128]{1,0:T(8,128)(2,1)S(1)}, bf16[256,128]{1,0:T(8,128)(2,1)S(1)}, u32[]{:S(2)}, u32[]{:S(2)}) collective-permute-start(bf16[256,128]{1,0:T(8,128)(2,1)S(1)} %pad_maximum_fusion.3), channel_id=1, source_target_pairs={{0,24},{8,16},{16,8},{24,0},{1,25},{9,17},{17,9},{25,1},{2,26},{10... | collective-permute-start | bytes 196616 | tf_op jit(solution)/shard_map/ppermute | solution.py:361
  10.2 1.7 collective-permute-done.3.h2
  12.6 1.3 collective-permute-start.4
  14.7 1.8 collective-permute-done.4.h3
  17.3 2.6 %collective-permute-start.5 = (bf16[1024,128]{1,0:T(8,128)(2,1)S(1)}, bf16[1024,128]{1,0:T(8,128)(2,1)S(1)}, u32[]{:S(2)}, u32[]{:S(2)}) collective-permute-start(bf16[1024,128]{1,0:T(8,128)(2,1)S(1)} %pad_maximum_fusion), channel_id=1, source_target_pairs={{0,6},{2,4},{4,2},{6,0},{1,7},{3,5},{5,3},{7,1},{8,14},{10,12},{12... | collective-permute-start | bytes 786440 | tf_op jit(solution)/shard_map/ppermute | solution.py:361
  19.9 3.9 %collective-permute-done.5.h4 = bf16[1024,128]{1,0:T(8,128)(2,1)S(1)} collective-permute-done((bf16[1024,128]{1,0:T(8,128)(2,1)S(1)}, bf16[1024,128]{1,0:T(8,128)(2,1)S(1)}, u32[]{:S(2)}, u32[]{:S(2)}) %collective-permute-start.5) | collective-permute-done | bytes 262176 | tf_op jit(solution)/shard_map/ppermute | solution.py:361
  23.9 5.2 %collective-permute-start.6 = (bf16[2048,128]{1,0:T(8,128)(2,1)S(1)}, bf16[2048,128]{1,0:T(8,128)(2,1)S(1)}, u32[]{:S(2)}, u32[]{:S(2)}) collective-permute-start(bf16[2048,128]{1,0:T(8,128)(2,1)S(1)} %constant_dynamic-update-slice_fusion), channel_id=1, source_target_pairs={{0,1},{1,0},{2,3},{3,2},{4,5},{5,4},{6,7},{7,6},{8,9},{9,8},{10,11... | collective-permute-start | bytes 1572872 | tf_op jit(solution)/shard_map/ppermute | solution.py:361
  29.1 3.6 %collective-permute-start = (bf16[1024,128]{1,0:T(8,128)(2,1)S(1)}, bf16[1024,128]{1,0:T(8,128)(2,1)S(1)}, u32[]{:S(2)}, u32[]{:S(2)}) collective-permute-start(bf16[1024,128]{1,0:T(8,128)(2,1)S(1)} %get-tuple-element.26), channel_id=1, source_target_pairs={{0,32},{32,64},{64,96},{1,33},{33,65},{65,97},{2,34},{34,66},{66,9... | collective-permute-start | bytes 786440 | tf_op jit(solution)/shard_map/ppermute | solution.py:367
  32.8 1.3 collective-permute-start.1
  34.1 2.4 %order_nodes.1 = (s32[32,128]{1,0:T(8,128)}, s32[1,128]{1,0:T(1,128)}) custom-call(s32[32,128]{1,0:T(8,128)} %bitcast.9), custom_call_target="tpu_custom_call" | custom-call | tf_op jit(solution)/shard_map/order_nodes/pallas_call | solution.py:109
  36.5 1.9 %collective-permute-done.lower = bf16[1024,128]{1,0:T(8,128)(2,1)S(1)} collective-permute-done((bf16[1024,128]{1,0:T(8,128)(2,1)S(1)}, bf16[1024,128]{1,0:T(8,128)(2,1)S(1)}, u32[]{:S(2)}, u32[]{:S(2)}) %collective-permute-start) | collective-permute-done | bytes 262176 | tf_op jit(solution)/shard_map/ppermute | solution.py:367
  38.4 4.2 %collective-permute-done.1.upper = bf16[1024,128]{1,0:T(8,128)(2,1)S(1)} collective-permute-done((bf16[1024,128]{1,0:T(8,128)(2,1)S(1)}, bf16[1024,128]{1,0:T(8,128)(2,1)S(1)}, u32[]{:S(2)}, u32[]{:S(2)}) %collective-permute-start.1) | collective-permute-done | bytes 262176 | tf_op jit(solution)/shard_map/ppermute | solution.py:367
  43.5 53.0 %forward.1 = (bf16[4096,256]{1,0:T(8,128)(2,1)}, f32[4096,128]{1,0:T(8,128)}, f32[4096,128]{1,0:T(8,128)}, f32[272,256]{1,0:T(8,128)}) custom-call(s32[128]{0:T(128)} %bitcast.11, s32[4096]{0:T(1024)} %bitcast.7, s32[10,4096]{1,0:T(8,128)} %bitcast.5, bf16[4096,128]{1,0:T(8,128)(2,1)} %features.3, bf16[1024,128]{1,0:T(8,128)(2,1)} %copy-done.10, ...), custom_call_target="tpu_custom_call" | custom-call | tf_op jit(solution)/shard_map/forward/pallas_call | solution.py:227
  96.5 45.2 %scatter.1 = (bf16[1024,128]{1,0:T(8,128)(2,1)}, bf16[1024,128]{1,0:T(8,128)(2,1)}, bf16[4096,128]{1,0:T(8,128)(2,1)}, f32[4096,128]{1,0:T(8,128)}) custom-call(s32[128]{0:T(128)} %bitcast.12, s32[4096]{0:T(1024)} %bitcast.8, s32[10,4096]{1,0:T(8,128)} %bitcast.6, f32[4096,128]{1,0:T(8,128)} %get-tuple-element.18.src, f32[4096,128]{1,0:T(8,128)} %get-tuple-element.19.base), custom_call_target="tpu_custom_call" | custom-call | tf_op jit(solution)/shard_map/scatter/pallas_call | solution.py:301
  141.7 1.2 constant_dynamic-slice_fusion.1
  142.9 1.3 collective-permute-start.9
  144.3 1.6 collective-permute-done.14
  146.7 4.2 %collective-permute-done.15 = f32[136,256]{1,0:T(8,128)S(1)} collective-permute-done((f32[136,256]{1,0:T(8,128)S(1)}, f32[136,256]{1,0:T(8,128)S(1)}, u32[]{:S(2)}, u32[]{:S(2)}) %collective-permute-start.15) | collective-permute-done | bytes 139296 | tf_op jit(solution)/shard_map/ppermute | solution.py:361
  150.9 1.9 collective-permute-start.16
  153.0 3.0 %collective-permute-start.10 = (bf16[1024,128]{1,0:T(8,128)(2,1)S(1)}, bf16[1024,128]{1,0:T(8,128)(2,1)S(1)}, u32[]{:S(2)}, u32[]{:S(2)}) collective-permute-start(bf16[1024,128]{1,0:T(8,128)(2,1)S(1)} %dynamic-slice_convert_fusion), channel_id=1, source_target_pairs={{0,6},{2,4},{4,2},{6,0},{1,7},{3,5},{5,3},{7,1},{8,14},{10,12},{12... | collective-permute-start | bytes 786440 | tf_op jit(solution)/shard_map/ppermute | solution.py:361
  156.3 4.2 %collective-permute-done.17 = f32[136,256]{1,0:T(8,128)S(1)} collective-permute-done((f32[136,256]{1,0:T(8,128)S(1)}, f32[136,256]{1,0:T(8,128)S(1)}, u32[]{:S(2)}, u32[]{:S(2)}) %collective-permute-start.17) | collective-permute-done | bytes 139296 | tf_op jit(solution)/shard_map/ppermute | solution.py:361
  160.5 2.1 %collective-permute-start.18 = (f32[136,256]{1,0:T(8,128)S(1)}, f32[136,256]{1,0:T(8,128)S(1)}, u32[]{:S(2)}, u32[]{:S(2)}) collective-permute-start(f32[136,256]{1,0:T(8,128)S(1)} %add.103), channel_id=1, source_target_pairs={{0,6},{2,4},{4,2},{6,0},{1,7},{3,5},{5,3},{7,1},{8,14},{10,12},{12... | collective-permute-start | bytes 417800 | tf_op jit(solution)/shard_map/ppermute | solution.py:361
  162.8 2.9 %collective-permute-done.18 = f32[136,256]{1,0:T(8,128)S(1)} collective-permute-done((f32[136,256]{1,0:T(8,128)S(1)}, f32[136,256]{1,0:T(8,128)S(1)}, u32[]{:S(2)}, u32[]{:S(2)}) %collective-permute-start.18) | collective-permute-done | bytes 139296 | tf_op jit(solution)/shard_map/ppermute | solution.py:361
  166.8 2.9 %collective-permute-start.12 = (bf16[256,128]{1,0:T(8,128)(2,1)S(1)}, bf16[256,128]{1,0:T(8,128)(2,1)S(1)}, u32[]{:S(2)}, u32[]{:S(2)}) collective-permute-start(bf16[256,128]{1,0:T(8,128)(2,1)S(1)} %dynamic-slice_convert_fusion.2), channel_id=1, source_target_pairs={{0,24},{8,16},{16,8},{24,0},{1,25},{9,17},{17,9},{25,1},{2,26},{10... | collective-permute-start | bytes 196616 | tf_op jit(solution)/shard_map/ppermute | solution.py:361
  169.6 2.5 %collective-permute-start.7 = (bf16[1024,128]{1,0:T(8,128)(2,1)S(1)}, bf16[1024,128]{1,0:T(8,128)(2,1)S(1)}, u32[]{:S(2)}, u32[]{:S(2)}) collective-permute-start(bf16[1024,128]{1,0:T(8,128)(2,1)S(1)} %copy-done.13), channel_id=1, source_target_pairs={{0,32},{32,64},{64,96},{1,33},{33,65},{65,97},{2,34},{34,66},{66,9... | collective-permute-start | bytes 786440 | tf_op jit(solution)/shard_map/ppermute | solution.py:367
  172.2 1.3 collective-permute-start.8
  173.8 4.9 %collective-permute-done.20 = f32[136,256]{1,0:T(8,128)S(1)} collective-permute-done((f32[136,256]{1,0:T(8,128)S(1)}, f32[136,256]{1,0:T(8,128)S(1)}, u32[]{:S(2)}, u32[]{:S(2)}) %collective-permute-start.20) | collective-permute-done | bytes 139296 | tf_op jit(solution)/shard_map/ppermute | solution.py:361
  178.8 5.9 %collective-permute-start.21 = (f32[136,256]{1,0:T(8,128)S(1)}, f32[136,256]{1,0:T(8,128)S(1)}, u32[]{:S(2)}, u32[]{:S(2)}) collective-permute-start(f32[136,256]{1,0:T(8,128)S(1)} %add.106), channel_id=1, source_target_pairs={{0,1},{1,0},{2,3},{3,2},{4,5},{5,4},{6,7},{7,6},{8,9},{9,8},{10,11... | collective-permute-start | bytes 417800 | tf_op jit(solution)/shard_map/ppermute | solution.py:361
  186.1 3.5 %finish.1 = bf16[4096,128]{1,0:T(8,128)(2,1)} custom-call(s32[128]{0:T(128)} %hub_rows.3, f32[4096,128]{1,0:T(8,128)} %get-tuple-element.20.own, bf16[1024,128]{1,0:T(8,128)(2,1)} %copy-done.8, bf16[1024,128]{1,0:T(8,128)(2,1)} %copy-done.9, f32[128,128]{1,0:T(8,128)} %convert_add_fusion.4.share), custom_call_target="tpu_custom_call" | custom-call | tf_op jit(solution)/shard_map/finish/pallas_call | solution.py:348
  (75 shorter events, 9.8 us)
Async XLA Ops:
  0.6 28.4 %copy-start = (bf16[4096,128]{1,0:T(8,128)(2,1)S(1)}, bf16[4096,128]{1,0:T(8,128)(2,1)}, u32[]{:S(2)}) copy-start(bf16[4096,128]{1,0:T(8,128)(2,1)} %features.3) | copy-start | bytes 3145732
  2.9 3.6 %collective-permute-start.2 = (bf16[128,128]{1,0:T(8,128)(2,1)}, bf16[128,128]{1,0:T(8,128)(2,1)S(1)}, u32[]{:S(2)}, u32[]{:S(2)}) collective-permute-start(bf16[128,128]{1,0:T(8,128)(2,1)} %pick_hubs.1.h0), channel_id=1, source_target_pairs={{0,8},{8,0},{16,24},{24,16},{1,9},{9,1},{17,25},{25,17},{2,10},{10... | collective-permute-start | bytes 98312 | tf_op jit(solution)/shard_map/ppermute | solution.py:361
  6.5 36.1 %copy-start.5 = (bf16[128,128]{1,0:T(8,128)(2,1)}, bf16[128,128]{1,0:T(8,128)(2,1)S(1)}, u32[]{:S(2)}) copy-start(bf16[128,128]{1,0:T(8,128)(2,1)S(1)} %collective-permute-done.2.h1) | copy-start | bytes 98308
  7.3 4.6 %collective-permute-start.3 = (bf16[256,128]{1,0:T(8,128)(2,1)S(1)}, bf16[256,128]{1,0:T(8,128)(2,1)S(1)}, u32[]{:S(2)}, u32[]{:S(2)}) collective-permute-start(bf16[256,128]{1,0:T(8,128)(2,1)S(1)} %pad_maximum_fusion.3), channel_id=1, source_target_pairs={{0,24},{8,16},{16,8},{24,0},{1,25},{9,17},{17,9},{25,1},{2,26},{10... | collective-permute-start | bytes 196616 | tf_op jit(solution)/shard_map/ppermute | solution.py:361
  11.9 30.8 %copy-start.2 = (bf16[256,128]{1,0:T(8,128)(2,1)}, bf16[256,128]{1,0:T(8,128)(2,1)S(1)}, u32[]{:S(2)}) copy-start(bf16[256,128]{1,0:T(8,128)(2,1)S(1)} %collective-permute-done.3.h2) | copy-start | bytes 196612
  12.6 3.9 %collective-permute-start.4 = (bf16[512,128]{1,0:T(8,128)(2,1)S(1)}, bf16[512,128]{1,0:T(8,128)(2,1)S(1)}, u32[]{:S(2)}, u32[]{:S(2)}) collective-permute-start(bf16[512,128]{1,0:T(8,128)(2,1)S(1)} %pad_maximum_fusion.2), channel_id=1, source_target_pairs={{0,2},{2,0},{4,6},{6,4},{1,3},{3,1},{5,7},{7,5},{8,10},{10,8},{12,... | collective-permute-start | bytes 393224 | tf_op jit(solution)/shard_map/ppermute | solution.py:361
  16.5 26.1 %copy-start.1 = (bf16[512,128]{1,0:T(8,128)(2,1)}, bf16[512,128]{1,0:T(8,128)(2,1)S(1)}, u32[]{:S(2)}) copy-start(bf16[512,128]{1,0:T(8,128)(2,1)S(1)} %collective-permute-done.4.h3) | copy-start | bytes 393220
  17.3 6.5 %collective-permute-start.5 = (bf16[1024,128]{1,0:T(8,128)(2,1)S(1)}, bf16[1024,128]{1,0:T(8,128)(2,1)S(1)}, u32[]{:S(2)}, u32[]{:S(2)}) collective-permute-start(bf16[1024,128]{1,0:T(8,128)(2,1)S(1)} %pad_maximum_fusion), channel_id=1, source_target_pairs={{0,6},{2,4},{4,2},{6,0},{1,7},{3,5},{5,3},{7,1},{8,14},{10,12},{12... | collective-permute-start | bytes 786440 | tf_op jit(solution)/shard_map/ppermute | solution.py:361
  23.8 18.8 %copy-start.3 = (bf16[1024,128]{1,0:T(8,128)(2,1)}, bf16[1024,128]{1,0:T(8,128)(2,1)S(1)}, u32[]{:S(2)}) copy-start(bf16[1024,128]{1,0:T(8,128)(2,1)S(1)} %collective-permute-done.5.h4) | copy-start | bytes 786436
  23.9 18.8 %collective-permute-start.6 = (bf16[2048,128]{1,0:T(8,128)(2,1)S(1)}, bf16[2048,128]{1,0:T(8,128)(2,1)S(1)}, u32[]{:S(2)}, u32[]{:S(2)}) collective-permute-start(bf16[2048,128]{1,0:T(8,128)(2,1)S(1)} %constant_dynamic-update-slice_fusion), channel_id=1, source_target_pairs={{0,1},{1,0},{2,3},{3,2},{4,5},{5,4},{6,7},{7,6},{8,9},{9,8},{10,11... | collective-permute-start | bytes 1572872 | tf_op jit(solution)/shard_map/ppermute | solution.py:361
  29.1 9.3 %collective-permute-start = (bf16[1024,128]{1,0:T(8,128)(2,1)S(1)}, bf16[1024,128]{1,0:T(8,128)(2,1)S(1)}, u32[]{:S(2)}, u32[]{:S(2)}) collective-permute-start(bf16[1024,128]{1,0:T(8,128)(2,1)S(1)} %get-tuple-element.26), channel_id=1, source_target_pairs={{0,32},{32,64},{64,96},{1,33},{33,65},{65,97},{2,34},{34,66},{66,9... | collective-permute-start | bytes 786440 | tf_op jit(solution)/shard_map/ppermute | solution.py:367
  32.8 9.9 %collective-permute-start.1 = (bf16[1024,128]{1,0:T(8,128)(2,1)S(1)}, bf16[1024,128]{1,0:T(8,128)(2,1)S(1)}, u32[]{:S(2)}, u32[]{:S(2)}) collective-permute-start(bf16[1024,128]{1,0:T(8,128)(2,1)S(1)} %get-tuple-element.25), channel_id=1, source_target_pairs={{32,0},{64,32},{96,64},{33,1},{65,33},{97,65},{34,2},{66,34},{98,6... | collective-permute-start | bytes 786440 | tf_op jit(solution)/shard_map/ppermute | solution.py:367
  38.4 4.2 %copy-start.10 = (bf16[1024,128]{1,0:T(8,128)(2,1)}, bf16[1024,128]{1,0:T(8,128)(2,1)S(1)}, u32[]{:S(2)}) copy-start(bf16[1024,128]{1,0:T(8,128)(2,1)S(1)} %collective-permute-done.lower) | copy-start | bytes 786436
  96.5 47.7 %copy-start.7 = (f32[272,256]{1,0:T(8,128)S(1)}, f32[272,256]{1,0:T(8,128)}, u32[]{:S(2)}) copy-start(f32[272,256]{1,0:T(8,128)} %get-tuple-element.24) | copy-start | bytes 835588
  141.7 11.1 %copy-start.4 = (bf16[4096,128]{1,0:T(8,128)(2,1)S(1)}, bf16[4096,128]{1,0:T(8,128)(2,1)}, u32[]{:S(2)}) copy-start(bf16[4096,128]{1,0:T(8,128)(2,1)} %get-tuple-element.23) | copy-start | bytes 3145732
  142.9 9.9 %collective-permute-start.9 = (bf16[2048,128]{1,0:T(8,128)(2,1)S(1)}, bf16[2048,128]{1,0:T(8,128)(2,1)S(1)}, u32[]{:S(2)}, u32[]{:S(2)}) collective-permute-start(bf16[2048,128]{1,0:T(8,128)(2,1)S(1)} %constant_dynamic-slice_fusion.1), channel_id=1, source_target_pairs={{0,1},{1,0},{2,3},{3,2},{4,5},{5,4},{6,7},{7,6},{8,9},{9,8},{10,11... | collective-permute-start | bytes 1572872 | tf_op jit(solution)/shard_map/ppermute | solution.py:361
  144.2 1.7 collective-permute-start.14
  145.9 5.0 %collective-permute-start.15 = (f32[136,256]{1,0:T(8,128)S(1)}, f32[136,256]{1,0:T(8,128)S(1)}, u32[]{:S(2)}, u32[]{:S(2)}) collective-permute-start(f32[136,256]{1,0:T(8,128)S(1)} %dynamic-slice_add_fusion), channel_id=1, source_target_pairs={{0,32},{32,0},{64,96},{96,64},{1,33},{33,1},{65,97},{97,65},{2,34}... | collective-permute-start | bytes 417800 | tf_op jit(solution)/shard_map/ppermute | solution.py:361
  150.9 5.2 %collective-permute-start.16 = (f32[136,256]{1,0:T(8,128)S(1)}, f32[136,256]{1,0:T(8,128)S(1)}, u32[]{:S(2)}, u32[]{:S(2)}) collective-permute-start(f32[136,256]{1,0:T(8,128)S(1)} %add.101), channel_id=1, source_target_pairs={{0,96},{32,64},{64,32},{96,0},{1,97},{33,65},{65,33},{97,1},{2,98}... | collective-permute-start | bytes 417800 | tf_op jit(solution)/shard_map/ppermute | solution.py:361
  152.9 16.7 %copy-start.13 = (bf16[1024,128]{1,0:T(8,128)(2,1)S(1)}, bf16[1024,128]{1,0:T(8,128)(2,1)}, u32[]{:S(2)}) copy-start(bf16[1024,128]{1,0:T(8,128)(2,1)} %get-tuple-element.21) | copy-start | bytes 786436
  152.9 19.3 %copy-start.12 = (bf16[1024,128]{1,0:T(8,128)(2,1)S(1)}, bf16[1024,128]{1,0:T(8,128)(2,1)}, u32[]{:S(2)}) copy-start(bf16[1024,128]{1,0:T(8,128)(2,1)} %get-tuple-element.22) | copy-start | bytes 786436
  153.0 9.6 %collective-permute-start.10 = (bf16[1024,128]{1,0:T(8,128)(2,1)S(1)}, bf16[1024,128]{1,0:T(8,128)(2,1)S(1)}, u32[]{:S(2)}, u32[]{:S(2)}) collective-permute-start(bf16[1024,128]{1,0:T(8,128)(2,1)S(1)} %dynamic-slice_convert_fusion), channel_id=1, source_target_pairs={{0,6},{2,4},{4,2},{6,0},{1,7},{3,5},{5,3},{7,1},{8,14},{10,12},{12... | collective-permute-start | bytes 786440 | tf_op jit(solution)/shard_map/ppermute | solution.py:361
  156.2 4.3 %collective-permute-start.17 = (f32[136,256]{1,0:T(8,128)S(1)}, f32[136,256]{1,0:T(8,128)S(1)}, u32[]{:S(2)}, u32[]{:S(2)}) collective-permute-start(f32[136,256]{1,0:T(8,128)S(1)} %add.102), channel_id=1, source_target_pairs={{0,2},{2,0},{4,6},{6,4},{1,3},{3,1},{5,7},{7,5},{8,10},{10,8},{12,... | collective-permute-start | bytes 417800 | tf_op jit(solution)/shard_map/ppermute | solution.py:361
  160.5 5.2 %collective-permute-start.18 = (f32[136,256]{1,0:T(8,128)S(1)}, f32[136,256]{1,0:T(8,128)S(1)}, u32[]{:S(2)}, u32[]{:S(2)}) collective-permute-start(f32[136,256]{1,0:T(8,128)S(1)} %add.103), channel_id=1, source_target_pairs={{0,6},{2,4},{4,2},{6,0},{1,7},{3,5},{5,3},{7,1},{8,14},{10,12},{12... | collective-permute-start | bytes 417800 | tf_op jit(solution)/shard_map/ppermute | solution.py:361
  162.6 4.1 %collective-permute-start.11 = (bf16[512,128]{1,0:T(8,128)(2,1)S(1)}, bf16[512,128]{1,0:T(8,128)(2,1)S(1)}, u32[]{:S(2)}, u32[]{:S(2)}) collective-permute-start(bf16[512,128]{1,0:T(8,128)(2,1)S(1)} %dynamic-slice_convert_fusion.1), channel_id=1, source_target_pairs={{0,2},{2,0},{4,6},{6,4},{1,3},{3,1},{5,7},{7,5},{8,10},{10,8},{12,... | collective-permute-start | bytes 393224 | tf_op jit(solution)/shard_map/ppermute | solution.py:361
  165.7 7.8 %collective-permute-start.19 = (f32[136,256]{1,0:T(8,128)S(1)}, f32[136,256]{1,0:T(8,128)S(1)}, u32[]{:S(2)}, u32[]{:S(2)}) collective-permute-start(f32[136,256]{1,0:T(8,128)S(1)} %add.104), channel_id=1, source_target_pairs={{0,8},{8,0},{16,24},{24,16},{1,9},{9,1},{17,25},{25,17},{2,10},{10... | collective-permute-start | bytes 417800 | tf_op jit(solution)/shard_map/ppermute | solution.py:361
  166.8 6.9 %collective-permute-start.12 = (bf16[256,128]{1,0:T(8,128)(2,1)S(1)}, bf16[256,128]{1,0:T(8,128)(2,1)S(1)}, u32[]{:S(2)}, u32[]{:S(2)}) collective-permute-start(bf16[256,128]{1,0:T(8,128)(2,1)S(1)} %dynamic-slice_convert_fusion.2), channel_id=1, source_target_pairs={{0,24},{8,16},{16,8},{24,0},{1,25},{9,17},{17,9},{25,1},{2,26},{10... | collective-permute-start | bytes 196616 | tf_op jit(solution)/shard_map/ppermute | solution.py:361
  169.6 15.7 %collective-permute-start.7 = (bf16[1024,128]{1,0:T(8,128)(2,1)S(1)}, bf16[1024,128]{1,0:T(8,128)(2,1)S(1)}, u32[]{:S(2)}, u32[]{:S(2)}) collective-permute-start(bf16[1024,128]{1,0:T(8,128)(2,1)S(1)} %copy-done.13), channel_id=1, source_target_pairs={{0,32},{32,64},{64,96},{1,33},{33,65},{65,97},{2,34},{34,66},{66,9... | collective-permute-start | bytes 786440 | tf_op jit(solution)/shard_map/ppermute | solution.py:367
  172.2 13.1 %collective-permute-start.8 = (bf16[1024,128]{1,0:T(8,128)(2,1)S(1)}, bf16[1024,128]{1,0:T(8,128)(2,1)S(1)}, u32[]{:S(2)}, u32[]{:S(2)}) collective-permute-start(bf16[1024,128]{1,0:T(8,128)(2,1)S(1)} %copy-done.12), channel_id=1, source_target_pairs={{32,0},{64,32},{96,64},{33,1},{65,33},{97,65},{34,2},{66,34},{98,6... | collective-permute-start | bytes 786440 | tf_op jit(solution)/shard_map/ppermute | solution.py:367
  173.5 5.2 %collective-permute-start.20 = (f32[136,256]{1,0:T(8,128)S(1)}, f32[136,256]{1,0:T(8,128)S(1)}, u32[]{:S(2)}, u32[]{:S(2)}) collective-permute-start(f32[136,256]{1,0:T(8,128)S(1)} %add.105), channel_id=1, source_target_pairs={{0,24},{8,16},{16,8},{24,0},{1,25},{9,17},{17,9},{25,1},{2,26},{10... | collective-permute-start | bytes 417800 | tf_op jit(solution)/shard_map/ppermute | solution.py:361
  173.7 11.0 %collective-permute-start.13 = (bf16[128,128]{1,0:T(8,128)(2,1)S(1)}, bf16[128,128]{1,0:T(8,128)(2,1)S(1)}, u32[]{:S(2)}, u32[]{:S(2)}) collective-permute-start(bf16[128,128]{1,0:T(8,128)(2,1)S(1)} %dynamic-slice_convert_fusion.3), channel_id=1, source_target_pairs={{0,8},{8,0},{16,24},{24,16},{1,9},{9,1},{17,25},{25,17},{2,10},{10... | collective-permute-start | bytes 98312 | tf_op jit(solution)/shard_map/ppermute | solution.py:361
  178.8 10.9 %collective-permute-start.21 = (f32[136,256]{1,0:T(8,128)S(1)}, f32[136,256]{1,0:T(8,128)S(1)}, u32[]{:S(2)}, u32[]{:S(2)}) collective-permute-start(f32[136,256]{1,0:T(8,128)S(1)} %add.106), channel_id=1, source_target_pairs={{0,1},{1,0},{2,3},{3,2},{4,5},{5,4},{6,7},{7,6},{8,9},{9,8},{10,11... | collective-permute-start | bytes 417800 | tf_op jit(solution)/shard_map/ppermute | solution.py:361
  (4 other events, 3.1 us)

commit v2 on v1

v2 whole, which is shorter than its diff:
```python
import functools

import jax
import jax.numpy as jnp
from jax import lax
from jax.experimental import pallas as pl
from jax.experimental.pallas import tpu as pltpu
from jax.sharding import Mesh, PartitionSpec as P

F = 128
H = 256
NODES = 4096
HALO = 1024
HUB = 128
FANOUT = 10
COLS = 32
HUBS = HUB * COLS
OWN = HALO
UPPER = HALO + NODES
HUB_AT = 2 * HALO + NODES
EXTENT = HUB_AT + HUBS
LANES = 128
CHAINS = 8
VMEM_BYTES = 60 * 2**20
AXES = ("z", "y", "x", "core")

smem = pl.BlockSpec(memory_space=pltpu.SMEM)
vmem = pl.BlockSpec(memory_space=pltpu.VMEM)
params = pltpu.CompilerParams(vmem_limit_bytes=VMEM_BYTES)


def group_of(count):
    return 16 if count <= 3 else 8


def cost(us):
    return pl.CostEstimate(flops=int(us * 1e9), bytes_accessed=0, transcendentals=0)


def hub_kernel(hub_rows, features, out, wide, rows):
    @pl.loop(0, NODES // 512)
    def _(i):
        cut = pl.ds(i * 512, 512)
        wide[cut, :] = features[cut, :].astype(jnp.float32)

    @pl.loop(0, HUB // 16)
    def _(i):
        for u in range(16):
            rows[pl.ds(i * 16 + u, 1), :] = wide[pl.ds(hub_rows[i * 16 + u], 1), :]

    out[...] = rows[...].astype(jnp.bfloat16)


def pick_hubs(hub_rows, features):
    return pl.pallas_call(
        hub_kernel,
        out_shape=jax.ShapeDtypeStruct((HUB, F), jnp.bfloat16),
        in_specs=[smem, vmem],
        out_specs=vmem,
        scratch_shapes=[pltpu.VMEM((NODES, F), jnp.float32), pltpu.VMEM((HUB, F), jnp.float32)],
        compiler_params=params,
        cost_estimate=cost(2),
        name="pick_hubs",
    )(hub_rows, features)


ROWS = NODES // LANES


def order_by(count):
    lane_r = lax.broadcasted_iota(jnp.int32, (LANES, LANES), 0)
    lane_c = lax.broadcasted_iota(jnp.int32, (LANES, LANES), 1)
    before = (lane_r < lane_c).astype(jnp.bfloat16)
    row_r = lax.broadcasted_iota(jnp.int32, (ROWS, ROWS), 0)
    row_c = lax.broadcasted_iota(jnp.int32, (ROWS, ROWS), 1)
    above = (row_c < row_r).astype(jnp.bfloat16)
    lane = lax.broadcasted_iota(jnp.int32, (1, LANES), 1)
    hits = [(count == c).astype(jnp.float32) for c in range(FANOUT + 1)]
    stacked = jnp.concatenate(hits, axis=0).astype(jnp.bfloat16)
    in_rows = jnp.dot(stacked, before, preferred_element_type=jnp.float32)
    place = jnp.zeros((ROWS, LANES), jnp.float32)
    start = jnp.zeros((1, 1), jnp.float32)
    end_row = jnp.zeros((1, LANES), jnp.float32)
    for c in range(FANOUT + 1):
        hit = hits[c]
        per_row = jnp.sum(hit, axis=1, keepdims=True)
        earlier = jnp.dot(
            above,
            jnp.broadcast_to(per_row, (ROWS, LANES)).astype(jnp.bfloat16),
            preferred_element_type=jnp.float32,
        )
        in_row = in_rows[c * ROWS : (c + 1) * ROWS]
        place = place + hit * (in_row + earlier + start)
        start = start + jnp.sum(per_row, axis=0, keepdims=True)
        end_row = end_row + jnp.where(lane == c, start, 0.0)
    place = place.astype(jnp.int32)
    high = place >> 7
    low = place & (LANES - 1)
    slot_row = lax.broadcasted_iota(jnp.int32, (ROWS, LANES), 0)
    slot_lane = lax.broadcasted_iota(jnp.int32, (LANES, LANES), 0)
    own_lane = lax.broadcasted_iota(jnp.int32, (ROWS, LANES), 1).astype(jnp.float32)
    total = jnp.zeros((ROWS, LANES), jnp.float32)
    for r in range(ROWS):
        to_row = (high[r : r + 1, :] == slot_row).astype(jnp.float32)
        to_lane = (low[r : r + 1, :] == slot_lane).astype(jnp.bfloat16)
        both = jnp.concatenate([to_row * own_lane, to_row * float(r)], axis=0)
        found = lax.dot_general(
            both.astype(jnp.bfloat16),
            to_lane,
            (((1,), (1,)), ((), ())),
            preferred_element_type=jnp.float32,
        )
        total = total + found[:ROWS] + found[ROWS:] * float(LANES)
    return total.astype(jnp.int32), end_row.astype(jnp.int32)


def spread(neighbors, flat):
    for s in range(FANOUT):
        for r in range(ROWS):
            flat[s, r : r + 1, :] = neighbors[s : s + 1, r * LANES : (r + 1) * LANES]


def split(flat, count, out, is_front, is_back, front_value, back_value):
    fronts = jnp.zeros((ROWS, LANES), jnp.int32)
    backs = jnp.zeros((ROWS, LANES), jnp.int32)
    placed = [jnp.zeros((ROWS, LANES), jnp.int32) for _ in range(FANOUT)]
    for s in range(FANOUT):
        row = flat[s]
        live = count > s
        front = jnp.logical_and(live, is_front(row))
        back = jnp.logical_and(live, is_back(row))
        at_front = jnp.where(front, fronts, -1)
        at_back = jnp.where(back, backs, -1)
        for k in range(s + 1):
            placed[k] = jnp.where(at_front == k, front_value(row), placed[k])
            last = FANOUT - 1 - k
            placed[last] = jnp.where(at_back == k, back_value(row), placed[last])
        fronts = fronts + front.astype(jnp.int32)
        backs = backs + back.astype(jnp.int32)
    for s in range(FANOUT):
        out[s][...] = placed[s]
    return fronts, backs


def is_hub(row):
    return row >= HUB_AT


def is_own(row):
    return jnp.logical_and(row >= OWN, row < UPPER)


def near_kernel(neighbors, counts, *refs):
    out, (perm, ends, hub_counts, flat) = refs[:FANOUT], refs[FANOUT:]
    spread(neighbors, flat)
    near, hub = split(
        flat, counts[...], out,
        lambda row: jnp.logical_not(is_hub(row)), is_hub,
        lambda row: row, lambda row: row - HUB_AT,
    )
    hub_counts[...] = hub
    perm[...], ends[...] = order_by(near)


def hub_order_kernel(hub_counts, perm, ends):
    perm[...], ends[...] = order_by(hub_counts[...])


def back_kernel(neighbors, counts, *refs):
    out, (perm, ends, rim_perm, rim_ends, flat) = refs[:FANOUT], refs[FANOUT:]
    spread(neighbors, flat)
    own, rim = split(
        flat, counts[...], out,
        is_own, lambda row: jnp.logical_and(jnp.logical_not(is_own(row)), row < HUB_AT),
        lambda row: row - OWN, lambda row: jnp.where(row < OWN, row, row - NODES),
    )
    perm[...], ends[...] = order_by(own)
    rim_perm[...], rim_ends[...] = order_by(rim)


tile = jax.ShapeDtypeStruct((ROWS, LANES), jnp.int32)
line = jax.ShapeDtypeStruct((1, LANES), jnp.int32)
flat_slots = pltpu.VMEM((FANOUT, ROWS, LANES), jnp.int32)


def flat_order(perm, ends):
    return ends.reshape(LANES), perm.reshape(NODES)


def near_plan(neighbors, counts):
    *slots, perm, ends, hub_counts = pl.pallas_call(
        near_kernel,
        out_shape=(tile,) * FANOUT + (tile, line, tile),
        in_specs=[vmem] * 2,
        out_specs=(vmem,) * (FANOUT + 3),
        scratch_shapes=[flat_slots],
        compiler_params=params,
        cost_estimate=cost(4),
        name="near_plan",
    )(neighbors, counts)
    return [s.reshape(NODES) for s in slots], flat_order(perm, ends), hub_counts


def hub_plan(hub_counts):
    return flat_order(*pl.pallas_call(
        hub_order_kernel,
        out_shape=(tile, line),
        in_specs=[vmem],
        out_specs=(vmem,) * 2,
        compiler_params=params,
        cost_estimate=cost(3),
        name="hub_plan",
    )(hub_counts))


def back_plan(neighbors, counts):
    *slots, perm, ends, rim_perm, rim_ends = pl.pallas_call(
        back_kernel,
        out_shape=(tile,) * FANOUT + (tile, line) * 2,
        in_specs=[vmem] * 2,
        out_specs=(vmem,) * (FANOUT + 4),
        scratch_shapes=[flat_slots],
        compiler_params=params,
        cost_estimate=cost(6),
        name="back_plan",
    )(neighbors, counts)
    return [s.reshape(NODES) for s in slots], flat_order(perm, ends), flat_order(rim_perm, rim_ends)


def over_nodes(ends, perm, visit):
    for count in range(1, FANOUT + 1):
        size = group_of(count)
        first = ends[count - 1]
        groups = (ends[count] - first) // size
        rest = first + groups * size

        @pl.loop(0, groups)
        def _(g, count=count, size=size, first=first):
            at = first + g * size
            visit([perm[at + u] for u in range(size)], count)

        @pl.loop(rest, ends[count])
        def _(at, count=count):
            visit([perm[at]], count)


def gather_rows(ends, perm, slots, table, sums):
    def gather(nodes, count):
        for n in nodes:
            total = table[pl.ds(slots[0][n], 1), :]
            for s in range(1, count):
                total = total + table[pl.ds(slots[s][n], 1), :]
            sums[pl.ds(n, 1), :] = total

    over_nodes(ends, perm, gather)


def clear(ref, at, rows):
    step = 512

    @pl.loop(0, rows // step)
    def _(i):
        ref[pl.ds(at + i * step, step), :] = jnp.zeros((step, F), jnp.float32)


def near_gather_kernel(ends, perm, *refs):
    slots, (features, lower, upper, sums, table) = refs[:FANOUT], refs[FANOUT:]

    def widen(source, at, rows):
        step = 256

        @pl.loop(0, rows // step)
        def _(i):
            table[pl.ds(at + i * step, step), :] = source[pl.ds(i * step, step), :].astype(
                jnp.float32
            )

    widen(features, OWN, NODES)
    widen(lower, 0, HALO)
    widen(upper, UPPER, HALO)
    clear(sums, 0, NODES)
    gather_rows(ends, perm, slots, table, sums)


def near_gather(order, slots, features, lower, upper):
    return pl.pallas_call(
        near_gather_kernel,
        out_shape=jax.ShapeDtypeStruct((NODES, F), jnp.float32),
        in_specs=[smem] * (2 + FANOUT) + [vmem] * 3,
        out_specs=vmem,
        scratch_shapes=[pltpu.VMEM((HUB_AT, F), jnp.float32)],
        compiler_params=params,
        cost_estimate=cost(20),
        name="near_gather",
    )(*order, *slots, features, lower, upper)


def forward_kernel(ends, perm, *refs):
    slots = refs[:FANOUT][::-1]
    (
        h0, h1, h2, h3, h4, h5, near, features, counts, w_self, w_neigh, bias, cotangent,
        act, src, base, grads, table, sums,
    ) = refs[FANOUT:]
    y, x, core = lax.axis_index("y"), lax.axis_index("x"), lax.axis_index("core")
    position = 0
    for piece in (h0, h1, h2, h3, h4, h5):
        for i in range(piece.shape[0] // HUB):
            b = [(position >> k) & 1 for k in range(5)]
            owner_y = y ^ (b[0] * 1) ^ (b[1] * 3)
            owner_x = x ^ (b[2] * 1) ^ (b[3] * 3)
            owner = owner_y * 8 + owner_x * 2 + (core ^ b[4])
            table[pl.ds(owner * HUB, HUB), :] = piece[i * HUB : (i + 1) * HUB, :].astype(
                jnp.float32
            )
            position += 1

    clear(sums, 0, NODES)
    gather_rows(ends, perm, slots, table, sums)

    grads[...] = jnp.zeros_like(grads)
    contract_rows = (((0,), (0,)), ((), ()))
    contract_cols = (((1,), (1,)), ((), ()))
    block = 256

    @pl.loop(0, NODES // block)
    def _(i):
        cut = pl.ds(i * block, block)
        parts = []
        for k in range(block // LANES):
            row = counts[pl.ds(i * (block // LANES) + k, 1), :].astype(jnp.float32)
            parts.append(jnp.broadcast_to(row, (LANES, LANES)).T)
        divisor = jnp.concatenate(parts, axis=0)
        own = features[cut, :]
        agg = ((near[cut, :] + sums[cut, :]) / divisor).astype(jnp.bfloat16)
        z = (
            jnp.dot(own, w_self[...], preferred_element_type=jnp.float32)
            + jnp.dot(agg, w_neigh[...], preferred_element_type=jnp.float32)
            + bias[...]
        )
        scale = 0.7978845608028654
        squared = z * z
        t = jnp.tanh(scale * (z + 0.044715 * (squared * z)))
        half = 0.5 * (1.0 + t)
        act[cut, :] = (z * half).astype(jnp.bfloat16)
        slope = half + 0.5 * z * (1.0 - t * t) * (scale * (1.0 + 3 * 0.044715 * squared))
        dz_wide = cotangent[cut, :].astype(jnp.float32) * slope
        dz = dz_wide.astype(jnp.bfloat16)
        grads[0:F, :] += lax.dot_general(
            own, dz, contract_rows, preferred_element_type=jnp.float32
        )
        grads[F : 2 * F, :] += lax.dot_general(
            agg, dz, contract_rows, preferred_element_type=jnp.float32
        )
        partial = jnp.sum(
            dz.astype(jnp.float32).reshape(block // 8, 8, H), axis=0
        )
        grads[2 * F : 2 * F + 8, :] += partial
        src[cut, :] = (
            lax.dot_general(dz, w_neigh[...], contract_cols, preferred_element_type=jnp.float32)
            / divisor
        )
        base[cut, :] = lax.dot_general(
            dz, w_self[...], contract_cols, preferred_element_type=jnp.float32
        )


def forward(order, slots, hubs, near, features, counts, w_self, w_neigh, bias, cot):
    return pl.pallas_call(
        forward_kernel,
        out_shape=(
            jax.ShapeDtypeStruct((NODES, H), jnp.bfloat16),
            jax.ShapeDtypeStruct((NODES, F), jnp.float32),
            jax.ShapeDtypeStruct((NODES, F), jnp.float32),
            jax.ShapeDtypeStruct((2 * F + 16, H), jnp.float32),
        ),
        in_specs=[smem] * (2 + FANOUT) + [vmem] * (len(hubs) + 7),
        out_specs=(vmem,) * 4,
        scratch_shapes=[
            pltpu.VMEM((HUBS, F), jnp.float32),
            pltpu.VMEM((NODES, F), jnp.float32),
        ],
        compiler_params=params,
        cost_estimate=cost(16),
        name="forward",
    )(*order, *slots, *hubs, near, features, counts, w_self, w_neigh, bias, cot)


def scatter_rows(ends, perm, slots, src, chains):
    def scatter(nodes, count):
        turn = 0
        for n in nodes:
            row = src[pl.ds(n, 1), :]
            for s in range(count):
                chain = chains[turn % CHAINS]
                turn += 1
                at = pl.ds(slots[s][n], 1)
                chain[at, :] = chain[at, :] + row

    over_nodes(ends, perm, scatter)


def chain_sum(chains, cut):
    out = chains[0][cut, :]
    for chain in chains[1:]:
        out = out + chain[cut, :]
    return out


def hub_scatter_kernel(ends, perm, *refs):
    slots, (src, hub), chains = refs[:FANOUT][::-1], refs[FANOUT : FANOUT + 2], refs[FANOUT + 2 :]
    for chain in chains:
        clear(chain, 0, HUBS)
    scatter_rows(ends, perm, slots, src, chains)

    @pl.loop(0, COLS)
    def _(owner):
        y, x, core = owner >> 3, (owner >> 1) & 3, owner & 1
        at = (core * 16 + x * 4 + y) * HUB
        hub[pl.ds(at, HUB), :] = chain_sum(chains, pl.ds(owner * HUB, HUB)).astype(jnp.bfloat16)


def rim_scatter_kernel(ends, perm, *refs):
    slots, (src, rim), chains = refs[:FANOUT][::-1], refs[FANOUT : FANOUT + 2], refs[FANOUT + 2 :]
    for chain in chains:
        clear(chain, 0, 2 * HALO)
    scatter_rows(ends, perm, slots, src, chains)

    @pl.loop(0, 2 * HALO // HUB)
    def _(i):
        cut = pl.ds(i * HUB, HUB)
        rim[cut, :] = chain_sum(chains, cut).astype(jnp.bfloat16)


def own_scatter_kernel(ends, perm, *refs):
    slots, (src, base, own), chains = refs[:FANOUT], refs[FANOUT : FANOUT + 3], refs[FANOUT + 3 :]
    for chain in chains[1:]:
        clear(chain, 0, NODES)
    step = 512

    @pl.loop(0, NODES // step)
    def _(i):
        cut = pl.ds(i * step, step)
        chains[0][cut, :] = base[cut, :]

    scatter_rows(ends, perm, slots, src, chains)

    @pl.loop(0, NODES // HUB)
    def _(i):
        cut = pl.ds(i * HUB, HUB)
        own[cut, :] = chain_sum(chains, cut)


def scatter(kernel, rows, kind, us, order, slots, *inputs):
    return pl.pallas_call(
        kernel,
        out_shape=jax.ShapeDtypeStruct((rows, F), kind),
        in_specs=[smem] * (2 + FANOUT) + [vmem] * len(inputs),
        out_specs=vmem,
        scratch_shapes=[pltpu.VMEM((rows, F), jnp.float32)] * CHAINS,
        compiler_params=params,
        cost_estimate=cost(us),
        name=kernel.__name__,
    )(*order, *slots, *inputs)


def finish_kernel(hub_rows, own, from_above, from_below, share, out, total):
    step = 256

    @pl.loop(0, NODES // step)
    def _(i):
        cut = pl.ds(i * step, step)
        total[cut, :] = own[cut, :]

    @pl.loop(0, HALO // step)
    def _(i):
        cut = pl.ds(i * step, step)
        total[cut, :] = total[cut, :] + from_above[cut, :].astype(jnp.float32)

    @pl.loop(0, HALO // step)
    def _(i):
        cut = pl.ds(NODES - HALO + i * step, step)
        total[cut, :] = total[cut, :] + from_below[pl.ds(i * step, step), :].astype(jnp.float32)

    @pl.loop(0, HUB // 8)
    def _(i):
        for u in range(8):
            at = pl.ds(hub_rows[i * 8 + u], 1)
            total[at, :] = total[at, :] + share[pl.ds(i * 8 + u, 1), :]

    @pl.loop(0, NODES // step)
    def _(i):
        cut = pl.ds(i * step, step)
        out[cut, :] = total[cut, :].astype(jnp.bfloat16)


def finish(hub_rows, own, from_above, from_below, share):
    return pl.pallas_call(
        finish_kernel,
        out_shape=jax.ShapeDtypeStruct((NODES, F), jnp.bfloat16),
        in_specs=[smem] + [vmem] * 4,
        out_specs=vmem,
        scratch_shapes=[pltpu.VMEM((NODES, F), jnp.float32)],
        compiler_params=params,
        cost_estimate=cost(3),
        name="finish",
    )(hub_rows, own, from_above, from_below, share)


def swap(value, axis, flip):
    count = lax.axis_size(axis)
    return lax.ppermute(value, axis, [(i, i ^ flip) for i in range(count)])


def shifted(value, axis, by):
    count = lax.axis_size(axis)
    pairs = [(i, i + by) for i in range(count) if 0 <= i + by < count]
    return lax.ppermute(value, axis, pairs)


def halves(value, bit):
    rows = value.shape[0] // 2
    keep = lax.dynamic_slice_in_dim(value, bit * rows, rows, axis=0)
    give = lax.dynamic_slice_in_dim(value, (1 - bit) * rows, rows, axis=0)
    return keep, give


def halve(value, axis, flip, bit):
    keep, give = halves(value, bit)
    got = swap(give.astype(jnp.bfloat16), axis, flip)
    return keep.astype(jnp.float32) + got.astype(jnp.float32)


def tie(*values):
    return lax.optimization_barrier(values)


def on_device(features, neighbors, counts, hub_rows, w_self, w_neigh, out_bias, cotangent):
    x, y, core = lax.axis_index("x"), lax.axis_index("y"), lax.axis_index("core")
    slots = neighbors.T
    counts = counts.reshape(ROWS, LANES)

    h0 = pick_hubs(hub_rows, features)
    h1 = swap(h0, "y", 1)
    near_slots, near_order, hub_counts = near_plan(slots, counts)
    lower = shifted(features[NODES - HALO :], "z", 1)
    upper = shifted(features[:HALO], "z", -1)
    h1, hub_counts = tie(h1, hub_counts)
    held = jnp.concatenate([h0, h1], axis=0)
    h2 = swap(held, "y", 3)
    hub_order = hub_plan(hub_counts)
    h2, slots, *hub_order = tie(h2, slots, *hub_order)
    held = jnp.concatenate([held, h2], axis=0)
    h3 = swap(held, "x", 1)
    back_slots, own_order, rim_order = back_plan(slots, counts)
    h3, lower, upper, own_order, rim_order = tie(h3, lower, upper, own_order, rim_order)
    held = jnp.concatenate([held, h3], axis=0)
    h4 = swap(held, "x", 3)
    near = near_gather(near_order, near_slots, features, lower, upper)
    h4, near = tie(h4, near)
    held = jnp.concatenate([held, h4], axis=0)
    h5 = swap(held, "core", 1)

    act, src, base, grads = forward(
        hub_order, near_slots, (h0, h1, h2, h3, h4, h5), near, features, counts,
        w_self, w_neigh, out_bias.reshape(1, H), cotangent,
    )

    keep, give = halves(grads, core)
    grads = keep + swap(give, "core", 1)
    src, grads = tie(src, grads)
    other = swap(grads, "z", 1)
    hub = scatter(hub_scatter_kernel, HUBS, jnp.bfloat16, 8, hub_order, near_slots, src)
    hub, src, other = tie(hub, src, other)
    grads = grads + other
    other = swap(grads, "z", 3)
    hub = halve(hub, "core", 1, core)
    rim = scatter(rim_scatter_kernel, 2 * HALO, jnp.bfloat16, 8, rim_order, back_slots, src)
    hub, src, other, rim = tie(hub, src, other, rim)
    grads = grads + other
    other = swap(grads, "x", 3)
    hub = halve(hub, "x", 3, x // 2)
    from_below = shifted(rim[:HALO], "z", -1)
    from_above = shifted(rim[HALO:], "z", 1)
    own = scatter(own_scatter_kernel, NODES, jnp.float32, 20, own_order, back_slots, src, base)
    hub, other, own, from_above, from_below = tie(hub, other, own, from_above, from_below)
    grads = grads + other
    grads = grads + swap(grads, "x", 1)
    hub = halve(hub, "x", 1, x % 2)
    grads = grads + swap(grads, "y", 3)
    hub = halve(hub, "y", 3, y // 2)
    grads = grads + swap(grads, "y", 1)
    share = halve(hub, "y", 1, y % 2)
    other = swap(grads, "core", 1)
    grads = jnp.concatenate(
        [jnp.where(core == 0, grads, other), jnp.where(core == 0, other, grads)], axis=0
    )
    grad_features = finish(hub_rows, own, from_above, from_below, share)
    grad_bias = jnp.sum(grads[2 * F :], axis=0)
    return act, grad_features, grads[:F], grads[F : 2 * F], grad_bias


def solution(mesh):
    mesh = Mesh(mesh.devices.reshape(4, 4, 4, 2), AXES)
    rows = P(AXES, None)
    placed = (rows, rows, P(AXES), P(AXES), P(), P(), P(), rows)
    return jax.shard_map(
        on_device,
        mesh=mesh,
        in_specs=placed,
        out_specs=(rows, rows, P(), P(), P()),
        check_vma=False,
    )
```

time: 191 us -> 167 us (0.87)
  waiting for transfers between devices: 33 us -> 13.2 us
  starting transfers between devices: 42.2 us -> 37.8 us
  Pallas kernels: 106 us -> 108 us
    pallas_call x2 -> x7, Pallas kernels: 47.7 us -> 79.7 us  [the longest x3 46.4 us: scatter(): pl.pallas_call(kernel, out_shape=jax.ShapeDtypeStruct((rows, F), kind), i...]
    pallas_call x1, Pallas kernels: 53 us -> 22.9 us  [forward(): pl.pallas_call(forward_kernel, out_shape=(jax.ShapeDtypeStruct((NODES, H)...]
    ppermute x18, waiting for transfers between devices: 26.9 us -> 13.2 us  [swap(): return lax.ppermute(value, axis, [(i, i ^ flip) for i in range(count)])]
    ppermute x4, waiting for transfers between devices: 6.11 us -> 0.01 us  [shifted(): return lax.ppermute(value, axis, pairs)]
    ppermute x18, starting transfers between devices: 33.4 us -> 29.1 us  [swap(): return lax.ppermute(value, axis, [(i, i ^ flip) for i in range(count)])]
    concatenate x4, other arithmetic: 3.05 us -> 0.77 us  [the longest x1 0.73 us: on_device(): jnp.concatenate([jnp.where(core == 0, grads, other), jnp.where(core == 0,...]
  transfers between devices with their start and end apart: 22 -> 22, of which waited for: 12 -> 6; matrix products, arithmetic and copies ran while one was open for 1% -> 1% of each run, Pallas kernels for 3% -> 50%
where the time goes in v2:
time: 167 us
  Pallas kernels  108 us (65%)
  starting transfers between devices  37.8 us (23%)
  waiting for transfers between devices  13.2 us (8%)
  other arithmetic  3.28 us (2%)
  local copies, waits for them, and re-layouts  3.09 us (2%)
    pallas_call x3, Pallas kernels, scatter(): pl.pallas_call(kernel, out_shape=jax.ShapeDtypeStruct((rows, F), kind), i...  46.4 us
    ppermute x18, starting transfers between devices, swap(): return lax.ppermute(value, axis, [(i, i ^ flip) for i in range(count)])  29.1 us
    pallas_call x1, Pallas kernels, near_gather(): pl.pallas_call(near_gather_kernel, out_shape=jax.ShapeDtypeStruct((NODES,...  23.3 us
    pallas_call x1, Pallas kernels, forward(): pl.pallas_call(forward_kernel, out_shape=(jax.ShapeDtypeStruct((NODES, H)...  22.9 us
    ppermute x18, waiting for transfers between devices, swap(): return lax.ppermute(value, axis, [(i, i ^ flip) for i in range(count)])  13.2 us
    ppermute x4, starting transfers between devices, shifted(): return lax.ppermute(value, axis, pairs)  8.69 us
    pallas_call x1, Pallas kernels, back_plan(): pl.pallas_call(back_kernel, out_shape=(tile,) * FANOUT + (tile, line) * 2...  4.61 us
    pallas_call x1, Pallas kernels, finish(): pl.pallas_call(finish_kernel, out_shape=jax.ShapeDtypeStruct((NODES, F),...  3.49 us
  transfers between devices with their start and end apart: 22, of which 6 were waited for; matrix products, arithmetic and copies ran while one was open for 1% of the time, Pallas kernels for 50%

profile of v2, /device:TPU:1, one launch (start us, length us, event | category | flops | bytes accessed | tf_op | source)
XLA Modules:
  0.0 166.7 jit_solution(9720881840174153902)
XLA Ops:
  0.6 2.2 %pick_hubs.1.refs_10_ = bf16[128,128]{1,0:T(8,128)(2,1)} custom-call(s32[128]{0:T(128)} %hub_rows.3, bf16[4096,128]{1,0:T(8,128)(2,1)} %refs_17_.1), custom_call_target="tpu_custom_call" | custom-call | flops 2000000000 | tf_op jit(solution)/shard_map/pick_hubs/pallas_call | solution.py:55
  2.9 2.1 %collective-permute-start = (bf16[128,128]{1,0:T(8,128)(2,1)}, bf16[128,128]{1,0:T(8,128)(2,1)S(1)}, u32[]{:S(2)}, u32[]{:S(2)}) collective-permute-start(bf16[128,128]{1,0:T(8,128)(2,1)} %pick_hubs.1.refs_10_), channel_id=1, source_target_pairs={{0,8},{8,0},{16,24},{24,16},{1,9},{9,1},{17,25},{25,17},{2,10},{10... | collective-permute-start | bytes 98312 | tf_op jit(solution)/shard_map/ppermute | solution.py:511
  5.0 3.6 %collective-permute-start.3 = (bf16[1024,128]{1,0:T(8,128)(2,1)S(1)}, bf16[1024,128]{1,0:T(8,128)(2,1)S(1)}, u32[]{:S(2)}, u32[]{:S(2)}) collective-permute-start(bf16[1024,128]{1,0:T(8,128)(2,1)S(1)} %get-tuple-element.130), channel_id=1, source_target_pairs={{0,32},{32,64},{64,96},{1,33},{33,65},{65,97},{2,34},{34,66},{66,9... | collective-permute-start | bytes 786440 | tf_op jit(solution)/shard_map/ppermute | solution.py:517
  8.6 1.3 collective-permute-start.4
  9.9 3.0 %near_plan.1 = (s32[32,128]{1,0:T(8,128)}, s32[32,128]{1,0:T(8,128)}, s32[32,128]{1,0:T(8,128)}, s32[32,128]{1,0:T(8,128)}, s32[32,128]{1,0:T(8,128)}, /*index=5...) custom-call(s32[10,4096]{1,0:T(8,128)} %bitcast.31, ...), custom_call_target="tpu_custom_call" | custom-call | flops 4000000000 | tf_op jit(solution)/shard_map/near_plan/pallas_call | solution.py:191
  12.9 2.0 %collective-permute-start.1 = (bf16[256,128]{1,0:T(8,128)(2,1)S(1)}, bf16[256,128]{1,0:T(8,128)(2,1)S(1)}, u32[]{:S(2)}, u32[]{:S(2)}) collective-permute-start(bf16[256,128]{1,0:T(8,128)(2,1)S(1)} %pad_maximum_fusion.3), channel_id=1, source_target_pairs={{0,24},{8,16},{16,8},{24,0},{1,25},{9,17},{17,9},{25,1},{2,26},{10... | collective-permute-start | bytes 196616 | tf_op jit(solution)/shard_map/ppermute | solution.py:511
  14.9 2.4 %hub_plan.1 = (s32[32,128]{1,0:T(8,128)}, s32[1,128]{1,0:T(1,128)}) custom-call(s32[32,128]{1,0:T(8,128)} %get-tuple-element.69.hub_counts), custom_call_target="tpu_custom_call" | custom-call | flops 3000000000 | tf_op jit(solution)/shard_map/hub_plan/pallas_call | solution.py:205
  17.4 1.3 collective-permute-start.2
  18.7 4.6 %back_plan.1 = (s32[32,128]{1,0:T(8,128)}, s32[32,128]{1,0:T(8,128)}, s32[32,128]{1,0:T(8,128)}, s32[32,128]{1,0:T(8,128)}, s32[32,128]{1,0:T(8,128)}, /*index=5...) custom-call(s32[10,4096]{1,0:T(8,128)} %bitcast.32, ...), custom_call_target="tpu_custom_call" | custom-call | flops 6000000000 | tf_op jit(solution)/shard_map/back_plan/pallas_call | solution.py:217
  23.4 1.9 %collective-permute-start.5 = (bf16[1024,128]{1,0:T(8,128)(2,1)S(1)}, bf16[1024,128]{1,0:T(8,128)(2,1)S(1)}, u32[]{:S(2)}, u32[]{:S(2)}) collective-permute-start(bf16[1024,128]{1,0:T(8,128)(2,1)S(1)} %pad_maximum_fusion), channel_id=1, source_target_pairs={{0,6},{2,4},{4,2},{6,0},{1,7},{3,5},{5,3},{7,1},{8,14},{10,12},{12... | collective-permute-start | bytes 786440 | tf_op jit(solution)/shard_map/ppermute | solution.py:511
  25.3 23.3 %near_gather.1.refs_16_ = f32[4096,128]{1,0:T(8,128)} custom-call(s32[128]{0:T(128)} %bitcast.96, s32[4096]{0:T(1024)} %bitcast.91, s32[4096]{0:T(1024)} %bitcast.58, s32[4096]{0:T(1024)} %bitcast.61, s32[4096]{0:T(1024)} %bitcast.64, s32[4096]{0:T(1024)} %bitcast.67, s32[4096]{0:T(1024)} %bitcast.70, s32[4096]{0:T(1024)} %bitcast.73, s32[4096]{0:T(1024)} %bitcast.76, ...), custom_call_target="tpu_custom_call" | custom-call | flops 20000000000 | tf_op jit(solution)/shard_map/near_gather/pallas_call | solution.py:286
  48.7 3.2 %collective-permute-start.6 = (bf16[2048,128]{1,0:T(8,128)(2,1)S(1)}, bf16[2048,128]{1,0:T(8,128)(2,1)S(1)}, u32[]{:S(2)}, u32[]{:S(2)}) collective-permute-start(bf16[2048,128]{1,0:T(8,128)(2,1)S(1)} %constant_dynamic-update-slice_fusion), channel_id=1, source_target_pairs={{0,1},{1,0},{2,3},{3,2},{4,5},{5,4},{6,7},{7,6},{8,9},{9,8},{10,11... | collective-permute-start | bytes 1572872 | tf_op jit(solution)/shard_map/ppermute | solution.py:511
  51.9 1.5 collective-permute-done.6.refs_15_
  54.3 22.9 %forward.1 = (bf16[4096,256]{1,0:T(8,128)(2,1)}, f32[4096,128]{1,0:T(8,128)}, f32[4096,128]{1,0:T(8,128)}, f32[272,256]{1,0:T(8,128)}) custom-call(s32[128]{0:T(128)} %bitcast.94, s32[4096]{0:T(1024)} %bitcast.89, s32[4096]{0:T(1024)} %bitcast.59, s32[4096]{0:T(1024)} %bitcast.62, s32[4096]{0:T(1024)} %bitcast.65, s32[4096]{0:T(1024)} %bitcast.68, ...), custom_call_target="tpu_custom_call" | custom-call | flops 16000000000 | tf_op jit(solution)/shard_map/forward/pallas_call | solution.py:368
  78.6 1.0 collective-permute-done.7
  80.5 1.9 %collective-permute-start.8 = (f32[136,256]{1,0:T(8,128)S(1)}, f32[136,256]{1,0:T(8,128)S(1)}, u32[]{:S(2)}, u32[]{:S(2)}) collective-permute-start(f32[136,256]{1,0:T(8,128)S(1)} %dynamic-slice_add_fusion), channel_id=1, source_target_pairs={{0,32},{32,0},{64,96},{96,64},{1,33},{33,1},{65,97},{97,65},{2,34}... | collective-permute-start | bytes 417800 | tf_op jit(solution)/shard_map/ppermute | solution.py:511
  82.3 12.4 %hub_scatter_kernel.1 = bf16[4096,128]{1,0:T(8,128)(2,1)} custom-call(s32[128]{0:T(128)} %bitcast.95, s32[4096]{0:T(1024)} %bitcast.90, s32[4096]{0:T(1024)} %bitcast.60, s32[4096]{0:T(1024)} %bitcast.63, s32[4096]{0:T(1024)} %bitcast.66, s32[4096]{0:T(1024)} %bitcast.69, s32[4096]{0:T(1024)} %bitcast.72, s32[4096]{0:T(1024)} %bitcast.75, s32[4096]{0:T(1024)} %bitcast.78, ...), custom_call_target="tpu_custom_call" | custom-call | flops 8000000000 | tf_op jit(solution)/shard_map/hub_scatter_kernel/pallas_call | solution.py:454
  94.7 1.1 constant_dynamic-slice_fusion
  96.6 2.4 %collective-permute-start.10 = (f32[136,256]{1,0:T(8,128)S(1)}, f32[136,256]{1,0:T(8,128)S(1)}, u32[]{:S(2)}, u32[]{:S(2)}) collective-permute-start(f32[136,256]{1,0:T(8,128)S(1)} %add.87), channel_id=1, source_target_pairs={{0,96},{32,64},{64,32},{96,0},{1,97},{33,65},{65,33},{97,1},{2,98}... | collective-permute-start | bytes 417800 | tf_op jit(solution)/shard_map/ppermute | solution.py:511
  99.0 11.2 %rim_scatter_kernel.1 = bf16[2048,128]{1,0:T(8,128)(2,1)} custom-call(s32[128]{0:T(128)} %bitcast.93, s32[4096]{0:T(1024)} %bitcast.88, s32[4096]{0:T(1024)} %bitcast.37, s32[4096]{0:T(1024)} %bitcast.39, s32[4096]{0:T(1024)} %bitcast.41, s32[4096]{0:T(1024)} %bitcast.43, s32[4096]{0:T(1024)} %bitcast.45, s32[4096]{0:T(1024)} %bitcast.47, s32[4096]{0:T(1024)} %bitcast.49, ...), custom_call_target="tpu_custom_call" | custom-call | flops 8000000000 | tf_op jit(solution)/shard_map/rim_scatter_kernel/pallas_call | solution.py:454
  111.3 2.0 %collective-permute-start.12 = (f32[136,256]{1,0:T(8,128)S(1)}, f32[136,256]{1,0:T(8,128)S(1)}, u32[]{:S(2)}, u32[]{:S(2)}) collective-permute-start(f32[136,256]{1,0:T(8,128)S(1)} %add.91), channel_id=1, source_target_pairs={{0,6},{2,4},{4,2},{6,0},{1,7},{3,5},{5,3},{7,1},{8,14},{10,12},{12... | collective-permute-start | bytes 417800 | tf_op jit(solution)/shard_map/ppermute | solution.py:511
  113.3 2.4 %collective-permute-start.13 = (bf16[1024,128]{1,0:T(8,128)(2,1)S(1)}, bf16[1024,128]{1,0:T(8,128)(2,1)S(1)}, u32[]{:S(2)}, u32[]{:S(2)}) collective-permute-start(bf16[1024,128]{1,0:T(8,128)(2,1)S(1)} %get-tuple-element.132), channel_id=1, source_target_pairs={{0,32},{32,64},{64,96},{1,33},{33,65},{65,97},{2,34},{34,66},{66,9... | collective-permute-start | bytes 786440 | tf_op jit(solution)/shard_map/ppermute | solution.py:517
  115.7 1.5 collective-permute-start.14
  117.2 22.8 %own_scatter_kernel.1.own = f32[4096,128]{1,0:T(8,128)} custom-call(s32[128]{0:T(128)} %bitcast.92, s32[4096]{0:T(1024)} %bitcast.57, s32[4096]{0:T(1024)} %bitcast.38, s32[4096]{0:T(1024)} %bitcast.40, s32[4096]{0:T(1024)} %bitcast.42, s32[4096]{0:T(1024)} %bitcast.44, s32[4096]{0:T(1024)} %bitcast.46, s32[4096]{0:T(1024)} %bitcast.48, s32[4096]{0:T(1024)} %bitcast.50, ...), custom_call_target="tpu_custom_call" | custom-call | flops 20000000000 | tf_op jit(solution)/shard_map/own_scatter_kernel/pallas_call | solution.py:454
  140.3 1.5 collective-permute-start.18
  141.8 2.6 %collective-permute-done.15 = bf16[512,128]{1,0:T(8,128)(2,1)S(1)} collective-permute-done((bf16[512,128]{1,0:T(8,128)(2,1)S(1)}, bf16[512,128]{1,0:T(8,128)(2,1)S(1)}, u32[]{:S(2)}, u32[]{:S(2)}) %collective-permute-start.15) | collective-permute-done | bytes 131104 | tf_op jit(solution)/shard_map/ppermute | solution.py:511
  144.4 2.1 %collective-permute-start.16 = (bf16[256,128]{1,0:T(8,128)(2,1)S(1)}, bf16[256,128]{1,0:T(8,128)(2,1)S(1)}, u32[]{:S(2)}, u32[]{:S(2)}) collective-permute-start(bf16[256,128]{1,0:T(8,128)(2,1)S(1)} %dynamic-slice_convert_fusion.2), channel_id=1, source_target_pairs={{0,24},{8,16},{16,8},{24,0},{1,25},{9,17},{17,9},{25,1},{2,26},{10... | collective-permute-start | bytes 196616 | tf_op jit(solution)/shard_map/ppermute | solution.py:511
  147.3 2.3 %collective-permute-start.19 = (f32[136,256]{1,0:T(8,128)S(1)}, f32[136,256]{1,0:T(8,128)S(1)}, u32[]{:S(2)}, u32[]{:S(2)}) collective-permute-start(f32[136,256]{1,0:T(8,128)S(1)} %add.104), channel_id=1, source_target_pairs={{0,24},{8,16},{16,8},{24,0},{1,25},{9,17},{17,9},{25,1},{2,26},{10... | collective-permute-start | bytes 417800 | tf_op jit(solution)/shard_map/ppermute | solution.py:511
  149.8 3.6 %collective-permute-done.19 = f32[136,256]{1,0:T(8,128)S(1)} collective-permute-done((f32[136,256]{1,0:T(8,128)S(1)}, f32[136,256]{1,0:T(8,128)S(1)}, u32[]{:S(2)}, u32[]{:S(2)}) %collective-permute-start.19) | collective-permute-done | bytes 139296 | tf_op jit(solution)/shard_map/ppermute | solution.py:511
  154.1 3.6 %collective-permute-done.20 = f32[136,256]{1,0:T(8,128)S(1)} collective-permute-done((f32[136,256]{1,0:T(8,128)S(1)}, f32[136,256]{1,0:T(8,128)S(1)}, u32[]{:S(2)}, u32[]{:S(2)}) %collective-permute-start.20) | collective-permute-done | bytes 139296 | tf_op jit(solution)/shard_map/ppermute | solution.py:511
  157.7 4.2 %collective-permute-start.21 = (f32[136,256]{1,0:T(8,128)S(1)}, f32[136,256]{1,0:T(8,128)S(1)}, u32[]{:S(2)}, u32[]{:S(2)}) collective-permute-start(f32[136,256]{1,0:T(8,128)S(1)} %add.106), channel_id=1, source_target_pairs={{0,1},{1,0},{2,3},{3,2},{4,5},{5,4},{6,7},{7,6},{8,9},{9,8},{10,11... | collective-permute-start | bytes 417800 | tf_op jit(solution)/shard_map/ppermute | solution.py:511
  161.9 3.5 %finish.1 = bf16[4096,128]{1,0:T(8,128)(2,1)} custom-call(s32[128]{0:T(128)} %hub_rows.3, f32[4096,128]{1,0:T(8,128)} %own_scatter_kernel.1.own, bf16[1024,128]{1,0:T(8,128)(2,1)} %copy-done.9, bf16[1024,128]{1,0:T(8,128)(2,1)} %copy-done.10, f32[128,128]{1,0:T(8,128)} %convert_add_fusion.4.share), custom_call_target="tpu_custom_call" | custom-call | flops 3000000000 | tf_op jit(solution)/shard_map/finish/pallas_call | solution.py:497
  (79 shorter events, 8.6 us)
Async XLA Ops:
  0.6 4.4 %copy-start.6 = (bf16[4096,128]{1,0:T(8,128)(2,1)S(1)}, bf16[4096,128]{1,0:T(8,128)(2,1)}, u32[]{:S(2)}) copy-start(bf16[4096,128]{1,0:T(8,128)(2,1)} %refs_17_.1) | copy-start | bytes 3145732
  2.9 10.0 %collective-permute-start = (bf16[128,128]{1,0:T(8,128)(2,1)}, bf16[128,128]{1,0:T(8,128)(2,1)S(1)}, u32[]{:S(2)}, u32[]{:S(2)}) collective-permute-start(bf16[128,128]{1,0:T(8,128)(2,1)} %pick_hubs.1.refs_10_), channel_id=1, source_target_pairs={{0,8},{8,0},{16,24},{24,16},{1,9},{9,1},{17,25},{25,17},{2,10},{10... | collective-permute-start | bytes 98312 | tf_op jit(solution)/shard_map/ppermute | solution.py:511
  5.0 18.3 %collective-permute-start.3 = (bf16[1024,128]{1,0:T(8,128)(2,1)S(1)}, bf16[1024,128]{1,0:T(8,128)(2,1)S(1)}, u32[]{:S(2)}, u32[]{:S(2)}) collective-permute-start(bf16[1024,128]{1,0:T(8,128)(2,1)S(1)} %get-tuple-element.130), channel_id=1, source_target_pairs={{0,32},{32,64},{64,96},{1,33},{33,65},{65,97},{2,34},{34,66},{66,9... | collective-permute-start | bytes 786440 | tf_op jit(solution)/shard_map/ppermute | solution.py:517
  8.6 14.7 %collective-permute-start.4 = (bf16[1024,128]{1,0:T(8,128)(2,1)S(1)}, bf16[1024,128]{1,0:T(8,128)(2,1)S(1)}, u32[]{:S(2)}, u32[]{:S(2)}) collective-permute-start(bf16[1024,128]{1,0:T(8,128)(2,1)S(1)} %get-tuple-element.129), channel_id=1, source_target_pairs={{32,0},{64,32},{96,64},{33,1},{65,33},{97,65},{34,2},{66,34},{98,6... | collective-permute-start | bytes 786440 | tf_op jit(solution)/shard_map/ppermute | solution.py:517
  9.9 3.0 %copy-start.4 = (bf16[128,128]{1,0:T(8,128)(2,1)S(1)}, bf16[128,128]{1,0:T(8,128)(2,1)}, u32[]{:S(2)}) copy-start(bf16[128,128]{1,0:T(8,128)(2,1)} %pick_hubs.1.refs_10_) | copy-start | bytes 98308
  12.9 10.5 %copy-start.5 = (bf16[128,128]{1,0:T(8,128)(2,1)}, bf16[128,128]{1,0:T(8,128)(2,1)S(1)}, u32[]{:S(2)}) copy-start(bf16[128,128]{1,0:T(8,128)(2,1)S(1)} %collective-permute-done.refs_11_) | copy-start | bytes 98308
  12.9 4.4 %collective-permute-start.1 = (bf16[256,128]{1,0:T(8,128)(2,1)S(1)}, bf16[256,128]{1,0:T(8,128)(2,1)S(1)}, u32[]{:S(2)}, u32[]{:S(2)}) collective-permute-start(bf16[256,128]{1,0:T(8,128)(2,1)S(1)} %pad_maximum_fusion.3), channel_id=1, source_target_pairs={{0,24},{8,16},{16,8},{24,0},{1,25},{9,17},{17,9},{25,1},{2,26},{10... | collective-permute-start | bytes 196616 | tf_op jit(solution)/shard_map/ppermute | solution.py:511
  17.4 6.0 %copy-start.1 = (bf16[256,128]{1,0:T(8,128)(2,1)}, bf16[256,128]{1,0:T(8,128)(2,1)S(1)}, u32[]{:S(2)}) copy-start(bf16[256,128]{1,0:T(8,128)(2,1)S(1)} %collective-permute-done.1.refs_12_) | copy-start | bytes 196612
  17.4 5.9 %collective-permute-start.2 = (bf16[512,128]{1,0:T(8,128)(2,1)S(1)}, bf16[512,128]{1,0:T(8,128)(2,1)S(1)}, u32[]{:S(2)}, u32[]{:S(2)}) collective-permute-start(bf16[512,128]{1,0:T(8,128)(2,1)S(1)} %pad_maximum_fusion.2), channel_id=1, source_target_pairs={{0,2},{2,0},{4,6},{6,4},{1,3},{3,1},{5,7},{7,5},{8,10},{10,8},{12,... | collective-permute-start | bytes 393224 | tf_op jit(solution)/shard_map/ppermute | solution.py:511
  23.3 25.3 %copy-start.3 = (bf16[512,128]{1,0:T(8,128)(2,1)}, bf16[512,128]{1,0:T(8,128)(2,1)S(1)}, u32[]{:S(2)}) copy-start(bf16[512,128]{1,0:T(8,128)(2,1)S(1)} %collective-permute-done.2.refs_13_) | copy-start | bytes 393220
  23.4 25.2 %collective-permute-start.5 = (bf16[1024,128]{1,0:T(8,128)(2,1)S(1)}, bf16[1024,128]{1,0:T(8,128)(2,1)S(1)}, u32[]{:S(2)}, u32[]{:S(2)}) collective-permute-start(bf16[1024,128]{1,0:T(8,128)(2,1)S(1)} %pad_maximum_fusion), channel_id=1, source_target_pairs={{0,6},{2,4},{4,2},{6,0},{1,7},{3,5},{5,3},{7,1},{8,14},{10,12},{12... | collective-permute-start | bytes 786440 | tf_op jit(solution)/shard_map/ppermute | solution.py:511
  48.7 4.8 %copy-start.7 = (bf16[1024,128]{1,0:T(8,128)(2,1)}, bf16[1024,128]{1,0:T(8,128)(2,1)S(1)}, u32[]{:S(2)}) copy-start(bf16[1024,128]{1,0:T(8,128)(2,1)S(1)} %collective-permute-done.5.refs_14_) | copy-start | bytes 786436
  48.7 4.7 %collective-permute-start.6 = (bf16[2048,128]{1,0:T(8,128)(2,1)S(1)}, bf16[2048,128]{1,0:T(8,128)(2,1)S(1)}, u32[]{:S(2)}, u32[]{:S(2)}) collective-permute-start(bf16[2048,128]{1,0:T(8,128)(2,1)S(1)} %constant_dynamic-update-slice_fusion), channel_id=1, source_target_pairs={{0,1},{1,0},{2,3},{3,2},{4,5},{5,4},{6,7},{7,6},{8,9},{9,8},{10,11... | collective-permute-start | bytes 1572872 | tf_op jit(solution)/shard_map/ppermute | solution.py:511
  78.1 1.5 collective-permute-start.7
  80.5 14.2 %collective-permute-start.8 = (f32[136,256]{1,0:T(8,128)S(1)}, f32[136,256]{1,0:T(8,128)S(1)}, u32[]{:S(2)}, u32[]{:S(2)}) collective-permute-start(f32[136,256]{1,0:T(8,128)S(1)} %dynamic-slice_add_fusion), channel_id=1, source_target_pairs={{0,32},{32,0},{64,96},{96,64},{1,33},{33,1},{65,97},{97,65},{2,34}... | collective-permute-start | bytes 417800 | tf_op jit(solution)/shard_map/ppermute | solution.py:511
  95.8 14.4 %collective-permute-start.9 = (bf16[2048,128]{1,0:T(8,128)(2,1)S(1)}, bf16[2048,128]{1,0:T(8,128)(2,1)S(1)}, u32[]{:S(2)}, u32[]{:S(2)}) collective-permute-start(bf16[2048,128]{1,0:T(8,128)(2,1)S(1)} %constant_dynamic-slice_fusion), channel_id=1, source_target_pairs={{0,1},{1,0},{2,3},{3,2},{4,5},{5,4},{6,7},{7,6},{8,9},{9,8},{10,11... | collective-permute-start | bytes 1572872 | tf_op jit(solution)/shard_map/ppermute | solution.py:511
  96.6 13.8 %collective-permute-start.10 = (f32[136,256]{1,0:T(8,128)S(1)}, f32[136,256]{1,0:T(8,128)S(1)}, u32[]{:S(2)}, u32[]{:S(2)}) collective-permute-start(f32[136,256]{1,0:T(8,128)S(1)} %add.87), channel_id=1, source_target_pairs={{0,96},{32,64},{64,32},{96,0},{1,97},{33,65},{65,33},{97,1},{2,98}... | collective-permute-start | bytes 417800 | tf_op jit(solution)/shard_map/ppermute | solution.py:511
  99.0 11.3 %copy-start = (bf16[4096,128]{1,0:T(8,128)(2,1)S(1)}, bf16[4096,128]{1,0:T(8,128)(2,1)}, u32[]{:S(2)}) copy-start(bf16[4096,128]{1,0:T(8,128)(2,1)} %hub_scatter_kernel.1) | copy-start | bytes 3145732
  110.2 3.1 %copy-start.2 = (bf16[2048,128]{1,0:T(8,128)(2,1)S(1)}, bf16[2048,128]{1,0:T(8,128)(2,1)}, u32[]{:S(2)}) copy-start(bf16[2048,128]{1,0:T(8,128)(2,1)} %rim_scatter_kernel.1) | copy-start | bytes 1572868
  110.4 29.6 %collective-permute-start.11 = (bf16[1024,128]{1,0:T(8,128)(2,1)S(1)}, bf16[1024,128]{1,0:T(8,128)(2,1)S(1)}, u32[]{:S(2)}, u32[]{:S(2)}) collective-permute-start(bf16[1024,128]{1,0:T(8,128)(2,1)S(1)} %dynamic-slice_convert_fusion), channel_id=1, source_target_pairs={{0,6},{2,4},{4,2},{6,0},{1,7},{3,5},{5,3},{7,1},{8,14},{10,12},{12... | collective-permute-start | bytes 786440 | tf_op jit(solution)/shard_map/ppermute | solution.py:511
  111.3 28.7 %collective-permute-start.12 = (f32[136,256]{1,0:T(8,128)S(1)}, f32[136,256]{1,0:T(8,128)S(1)}, u32[]{:S(2)}, u32[]{:S(2)}) collective-permute-start(f32[136,256]{1,0:T(8,128)S(1)} %add.91), channel_id=1, source_target_pairs={{0,6},{2,4},{4,2},{6,0},{1,7},{3,5},{5,3},{7,1},{8,14},{10,12},{12... | collective-permute-start | bytes 417800 | tf_op jit(solution)/shard_map/ppermute | solution.py:511
  113.3 26.7 %collective-permute-start.13 = (bf16[1024,128]{1,0:T(8,128)(2,1)S(1)}, bf16[1024,128]{1,0:T(8,128)(2,1)S(1)}, u32[]{:S(2)}, u32[]{:S(2)}) collective-permute-start(bf16[1024,128]{1,0:T(8,128)(2,1)S(1)} %get-tuple-element.132), channel_id=1, source_target_pairs={{0,32},{32,64},{64,96},{1,33},{33,65},{65,97},{2,34},{34,66},{66,9... | collective-permute-start | bytes 786440 | tf_op jit(solution)/shard_map/ppermute | solution.py:517
  115.7 24.4 %collective-permute-start.14 = (bf16[1024,128]{1,0:T(8,128)(2,1)S(1)}, bf16[1024,128]{1,0:T(8,128)(2,1)S(1)}, u32[]{:S(2)}, u32[]{:S(2)}) collective-permute-start(bf16[1024,128]{1,0:T(8,128)(2,1)S(1)} %get-tuple-element.131), channel_id=1, source_target_pairs={{32,0},{64,32},{96,64},{33,1},{65,33},{97,65},{34,2},{66,34},{98,6... | collective-permute-start | bytes 786440 | tf_op jit(solution)/shard_map/ppermute | solution.py:517
  140.0 21.9 %copy-start.9 = (bf16[1024,128]{1,0:T(8,128)(2,1)}, bf16[1024,128]{1,0:T(8,128)(2,1)S(1)}, u32[]{:S(2)}) copy-start(bf16[1024,128]{1,0:T(8,128)(2,1)S(1)} %collective-permute-done.13.from_above) | copy-start | bytes 786436
  140.1 21.8 %copy-start.10 = (bf16[1024,128]{1,0:T(8,128)(2,1)}, bf16[1024,128]{1,0:T(8,128)(2,1)S(1)}, u32[]{:S(2)}) copy-start(bf16[1024,128]{1,0:T(8,128)(2,1)S(1)} %collective-permute-done.14.from_below) | copy-start | bytes 786436
  140.1 4.2 %collective-permute-start.15 = (bf16[512,128]{1,0:T(8,128)(2,1)S(1)}, bf16[512,128]{1,0:T(8,128)(2,1)S(1)}, u32[]{:S(2)}, u32[]{:S(2)}) collective-permute-start(bf16[512,128]{1,0:T(8,128)(2,1)S(1)} %dynamic-slice_convert_fusion.1), channel_id=1, source_target_pairs={{0,2},{2,0},{4,6},{6,4},{1,3},{3,1},{5,7},{7,5},{8,10},{10,8},{12,... | collective-permute-start | bytes 393224 | tf_op jit(solution)/shard_map/ppermute | solution.py:511
  140.3 7.0 %collective-permute-start.18 = (f32[136,256]{1,0:T(8,128)S(1)}, f32[136,256]{1,0:T(8,128)S(1)}, u32[]{:S(2)}, u32[]{:S(2)}) collective-permute-start(f32[136,256]{1,0:T(8,128)S(1)} %add.103), channel_id=1, source_target_pairs={{0,2},{2,0},{4,6},{6,4},{1,3},{3,1},{5,7},{7,5},{8,10},{10,8},{12,... | collective-permute-start | bytes 417800 | tf_op jit(solution)/shard_map/ppermute | solution.py:511
  144.4 5.2 %collective-permute-start.16 = (bf16[256,128]{1,0:T(8,128)(2,1)S(1)}, bf16[256,128]{1,0:T(8,128)(2,1)S(1)}, u32[]{:S(2)}, u32[]{:S(2)}) collective-permute-start(bf16[256,128]{1,0:T(8,128)(2,1)S(1)} %dynamic-slice_convert_fusion.2), channel_id=1, source_target_pairs={{0,24},{8,16},{16,8},{24,0},{1,25},{9,17},{17,9},{25,1},{2,26},{10... | collective-permute-start | bytes 196616 | tf_op jit(solution)/shard_map/ppermute | solution.py:511
  147.3 6.0 %collective-permute-start.19 = (f32[136,256]{1,0:T(8,128)S(1)}, f32[136,256]{1,0:T(8,128)S(1)}, u32[]{:S(2)}, u32[]{:S(2)}) collective-permute-start(f32[136,256]{1,0:T(8,128)S(1)} %add.104), channel_id=1, source_target_pairs={{0,24},{8,16},{16,8},{24,0},{1,25},{9,17},{17,9},{25,1},{2,26},{10... | collective-permute-start | bytes 417800 | tf_op jit(solution)/shard_map/ppermute | solution.py:511
  149.7 3.8 %collective-permute-start.17 = (bf16[128,128]{1,0:T(8,128)(2,1)S(1)}, bf16[128,128]{1,0:T(8,128)(2,1)S(1)}, u32[]{:S(2)}, u32[]{:S(2)}) collective-permute-start(bf16[128,128]{1,0:T(8,128)(2,1)S(1)} %dynamic-slice_convert_fusion.3), channel_id=1, source_target_pairs={{0,8},{8,0},{16,24},{24,16},{1,9},{9,1},{17,25},{25,17},{2,10},{10... | collective-permute-start | bytes 98312 | tf_op jit(solution)/shard_map/ppermute | solution.py:511
  153.4 4.3 %collective-permute-start.20 = (f32[136,256]{1,0:T(8,128)S(1)}, f32[136,256]{1,0:T(8,128)S(1)}, u32[]{:S(2)}, u32[]{:S(2)}) collective-permute-start(f32[136,256]{1,0:T(8,128)S(1)} %add.105), channel_id=1, source_target_pairs={{0,8},{8,0},{16,24},{24,16},{1,9},{9,1},{17,25},{25,17},{2,10},{10... | collective-permute-start | bytes 417800 | tf_op jit(solution)/shard_map/ppermute | solution.py:511
  157.7 7.7 %collective-permute-start.21 = (f32[136,256]{1,0:T(8,128)S(1)}, f32[136,256]{1,0:T(8,128)S(1)}, u32[]{:S(2)}, u32[]{:S(2)}) collective-permute-start(f32[136,256]{1,0:T(8,128)S(1)} %add.106), channel_id=1, source_target_pairs={{0,1},{1,0},{2,3},{3,2},{4,5},{5,4},{6,7},{7,6},{8,9},{9,8},{10,11... | collective-permute-start | bytes 417800 | tf_op jit(solution)/shard_map/ppermute | solution.py:511
  (3 other events, 4.7 us)

commit v3 on v2

v3 whole, which is shorter than its diff:
```python
import functools

import jax
import jax.numpy as jnp
from jax import lax
from jax.experimental import pallas as pl
from jax.experimental.pallas import tpu as pltpu
from jax.sharding import Mesh, PartitionSpec as P

F = 128
H = 256
NODES = 4096
HALO = 1024
HUB = 128
FANOUT = 10
COLS = 32
HUBS = HUB * COLS
OWN = HALO
UPPER = HALO + NODES
HUB_AT = 2 * HALO + NODES
EXTENT = HUB_AT + HUBS
LANES = 128
CHAINS = 8
VMEM_BYTES = 60 * 2**20
AXES = ("z", "y", "x", "core")

smem = pl.BlockSpec(memory_space=pltpu.SMEM)
vmem = pl.BlockSpec(memory_space=pltpu.VMEM)
hbm = pl.BlockSpec(memory_space=pl.ANY)
params = pltpu.CompilerParams(vmem_limit_bytes=VMEM_BYTES)


def group_of(count):
    return 16 if count <= 3 else 8


def cost(us):
    return pl.CostEstimate(flops=int(us * 1e9), bytes_accessed=0, transcendentals=0)


def hub_kernel(hub_rows, features, out, wide, rows):
    @pl.loop(0, NODES // 512)
    def _(i):
        cut = pl.ds(i * 512, 512)
        wide[cut, :] = features[cut, :].astype(jnp.float32)

    @pl.loop(0, HUB // 16)
    def _(i):
        for u in range(16):
            rows[pl.ds(i * 16 + u, 1), :] = wide[pl.ds(hub_rows[i * 16 + u], 1), :]

    out[...] = rows[...].astype(jnp.bfloat16)


def pick_hubs(hub_rows, features):
    return pl.pallas_call(
        hub_kernel,
        out_shape=jax.ShapeDtypeStruct((HUB, F), jnp.bfloat16),
        in_specs=[smem, vmem],
        out_specs=vmem,
        scratch_shapes=[pltpu.VMEM((NODES, F), jnp.float32), pltpu.VMEM((HUB, F), jnp.float32)],
        compiler_params=params,
        cost_estimate=cost(2),
        name="pick_hubs",
    )(hub_rows, features)


ROWS = NODES // LANES


def order_by(count):
    lane_r = lax.broadcasted_iota(jnp.int32, (LANES, LANES), 0)
    lane_c = lax.broadcasted_iota(jnp.int32, (LANES, LANES), 1)
    before = (lane_r < lane_c).astype(jnp.bfloat16)
    row_r = lax.broadcasted_iota(jnp.int32, (ROWS, ROWS), 0)
    row_c = lax.broadcasted_iota(jnp.int32, (ROWS, ROWS), 1)
    above = (row_c < row_r).astype(jnp.bfloat16)
    lane = lax.broadcasted_iota(jnp.int32, (1, LANES), 1)
    hits = [(count == c).astype(jnp.float32) for c in range(FANOUT + 1)]
    stacked = jnp.concatenate(hits, axis=0).astype(jnp.bfloat16)
    in_rows = jnp.dot(stacked, before, preferred_element_type=jnp.float32)
    place = jnp.zeros((ROWS, LANES), jnp.float32)
    start = jnp.zeros((1, 1), jnp.float32)
    end_row = jnp.zeros((1, LANES), jnp.float32)
    for c in range(FANOUT + 1):
        hit = hits[c]
        per_row = jnp.sum(hit, axis=1, keepdims=True)
        earlier = jnp.dot(
            above,
            jnp.broadcast_to(per_row, (ROWS, LANES)).astype(jnp.bfloat16),
            preferred_element_type=jnp.float32,
        )
        in_row = in_rows[c * ROWS : (c + 1) * ROWS]
        place = place + hit * (in_row + earlier + start)
        start = start + jnp.sum(per_row, axis=0, keepdims=True)
        end_row = end_row + jnp.where(lane == c, start, 0.0)
    place = place.astype(jnp.int32)
    high = place >> 7
    low = place & (LANES - 1)
    slot_row = lax.broadcasted_iota(jnp.int32, (ROWS, LANES), 0)
    slot_lane = lax.broadcasted_iota(jnp.int32, (LANES, LANES), 0)
    own_lane = lax.broadcasted_iota(jnp.int32, (ROWS, LANES), 1).astype(jnp.float32)
    total = jnp.zeros((ROWS, LANES), jnp.float32)
    for r in range(ROWS):
        to_row = (high[r : r + 1, :] == slot_row).astype(jnp.float32)
        to_lane = (low[r : r + 1, :] == slot_lane).astype(jnp.bfloat16)
        both = jnp.concatenate([to_row * own_lane, to_row * float(r)], axis=0)
        found = lax.dot_general(
            both.astype(jnp.bfloat16),
            to_lane,
            (((1,), (1,)), ((), ())),
            preferred_element_type=jnp.float32,
        )
        total = total + found[:ROWS] + found[ROWS:] * float(LANES)
    return total.astype(jnp.int32), end_row.astype(jnp.int32)


def compact(flat, count, is_kind, value, backwards, placed):
    found = jnp.zeros((ROWS, LANES), jnp.int32)
    for s in range(FANOUT):
        row = flat[s * ROWS : (s + 1) * ROWS, :]
        hit = jnp.logical_and(count > s, is_kind(row))
        at = jnp.where(hit, found, -1)
        for k in range(s + 1):
            place = FANOUT - 1 - k if backwards else k
            placed[place] = jnp.where(at == k, value(row), placed[place])
        found = found + hit.astype(jnp.int32)
    return found


def nothing_placed():
    return [jnp.zeros((ROWS, LANES), jnp.int32) for _ in range(FANOUT)]


def is_own(row):
    return jnp.logical_and(row >= OWN, row < UPPER)


def is_rim(row):
    return jnp.logical_or(row < OWN, jnp.logical_and(row >= UPPER, row < HUB_AT))


def all_plan_kernel(neighbors, counts, flat, perm, ends):
    for s in range(FANOUT):
        for r in range(ROWS):
            at = s * ROWS + r
            flat[at : at + 1, :] = neighbors[s : s + 1, r * LANES : (r + 1) * LANES]
    perm[...], ends[...] = order_by(counts[...])


def hub_plan_kernel(flat, counts, slots, perm, ends):
    placed = nothing_placed()
    hubs = compact(
        flat, counts[...], lambda row: row >= HUB_AT, lambda row: row - HUB_AT, False, placed
    )
    for s in range(FANOUT):
        slots[s * ROWS : (s + 1) * ROWS, :] = placed[s]
    perm[...], ends[...] = order_by(hubs)


def rim_plan_kernel(flat, counts, slots, perm, ends, own_counts):
    placed = nothing_placed()
    own_counts[...] = compact(flat, counts[...], is_own, lambda row: row - OWN, False, placed)
    rims = compact(
        flat, counts[...], is_rim, lambda row: jnp.where(row < OWN, row, row - NODES), True, placed
    )
    for s in range(FANOUT):
        slots[s * ROWS : (s + 1) * ROWS, :] = placed[s]
    perm[...], ends[...] = order_by(rims)


def own_plan_kernel(own_counts, perm, ends):
    perm[...], ends[...] = order_by(own_counts[...])


tile = jax.ShapeDtypeStruct((ROWS, LANES), jnp.int32)
line = jax.ShapeDtypeStruct((1, LANES), jnp.int32)
tiles = jax.ShapeDtypeStruct((FANOUT * ROWS, LANES), jnp.int32)


def plan(kernel, outs, us, *inputs):
    return pl.pallas_call(
        kernel,
        out_shape=outs,
        in_specs=[vmem] * len(inputs),
        out_specs=(vmem,) * len(outs),
        compiler_params=params,
        cost_estimate=cost(us),
        name=kernel.__name__,
    )(*inputs)


def lists(perm, ends, slots):
    return ends.reshape(LANES), perm.reshape(NODES), slots.reshape(FANOUT * NODES)


list_specs = [smem, hbm, hbm]
list_scratch = [pltpu.SMEM((NODES,), jnp.int32)] * (1 + FANOUT) + [
    pltpu.SemaphoreType.DMA((1 + FANOUT,))
]


class Lists:
    def __init__(self, ends, perm, slots, perm_at, *rest):
        slots_at, sems = rest[:FANOUT], rest[FANOUT]
        self.ends, self.perm, self.slots = ends, perm_at, slots_at
        self.copies = [pltpu.make_async_copy(perm, perm_at, sems.at[0])]
        for s in range(FANOUT):
            part = slots.at[pl.ds(s * NODES, NODES)]
            self.copies.append(pltpu.make_async_copy(part, slots_at[s], sems.at[1 + s]))
        for copy in self.copies:
            copy.start()

    def visit(self, act, backwards=False):
        slots = self.slots[::-1] if backwards else self.slots
        copies = self.copies[:0:-1] if backwards else self.copies[1:]
        self.copies[0].wait()
        for count in range(1, FANOUT + 1):
            copies[count - 1].wait()
            size = group_of(count)
            first = self.ends[count - 1]
            last = self.ends[count]
            groups = (last - first) // size
            rest = first + groups * size

            @pl.loop(0, groups)
            def _(g, count=count, size=size, first=first):
                at = first + g * size
                act([self.perm[at + u] for u in range(size)], count, slots)

            @pl.loop(rest, last)
            def _(at, count=count):
                act([self.perm[at]], count, slots)


def clear(ref, at, rows):
    step = 512

    @pl.loop(0, rows // step)
    def _(i):
        ref[pl.ds(at + i * step, step), :] = jnp.zeros((step, F), jnp.float32)


BLOCK = 256
HUB_PIECES = (1, 1, 2, 4, 8, 16)


def forward_kernel(ends, perm, slots, features, lower, upper, *refs):
    pieces, refs = refs[:6], refs[6:]
    counts, w_self, w_neigh, bias, cotangent, act, src, base, grads = refs[:9]
    table, sums, features_at, rims_at, hubs_at, cot_at, act_at, src_at, base_at, weights = refs[9:19]
    lists_at, (sem_in, sem_out) = refs[19:-2], refs[-2:]
    copies = [
        pltpu.make_async_copy(features, features_at, sem_in.at[0]),
        pltpu.make_async_copy(lower, rims_at.at[pl.ds(0, HALO)], sem_in.at[1]),
        pltpu.make_async_copy(upper, rims_at.at[pl.ds(HALO, HALO)], sem_in.at[2]),
    ]
    at = 0
    for k, piece in enumerate(pieces):
        rows = HUB_PIECES[k] * HUB
        copies.append(
            pltpu.make_async_copy(piece, hubs_at.at[pl.ds(at, rows)], sem_in.at[3 + k])
        )
        at += rows
    for copy in copies:
        copy.start()
    todo = Lists(ends, perm, slots, *lists_at)
    cot_copy = pltpu.make_async_copy(cotangent, cot_at, sem_in.at[9])
    cot_copy.start()

    weights[0:F, :] = w_self[...]
    weights[F : 2 * F, :] = w_neigh[...]
    grads[...] = jnp.zeros_like(grads)

    def widen(source, start, at, rows):
        step = 256

        @pl.loop(0, rows // step)
        def _(i):
            table[pl.ds(at + i * step, step), :] = source[
                pl.ds(start + i * step, step), :
            ].astype(jnp.float32)

    copies[0].wait()
    widen(features_at, 0, OWN, NODES)
    copies[1].wait()
    widen(rims_at, 0, 0, HALO)
    copies[2].wait()
    widen(rims_at, HALO, UPPER, HALO)
    y, x, core = lax.axis_index("y"), lax.axis_index("x"), lax.axis_index("core")
    position = 0
    for k in range(6):
        copies[3 + k].wait()
        for _ in range(HUB_PIECES[k]):
            b = [(position >> k) & 1 for k in range(5)]
            owner_y = y ^ (b[0] * 1) ^ (b[1] * 3)
            owner_x = x ^ (b[2] * 1) ^ (b[3] * 3)
            owner = owner_y * 8 + owner_x * 2 + (core ^ b[4])
            table[pl.ds(HUB_AT + owner * HUB, HUB), :] = hubs_at[
                position * HUB : (position + 1) * HUB, :
            ].astype(jnp.float32)
            position += 1

    def gather(nodes, count, slots):
        for n in nodes:
            total = table[pl.ds(slots[0][n], 1), :]
            for s in range(1, count):
                total = total + table[pl.ds(slots[s][n], 1), :]
            sums[pl.ds(n, 1), :] = total

    todo.visit(gather)
    cot_copy.wait()

    @pl.loop(0, NODES // BLOCK)
    def _(i):
        cut = pl.ds(i * BLOCK, BLOCK)
        parts = []
        for k in range(BLOCK // LANES):
            row = counts[pl.ds(i * (BLOCK // LANES) + k, 1), :].astype(jnp.float32)
            parts.append(jnp.broadcast_to(row, (LANES, LANES)).T)
        divisor = jnp.concatenate(parts, axis=0)
        agg = (sums[cut, :] / divisor).astype(jnp.bfloat16)
        both = jnp.concatenate([features_at[cut, :], agg], axis=1)
        z = jnp.dot(both, weights[...], preferred_element_type=jnp.float32) + bias[...]
        scale = 0.7978845608028654
        cubic = 0.044715 * scale
        squared = z * z
        t = jnp.tanh(z * (scale + cubic * squared))
        half = 0.5 * z
        rest = half * t
        act_at[cut, :] = (half + rest).astype(jnp.bfloat16)
        slope = (0.5 + 0.5 * t) + (half - rest * t) * (scale + 3 * cubic * squared)
        dz = (cot_at[cut, :].astype(jnp.float32) * slope).astype(jnp.bfloat16)
        grads[0 : 2 * F, :] += lax.dot_general(
            both, dz, (((0,), (0,)), ((), ())), preferred_element_type=jnp.float32
        )
        grads[2 * F : 2 * F + 8, :] += jnp.sum(
            dz.astype(jnp.float32).reshape(BLOCK // 8, 8, H), axis=0
        )
        back = lax.dot_general(
            dz, weights[...], (((1,), (1,)), ((), ())), preferred_element_type=jnp.float32
        )
        base_at[cut, :] = back[:, :F]
        src_at[cut, :] = back[:, F:] / divisor
        for k, (here, there) in enumerate(((act_at, act), (src_at, src), (base_at, base))):
            pltpu.make_async_copy(here.at[cut], there.at[cut], sem_out.at[k]).start()

    for k, (here, there) in enumerate(((act_at, act), (src_at, src), (base_at, base))):
        pltpu.make_async_copy(here, there, sem_out.at[k]).wait()


def forward(lists, features, lower, upper, hubs, counts, w_self, w_neigh, bias, cot):
    return pl.pallas_call(
        forward_kernel,
        out_shape=(
            jax.ShapeDtypeStruct((NODES, H), jnp.bfloat16),
            jax.ShapeDtypeStruct((NODES, F), jnp.float32),
            jax.ShapeDtypeStruct((NODES, F), jnp.float32),
            jax.ShapeDtypeStruct((2 * F + 16, H), jnp.float32),
        ),
        in_specs=list_specs + [hbm] * (3 + len(hubs)) + [vmem] * 4 + [hbm],
        out_specs=(hbm, hbm, hbm, vmem),
        scratch_shapes=[
            pltpu.VMEM((EXTENT, F), jnp.float32),
            pltpu.VMEM((NODES, F), jnp.float32),
            pltpu.VMEM((NODES, F), jnp.bfloat16),
            pltpu.VMEM((2 * HALO, F), jnp.bfloat16),
            pltpu.VMEM((HUBS, F), jnp.bfloat16),
            pltpu.VMEM((NODES, H), jnp.bfloat16),
            pltpu.VMEM((NODES, H), jnp.bfloat16),
            pltpu.VMEM((NODES, F), jnp.float32),
            pltpu.VMEM((NODES, F), jnp.float32),
            pltpu.VMEM((2 * F, H), jnp.bfloat16),
        ]
        + list_scratch
        + [pltpu.SemaphoreType.DMA((10,)), pltpu.SemaphoreType.DMA((3,))],
        compiler_params=params,
        cost_estimate=cost(30),
        name="forward",
    )(*lists, features, lower, upper, *hubs, counts, w_self, w_neigh, bias, cot)


def chain_sum(chains, cut):
    out = chains[0][cut, :]
    for chain in chains[1:]:
        out = out + chain[cut, :]
    return out


def scatter_kernel(place, backwards, based, ends, perm, slots, src, *refs):
    if based:
        base, refs = refs[0], refs[1:]
    out, refs = refs[0], refs[1:]
    chains, refs = refs[:CHAINS], refs[CHAINS:]
    src_at, out_at = refs[:2]
    lists_at, sems = refs[2:-1], refs[-1]
    todo = Lists(ends, perm, slots, *lists_at)
    src_copy = pltpu.make_async_copy(src, src_at, sems.at[0])
    src_copy.start()
    rows = out_at.shape[0]
    if based:
        base_copy = pltpu.make_async_copy(base, chains[0], sems.at[1])
        base_copy.start()
    for chain in chains[1 if based else 0 :]:
        clear(chain, 0, rows)
    if based:
        base_copy.wait()
    src_copy.wait()

    def scatter(nodes, count, slots):
        turn = 0
        for n in nodes:
            row = src_at[pl.ds(n, 1), :]
            for s in range(count):
                chain = chains[turn % CHAINS]
                turn += 1
                at = pl.ds(slots[s][n], 1)
                chain[at, :] = chain[at, :] + row

    todo.visit(scatter, backwards)

    @pl.loop(0, rows // HUB)
    def _(i):
        to = pl.ds(place(i) * HUB, HUB)
        out_at[to, :] = chain_sum(chains, pl.ds(i * HUB, HUB)).astype(out_at.dtype)
        pltpu.make_async_copy(out_at.at[to], out.at[to], sems.at[2]).start()

    pltpu.make_async_copy(out_at, out, sems.at[2]).wait()


def hub_place(owner):
    return (owner & 1) * 16 + ((owner >> 1) & 3) * 4 + (owner >> 3)


def scatter(name, rows, kind, us, place, backwards, lists, *inputs):
    return pl.pallas_call(
        functools.partial(scatter_kernel, place, backwards, len(inputs) > 1),
        out_shape=jax.ShapeDtypeStruct((rows, F), kind),
        in_specs=list_specs + [hbm] * len(inputs),
        out_specs=hbm,
        scratch_shapes=[pltpu.VMEM((rows, F), jnp.float32)] * CHAINS
        + [pltpu.VMEM((NODES, F), jnp.float32), pltpu.VMEM((rows, F), kind)]
        + list_scratch
        + [pltpu.SemaphoreType.DMA((3,))],
        compiler_params=params,
        cost_estimate=cost(us),
        name=name,
    )(*lists, *inputs)


def finish_kernel(hub_rows, own, from_above, from_below, share, out, total):
    step = 256

    @pl.loop(0, NODES // step)
    def _(i):
        cut = pl.ds(i * step, step)
        total[cut, :] = own[cut, :]

    @pl.loop(0, HALO // step)
    def _(i):
        cut = pl.ds(i * step, step)
        total[cut, :] = total[cut, :] + from_above[cut, :].astype(jnp.float32)

    @pl.loop(0, HALO // step)
    def _(i):
        cut = pl.ds(NODES - HALO + i * step, step)
        total[cut, :] = total[cut, :] + from_below[pl.ds(i * step, step), :].astype(jnp.float32)

    @pl.loop(0, HUB // 8)
    def _(i):
        for u in range(8):
            at = pl.ds(hub_rows[i * 8 + u], 1)
            total[at, :] = total[at, :] + share[pl.ds(i * 8 + u, 1), :]

    @pl.loop(0, NODES // step)
    def _(i):
        cut = pl.ds(i * step, step)
        out[cut, :] = total[cut, :].astype(jnp.bfloat16)


def finish(hub_rows, own, from_above, from_below, share):
    return pl.pallas_call(
        finish_kernel,
        out_shape=jax.ShapeDtypeStruct((NODES, F), jnp.bfloat16),
        in_specs=[smem] + [vmem] * 4,
        out_specs=vmem,
        scratch_shapes=[pltpu.VMEM((NODES, F), jnp.float32)],
        compiler_params=params,
        cost_estimate=cost(3),
        name="finish",
    )(hub_rows, own, from_above, from_below, share)


def swap(value, axis, flip):
    count = lax.axis_size(axis)
    return lax.ppermute(value, axis, [(i, i ^ flip) for i in range(count)])


def shifted(value, axis, by):
    count = lax.axis_size(axis)
    pairs = [(i, i + by) for i in range(count) if 0 <= i + by < count]
    return lax.ppermute(value, axis, pairs)


def halves(value, bit):
    rows = value.shape[0] // 2
    keep = lax.dynamic_slice_in_dim(value, bit * rows, rows, axis=0)
    give = lax.dynamic_slice_in_dim(value, (1 - bit) * rows, rows, axis=0)
    return keep, give


def halve(value, axis, flip, bit):
    keep, give = halves(value, bit)
    got = swap(give.astype(jnp.bfloat16), axis, flip)
    return keep.astype(jnp.float32) + got.astype(jnp.float32)


def tie(*values):
    return lax.optimization_barrier(values)


def on_device(features, neighbors, counts, hub_rows, w_self, w_neigh, out_bias, cotangent):
    x, y, core = lax.axis_index("x"), lax.axis_index("y"), lax.axis_index("core")
    counts = counts.reshape(ROWS, LANES)

    h0 = pick_hubs(hub_rows, features)
    h1 = swap(h0, "y", 1)
    lower = shifted(features[NODES - HALO :], "z", 1)
    upper = shifted(features[:HALO], "z", -1)
    flat, perm, ends = plan(all_plan_kernel, (tiles, tile, line), 4, neighbors.T, counts)
    all_lists = lists(perm, ends, flat)
    h1, flat = tie(h1, flat)
    held = jnp.concatenate([h0, h1], axis=0)
    h2 = swap(held, "y", 3)
    slots, perm, ends = plan(hub_plan_kernel, (tiles, tile, line), 4, flat, counts)
    hub_lists = lists(perm, ends, slots)
    h2, flat, *hub_lists = tie(h2, flat, *hub_lists)
    held = jnp.concatenate([held, h2], axis=0)
    h3 = swap(held, "x", 1)
    slots, perm, ends, own_counts = plan(
        rim_plan_kernel, (tiles, tile, line, tile), 4, flat, counts
    )
    rim_lists = lists(perm, ends, slots)
    h3, lower, upper, own_counts, rim_lists = tie(h3, lower, upper, own_counts, rim_lists)
    held = jnp.concatenate([held, h3], axis=0)
    h4 = swap(held, "x", 3)
    perm, ends = plan(own_plan_kernel, (tile, line), 4, own_counts)
    own_lists = lists(perm, ends, slots)
    h4, *own_lists = tie(h4, *own_lists)
    held = jnp.concatenate([held, h4], axis=0)
    h5 = swap(held, "core", 1)

    act, src, base, grads = forward(
        all_lists, features, lower, upper, (h0, h1, h2, h3, h4, h5), counts,
        w_self, w_neigh, out_bias.reshape(1, H), cotangent,
    )

    keep, give = halves(grads, core)
    other = swap(give, "core", 1)
    hub = scatter("hub_scatter", HUBS, jnp.bfloat16, 8, hub_place, False, hub_lists, src)
    hub, src, other = tie(hub, src, other)
    grads = keep + other
    other = swap(grads, "z", 1)
    hub = halve(hub, "core", 1, core)
    rim = scatter(
        "rim_scatter", 2 * HALO, jnp.bfloat16, 8, lambda i: i, True, rim_lists, src
    )
    hub, src, other, rim = tie(hub, src, other, rim)
    grads = grads + other
    other = swap(grads, "z", 3)
    hub = halve(hub, "x", 3, x // 2)
    from_below = shifted(rim[:HALO], "z", -1)
    from_above = shifted(rim[HALO:], "z", 1)
    own = scatter(
        "own_scatter", NODES, jnp.float32, 20, lambda i: i, False, own_lists, src, base
    )
    hub, other, own, from_above, from_below = tie(hub, other, own, from_above, from_below)
    grads = grads + other
    grads = grads + swap(grads, "x", 3)
    hub = halve(hub, "x", 1, x % 2)
    grads = grads + swap(grads, "x", 1)
    hub = halve(hub, "y", 3, y // 2)
    grads = grads + swap(grads, "y", 3)
    share = halve(hub, "y", 1, y % 2)
    grads = grads + swap(grads, "y", 1)
    other = swap(grads, "core", 1)
    grads = jnp.concatenate(
        [jnp.where(core == 0, grads, other), jnp.where(core == 0, other, grads)], axis=0
    )
    grad_features = finish(hub_rows, own, from_above, from_below, share)
    grad_bias = jnp.sum(grads[2 * F :], axis=0)
    return act, grad_features, grads[:F], grads[F : 2 * F], grad_bias


def solution(mesh):
    mesh = Mesh(mesh.devices.reshape(4, 4, 4, 2), AXES)
    rows = P(AXES, None)
    placed = (rows, rows, P(AXES), P(AXES), P(), P(), P(), rows)
    return jax.shard_map(
        on_device,
        mesh=mesh,
        in_specs=placed,
        out_specs=(rows, rows, P(), P(), P()),
        check_vma=False,
    )
```

time: 167 us -> 156 us (0.934)
  Pallas kernels: 108 us -> 92.5 us
  waiting for transfers between devices: 13.2 us -> 18.5 us
    pallas_call x7, Pallas kernels: 79.7 us -> 52.4 us  [the longest x3 41.7 us: scatter(): pl.pallas_call(functools.partial(scatter_kernel, place, backwards, len(in...]
    pallas_call x1, Pallas kernels: 22.9 us -> 34.4 us  [forward(): pl.pallas_call(forward_kernel, out_shape=(jax.ShapeDtypeStruct((NODES, H)...]
    ppermute x18, waiting for transfers between devices: 13.2 us -> 18.5 us  [swap(): return lax.ppermute(value, axis, [(i, i ^ flip) for i in range(count)])]
  transfers between devices with their start and end apart: 22 -> 22, of which waited for: 6 -> 8; matrix products, arithmetic and copies ran while one was open for 1% -> 1% of each run, Pallas kernels for 50% -> 36%
where the time goes in v3:
time: 156 us; the launch traced here: 155 us
  Pallas kernels  92.5 us (59%)
  starting transfers between devices  37.6 us (24%)
  waiting for transfers between devices  18.5 us (12%)
  local copies, waits for them, and re-layouts  3.09 us (2%)
  other arithmetic  2.39 us (2%)
    pallas_call x3, Pallas kernels, scatter(): pl.pallas_call(functools.partial(scatter_kernel, place, backwards, len(in...  41.7 us
    pallas_call x1, Pallas kernels, forward(): pl.pallas_call(forward_kernel, out_shape=(jax.ShapeDtypeStruct((NODES, H)...  34.4 us
    ppermute x18, starting transfers between devices, swap(): return lax.ppermute(value, axis, [(i, i ^ flip) for i in range(count)])  28.7 us
    ppermute x18, waiting for transfers between devices, swap(): return lax.ppermute(value, axis, [(i, i ^ flip) for i in range(count)])  18.5 us
    pallas_call x4, Pallas kernels, plan(): pl.pallas_call(kernel, out_shape=outs, in_specs=[vmem] * len(inputs), out...  10.7 us
    ppermute x4, starting transfers between devices, shifted(): return lax.ppermute(value, axis, pairs)  8.89 us
    pallas_call x1, Pallas kernels, finish(): pl.pallas_call(finish_kernel, out_shape=jax.ShapeDtypeStruct((NODES, F),...  3.49 us
  transfers between devices with their start and end apart: 22, of which 8 were waited for; matrix products, arithmetic and copies ran while one was open for 1% of the time, Pallas kernels for 36%

profile of v3, /device:TPU:1, one launch (start us, length us, event | category | flops | bytes accessed | tf_op | source)
XLA Modules:
  0.0 155.2 jit_solution(9172726994665278535)
XLA Ops:
  0.6 2.2 %pick_hubs.1.refs_0_ = bf16[128,128]{1,0:T(8,128)(2,1)} custom-call(s32[128]{0:T(128)} %hub_rows.3, bf16[4096,128]{1,0:T(8,128)(2,1)} %features.3), custom_call_target="tpu_custom_call" | custom-call | flops 2000000000 | tf_op jit(solution)/shard_map/pick_hubs/pallas_call | solution.py:56
  2.9 2.1 %collective-permute-start = (bf16[128,128]{1,0:T(8,128)(2,1)}, bf16[128,128]{1,0:T(8,128)(2,1)S(1)}, u32[]{:S(2)}, u32[]{:S(2)}) collective-permute-start(bf16[128,128]{1,0:T(8,128)(2,1)} %pick_hubs.1.refs_0_), channel_id=1, source_target_pairs={{0,8},{8,0},{16,24},{24,16},{1,9},{9,1},{17,25},{25,17},{2,10},{10... | collective-permute-start | bytes 98312 | tf_op jit(solution)/shard_map/ppermute | solution.py:496
  5.0 3.6 %collective-permute-start.3 = (bf16[1024,128]{1,0:T(8,128)(2,1)S(1)}, bf16[1024,128]{1,0:T(8,128)(2,1)S(1)}, u32[]{:S(2)}, u32[]{:S(2)}) collective-permute-start(bf16[1024,128]{1,0:T(8,128)(2,1)S(1)} %get-tuple-element.98), channel_id=1, source_target_pairs={{0,32},{32,64},{64,96},{1,33},{33,65},{65,97},{2,34},{34,66},{66,9... | collective-permute-start | bytes 786440 | tf_op jit(solution)/shard_map/ppermute | solution.py:502
  8.6 1.3 collective-permute-start.4
  9.9 2.7 %all_plan_kernel.1 = (s32[320,128]{1,0:T(8,128)}, s32[32,128]{1,0:T(8,128)}, s32[1,128]{1,0:T(1,128)}) custom-call(s32[10,4096]{1,0:T(8,128)} %bitcast.14, s32[32,128]{1,0:T(8,128)} %bitcast.15), custom_call_target="tpu_custom_call" | custom-call | flops 4000000000 | tf_op jit(solution)/shard_map/all_plan_kernel/pallas_call | solution.py:182
  12.7 2.0 %collective-permute-start.1 = (bf16[256,128]{1,0:T(8,128)(2,1)S(1)}, bf16[256,128]{1,0:T(8,128)(2,1)S(1)}, u32[]{:S(2)}, u32[]{:S(2)}) collective-permute-start(bf16[256,128]{1,0:T(8,128)(2,1)S(1)} %pad_maximum_fusion.3), channel_id=1, source_target_pairs={{0,24},{8,16},{16,8},{24,0},{1,25},{9,17},{17,9},{25,1},{2,26},{10... | collective-permute-start | bytes 196616 | tf_op jit(solution)/shard_map/ppermute | solution.py:496
  14.7 2.7 %hub_plan_kernel.1 = (s32[320,128]{1,0:T(8,128)}, s32[32,128]{1,0:T(8,128)}, s32[1,128]{1,0:T(1,128)}) custom-call(s32[320,128]{1,0:T(8,128)} %get-tuple-element.60.flat, s32[32,128]{1,0:T(8,128)} %bitcast.16), custom_call_target="tpu_custom_call" | custom-call | flops 4000000000 | tf_op jit(solution)/shard_map/hub_plan_kernel/pallas_call | solution.py:182
  17.4 1.3 collective-permute-start.2
  18.7 2.8 %rim_plan_kernel.1 = (s32[320,128]{1,0:T(8,128)}, s32[32,128]{1,0:T(8,128)}, s32[1,128]{1,0:T(1,128)}, s32[32,128]{1,0:T(8,128)}) custom-call(s32[320,128]{1,0:T(8,128)} %get-tuple-element.60.flat, s32[32,128]{1,0:T(8,128)} %bitcast.17), custom_call_target="tpu_custom_call" | custom-call | flops 4000000000 | tf_op jit(solution)/shard_map/rim_plan_kernel/pallas_call | solution.py:182
  21.7 2.3 %collective-permute-start.5 = (bf16[1024,128]{1,0:T(8,128)(2,1)S(1)}, bf16[1024,128]{1,0:T(8,128)(2,1)S(1)}, u32[]{:S(2)}, u32[]{:S(2)}) collective-permute-start(bf16[1024,128]{1,0:T(8,128)(2,1)S(1)} %pad_maximum_fusion), channel_id=1, source_target_pairs={{0,6},{2,4},{4,2},{6,0},{1,7},{3,5},{5,3},{7,1},{8,14},{10,12},{12... | collective-permute-start | bytes 786440 | tf_op jit(solution)/shard_map/ppermute | solution.py:496
  24.0 2.4 %own_plan_kernel.1 = (s32[32,128]{1,0:T(8,128)}, s32[1,128]{1,0:T(1,128)}) custom-call(s32[32,128]{1,0:T(8,128)} %get-tuple-element.68.own_counts), custom_call_target="tpu_custom_call" | custom-call | flops 4000000000 | tf_op jit(solution)/shard_map/own_plan_kernel/pallas_call | solution.py:182
  26.4 1.8 %collective-permute-done.5.refs_4_ = bf16[1024,128]{1,0:T(8,128)(2,1)S(1)} collective-permute-done((bf16[1024,128]{1,0:T(8,128)(2,1)S(1)}, bf16[1024,128]{1,0:T(8,128)(2,1)S(1)}, u32[]{:S(2)}, u32[]{:S(2)}) %collective-permute-start.5) | collective-permute-done | bytes 262176 | tf_op jit(solution)/shard_map/ppermute | solution.py:496
  28.3 4.1 %collective-permute-start.6 = (bf16[2048,128]{1,0:T(8,128)(2,1)S(1)}, bf16[2048,128]{1,0:T(8,128)(2,1)S(1)}, u32[]{:S(2)}, u32[]{:S(2)}) collective-permute-start(bf16[2048,128]{1,0:T(8,128)(2,1)S(1)} %constant_dynamic-update-slice_fusion), channel_id=1, source_target_pairs={{0,1},{1,0},{2,3},{3,2},{4,5},{5,4},{6,7},{7,6},{8,9},{9,8},{10,11... | collective-permute-start | bytes 1572872 | tf_op jit(solution)/shard_map/ppermute | solution.py:496
  32.4 1.5 collective-permute-done.6.refs_5_
  34.7 34.4 %forward.1 = (bf16[4096,256]{1,0:T(8,128)(2,1)}, f32[4096,128]{1,0:T(8,128)}, f32[4096,128]{1,0:T(8,128)}, f32[272,256]{1,0:T(8,128)}) custom-call(s32[128]{0:T(128)} %bitcast.31, s32[4096]{0:T(1024)} %bitcast.27, s32[40960]{0:T(1024)} %bitcast.23, bf16[4096,128]{1,0:T(8,128)(2,1)} %features.3, bf16[1024,128]{1,0:T(8,128)(2,1)} %copy-done.12, ...), custom_call_target="tpu_custom_call" | custom-call | flops 30000001024 | tf_op jit(solution)/shard_map/forward/pallas_call | solution.py:353
  70.2 9.9 %hub_scatter.1 = bf16[4096,128]{1,0:T(8,128)(2,1)} custom-call(s32[128]{0:T(128)} %bitcast.30, s32[4096]{0:T(1024)} %bitcast.26, s32[40960]{0:T(1024)} %bitcast.22, f32[4096,128]{1,0:T(8,128)} %get-tuple-element.89.src), custom_call_target="tpu_custom_call" | custom-call | flops 8000000000 | tf_op jit(solution)/shard_map/hub_scatter/pallas_call | solution.py:436
  80.2 1.1 constant_dynamic-slice_fusion
  81.6 2.5 %collective-permute-start.9 = (f32[136,256]{1,0:T(8,128)S(1)}, f32[136,256]{1,0:T(8,128)S(1)}, u32[]{:S(2)}, u32[]{:S(2)}) collective-permute-start(f32[136,256]{1,0:T(8,128)S(1)} %dynamic-slice_add_fusion), channel_id=1, source_target_pairs={{0,32},{32,0},{64,96},{96,64},{1,33},{33,1},{65,97},{97,65},{2,34}... | collective-permute-start | bytes 417800 | tf_op jit(solution)/shard_map/ppermute | solution.py:496
  84.1 11.0 %rim_scatter.1 = bf16[2048,128]{1,0:T(8,128)(2,1)} custom-call(s32[128]{0:T(128)} %bitcast.29, s32[4096]{0:T(1024)} %bitcast.25, s32[40960]{0:T(1024)} %bitcast.20, f32[4096,128]{1,0:T(8,128)} %get-tuple-element.89.src), custom_call_target="tpu_custom_call" | custom-call | flops 8000000000 | tf_op jit(solution)/shard_map/rim_scatter/pallas_call | solution.py:436
  95.3 2.6 %collective-permute-start.10 = (bf16[1024,128]{1,0:T(8,128)(2,1)S(1)}, bf16[1024,128]{1,0:T(8,128)(2,1)S(1)}, u32[]{:S(2)}, u32[]{:S(2)}) collective-permute-start(bf16[1024,128]{1,0:T(8,128)(2,1)S(1)} %dynamic-slice_convert_fusion), channel_id=1, source_target_pairs={{0,6},{2,4},{4,2},{6,0},{1,7},{3,5},{5,3},{7,1},{8,14},{10,12},{12... | collective-permute-start | bytes 786440 | tf_op jit(solution)/shard_map/ppermute | solution.py:496
  98.0 2.7 %collective-permute-start.11 = (f32[136,256]{1,0:T(8,128)S(1)}, f32[136,256]{1,0:T(8,128)S(1)}, u32[]{:S(2)}, u32[]{:S(2)}) collective-permute-start(f32[136,256]{1,0:T(8,128)S(1)} %add.90), channel_id=1, source_target_pairs={{0,96},{32,64},{64,32},{96,0},{1,97},{33,65},{65,33},{97,1},{2,98}... | collective-permute-start | bytes 417800 | tf_op jit(solution)/shard_map/ppermute | solution.py:496
  100.7 2.7 %collective-permute-start.12 = (bf16[1024,128]{1,0:T(8,128)(2,1)S(1)}, bf16[1024,128]{1,0:T(8,128)(2,1)S(1)}, u32[]{:S(2)}, u32[]{:S(2)}) collective-permute-start(bf16[1024,128]{1,0:T(8,128)(2,1)S(1)} %get-tuple-element.100), channel_id=1, source_target_pairs={{0,32},{32,64},{64,96},{1,33},{33,65},{65,97},{2,34},{34,66},{66,9... | collective-permute-start | bytes 786440 | tf_op jit(solution)/shard_map/ppermute | solution.py:502
  103.4 1.3 collective-permute-start.13
  104.7 20.7 %own_scatter.1.own = f32[4096,128]{1,0:T(8,128)} custom-call(s32[128]{0:T(128)} %bitcast.28, s32[4096]{0:T(1024)} %bitcast.24, s32[40960]{0:T(1024)} %bitcast.21, f32[4096,128]{1,0:T(8,128)} %get-tuple-element.89.src, f32[4096,128]{1,0:T(8,128)} %get-tuple-element.90.refs_0_), custom_call_target="tpu_custom_call" | custom-call | flops 20000000000 | tf_op jit(solution)/shard_map/own_scatter/pallas_call | solution.py:436
  125.8 3.7 %collective-permute-done.14 = bf16[512,128]{1,0:T(8,128)(2,1)S(1)} collective-permute-done((bf16[512,128]{1,0:T(8,128)(2,1)S(1)}, bf16[512,128]{1,0:T(8,128)(2,1)S(1)}, u32[]{:S(2)}, u32[]{:S(2)}) %collective-permute-start.14) | collective-permute-done | bytes 131104 | tf_op jit(solution)/shard_map/ppermute | solution.py:496
  129.5 1.0 collective-permute-start.15
  131.3 2.7 %collective-permute-done.15 = bf16[256,128]{1,0:T(8,128)(2,1)S(1)} collective-permute-done((bf16[256,128]{1,0:T(8,128)(2,1)S(1)}, bf16[256,128]{1,0:T(8,128)(2,1)S(1)}, u32[]{:S(2)}, u32[]{:S(2)}) %collective-permute-start.15) | collective-permute-done | bytes 65568 | tf_op jit(solution)/shard_map/ppermute | solution.py:496
  134.9 1.4 collective-permute-start.19
  136.4 3.7 %collective-permute-done.19 = f32[136,256]{1,0:T(8,128)S(1)} collective-permute-done((f32[136,256]{1,0:T(8,128)S(1)}, f32[136,256]{1,0:T(8,128)S(1)}, u32[]{:S(2)}, u32[]{:S(2)}) %collective-permute-start.19) | collective-permute-done | bytes 139296 | tf_op jit(solution)/shard_map/ppermute | solution.py:496
  140.9 3.8 %collective-permute-done.20 = f32[136,256]{1,0:T(8,128)S(1)} collective-permute-done((f32[136,256]{1,0:T(8,128)S(1)}, f32[136,256]{1,0:T(8,128)S(1)}, u32[]{:S(2)}, u32[]{:S(2)}) %collective-permute-start.20) | collective-permute-done | bytes 139296 | tf_op jit(solution)/shard_map/ppermute | solution.py:496
  144.7 5.6 %collective-permute-start.21 = (f32[136,256]{1,0:T(8,128)S(1)}, f32[136,256]{1,0:T(8,128)S(1)}, u32[]{:S(2)}, u32[]{:S(2)}) collective-permute-start(f32[136,256]{1,0:T(8,128)S(1)} %add.106), channel_id=1, source_target_pairs={{0,1},{1,0},{2,3},{3,2},{4,5},{5,4},{6,7},{7,6},{8,9},{9,8},{10,11... | collective-permute-start | bytes 417800 | tf_op jit(solution)/shard_map/ppermute | solution.py:496
  150.3 3.5 %finish.1 = bf16[4096,128]{1,0:T(8,128)(2,1)} custom-call(s32[128]{0:T(128)} %hub_rows.3, f32[4096,128]{1,0:T(8,128)} %own_scatter.1.own, bf16[1024,128]{1,0:T(8,128)(2,1)} %copy-done.10, bf16[1024,128]{1,0:T(8,128)(2,1)} %copy-done.11, f32[128,128]{1,0:T(8,128)} %convert_add_fusion.4.share), custom_call_target="tpu_custom_call" | custom-call | flops 3000000000 | tf_op jit(solution)/shard_map/finish/pallas_call | solution.py:482
  (81 shorter events, 6.9 us)
Async XLA Ops:
  2.9 9.8 %collective-permute-start = (bf16[128,128]{1,0:T(8,128)(2,1)}, bf16[128,128]{1,0:T(8,128)(2,1)S(1)}, u32[]{:S(2)}, u32[]{:S(2)}) collective-permute-start(bf16[128,128]{1,0:T(8,128)(2,1)} %pick_hubs.1.refs_0_), channel_id=1, source_target_pairs={{0,8},{8,0},{16,24},{24,16},{1,9},{9,1},{17,25},{25,17},{2,10},{10... | collective-permute-start | bytes 98312 | tf_op jit(solution)/shard_map/ppermute | solution.py:496
  5.0 16.6 %collective-permute-start.3 = (bf16[1024,128]{1,0:T(8,128)(2,1)S(1)}, bf16[1024,128]{1,0:T(8,128)(2,1)S(1)}, u32[]{:S(2)}, u32[]{:S(2)}) collective-permute-start(bf16[1024,128]{1,0:T(8,128)(2,1)S(1)} %get-tuple-element.98), channel_id=1, source_target_pairs={{0,32},{32,64},{64,96},{1,33},{33,65},{65,97},{2,34},{34,66},{66,9... | collective-permute-start | bytes 786440 | tf_op jit(solution)/shard_map/ppermute | solution.py:502
  8.6 13.0 %collective-permute-start.4 = (bf16[1024,128]{1,0:T(8,128)(2,1)S(1)}, bf16[1024,128]{1,0:T(8,128)(2,1)S(1)}, u32[]{:S(2)}, u32[]{:S(2)}) collective-permute-start(bf16[1024,128]{1,0:T(8,128)(2,1)S(1)} %get-tuple-element.97), channel_id=1, source_target_pairs={{32,0},{64,32},{96,64},{33,1},{65,33},{97,65},{34,2},{66,34},{98,6... | collective-permute-start | bytes 786440 | tf_op jit(solution)/shard_map/ppermute | solution.py:502
  12.7 9.0 %copy-start.5 = (bf16[128,128]{1,0:T(8,128)(2,1)}, bf16[128,128]{1,0:T(8,128)(2,1)S(1)}, u32[]{:S(2)}) copy-start(bf16[128,128]{1,0:T(8,128)(2,1)S(1)} %collective-permute-done.refs_1_) | copy-start | bytes 98308
  12.7 4.7 %collective-permute-start.1 = (bf16[256,128]{1,0:T(8,128)(2,1)S(1)}, bf16[256,128]{1,0:T(8,128)(2,1)S(1)}, u32[]{:S(2)}, u32[]{:S(2)}) collective-permute-start(bf16[256,128]{1,0:T(8,128)(2,1)S(1)} %pad_maximum_fusion.3), channel_id=1, source_target_pairs={{0,24},{8,16},{16,8},{24,0},{1,25},{9,17},{17,9},{25,1},{2,26},{10... | collective-permute-start | bytes 196616 | tf_op jit(solution)/shard_map/ppermute | solution.py:496
  17.4 4.2 %collective-permute-start.2 = (bf16[512,128]{1,0:T(8,128)(2,1)S(1)}, bf16[512,128]{1,0:T(8,128)(2,1)S(1)}, u32[]{:S(2)}, u32[]{:S(2)}) collective-permute-start(bf16[512,128]{1,0:T(8,128)(2,1)S(1)} %pad_maximum_fusion.2), channel_id=1, source_target_pairs={{0,2},{2,0},{4,6},{6,4},{1,3},{3,1},{5,7},{7,5},{8,10},{10,8},{12,... | collective-permute-start | bytes 393224 | tf_op jit(solution)/shard_map/ppermute | solution.py:496
  21.6 4.8 %copy-start.3 = (bf16[512,128]{1,0:T(8,128)(2,1)}, bf16[512,128]{1,0:T(8,128)(2,1)S(1)}, u32[]{:S(2)}) copy-start(bf16[512,128]{1,0:T(8,128)(2,1)S(1)} %collective-permute-done.2.refs_3_) | copy-start | bytes 393220
  21.6 4.8 %copy-start.12 = (bf16[1024,128]{1,0:T(8,128)(2,1)}, bf16[1024,128]{1,0:T(8,128)(2,1)S(1)}, u32[]{:S(2)}) copy-start(bf16[1024,128]{1,0:T(8,128)(2,1)S(1)} %collective-permute-done.3.lower) | copy-start | bytes 786436
  21.7 4.8 %copy-start.13 = (bf16[1024,128]{1,0:T(8,128)(2,1)}, bf16[1024,128]{1,0:T(8,128)(2,1)S(1)}, u32[]{:S(2)}) copy-start(bf16[1024,128]{1,0:T(8,128)(2,1)S(1)} %collective-permute-done.4.upper) | copy-start | bytes 786436
  21.7 6.5 %collective-permute-start.5 = (bf16[1024,128]{1,0:T(8,128)(2,1)S(1)}, bf16[1024,128]{1,0:T(8,128)(2,1)S(1)}, u32[]{:S(2)}, u32[]{:S(2)}) collective-permute-start(bf16[1024,128]{1,0:T(8,128)(2,1)S(1)} %pad_maximum_fusion), channel_id=1, source_target_pairs={{0,6},{2,4},{4,2},{6,0},{1,7},{3,5},{5,3},{7,1},{8,14},{10,12},{12... | collective-permute-start | bytes 786440 | tf_op jit(solution)/shard_map/ppermute | solution.py:496
  28.2 5.7 %copy-start.8 = (bf16[1024,128]{1,0:T(8,128)(2,1)}, bf16[1024,128]{1,0:T(8,128)(2,1)S(1)}, u32[]{:S(2)}) copy-start(bf16[1024,128]{1,0:T(8,128)(2,1)S(1)} %collective-permute-done.5.refs_4_) | copy-start | bytes 786436
  28.3 5.7 %collective-permute-start.6 = (bf16[2048,128]{1,0:T(8,128)(2,1)S(1)}, bf16[2048,128]{1,0:T(8,128)(2,1)S(1)}, u32[]{:S(2)}, u32[]{:S(2)}) collective-permute-start(bf16[2048,128]{1,0:T(8,128)(2,1)S(1)} %constant_dynamic-update-slice_fusion), channel_id=1, source_target_pairs={{0,1},{1,0},{2,3},{3,2},{4,5},{5,4},{6,7},{7,6},{8,9},{9,8},{10,11... | collective-permute-start | bytes 1572872 | tf_op jit(solution)/shard_map/ppermute | solution.py:496
  70.0 10.1 %collective-permute-start.7 = (f32[136,256]{1,0:T(8,128)S(1)}, f32[136,256]{1,0:T(8,128)S(1)}, u32[]{:S(2)}, u32[]{:S(2)}) collective-permute-start(f32[136,256]{1,0:T(8,128)S(1)} %constant_dynamic-slice_fusion.1), channel_id=1, source_target_pairs={{0,1},{1,0},{2,3},{3,2},{4,5},{5,4},{6,7},{7,6},{8,9},{9,8},{10,11... | collective-permute-start | bytes 417800 | tf_op jit(solution)/shard_map/ppermute | solution.py:496
  70.2 11.4 %copy-start.6 = (f32[272,256]{1,0:T(8,128)S(1)}, f32[272,256]{1,0:T(8,128)}, u32[]{:S(2)}) copy-start(f32[272,256]{1,0:T(8,128)} %get-tuple-element.77) | copy-start | bytes 835588
  81.2 13.9 %collective-permute-start.8 = (bf16[2048,128]{1,0:T(8,128)(2,1)S(1)}, bf16[2048,128]{1,0:T(8,128)(2,1)S(1)}, u32[]{:S(2)}, u32[]{:S(2)}) collective-permute-start(bf16[2048,128]{1,0:T(8,128)(2,1)S(1)} %constant_dynamic-slice_fusion), channel_id=1, source_target_pairs={{0,1},{1,0},{2,3},{3,2},{4,5},{5,4},{6,7},{7,6},{8,9},{9,8},{10,11... | collective-permute-start | bytes 1572872 | tf_op jit(solution)/shard_map/ppermute | solution.py:496
  81.6 13.5 %copy-start = (bf16[4096,128]{1,0:T(8,128)(2,1)S(1)}, bf16[4096,128]{1,0:T(8,128)(2,1)}, u32[]{:S(2)}) copy-start(bf16[4096,128]{1,0:T(8,128)(2,1)} %hub_scatter.1) | copy-start | bytes 3145732
  81.6 13.7 %collective-permute-start.9 = (f32[136,256]{1,0:T(8,128)S(1)}, f32[136,256]{1,0:T(8,128)S(1)}, u32[]{:S(2)}, u32[]{:S(2)}) collective-permute-start(f32[136,256]{1,0:T(8,128)S(1)} %dynamic-slice_add_fusion), channel_id=1, source_target_pairs={{0,32},{32,0},{64,96},{96,64},{1,33},{33,1},{65,97},{97,65},{2,34}... | collective-permute-start | bytes 417800 | tf_op jit(solution)/shard_map/ppermute | solution.py:496
  95.1 5.5 %copy-start.2 = (bf16[2048,128]{1,0:T(8,128)(2,1)S(1)}, bf16[2048,128]{1,0:T(8,128)(2,1)}, u32[]{:S(2)}) copy-start(bf16[2048,128]{1,0:T(8,128)(2,1)} %rim_scatter.1) | copy-start | bytes 1572868
  95.3 30.1 %collective-permute-start.10 = (bf16[1024,128]{1,0:T(8,128)(2,1)S(1)}, bf16[1024,128]{1,0:T(8,128)(2,1)S(1)}, u32[]{:S(2)}, u32[]{:S(2)}) collective-permute-start(bf16[1024,128]{1,0:T(8,128)(2,1)S(1)} %dynamic-slice_convert_fusion), channel_id=1, source_target_pairs={{0,6},{2,4},{4,2},{6,0},{1,7},{3,5},{5,3},{7,1},{8,14},{10,12},{12... | collective-permute-start | bytes 786440 | tf_op jit(solution)/shard_map/ppermute | solution.py:496
  98.0 27.5 %collective-permute-start.11 = (f32[136,256]{1,0:T(8,128)S(1)}, f32[136,256]{1,0:T(8,128)S(1)}, u32[]{:S(2)}, u32[]{:S(2)}) collective-permute-start(f32[136,256]{1,0:T(8,128)S(1)} %add.90), channel_id=1, source_target_pairs={{0,96},{32,64},{64,32},{96,0},{1,97},{33,65},{65,33},{97,1},{2,98}... | collective-permute-start | bytes 417800 | tf_op jit(solution)/shard_map/ppermute | solution.py:496
  100.7 24.8 %collective-permute-start.12 = (bf16[1024,128]{1,0:T(8,128)(2,1)S(1)}, bf16[1024,128]{1,0:T(8,128)(2,1)S(1)}, u32[]{:S(2)}, u32[]{:S(2)}) collective-permute-start(bf16[1024,128]{1,0:T(8,128)(2,1)S(1)} %get-tuple-element.100), channel_id=1, source_target_pairs={{0,32},{32,64},{64,96},{1,33},{33,65},{65,97},{2,34},{34,66},{66,9... | collective-permute-start | bytes 786440 | tf_op jit(solution)/shard_map/ppermute | solution.py:502
  103.4 22.1 %collective-permute-start.13 = (bf16[1024,128]{1,0:T(8,128)(2,1)S(1)}, bf16[1024,128]{1,0:T(8,128)(2,1)S(1)}, u32[]{:S(2)}, u32[]{:S(2)}) collective-permute-start(bf16[1024,128]{1,0:T(8,128)(2,1)S(1)} %get-tuple-element.99), channel_id=1, source_target_pairs={{32,0},{64,32},{96,64},{33,1},{65,33},{97,65},{34,2},{66,34},{98,6... | collective-permute-start | bytes 786440 | tf_op jit(solution)/shard_map/ppermute | solution.py:502
  125.5 24.8 %copy-start.10 = (bf16[1024,128]{1,0:T(8,128)(2,1)}, bf16[1024,128]{1,0:T(8,128)(2,1)S(1)}, u32[]{:S(2)}) copy-start(bf16[1024,128]{1,0:T(8,128)(2,1)S(1)} %collective-permute-done.12.from_above) | copy-start | bytes 786436
  125.5 24.8 %copy-start.11 = (bf16[1024,128]{1,0:T(8,128)(2,1)}, bf16[1024,128]{1,0:T(8,128)(2,1)S(1)}, u32[]{:S(2)}) copy-start(bf16[1024,128]{1,0:T(8,128)(2,1)S(1)} %collective-permute-done.13.from_below) | copy-start | bytes 786436
  125.6 3.9 %collective-permute-start.14 = (bf16[512,128]{1,0:T(8,128)(2,1)S(1)}, bf16[512,128]{1,0:T(8,128)(2,1)S(1)}, u32[]{:S(2)}, u32[]{:S(2)}) collective-permute-start(bf16[512,128]{1,0:T(8,128)(2,1)S(1)} %dynamic-slice_convert_fusion.1), channel_id=1, source_target_pairs={{0,2},{2,0},{4,6},{6,4},{1,3},{3,1},{5,7},{7,5},{8,10},{10,8},{12,... | collective-permute-start | bytes 393224 | tf_op jit(solution)/shard_map/ppermute | solution.py:496
  125.7 5.2 %collective-permute-start.17 = (f32[136,256]{1,0:T(8,128)S(1)}, f32[136,256]{1,0:T(8,128)S(1)}, u32[]{:S(2)}, u32[]{:S(2)}) collective-permute-start(f32[136,256]{1,0:T(8,128)S(1)} %add.102), channel_id=1, source_target_pairs={{0,6},{2,4},{4,2},{6,0},{1,7},{3,5},{5,3},{7,1},{8,14},{10,12},{12... | collective-permute-start | bytes 417800 | tf_op jit(solution)/shard_map/ppermute | solution.py:496
  129.5 4.4 %collective-permute-start.15 = (bf16[256,128]{1,0:T(8,128)(2,1)S(1)}, bf16[256,128]{1,0:T(8,128)(2,1)S(1)}, u32[]{:S(2)}, u32[]{:S(2)}) collective-permute-start(bf16[256,128]{1,0:T(8,128)(2,1)S(1)} %dynamic-slice_convert_fusion.2), channel_id=1, source_target_pairs={{0,24},{8,16},{16,8},{24,0},{1,25},{9,17},{17,9},{25,1},{2,26},{10... | collective-permute-start | bytes 196616 | tf_op jit(solution)/shard_map/ppermute | solution.py:496
  130.9 4.0 %collective-permute-start.18 = (f32[136,256]{1,0:T(8,128)S(1)}, f32[136,256]{1,0:T(8,128)S(1)}, u32[]{:S(2)}, u32[]{:S(2)}) collective-permute-start(f32[136,256]{1,0:T(8,128)S(1)} %add.103), channel_id=1, source_target_pairs={{0,2},{2,0},{4,6},{6,4},{1,3},{3,1},{5,7},{7,5},{8,10},{10,8},{12,... | collective-permute-start | bytes 417800 | tf_op jit(solution)/shard_map/ppermute | solution.py:496
  134.9 5.2 %collective-permute-start.19 = (f32[136,256]{1,0:T(8,128)S(1)}, f32[136,256]{1,0:T(8,128)S(1)}, u32[]{:S(2)}, u32[]{:S(2)}) collective-permute-start(f32[136,256]{1,0:T(8,128)S(1)} %add.104), channel_id=1, source_target_pairs={{0,24},{8,16},{16,8},{24,0},{1,25},{9,17},{17,9},{25,1},{2,26},{10... | collective-permute-start | bytes 417800 | tf_op jit(solution)/shard_map/ppermute | solution.py:496
  136.4 3.9 %collective-permute-start.16 = (bf16[128,128]{1,0:T(8,128)(2,1)S(1)}, bf16[128,128]{1,0:T(8,128)(2,1)S(1)}, u32[]{:S(2)}, u32[]{:S(2)}) collective-permute-start(bf16[128,128]{1,0:T(8,128)(2,1)S(1)} %dynamic-slice_convert_fusion.3), channel_id=1, source_target_pairs={{0,8},{8,0},{16,24},{24,16},{1,9},{9,1},{17,25},{25,17},{2,10},{10... | collective-permute-start | bytes 98312 | tf_op jit(solution)/shard_map/ppermute | solution.py:496
  140.2 4.5 %collective-permute-start.20 = (f32[136,256]{1,0:T(8,128)S(1)}, f32[136,256]{1,0:T(8,128)S(1)}, u32[]{:S(2)}, u32[]{:S(2)}) collective-permute-start(f32[136,256]{1,0:T(8,128)S(1)} %add.105), channel_id=1, source_target_pairs={{0,8},{8,0},{16,24},{24,16},{1,9},{9,1},{17,25},{25,17},{2,10},{10... | collective-permute-start | bytes 417800 | tf_op jit(solution)/shard_map/ppermute | solution.py:496
  144.7 9.1 %collective-permute-start.21 = (f32[136,256]{1,0:T(8,128)S(1)}, f32[136,256]{1,0:T(8,128)S(1)}, u32[]{:S(2)}, u32[]{:S(2)}) collective-permute-start(f32[136,256]{1,0:T(8,128)S(1)} %add.106), channel_id=1, source_target_pairs={{0,1},{1,0},{2,3},{3,2},{4,5},{5,4},{6,7},{7,6},{8,9},{9,8},{10,11... | collective-permute-start | bytes 417800 | tf_op jit(solution)/shard_map/ppermute | solution.py:496
  (4 other events, 12.2 us)

commit v4 on v3

--- a/solution.py
+++ b/solution.py
@@ -22,11 +22,12 @@
 LANES = 128
 CHAINS = 8
 VMEM_BYTES = 60 * 2**20
+HALF = F + 8
 AXES = ("z", "y", "x", "core")
 
 smem = pl.BlockSpec(memory_space=pltpu.SMEM)
 vmem = pl.BlockSpec(memory_space=pltpu.VMEM)
-hbm = pl.BlockSpec(memory_space=pl.ANY)
+hbm = pl.BlockSpec(memory_space=pltpu.HBM)
 params = pltpu.CompilerParams(vmem_limit_bytes=VMEM_BYTES)
 
 
@@ -158,19 +159,16 @@
     perm[...], ends[...] = order_by(hubs)
 
 
-def rim_plan_kernel(flat, counts, slots, perm, ends, own_counts):
+def rim_plan_kernel(flat, counts, slots, perm, ends, own_perm, own_ends):
     placed = nothing_placed()
-    own_counts[...] = compact(flat, counts[...], is_own, lambda row: row - OWN, False, placed)
+    owns = compact(flat, counts[...], is_own, lambda row: row - OWN, False, placed)
     rims = compact(
         flat, counts[...], is_rim, lambda row: jnp.where(row < OWN, row, row - NODES), True, placed
     )
     for s in range(FANOUT):
         slots[s * ROWS : (s + 1) * ROWS, :] = placed[s]
     perm[...], ends[...] = order_by(rims)
-
-
-def own_plan_kernel(own_counts, perm, ends):
-    perm[...], ends[...] = order_by(own_counts[...])
+    own_perm[...], own_ends[...] = order_by(owns)
 
 
 tile = jax.ShapeDtypeStruct((ROWS, LANES), jnp.int32)
@@ -201,19 +199,21 @@
 
 
 class Lists:
-    def __init__(self, ends, perm, slots, perm_at, *rest):
+    def __init__(self, backwards, ends, perm, slots, perm_at, *rest):
         slots_at, sems = rest[:FANOUT], rest[FANOUT]
         self.ends, self.perm, self.slots = ends, perm_at, slots_at
         self.copies = [pltpu.make_async_copy(perm, perm_at, sems.at[0])]
         for s in range(FANOUT):
             part = slots.at[pl.ds(s * NODES, NODES)]
             self.copies.append(pltpu.make_async_copy(part, slots_at[s], sems.at[1 + s]))
+        if backwards:
+            self.slots = self.slots[::-1]
+            self.copies[1:] = self.copies[:0:-1]
         for copy in self.copies:
             copy.start()
 
-    def visit(self, act, backwards=False):
-        slots = self.slots[::-1] if backwards else self.slots
-        copies = self.copies[:0:-1] if backwards else self.copies[1:]
+    def visit(self, act):
+        slots, copies = self.slots, self.copies[1:]
         self.copies[0].wait()
         for count in range(1, FANOUT + 1):
             copies[count - 1].wait()
@@ -241,7 +241,7 @@
         ref[pl.ds(at + i * step, step), :] = jnp.zeros((step, F), jnp.float32)
 
 
-BLOCK = 256
+BLOCK = 512
 HUB_PIECES = (1, 1, 2, 4, 8, 16)
 
 
@@ -264,7 +264,7 @@
         at += rows
     for copy in copies:
         copy.start()
-    todo = Lists(ends, perm, slots, *lists_at)
+    todo = Lists(False, ends, perm, slots, *lists_at)
     cot_copy = pltpu.make_async_copy(cotangent, cot_at, sem_in.at[9])
     cot_copy.start()
 
@@ -331,10 +331,12 @@
         act_at[cut, :] = (half + rest).astype(jnp.bfloat16)
         slope = (0.5 + 0.5 * t) + (half - rest * t) * (scale + 3 * cubic * squared)
         dz = (cot_at[cut, :].astype(jnp.float32) * slope).astype(jnp.bfloat16)
-        grads[0 : 2 * F, :] += lax.dot_general(
+        products = lax.dot_general(
             both, dz, (((0,), (0,)), ((), ())), preferred_element_type=jnp.float32
         )
-        grads[2 * F : 2 * F + 8, :] += jnp.sum(
+        grads[0:F, :] += products[:F]
+        grads[HALF : HALF + F, :] += products[F:]
+        grads[F:HALF, :] += jnp.sum(
             dz.astype(jnp.float32).reshape(BLOCK // 8, 8, H), axis=0
         )
         back = lax.dot_general(
@@ -356,7 +358,7 @@
             jax.ShapeDtypeStruct((NODES, H), jnp.bfloat16),
             jax.ShapeDtypeStruct((NODES, F), jnp.float32),
             jax.ShapeDtypeStruct((NODES, F), jnp.float32),
-            jax.ShapeDtypeStruct((2 * F + 16, H), jnp.float32),
+            jax.ShapeDtypeStruct((2 * HALF, H), jnp.float32),
         ),
         in_specs=list_specs + [hbm] * (3 + len(hubs)) + [vmem] * 4 + [hbm],
         out_specs=(hbm, hbm, hbm, vmem),
@@ -387,23 +389,23 @@
     return out
 
 
-def scatter_kernel(place, backwards, based, ends, perm, slots, src, *refs):
-    if based:
+def scatter_kernel(kind, ends, perm, slots, src, *refs):
+    if kind == "own":
         base, refs = refs[0], refs[1:]
-    out, refs = refs[0], refs[1:]
-    chains, refs = refs[:CHAINS], refs[CHAINS:]
-    src_at, out_at = refs[:2]
-    lists_at, sems = refs[2:-1], refs[-1]
-    todo = Lists(ends, perm, slots, *lists_at)
+    outs, refs = refs[: 2 if kind == "hub" else 1], refs[2 if kind == "hub" else 1 :]
+    lists_at, (src_at, out_at, sems), chains = refs[: FANOUT + 2], refs[FANOUT + 2 : FANOUT + 5], refs[
+        FANOUT + 5 :
+    ]
+    todo = Lists(kind == "rim", ends, perm, slots, *lists_at)
     src_copy = pltpu.make_async_copy(src, src_at, sems.at[0])
     src_copy.start()
     rows = out_at.shape[0]
-    if based:
+    if kind == "own":
         base_copy = pltpu.make_async_copy(base, chains[0], sems.at[1])
         base_copy.start()
-    for chain in chains[1 if based else 0 :]:
+    for chain in chains[1 if kind == "own" else 0 :]:
         clear(chain, 0, rows)
-    if based:
+    if kind == "own":
         base_copy.wait()
     src_copy.wait()
 
@@ -412,65 +414,71 @@
         for n in nodes:
             row = src_at[pl.ds(n, 1), :]
             for s in range(count):
-                chain = chains[turn % CHAINS]
+                chain = chains[turn % len(chains)]
                 turn += 1
                 at = pl.ds(slots[s][n], 1)
                 chain[at, :] = chain[at, :] + row
 
-    todo.visit(scatter, backwards)
-
-    @pl.loop(0, rows // HUB)
-    def _(i):
-        to = pl.ds(place(i) * HUB, HUB)
-        out_at[to, :] = chain_sum(chains, pl.ds(i * HUB, HUB)).astype(out_at.dtype)
-        pltpu.make_async_copy(out_at.at[to], out.at[to], sems.at[2]).start()
-
-    pltpu.make_async_copy(out_at, out, sems.at[2]).wait()
-
-
-def hub_place(owner):
-    return (owner & 1) * 16 + ((owner >> 1) & 3) * 4 + (owner >> 3)
-
-
-def scatter(name, rows, kind, us, place, backwards, lists, *inputs):
+    todo.visit(scatter)
+
+    part = rows // len(outs)
+    for half, out in enumerate(outs):
+
+        @pl.loop(0, part // HUB)
+        def _(i, half=half, out=out):
+            if kind == "hub":
+                core = lax.axis_index("core") ^ half
+                taken = (((i & 3) * 4) + (i >> 2)) * 2 + core
+            else:
+                taken = i
+            to = pl.ds(i * HUB, HUB)
+            at = pl.ds(half * part + i * HUB, HUB)
+            out_at[at, :] = chain_sum(chains, pl.ds(taken * HUB, HUB)).astype(out_at.dtype)
+            pltpu.make_async_copy(out_at.at[at], out.at[to], sems.at[2 + half]).start()
+
+    for half, out in enumerate(outs):
+        at = pl.ds(half * part, part)
+        pltpu.make_async_copy(out_at.at[at], out, sems.at[2 + half]).wait()
+
+
+def scatter(kind, rows, dtype, us, chains, lists, *inputs):
+    parts = 2 if kind == "hub" else 1
     return pl.pallas_call(
-        functools.partial(scatter_kernel, place, backwards, len(inputs) > 1),
-        out_shape=jax.ShapeDtypeStruct((rows, F), kind),
+        functools.partial(scatter_kernel, kind),
+        out_shape=(jax.ShapeDtypeStruct((rows // parts, F), dtype),) * parts,
         in_specs=list_specs + [hbm] * len(inputs),
-        out_specs=hbm,
-        scratch_shapes=[pltpu.VMEM((rows, F), jnp.float32)] * CHAINS
-        + [pltpu.VMEM((NODES, F), jnp.float32), pltpu.VMEM((rows, F), kind)]
-        + list_scratch
-        + [pltpu.SemaphoreType.DMA((3,))],
+        out_specs=(hbm,) * parts,
+        scratch_shapes=list_scratch
+        + [
+            pltpu.VMEM((NODES, F), jnp.float32),
+            pltpu.VMEM((rows, F), dtype),
+            pltpu.SemaphoreType.DMA((4,)),
+        ]
+        + [pltpu.VMEM((rows, F), jnp.float32)] * chains,
         compiler_params=params,
         cost_estimate=cost(us),
-        name=name,
+        name=kind + "_scatter",
     )(*lists, *inputs)
 
 
-def finish_kernel(hub_rows, own, from_above, from_below, share, out, total):
+def finish_kernel(hub_rows, own, from_above, from_below, share, out, total, sem):
+    copy = pltpu.make_async_copy(own, total, sem)
+    copy.start()
     step = 256
-
-    @pl.loop(0, NODES // step)
-    def _(i):
-        cut = pl.ds(i * step, step)
-        total[cut, :] = own[cut, :]
+    copy.wait()
 
     @pl.loop(0, HALO // step)
     def _(i):
         cut = pl.ds(i * step, step)
         total[cut, :] = total[cut, :] + from_above[cut, :].astype(jnp.float32)
-
-    @pl.loop(0, HALO // step)
+        low = pl.ds(NODES - HALO + i * step, step)
+        total[low, :] = total[low, :] + from_below[cut, :].astype(jnp.float32)
+
+    @pl.loop(0, HUB // 16)
     def _(i):
-        cut = pl.ds(NODES - HALO + i * step, step)
-        total[cut, :] = total[cut, :] + from_below[pl.ds(i * step, step), :].astype(jnp.float32)
-
-    @pl.loop(0, HUB // 8)
-    def _(i):
-        for u in range(8):
-            at = pl.ds(hub_rows[i * 8 + u], 1)
-            total[at, :] = total[at, :] + share[pl.ds(i * 8 + u, 1), :]
+        for u in range(16):
+            at = pl.ds(hub_rows[i * 16 + u], 1)
+            total[at, :] = total[at, :] + share[pl.ds(i * 16 + u, 1), :]
 
     @pl.loop(0, NODES // step)
     def _(i):
@@ -482,9 +490,9 @@
     return pl.pallas_call(
         finish_kernel,
         out_shape=jax.ShapeDtypeStruct((NODES, F), jnp.bfloat16),
-        in_specs=[smem] + [vmem] * 4,
+        in_specs=[smem, hbm] + [vmem] * 3,
         out_specs=vmem,
-        scratch_shapes=[pltpu.VMEM((NODES, F), jnp.float32)],
+        scratch_shapes=[pltpu.VMEM((NODES, F), jnp.float32), pltpu.SemaphoreType.DMA],
         compiler_params=params,
         cost_estimate=cost(3),
         name="finish",
@@ -511,7 +519,10 @@
 
 def halve(value, axis, flip, bit):
     keep, give = halves(value, bit)
-    got = swap(give.astype(jnp.bfloat16), axis, flip)
+    return keep, swap(give.astype(jnp.bfloat16), axis, flip)
+
+
+def plus(keep, got):
     return keep.astype(jnp.float32) + got.astype(jnp.float32)
 
 
@@ -525,28 +536,27 @@
 
     h0 = pick_hubs(hub_rows, features)
     h1 = swap(h0, "y", 1)
+    flat, perm, ends = plan(all_plan_kernel, (tiles, tile, line), 4, neighbors.T, counts)
+    all_lists = lists(perm, ends, flat)
+    h1, flat, features = tie(h1, flat, features)
+    held = jnp.concatenate([h0, h1], axis=0)
+    h2 = swap(held, "y", 3)
     lower = shifted(features[NODES - HALO :], "z", 1)
     upper = shifted(features[:HALO], "z", -1)
-    flat, perm, ends = plan(all_plan_kernel, (tiles, tile, line), 4, neighbors.T, counts)
-    all_lists = lists(perm, ends, flat)
-    h1, flat = tie(h1, flat)
-    held = jnp.concatenate([h0, h1], axis=0)
-    h2 = swap(held, "y", 3)
+    h2, flat = tie(h2, flat)
+    held = jnp.concatenate([held, h2], axis=0)
+    h3 = swap(held, "x", 1)
     slots, perm, ends = plan(hub_plan_kernel, (tiles, tile, line), 4, flat, counts)
     hub_lists = lists(perm, ends, slots)
-    h2, flat, *hub_lists = tie(h2, flat, *hub_lists)
-    held = jnp.concatenate([held, h2], axis=0)
-    h3 = swap(held, "x", 1)
-    slots, perm, ends, own_counts = plan(
-        rim_plan_kernel, (tiles, tile, line, tile), 4, flat, counts
+    h3, lower, upper, flat, *hub_lists = tie(h3, lower, upper, flat, *hub_lists)
+    held = jnp.concatenate([held, h3], axis=0)
+    h4 = swap(held, "x", 3)
+    slots, perm, ends, own_perm, own_ends = plan(
+        rim_plan_kernel, (tiles, tile, line, tile, line), 5, flat, counts
     )
     rim_lists = lists(perm, ends, slots)
-    h3, lower, upper, own_counts, rim_lists = tie(h3, lower, upper, own_counts, rim_lists)
-    held = jnp.concatenate([held, h3], axis=0)
-    h4 = swap(held, "x", 3)
-    perm, ends = plan(own_plan_kernel, (tile, line), 4, own_counts)
-    own_lists = lists(perm, ends, slots)
-    h4, *own_lists = tie(h4, *own_lists)
+    own_lists = lists(own_perm, own_ends, slots)
+    h4, rim_lists, own_lists = tie(h4, rim_lists, own_lists)
     held = jnp.concatenate([held, h4], axis=0)
     h5 = swap(held, "core", 1)
 
@@ -555,41 +565,45 @@
         w_self, w_neigh, out_bias.reshape(1, H), cotangent,
     )
 
-    keep, give = halves(grads, core)
+    other = swap(grads, "z", 1)
+    keep, give = scatter("hub", HUBS, jnp.bfloat16, 8, 6, hub_lists, src)
+    keep, give, src, other = tie(keep, give, src, other)
+    grads = grads + other
+    got = swap(give, "core", 1)
+    other = swap(grads, "z", 3)
+    got, src = tie(got, src)
+    keep, got = halve(plus(keep, got), "x", 3, x // 2)
+    (rim,) = scatter("rim", 2 * HALO, jnp.bfloat16, 8, 6, rim_lists, src)
+    keep, got, src, other, rim = tie(keep, got, src, other, rim)
+
+    grads, give = halves(grads + other, core)
     other = swap(give, "core", 1)
-    hub = scatter("hub_scatter", HUBS, jnp.bfloat16, 8, hub_place, False, hub_lists, src)
-    hub, src, other = tie(hub, src, other)
-    grads = keep + other
-    other = swap(grads, "z", 1)
-    hub = halve(hub, "core", 1, core)
-    rim = scatter(
-        "rim_scatter", 2 * HALO, jnp.bfloat16, 8, lambda i: i, True, rim_lists, src
-    )
-    hub, src, other, rim = tie(hub, src, other, rim)
+    keep, got = halve(plus(keep, got), "x", 1, x % 2)
+    other, src = tie(other, src)
     grads = grads + other
-    other = swap(grads, "z", 3)
-    hub = halve(hub, "x", 3, x // 2)
+    other = swap(grads, "x", 3)
+    (own,) = scatter("own", NODES, jnp.float32, 20, CHAINS, own_lists, src, base)
+    keep, got, other, rim, own = tie(keep, got, other, rim, own)
+
+    keep, got = halve(plus(keep, got), "y", 3, y // 2)
+    grads = grads + other
+    other = swap(grads, "x", 1)
     from_below = shifted(rim[:HALO], "z", -1)
     from_above = shifted(rim[HALO:], "z", 1)
-    own = scatter(
-        "own_scatter", NODES, jnp.float32, 20, lambda i: i, False, own_lists, src, base
-    )
-    hub, other, own, from_above, from_below = tie(hub, other, own, from_above, from_below)
+    keep, got, other, from_below, from_above = tie(keep, got, other, from_below, from_above)
+    keep, got = halve(plus(keep, got), "y", 1, y % 2)
     grads = grads + other
-    grads = grads + swap(grads, "x", 3)
-    hub = halve(hub, "x", 1, x % 2)
-    grads = grads + swap(grads, "x", 1)
-    hub = halve(hub, "y", 3, y // 2)
-    grads = grads + swap(grads, "y", 3)
-    share = halve(hub, "y", 1, y % 2)
-    grads = grads + swap(grads, "y", 1)
+    other = swap(grads, "y", 3)
+    keep, got, other = tie(keep, got, other)
+    grads = grads + other
+    other = swap(grads, "y", 1)
+    grad_features = finish(hub_rows, own, from_above, from_below, plus(keep, got))
+    other, grad_features = tie(other, grad_features)
+    grads = grads + other
     other = swap(grads, "core", 1)
-    grads = jnp.concatenate(
-        [jnp.where(core == 0, grads, other), jnp.where(core == 0, other, grads)], axis=0
-    )
-    grad_features = finish(hub_rows, own, from_above, from_below, share)
-    grad_bias = jnp.sum(grads[2 * F :], axis=0)
-    return act, grad_features, grads[:F], grads[F : 2 * F], grad_bias
+    first = jnp.where(core == 0, grads, other)
+    second = jnp.where(core == 0, other, grads)
+    return act, grad_features, first[:F], second[:F], jnp.sum(first[F:], axis=0)
 
 
 def solution(mesh):

time: 156 us -> 143 us (0.917)
  Pallas kernels: 92.5 us -> 86.6 us
  waiting for transfers between devices: 18.5 us -> 13.6 us
  starting transfers between devices: 37.6 us -> 36 us
    ppermute x18, waiting for transfers between devices: 18.5 us -> 11.1 us  [swap(): return lax.ppermute(value, axis, [(i, i ^ flip) for i in range(count)])]
    pallas_call x1, Pallas kernels: 34.4 us -> 30.8 us  [forward(): pl.pallas_call(forward_kernel, out_shape=(jax.ShapeDtypeStruct((NODES, H)...]
    ppermute x18, starting transfers between devices: 28.7 us -> 25.9 us  [swap(): return lax.ppermute(value, axis, [(i, i ^ flip) for i in range(count)])]
    ppermute x4, waiting for transfers between devices: 0.01 us -> 2.58 us  [shifted(): return lax.ppermute(value, axis, pairs)]
    pallas_call x3, Pallas kernels: 41.7 us -> 39.4 us  [scatter(): pl.pallas_call(functools.partial(scatter_kernel, kind), out_shape=(jax.Sh...]
    dynamic_slice x2 -> x1, local copies, waits for them, and re-layouts: 2.01 us -> 0.02 us  [halves(): give = lax.dynamic_slice_in_dim(value, (1 - bit) * rows, rows, axis=0)]
    pallas_call x4 -> x3, Pallas kernels: 10.7 us -> 9.98 us  [plan(): pl.pallas_call(kernel, out_shape=outs, in_specs=[vmem] * len(inputs), out...]
  transfers between devices with their start and end apart: 22 -> 22, of which waited for: 8 -> 7; matrix products, arithmetic and copies ran while one was open for 1% -> 2% of each run, Pallas kernels for 36% -> 38%
where the time goes in v4:
time: 143 us
  Pallas kernels  86.6 us (61%)
  starting transfers between devices  36 us (25%)
  waiting for transfers between devices  13.6 us (10%)
  other arithmetic  3.38 us (2%)
  local copies, waits for them, and re-layouts  1.86 us (1%)
    pallas_call x3, Pallas kernels, scatter(): pl.pallas_call(functools.partial(scatter_kernel, kind), out_shape=(jax.Sh...  39.4 us
    pallas_call x1, Pallas kernels, forward(): pl.pallas_call(forward_kernel, out_shape=(jax.ShapeDtypeStruct((NODES, H)...  30.8 us
    ppermute x18, starting transfers between devices, swap(): return lax.ppermute(value, axis, [(i, i ^ flip) for i in range(count)])  25.9 us
    ppermute x18, waiting for transfers between devices, swap(): return lax.ppermute(value, axis, [(i, i ^ flip) for i in range(count)])  11.1 us
    ppermute x4, starting transfers between devices, shifted(): return lax.ppermute(value, axis, pairs)  10.1 us
    pallas_call x3, Pallas kernels, plan(): pl.pallas_call(kernel, out_shape=outs, in_specs=[vmem] * len(inputs), out...  9.98 us
    pallas_call x1, Pallas kernels, finish(): pl.pallas_call(finish_kernel, out_shape=jax.ShapeDtypeStruct((NODES, F),...  4.28 us
  transfers between devices with their start and end apart: 22, of which 7 were waited for; matrix products, arithmetic and copies ran while one was open for 2% of the time, Pallas kernels for 38%

profile of v4, /device:TPU:1, one launch (start us, length us, event | category | flops | bytes accessed | tf_op | source)
XLA Modules:
  0.0 142.6 jit_solution(8780830218605561692)
XLA Ops:
  0.6 2.2 %pick_hubs.1.refs_0_ = bf16[128,128]{1,0:T(8,128)(2,1)} custom-call(s32[128]{0:T(128)} %hub_rows.3, bf16[4096,128]{1,0:T(8,128)(2,1)} %features.2), custom_call_target="tpu_custom_call" | custom-call | flops 2000000000 | tf_op jit(solution)/shard_map/pick_hubs/pallas_call | solution.py:57
  2.8 2.1 %collective-permute-start = (bf16[128,128]{1,0:T(8,128)(2,1)}, bf16[128,128]{1,0:T(8,128)(2,1)S(1)}, u32[]{:S(2)}, u32[]{:S(2)}) collective-permute-start(bf16[128,128]{1,0:T(8,128)(2,1)} %pick_hubs.1.refs_0_), channel_id=1, source_target_pairs={{0,8},{8,0},{16,24},{24,16},{1,9},{9,1},{17,25},{25,17},{2,10},{10... | collective-permute-start | bytes 98312 | tf_op jit(solution)/shard_map/ppermute | solution.py:504
  4.9 2.8 %all_plan_kernel.1 = (s32[320,128]{1,0:T(8,128)}, s32[32,128]{1,0:T(8,128)}, s32[1,128]{1,0:T(1,128)}) custom-call(s32[10,4096]{1,0:T(8,128)} %bitcast.14, s32[32,128]{1,0:T(8,128)} %bitcast.15), custom_call_target="tpu_custom_call" | custom-call | flops 4000000000 | tf_op jit(solution)/shard_map/all_plan_kernel/pallas_call | solution.py:180
  7.8 2.0 %collective-permute-start.1 = (bf16[256,128]{1,0:T(8,128)(2,1)S(1)}, bf16[256,128]{1,0:T(8,128)(2,1)S(1)}, u32[]{:S(2)}, u32[]{:S(2)}) collective-permute-start(bf16[256,128]{1,0:T(8,128)(2,1)S(1)} %pad_maximum_fusion.2), channel_id=1, source_target_pairs={{0,24},{8,16},{16,8},{24,0},{1,25},{9,17},{17,9},{25,1},{2,26},{10... | collective-permute-start | bytes 196616 | tf_op jit(solution)/shard_map/ppermute | solution.py:504
  9.8 3.6 %collective-permute-start.3 = (bf16[1024,128]{1,0:T(8,128)(2,1)S(1)}, bf16[1024,128]{1,0:T(8,128)(2,1)S(1)}, u32[]{:S(2)}, u32[]{:S(2)}) collective-permute-start(bf16[1024,128]{1,0:T(8,128)(2,1)S(1)} %get-tuple-element.134), channel_id=1, source_target_pairs={{0,32},{32,64},{64,96},{1,33},{33,65},{65,97},{2,34},{34,66},{66,9... | collective-permute-start | bytes 786440 | tf_op jit(solution)/shard_map/ppermute | solution.py:510
  13.4 1.3 collective-permute-start.4
  14.7 1.3 collective-permute-start.2
  16.0 2.7 %hub_plan_kernel.1 = (s32[320,128]{1,0:T(8,128)}, s32[32,128]{1,0:T(8,128)}, s32[1,128]{1,0:T(1,128)}) custom-call(s32[320,128]{1,0:T(8,128)} %get-tuple-element.83.flat, s32[32,128]{1,0:T(8,128)} %bitcast.16), custom_call_target="tpu_custom_call" | custom-call | flops 4000000000 | tf_op jit(solution)/shard_map/hub_plan_kernel/pallas_call | solution.py:180
  18.8 2.6 %collective-permute-done.4.upper = bf16[1024,128]{1,0:T(8,128)(2,1)S(1)} collective-permute-done((bf16[1024,128]{1,0:T(8,128)(2,1)S(1)}, bf16[1024,128]{1,0:T(8,128)(2,1)S(1)}, u32[]{:S(2)}, u32[]{:S(2)}) %collective-permute-start.4) | collective-permute-done | bytes 262176 | tf_op jit(solution)/shard_map/ppermute | solution.py:510
  21.4 2.6 %collective-permute-start.5 = (bf16[1024,128]{1,0:T(8,128)(2,1)S(1)}, bf16[1024,128]{1,0:T(8,128)(2,1)S(1)}, u32[]{:S(2)}, u32[]{:S(2)}) collective-permute-start(bf16[1024,128]{1,0:T(8,128)(2,1)S(1)} %pad_maximum_fusion), channel_id=1, source_target_pairs={{0,6},{2,4},{4,2},{6,0},{1,7},{3,5},{5,3},{7,1},{8,14},{10,12},{12... | collective-permute-start | bytes 786440 | tf_op jit(solution)/shard_map/ppermute | solution.py:504
  24.0 4.4 %rim_plan_kernel.1 = (s32[320,128]{1,0:T(8,128)}, s32[32,128]{1,0:T(8,128)}, s32[1,128]{1,0:T(1,128)}, s32[32,128]{1,0:T(8,128)}, s32[1,128]{1,0:T(1,128)}) custom-call(s32[320,128]{1,0:T(8,128)} %get-tuple-element.83.flat, s32[32,128]{1,0:T(8,128)} %bitcast.17), custom_call_target="tpu_custom_call" | custom-call | flops 5000000000 | tf_op jit(solution)/shard_map/rim_plan_kernel/pallas_call | solution.py:180
  28.5 3.5 %collective-permute-start.6 = (bf16[2048,128]{1,0:T(8,128)(2,1)S(1)}, bf16[2048,128]{1,0:T(8,128)(2,1)S(1)}, u32[]{:S(2)}, u32[]{:S(2)}) collective-permute-start(bf16[2048,128]{1,0:T(8,128)(2,1)S(1)} %constant_dynamic-update-slice_fusion), channel_id=1, source_target_pairs={{0,1},{1,0},{2,3},{3,2},{4,5},{5,4},{6,7},{7,6},{8,9},{9,8},{10,11... | collective-permute-start | bytes 1572872 | tf_op jit(solution)/shard_map/ppermute | solution.py:504
  32.0 1.5 %collective-permute-done.6.refs_5_ = bf16[2048,128]{1,0:T(8,128)(2,1)S(1)} collective-permute-done((bf16[2048,128]{1,0:T(8,128)(2,1)S(1)}, bf16[2048,128]{1,0:T(8,128)(2,1)S(1)}, u32[]{:S(2)}, u32[]{:S(2)}) %collective-permute-start.6) | collective-permute-done | bytes 524320 | tf_op jit(solution)/shard_map/ppermute | solution.py:504
  34.3 30.8 %forward.1 = (bf16[4096,256]{1,0:T(8,128)(2,1)}, f32[4096,128]{1,0:T(8,128)}, f32[4096,128]{1,0:T(8,128)}, f32[272,256]{1,0:T(8,128)}) custom-call(s32[128]{0:T(128)} %bitcast.30, s32[4096]{0:T(1024)} %bitcast.26, s32[40960]{0:T(1024)} %bitcast.22, bf16[4096,128]{1,0:T(8,128)(2,1)} %features.2, bf16[1024,128]{1,0:T(8,128)(2,1)} %copy-done.9, ...), custom_call_target="tpu_custom_call" | custom-call | flops 30000001024 | tf_op jit(solution)/shard_map/forward/pallas_call | solution.py:355
  65.1 1.4 collective-permute-start.7
  66.5 9.6 %hub_scatter.1 = (bf16[2048,128]{1,0:T(8,128)(2,1)}, bf16[2048,128]{1,0:T(8,128)(2,1)}) custom-call(s32[128]{0:T(128)} %bitcast.31, s32[4096]{0:T(1024)} %bitcast.27, s32[40960]{0:T(1024)} %bitcast.23, f32[4096,128]{1,0:T(8,128)} %get-tuple-element.116.src), custom_call_target="tpu_custom_call" | custom-call | flops 8000000000 | tf_op jit(solution)/shard_map/hub_scatter/pallas_call | solution.py:446
  76.1 1.0 collective-permute-start.8
  77.2 1.7 %collective-permute-start.10 = (f32[272,256]{1,0:T(8,128)S(1)}, f32[272,256]{1,0:T(8,128)S(1)}, u32[]{:S(2)}, u32[]{:S(2)}) collective-permute-start(f32[272,256]{1,0:T(8,128)S(1)} %add.75), channel_id=1, source_target_pairs={{0,96},{32,64},{64,32},{96,0},{1,97},{33,65},{65,33},{97,1},{2,98}... | collective-permute-start | bytes 835592 | tf_op jit(solution)/shard_map/ppermute | solution.py:504
  78.9 1.1 convert_add_fusion
  80.1 3.2 %collective-permute-start.9 = (bf16[1024,128]{1,0:T(8,128)(2,1)S(1)}, bf16[1024,128]{1,0:T(8,128)(2,1)S(1)}, u32[]{:S(2)}, u32[]{:S(2)}) collective-permute-start(bf16[1024,128]{1,0:T(8,128)(2,1)S(1)} %dynamic-slice_convert_fusion), channel_id=1, source_target_pairs={{0,6},{2,4},{4,2},{6,0},{1,7},{3,5},{5,3},{7,1},{8,14},{10,12},{12... | collective-permute-start | bytes 786440 | tf_op jit(solution)/shard_map/ppermute | solution.py:504
  83.2 9.1 %rim_scatter.1 = bf16[2048,128]{1,0:T(8,128)(2,1)} custom-call(s32[128]{0:T(128)} %bitcast.29, s32[4096]{0:T(1024)} %bitcast.25, s32[40960]{0:T(1024)} %bitcast.20, f32[4096,128]{1,0:T(8,128)} %get-tuple-element.116.src), custom_call_target="tpu_custom_call" | custom-call | flops 8000000000 | tf_op jit(solution)/shard_map/rim_scatter/pallas_call | solution.py:446
  94.4 20.7 %own_scatter.1.own = f32[4096,128]{1,0:T(8,128)} custom-call(s32[128]{0:T(128)} %bitcast.28, s32[4096]{0:T(1024)} %bitcast.24, s32[40960]{0:T(1024)} %bitcast.21, f32[4096,128]{1,0:T(8,128)} %get-tuple-element.116.src, f32[4096,128]{1,0:T(8,128)} %get-tuple-element.117.refs_0_), custom_call_target="tpu_custom_call" | custom-call | flops 20000000000 | tf_op jit(solution)/shard_map/own_scatter/pallas_call | solution.py:446
  115.6 1.3 collective-permute-start.16
  116.9 4.0 %collective-permute-start.17 = (bf16[1024,128]{1,0:T(8,128)(2,1)S(1)}, bf16[1024,128]{1,0:T(8,128)(2,1)S(1)}, u32[]{:S(2)}, u32[]{:S(2)}) collective-permute-start(bf16[1024,128]{1,0:T(8,128)(2,1)S(1)} %get-tuple-element.135), channel_id=1, source_target_pairs={{0,32},{32,64},{64,96},{1,33},{33,65},{65,97},{2,34},{34,66},{66,9... | collective-permute-start | bytes 786440 | tf_op jit(solution)/shard_map/ppermute | solution.py:510
  121.0 0.9 collective-permute-start.14
  121.9 3.5 %collective-permute-done.14 = bf16[256,128]{1,0:T(8,128)(2,1)S(1)} collective-permute-done((bf16[256,128]{1,0:T(8,128)(2,1)S(1)}, bf16[256,128]{1,0:T(8,128)(2,1)S(1)}, u32[]{:S(2)}, u32[]{:S(2)}) %collective-permute-start.14) | collective-permute-done | bytes 65568 | tf_op jit(solution)/shard_map/ppermute | solution.py:504
  125.5 0.9 collective-permute-start.19
  126.5 2.7 %collective-permute-done.18 = bf16[128,128]{1,0:T(8,128)(2,1)S(1)} collective-permute-done((bf16[128,128]{1,0:T(8,128)(2,1)S(1)}, bf16[128,128]{1,0:T(8,128)(2,1)S(1)}, u32[]{:S(2)}, u32[]{:S(2)}) %collective-permute-start.18) | collective-permute-done | bytes 32800 | tf_op jit(solution)/shard_map/ppermute | solution.py:504
  129.2 1.5 %collective-permute-done.19 = f32[136,256]{1,0:T(8,128)S(1)} collective-permute-done((f32[136,256]{1,0:T(8,128)S(1)}, f32[136,256]{1,0:T(8,128)S(1)}, u32[]{:S(2)}, u32[]{:S(2)}) %collective-permute-start.19) | collective-permute-done | bytes 139296 | tf_op jit(solution)/shard_map/ppermute | solution.py:504
  131.4 4.3 %finish.1 = bf16[4096,128]{1,0:T(8,128)(2,1)} custom-call(s32[128]{0:T(128)} %hub_rows.3, f32[4096,128]{1,0:T(8,128)} %own_scatter.1.own, bf16[1024,128]{1,0:T(8,128)(2,1)} %copy-done.12, bf16[1024,128]{1,0:T(8,128)(2,1)} %copy-done.11, f32[128,128]{1,0:T(8,128)} %convert_add_fusion.4.share), custom_call_target="tpu_custom_call" | custom-call | flops 3000000000 | tf_op jit(solution)/shard_map/finish/pallas_call | solution.py:490
  135.8 3.9 %collective-permute-start.21 = (f32[136,256]{1,0:T(8,128)S(1)}, f32[136,256]{1,0:T(8,128)S(1)}, u32[]{:S(2)}, u32[]{:S(2)}) collective-permute-start(f32[136,256]{1,0:T(8,128)S(1)} %add.98), channel_id=1, source_target_pairs={{0,1},{1,0},{2,3},{3,2},{4,5},{5,4},{6,7},{7,6},{8,9},{9,8},{10,11... | collective-permute-start | bytes 417800 | tf_op jit(solution)/shard_map/ppermute | solution.py:504
  139.6 1.0 collective-permute-done.21
  (82 shorter events, 6.5 us)
Async XLA Ops:
  2.8 5.0 %collective-permute-start = (bf16[128,128]{1,0:T(8,128)(2,1)}, bf16[128,128]{1,0:T(8,128)(2,1)S(1)}, u32[]{:S(2)}, u32[]{:S(2)}) collective-permute-start(bf16[128,128]{1,0:T(8,128)(2,1)} %pick_hubs.1.refs_0_), channel_id=1, source_target_pairs={{0,8},{8,0},{16,24},{24,16},{1,9},{9,1},{17,25},{25,17},{2,10},{10... | collective-permute-start | bytes 98312 | tf_op jit(solution)/shard_map/ppermute | solution.py:504
  7.8 13.6 %copy-start.4 = (bf16[128,128]{1,0:T(8,128)(2,1)}, bf16[128,128]{1,0:T(8,128)(2,1)S(1)}, u32[]{:S(2)}) copy-start(bf16[128,128]{1,0:T(8,128)(2,1)S(1)} %collective-permute-done.refs_1_) | copy-start | bytes 98308
  7.8 6.9 %collective-permute-start.1 = (bf16[256,128]{1,0:T(8,128)(2,1)S(1)}, bf16[256,128]{1,0:T(8,128)(2,1)S(1)}, u32[]{:S(2)}, u32[]{:S(2)}) collective-permute-start(bf16[256,128]{1,0:T(8,128)(2,1)S(1)} %pad_maximum_fusion.2), channel_id=1, source_target_pairs={{0,24},{8,16},{16,8},{24,0},{1,25},{9,17},{17,9},{25,1},{2,26},{10... | collective-permute-start | bytes 196616 | tf_op jit(solution)/shard_map/ppermute | solution.py:504
  9.8 9.0 %collective-permute-start.3 = (bf16[1024,128]{1,0:T(8,128)(2,1)S(1)}, bf16[1024,128]{1,0:T(8,128)(2,1)S(1)}, u32[]{:S(2)}, u32[]{:S(2)}) collective-permute-start(bf16[1024,128]{1,0:T(8,128)(2,1)S(1)} %get-tuple-element.134), channel_id=1, source_target_pairs={{0,32},{32,64},{64,96},{1,33},{33,65},{65,97},{2,34},{34,66},{66,9... | collective-permute-start | bytes 786440 | tf_op jit(solution)/shard_map/ppermute | solution.py:510
  13.4 8.0 %collective-permute-start.4 = (bf16[1024,128]{1,0:T(8,128)(2,1)S(1)}, bf16[1024,128]{1,0:T(8,128)(2,1)S(1)}, u32[]{:S(2)}, u32[]{:S(2)}) collective-permute-start(bf16[1024,128]{1,0:T(8,128)(2,1)S(1)} %get-tuple-element.133), channel_id=1, source_target_pairs={{32,0},{64,32},{96,64},{33,1},{65,33},{97,65},{34,2},{66,34},{98,6... | collective-permute-start | bytes 786440 | tf_op jit(solution)/shard_map/ppermute | solution.py:510
  14.7 6.7 %copy-start = (bf16[256,128]{1,0:T(8,128)(2,1)}, bf16[256,128]{1,0:T(8,128)(2,1)S(1)}, u32[]{:S(2)}) copy-start(bf16[256,128]{1,0:T(8,128)(2,1)S(1)} %collective-permute-done.1.refs_2_) | copy-start | bytes 196612
  14.7 4.0 %collective-permute-start.2 = (bf16[512,128]{1,0:T(8,128)(2,1)S(1)}, bf16[512,128]{1,0:T(8,128)(2,1)S(1)}, u32[]{:S(2)}, u32[]{:S(2)}) collective-permute-start(bf16[512,128]{1,0:T(8,128)(2,1)S(1)} %pad_maximum_fusion.1), channel_id=1, source_target_pairs={{0,2},{2,0},{4,6},{6,4},{1,3},{3,1},{5,7},{7,5},{8,10},{10,8},{12,... | collective-permute-start | bytes 393224 | tf_op jit(solution)/shard_map/ppermute | solution.py:504
  18.8 9.6 %copy-start.2 = (bf16[512,128]{1,0:T(8,128)(2,1)}, bf16[512,128]{1,0:T(8,128)(2,1)S(1)}, u32[]{:S(2)}) copy-start(bf16[512,128]{1,0:T(8,128)(2,1)S(1)} %collective-permute-done.2.refs_3_) | copy-start | bytes 393220
  18.8 9.6 %copy-start.9 = (bf16[1024,128]{1,0:T(8,128)(2,1)}, bf16[1024,128]{1,0:T(8,128)(2,1)S(1)}, u32[]{:S(2)}) copy-start(bf16[1024,128]{1,0:T(8,128)(2,1)S(1)} %collective-permute-done.3.lower) | copy-start | bytes 786436
  21.4 7.0 %copy-start.10 = (bf16[1024,128]{1,0:T(8,128)(2,1)}, bf16[1024,128]{1,0:T(8,128)(2,1)S(1)}, u32[]{:S(2)}) copy-start(bf16[1024,128]{1,0:T(8,128)(2,1)S(1)} %collective-permute-done.4.upper) | copy-start | bytes 786436
  21.4 7.0 %collective-permute-start.5 = (bf16[1024,128]{1,0:T(8,128)(2,1)S(1)}, bf16[1024,128]{1,0:T(8,128)(2,1)S(1)}, u32[]{:S(2)}, u32[]{:S(2)}) collective-permute-start(bf16[1024,128]{1,0:T(8,128)(2,1)S(1)} %pad_maximum_fusion), channel_id=1, source_target_pairs={{0,6},{2,4},{4,2},{6,0},{1,7},{3,5},{5,3},{7,1},{8,14},{10,12},{12... | collective-permute-start | bytes 786440 | tf_op jit(solution)/shard_map/ppermute | solution.py:504
  28.5 5.1 %copy-start.7 = (bf16[1024,128]{1,0:T(8,128)(2,1)}, bf16[1024,128]{1,0:T(8,128)(2,1)S(1)}, u32[]{:S(2)}) copy-start(bf16[1024,128]{1,0:T(8,128)(2,1)S(1)} %collective-permute-done.5.refs_4_) | copy-start | bytes 786436
  28.5 5.0 %collective-permute-start.6 = (bf16[2048,128]{1,0:T(8,128)(2,1)S(1)}, bf16[2048,128]{1,0:T(8,128)(2,1)S(1)}, u32[]{:S(2)}, u32[]{:S(2)}) collective-permute-start(bf16[2048,128]{1,0:T(8,128)(2,1)S(1)} %constant_dynamic-update-slice_fusion), channel_id=1, source_target_pairs={{0,1},{1,0},{2,3},{3,2},{4,5},{5,4},{6,7},{7,6},{8,9},{9,8},{10,11... | collective-permute-start | bytes 1572872 | tf_op jit(solution)/shard_map/ppermute | solution.py:504
  65.1 11.0 %collective-permute-start.7 = (f32[272,256]{1,0:T(8,128)}, f32[272,256]{1,0:T(8,128)S(1)}, u32[]{:S(2)}, u32[]{:S(2)}) collective-permute-start(f32[272,256]{1,0:T(8,128)} %get-tuple-element.91), channel_id=1, source_target_pairs={{0,32},{32,0},{64,96},{96,64},{1,33},{33,1},{65,97},{97,65},{2,34}... | collective-permute-start | bytes 835592 | tf_op jit(solution)/shard_map/ppermute | solution.py:504
  66.5 10.6 %copy-start.5 = (f32[272,256]{1,0:T(8,128)S(1)}, f32[272,256]{1,0:T(8,128)}, u32[]{:S(2)}) copy-start(f32[272,256]{1,0:T(8,128)} %get-tuple-element.91) | copy-start | bytes 835588
  76.1 2.8 %collective-permute-start.8 = (bf16[2048,128]{1,0:T(8,128)(2,1)}, bf16[2048,128]{1,0:T(8,128)(2,1)S(1)}, u32[]{:S(2)}, u32[]{:S(2)}) collective-permute-start(bf16[2048,128]{1,0:T(8,128)(2,1)} %get-tuple-element.100), channel_id=1, source_target_pairs={{0,1},{1,0},{2,3},{3,2},{4,5},{5,4},{6,7},{7,6},{8,9},{9,8},{10,11... | collective-permute-start | bytes 1572872 | tf_op jit(solution)/shard_map/ppermute | solution.py:504
  77.2 15.2 %collective-permute-start.10 = (f32[272,256]{1,0:T(8,128)S(1)}, f32[272,256]{1,0:T(8,128)S(1)}, u32[]{:S(2)}, u32[]{:S(2)}) collective-permute-start(f32[272,256]{1,0:T(8,128)S(1)} %add.75), channel_id=1, source_target_pairs={{0,96},{32,64},{64,32},{96,0},{1,97},{33,65},{65,33},{97,1},{2,98}... | collective-permute-start | bytes 835592 | tf_op jit(solution)/shard_map/ppermute | solution.py:504
  80.1 12.3 %collective-permute-start.9 = (bf16[1024,128]{1,0:T(8,128)(2,1)S(1)}, bf16[1024,128]{1,0:T(8,128)(2,1)S(1)}, u32[]{:S(2)}, u32[]{:S(2)}) collective-permute-start(bf16[1024,128]{1,0:T(8,128)(2,1)S(1)} %dynamic-slice_convert_fusion), channel_id=1, source_target_pairs={{0,6},{2,4},{4,2},{6,0},{1,7},{3,5},{5,3},{7,1},{8,14},{10,12},{12... | collective-permute-start | bytes 786440 | tf_op jit(solution)/shard_map/ppermute | solution.py:504
  92.5 1.6 %collective-permute-start.11 = (f32[136,256]{1,0:T(8,128)S(1)}, f32[136,256]{1,0:T(8,128)S(1)}, u32[]{:S(2)}, u32[]{:S(2)}) collective-permute-start(f32[136,256]{1,0:T(8,128)S(1)} %constant_dynamic-slice_fusion.3), channel_id=1, source_target_pairs={{0,1},{1,0},{2,3},{3,2},{4,5},{5,4},{6,7},{7,6},{8,9},{9,8},{10,11... | collective-permute-start | bytes 417800 | tf_op jit(solution)/shard_map/ppermute | solution.py:504
  93.2 22.0 %collective-permute-start.12 = (bf16[512,128]{1,0:T(8,128)(2,1)S(1)}, bf16[512,128]{1,0:T(8,128)(2,1)S(1)}, u32[]{:S(2)}, u32[]{:S(2)}) collective-permute-start(bf16[512,128]{1,0:T(8,128)(2,1)S(1)} %dynamic-slice_convert_fusion.1), channel_id=1, source_target_pairs={{0,2},{2,0},{4,6},{6,4},{1,3},{3,1},{5,7},{7,5},{8,10},{10,8},{12,... | collective-permute-start | bytes 393224 | tf_op jit(solution)/shard_map/ppermute | solution.py:504
  94.1 21.1 %collective-permute-start.13 = (f32[136,256]{1,0:T(8,128)S(1)}, f32[136,256]{1,0:T(8,128)S(1)}, u32[]{:S(2)}, u32[]{:S(2)}) collective-permute-start(f32[136,256]{1,0:T(8,128)S(1)} %dynamic-slice_add_fusion), channel_id=1, source_target_pairs={{0,6},{2,4},{4,2},{6,0},{1,7},{3,5},{5,3},{7,1},{8,14},{10,12},{12... | collective-permute-start | bytes 417800 | tf_op jit(solution)/shard_map/ppermute | solution.py:504
  94.4 21.2 %copy-start.1 = (bf16[2048,128]{1,0:T(8,128)(2,1)S(1)}, bf16[2048,128]{1,0:T(8,128)(2,1)}, u32[]{:S(2)}) copy-start(bf16[2048,128]{1,0:T(8,128)(2,1)} %rim_scatter.1) | copy-start | bytes 1572868
  115.2 10.2 %collective-permute-start.15 = (f32[136,256]{1,0:T(8,128)S(1)}, f32[136,256]{1,0:T(8,128)S(1)}, u32[]{:S(2)}, u32[]{:S(2)}) collective-permute-start(f32[136,256]{1,0:T(8,128)S(1)} %add.87), channel_id=1, source_target_pairs={{0,2},{2,0},{4,6},{6,4},{1,3},{3,1},{5,7},{7,5},{8,10},{10,8},{12,... | collective-permute-start | bytes 417800 | tf_op jit(solution)/shard_map/ppermute | solution.py:504
  115.6 9.8 %collective-permute-start.16 = (bf16[1024,128]{1,0:T(8,128)(2,1)S(1)}, bf16[1024,128]{1,0:T(8,128)(2,1)S(1)}, u32[]{:S(2)}, u32[]{:S(2)}) collective-permute-start(bf16[1024,128]{1,0:T(8,128)(2,1)S(1)} %get-tuple-element.136), channel_id=1, source_target_pairs={{32,0},{64,32},{96,64},{33,1},{65,33},{97,65},{34,2},{66,34},{98,6... | collective-permute-start | bytes 786440 | tf_op jit(solution)/shard_map/ppermute | solution.py:510
  116.9 8.5 %collective-permute-start.17 = (bf16[1024,128]{1,0:T(8,128)(2,1)S(1)}, bf16[1024,128]{1,0:T(8,128)(2,1)S(1)}, u32[]{:S(2)}, u32[]{:S(2)}) collective-permute-start(bf16[1024,128]{1,0:T(8,128)(2,1)S(1)} %get-tuple-element.135), channel_id=1, source_target_pairs={{0,32},{32,64},{64,96},{1,33},{33,65},{65,97},{2,34},{34,66},{66,9... | collective-permute-start | bytes 786440 | tf_op jit(solution)/shard_map/ppermute | solution.py:510
  121.0 4.4 %collective-permute-start.14 = (bf16[256,128]{1,0:T(8,128)(2,1)S(1)}, bf16[256,128]{1,0:T(8,128)(2,1)S(1)}, u32[]{:S(2)}, u32[]{:S(2)}) collective-permute-start(bf16[256,128]{1,0:T(8,128)(2,1)S(1)} %dynamic-slice_convert_fusion.2), channel_id=1, source_target_pairs={{0,24},{8,16},{16,8},{24,0},{1,25},{9,17},{17,9},{25,1},{2,26},{10... | collective-permute-start | bytes 196616 | tf_op jit(solution)/shard_map/ppermute | solution.py:504
  125.4 6.0 %copy-start.11 = (bf16[1024,128]{1,0:T(8,128)(2,1)}, bf16[1024,128]{1,0:T(8,128)(2,1)S(1)}, u32[]{:S(2)}) copy-start(bf16[1024,128]{1,0:T(8,128)(2,1)S(1)} %collective-permute-done.16.from_below) | copy-start | bytes 786436
  125.4 6.0 %copy-start.12 = (bf16[1024,128]{1,0:T(8,128)(2,1)}, bf16[1024,128]{1,0:T(8,128)(2,1)S(1)}, u32[]{:S(2)}) copy-start(bf16[1024,128]{1,0:T(8,128)(2,1)S(1)} %collective-permute-done.17.from_above) | copy-start | bytes 786436
  125.5 5.2 %collective-permute-start.19 = (f32[136,256]{1,0:T(8,128)S(1)}, f32[136,256]{1,0:T(8,128)S(1)}, u32[]{:S(2)}, u32[]{:S(2)}) collective-permute-start(f32[136,256]{1,0:T(8,128)S(1)} %add.91), channel_id=1, source_target_pairs={{0,24},{8,16},{16,8},{24,0},{1,25},{9,17},{17,9},{25,1},{2,26},{10... | collective-permute-start | bytes 417800 | tf_op jit(solution)/shard_map/ppermute | solution.py:504
  126.4 2.8 %collective-permute-start.18 = (bf16[128,128]{1,0:T(8,128)(2,1)S(1)}, bf16[128,128]{1,0:T(8,128)(2,1)S(1)}, u32[]{:S(2)}, u32[]{:S(2)}) collective-permute-start(bf16[128,128]{1,0:T(8,128)(2,1)S(1)} %dynamic-slice_convert_fusion.3), channel_id=1, source_target_pairs={{0,8},{8,0},{16,24},{24,16},{1,9},{9,1},{17,25},{25,17},{2,10},{10... | collective-permute-start | bytes 98312 | tf_op jit(solution)/shard_map/ppermute | solution.py:504
  130.7 5.0 %collective-permute-start.20 = (f32[136,256]{1,0:T(8,128)S(1)}, f32[136,256]{1,0:T(8,128)S(1)}, u32[]{:S(2)}, u32[]{:S(2)}) collective-permute-start(f32[136,256]{1,0:T(8,128)S(1)} %add.96), channel_id=1, source_target_pairs={{0,8},{8,0},{16,24},{24,16},{1,9},{9,1},{17,25},{25,17},{2,10},{10... | collective-permute-start | bytes 417800 | tf_op jit(solution)/shard_map/ppermute | solution.py:504
  135.8 4.9 %collective-permute-start.21 = (f32[136,256]{1,0:T(8,128)S(1)}, f32[136,256]{1,0:T(8,128)S(1)}, u32[]{:S(2)}, u32[]{:S(2)}) collective-permute-start(f32[136,256]{1,0:T(8,128)S(1)} %add.98), channel_id=1, source_target_pairs={{0,1},{1,0},{2,3},{3,2},{4,5},{5,4},{6,7},{7,6},{8,9},{9,8},{10,11... | collective-permute-start | bytes 417800 | tf_op jit(solution)/shard_map/ppermute | solution.py:504
  (3 other events, 8.5 us)

commit v5 on v4

--- a/solution.py
+++ b/solution.py
@@ -28,6 +28,7 @@
 smem = pl.BlockSpec(memory_space=pltpu.SMEM)
 vmem = pl.BlockSpec(memory_space=pltpu.VMEM)
 hbm = pl.BlockSpec(memory_space=pltpu.HBM)
+anywhere = pl.BlockSpec(memory_space=pl.ANY)
 params = pltpu.CompilerParams(vmem_limit_bytes=VMEM_BYTES)
 
 
@@ -39,11 +40,33 @@
     return pl.CostEstimate(flops=int(us * 1e9), bytes_accessed=0, transcendentals=0)
 
 
-def hub_kernel(hub_rows, features, out, wide, rows):
-    @pl.loop(0, NODES // 512)
-    def _(i):
-        cut = pl.ds(i * 512, 512)
-        wide[cut, :] = features[cut, :].astype(jnp.float32)
+def faces_up(half):
+    return (lax.axis_index("z") & 1) ^ (1 - half)
+
+
+def hub_kernel(hub_rows, features, out, *refs):
+    rims, (here, wide, rows, sems) = refs[:2], refs[2:]
+    part = NODES // 4
+    copies = []
+    for k in range(4):
+        cut = pl.ds(k * part, part)
+        copies.append(pltpu.make_async_copy(features.at[cut], here.at[cut], sems.at[k]))
+        copies[k].start()
+    for k in range(4):
+        copies[k].wait()
+
+        @pl.loop(0, part // 512)
+        def _(i, k=k):
+            cut = pl.ds(k * part + i * 512, 512)
+            wide[cut, :] = here[cut, :].astype(jnp.float32)
+
+    sends = []
+    for half in range(2):
+        at = pl.multiple_of(faces_up(half) * (NODES - HALO), HALO)
+        sends.append(
+            pltpu.make_async_copy(here.at[pl.ds(at, HALO)], rims[half], sems.at[4 + half])
+        )
+        sends[half].start()
 
     @pl.loop(0, HUB // 16)
     def _(i):
@@ -51,15 +74,23 @@
             rows[pl.ds(i * 16 + u, 1), :] = wide[pl.ds(hub_rows[i * 16 + u], 1), :]
 
     out[...] = rows[...].astype(jnp.bfloat16)
+    for send in sends:
+        send.wait()
 
 
 def pick_hubs(hub_rows, features):
     return pl.pallas_call(
         hub_kernel,
-        out_shape=jax.ShapeDtypeStruct((HUB, F), jnp.bfloat16),
-        in_specs=[smem, vmem],
-        out_specs=vmem,
-        scratch_shapes=[pltpu.VMEM((NODES, F), jnp.float32), pltpu.VMEM((HUB, F), jnp.float32)],
+        out_shape=(jax.ShapeDtypeStruct((HUB, F), jnp.bfloat16),)
+        + (jax.ShapeDtypeStruct((HALO, F), jnp.bfloat16),) * 2,
+        in_specs=[smem, hbm],
+        out_specs=(vmem, hbm, hbm),
+        scratch_shapes=[
+            pltpu.VMEM((NODES, F), jnp.bfloat16),
+            pltpu.VMEM((NODES, F), jnp.float32),
+            pltpu.VMEM((HUB, F), jnp.float32),
+            pltpu.SemaphoreType.DMA((6,)),
+        ],
         compiler_params=params,
         cost_estimate=cost(2),
         name="pick_hubs",
@@ -69,7 +100,7 @@
 ROWS = NODES // LANES
 
 
-def order_by(count):
+def order_by(count, order):
     lane_r = lax.broadcasted_iota(jnp.int32, (LANES, LANES), 0)
     lane_c = lax.broadcasted_iota(jnp.int32, (LANES, LANES), 1)
     before = (lane_r < lane_c).astype(jnp.bfloat16)
@@ -113,7 +144,8 @@
             preferred_element_type=jnp.float32,
         )
         total = total + found[:ROWS] + found[ROWS:] * float(LANES)
-    return total.astype(jnp.int32), end_row.astype(jnp.int32)
+    order[0:ROWS, :] = total.astype(jnp.int32)
+    order[ROWS : ROWS + 8, :] = jnp.broadcast_to(end_row, (8, LANES)).astype(jnp.int32)
 
 
 def compact(flat, count, is_kind, value, backwards, placed):
@@ -141,25 +173,25 @@
     return jnp.logical_or(row < OWN, jnp.logical_and(row >= UPPER, row < HUB_AT))
 
 
-def all_plan_kernel(neighbors, counts, flat, perm, ends):
+def all_plan_kernel(neighbors, counts, flat, order):
     for s in range(FANOUT):
         for r in range(ROWS):
             at = s * ROWS + r
             flat[at : at + 1, :] = neighbors[s : s + 1, r * LANES : (r + 1) * LANES]
-    perm[...], ends[...] = order_by(counts[...])
-
-
-def hub_plan_kernel(flat, counts, slots, perm, ends):
+    order_by(counts[...], order)
+
+
+def hub_plan_kernel(flat, counts, slots, order):
     placed = nothing_placed()
     hubs = compact(
         flat, counts[...], lambda row: row >= HUB_AT, lambda row: row - HUB_AT, False, placed
     )
     for s in range(FANOUT):
         slots[s * ROWS : (s + 1) * ROWS, :] = placed[s]
-    perm[...], ends[...] = order_by(hubs)
-
-
-def rim_plan_kernel(flat, counts, slots, perm, ends, own_perm, own_ends):
+    order_by(hubs, order)
+
+
+def rim_plan_kernel(flat, counts, slots, order, own_order):
     placed = nothing_placed()
     owns = compact(flat, counts[...], is_own, lambda row: row - OWN, False, placed)
     rims = compact(
@@ -167,12 +199,12 @@
     )
     for s in range(FANOUT):
         slots[s * ROWS : (s + 1) * ROWS, :] = placed[s]
-    perm[...], ends[...] = order_by(rims)
-    own_perm[...], own_ends[...] = order_by(owns)
-
-
-tile = jax.ShapeDtypeStruct((ROWS, LANES), jnp.int32)
-line = jax.ShapeDtypeStruct((1, LANES), jnp.int32)
+    order_by(rims, order)
+    order_by(owns, own_order)
+
+
+ORDER = NODES + 8 * LANES
+ordered = jax.ShapeDtypeStruct((ROWS + 8, LANES), jnp.int32)
 tiles = jax.ShapeDtypeStruct((FANOUT * ROWS, LANES), jnp.int32)
 
 
@@ -188,21 +220,21 @@
     )(*inputs)
 
 
-def lists(perm, ends, slots):
-    return ends.reshape(LANES), perm.reshape(NODES), slots.reshape(FANOUT * NODES)
-
-
-list_specs = [smem, hbm, hbm]
-list_scratch = [pltpu.SMEM((NODES,), jnp.int32)] * (1 + FANOUT) + [
+def lists(order, slots):
+    return order.reshape(ORDER), slots.reshape(FANOUT * NODES)
+
+
+list_specs = [hbm, hbm]
+list_scratch = [pltpu.SMEM((ORDER,), jnp.int32)] + [pltpu.SMEM((NODES,), jnp.int32)] * FANOUT + [
     pltpu.SemaphoreType.DMA((1 + FANOUT,))
 ]
 
 
 class Lists:
-    def __init__(self, backwards, ends, perm, slots, perm_at, *rest):
+    def __init__(self, backwards, order, slots, order_at, *rest):
         slots_at, sems = rest[:FANOUT], rest[FANOUT]
-        self.ends, self.perm, self.slots = ends, perm_at, slots_at
-        self.copies = [pltpu.make_async_copy(perm, perm_at, sems.at[0])]
+        self.order, self.slots = order_at, slots_at
+        self.copies = [pltpu.make_async_copy(order, order_at, sems.at[0])]
         for s in range(FANOUT):
             part = slots.at[pl.ds(s * NODES, NODES)]
             self.copies.append(pltpu.make_async_copy(part, slots_at[s], sems.at[1 + s]))
@@ -218,19 +250,19 @@
         for count in range(1, FANOUT + 1):
             copies[count - 1].wait()
             size = group_of(count)
-            first = self.ends[count - 1]
-            last = self.ends[count]
+            first = self.order[NODES + count - 1]
+            last = self.order[NODES + count]
             groups = (last - first) // size
             rest = first + groups * size
 
             @pl.loop(0, groups)
             def _(g, count=count, size=size, first=first):
                 at = first + g * size
-                act([self.perm[at + u] for u in range(size)], count, slots)
+                act([self.order[at + u] for u in range(size)], count, slots)
 
             @pl.loop(rest, last)
             def _(at, count=count):
-                act([self.perm[at]], count, slots)
+                act([self.order[at]], count, slots)
 
 
 def clear(ref, at, rows):
@@ -245,15 +277,16 @@
 HUB_PIECES = (1, 1, 2, 4, 8, 16)
 
 
-def forward_kernel(ends, perm, slots, features, lower, upper, *refs):
+def forward_kernel(order, slots, features, rim_up, rim_down, *refs):
     pieces, refs = refs[:6], refs[6:]
-    counts, w_self, w_neigh, bias, cotangent, act, src, base, grads = refs[:9]
-    table, sums, features_at, rims_at, hubs_at, cot_at, act_at, src_at, base_at, weights = refs[9:19]
-    lists_at, (sem_in, sem_out) = refs[19:-2], refs[-2:]
+    small, cotangent, (act, src, base, grads) = refs[:4], refs[4], refs[5:9]
+    table, sums, features_at, rims_at, hubs_at, cot_at, act_at, src_at, base_at = refs[9:18]
+    small_at, lists_at, (sem_in, sem_out) = refs[18:21], refs[21:-2], refs[-2:]
+    counts, weights, bias = small_at
     copies = [
         pltpu.make_async_copy(features, features_at, sem_in.at[0]),
-        pltpu.make_async_copy(lower, rims_at.at[pl.ds(0, HALO)], sem_in.at[1]),
-        pltpu.make_async_copy(upper, rims_at.at[pl.ds(HALO, HALO)], sem_in.at[2]),
+        pltpu.make_async_copy(rim_up, rims_at.at[pl.ds(0, HALO)], sem_in.at[1]),
+        pltpu.make_async_copy(rim_down, rims_at.at[pl.ds(HALO, HALO)], sem_in.at[2]),
     ]
     at = 0
     for k, piece in enumerate(pieces):
@@ -264,12 +297,14 @@
         at += rows
     for copy in copies:
         copy.start()
-    todo = Lists(False, ends, perm, slots, *lists_at)
+    todo = Lists(False, order, slots, *lists_at)
     cot_copy = pltpu.make_async_copy(cotangent, cot_at, sem_in.at[9])
     cot_copy.start()
-
-    weights[0:F, :] = w_self[...]
-    weights[F : 2 * F, :] = w_neigh[...]
+    to = (counts, weights.at[pl.ds(0, F)], weights.at[pl.ds(F, F)], bias)
+    late = [pltpu.make_async_copy(small[k], to[k], sem_in.at[10 + k]) for k in range(4)]
+    for copy in late:
+        copy.start()
+    late.append(cot_copy)
     grads[...] = jnp.zeros_like(grads)
 
     def widen(source, start, at, rows):
@@ -283,10 +318,9 @@
 
     copies[0].wait()
     widen(features_at, 0, OWN, NODES)
-    copies[1].wait()
-    widen(rims_at, 0, 0, HALO)
-    copies[2].wait()
-    widen(rims_at, HALO, UPPER, HALO)
+    for half in range(2):
+        copies[1 + half].wait()
+        widen(rims_at, half * HALO, pl.multiple_of(faces_up(half) * UPPER, HALO), HALO)
     y, x, core = lax.axis_index("y"), lax.axis_index("x"), lax.axis_index("core")
     position = 0
     for k in range(6):
@@ -309,7 +343,8 @@
             sums[pl.ds(n, 1), :] = total
 
     todo.visit(gather)
-    cot_copy.wait()
+    for copy in late:
+        copy.wait()
 
     @pl.loop(0, NODES // BLOCK)
     def _(i):
@@ -351,7 +386,7 @@
         pltpu.make_async_copy(here, there, sem_out.at[k]).wait()
 
 
-def forward(lists, features, lower, upper, hubs, counts, w_self, w_neigh, bias, cot):
+def forward(lists, features, rims, hubs, counts, w_self, w_neigh, bias, cot):
     return pl.pallas_call(
         forward_kernel,
         out_shape=(
@@ -360,7 +395,7 @@
             jax.ShapeDtypeStruct((NODES, F), jnp.float32),
             jax.ShapeDtypeStruct((2 * HALF, H), jnp.float32),
         ),
-        in_specs=list_specs + [hbm] * (3 + len(hubs)) + [vmem] * 4 + [hbm],
+        in_specs=list_specs + [anywhere] * (3 + len(hubs)) + [hbm] * 5,
         out_specs=(hbm, hbm, hbm, vmem),
         scratch_shapes=[
             pltpu.VMEM((EXTENT, F), jnp.float32),
@@ -372,14 +407,16 @@
             pltpu.VMEM((NODES, H), jnp.bfloat16),
             pltpu.VMEM((NODES, F), jnp.float32),
             pltpu.VMEM((NODES, F), jnp.float32),
+            pltpu.VMEM((ROWS, LANES), jnp.int32),
             pltpu.VMEM((2 * F, H), jnp.bfloat16),
+            pltpu.VMEM((1, H), jnp.float32),
         ]
         + list_scratch
-        + [pltpu.SemaphoreType.DMA((10,)), pltpu.SemaphoreType.DMA((3,))],
-        compiler_params=params,
+        + [pltpu.SemaphoreType.DMA((14,)), pltpu.SemaphoreType.DMA((3,))],
+        compiler_params=pltpu.CompilerParams(vmem_limit_bytes=40 * 2**20),
         cost_estimate=cost(30),
         name="forward",
-    )(*lists, features, lower, upper, *hubs, counts, w_self, w_neigh, bias, cot)
+    )(*lists, features, *rims, *hubs, counts, w_self, w_neigh, bias, cot)
 
 
 def chain_sum(chains, cut):
@@ -389,14 +426,15 @@
     return out
 
 
-def scatter_kernel(kind, ends, perm, slots, src, *refs):
+def scatter_kernel(kind, order, slots, src, *refs):
     if kind == "own":
         base, refs = refs[0], refs[1:]
-    outs, refs = refs[: 2 if kind == "hub" else 1], refs[2 if kind == "hub" else 1 :]
+    parts = 1 if kind == "own" else 2
+    outs, refs = refs[:parts], refs[parts:]
     lists_at, (src_at, out_at, sems), chains = refs[: FANOUT + 2], refs[FANOUT + 2 : FANOUT + 5], refs[
         FANOUT + 5 :
     ]
-    todo = Lists(kind == "rim", ends, perm, slots, *lists_at)
+    todo = Lists(kind == "rim", order, slots, *lists_at)
     src_copy = pltpu.make_async_copy(src, src_at, sems.at[0])
     src_copy.start()
     rows = out_at.shape[0]
@@ -429,6 +467,8 @@
             if kind == "hub":
                 core = lax.axis_index("core") ^ half
                 taken = (((i & 3) * 4) + (i >> 2)) * 2 + core
+            elif kind == "rim":
+                taken = i + faces_up(half) * (HALO // HUB)
             else:
                 taken = i
             to = pl.ds(i * HUB, HUB)
@@ -442,7 +482,7 @@
 
 
 def scatter(kind, rows, dtype, us, chains, lists, *inputs):
-    parts = 2 if kind == "hub" else 1
+    parts = 1 if kind == "own" else 2
     return pl.pallas_call(
         functools.partial(scatter_kernel, kind),
         out_shape=(jax.ShapeDtypeStruct((rows // parts, F), dtype),) * parts,
@@ -461,42 +501,59 @@
     )(*lists, *inputs)
 
 
-def finish_kernel(hub_rows, own, from_above, from_below, share, out, total, sem):
-    copy = pltpu.make_async_copy(own, total, sem)
-    copy.start()
+def finish_kernel(hub_rows, own, rim_0, rim_1, share, out, total, rims, share_at, out_at, rows, sems):
+    to = (total, rims.at[pl.ds(0, HALO)], rims.at[pl.ds(HALO, HALO)], share_at, rows)
+    copies = [
+        pltpu.make_async_copy(source, to[k], sems.at[k])
+        for k, source in enumerate((own, rim_0, rim_1, share, hub_rows))
+    ]
+    for copy in copies:
+        copy.start()
+    for copy in copies:
+        copy.wait()
     step = 256
-    copy.wait()
-
-    @pl.loop(0, HALO // step)
-    def _(i):
-        cut = pl.ds(i * step, step)
-        total[cut, :] = total[cut, :] + from_above[cut, :].astype(jnp.float32)
-        low = pl.ds(NODES - HALO + i * step, step)
-        total[low, :] = total[low, :] + from_below[cut, :].astype(jnp.float32)
+    for half in range(2):
+        start = pl.multiple_of(faces_up(half) * (NODES - HALO), HALO)
+
+        @pl.loop(0, HALO // step)
+        def _(i, half=half, start=start):
+            cut = pl.ds(start + i * step, step)
+            rim = rims[pl.ds(half * HALO + i * step, step), :]
+            total[cut, :] = total[cut, :] + rim.astype(jnp.float32)
 
     @pl.loop(0, HUB // 16)
     def _(i):
         for u in range(16):
-            at = pl.ds(hub_rows[i * 16 + u], 1)
-            total[at, :] = total[at, :] + share[pl.ds(i * 16 + u, 1), :]
-
-    @pl.loop(0, NODES // step)
+            at = pl.ds(rows[i * 16 + u], 1)
+            total[at, :] = total[at, :] + share_at[pl.ds(i * 16 + u, 1), :]
+
+    @pl.loop(0, NODES // 512)
     def _(i):
-        cut = pl.ds(i * step, step)
-        out[cut, :] = total[cut, :].astype(jnp.bfloat16)
-
-
-def finish(hub_rows, own, from_above, from_below, share):
+        cut = pl.ds(i * 512, 512)
+        out_at[cut, :] = total[cut, :].astype(jnp.bfloat16)
+        pltpu.make_async_copy(out_at.at[cut], out.at[cut], sems.at[5]).start()
+
+    pltpu.make_async_copy(out_at, out, sems.at[5]).wait()
+
+
+def finish(hub_rows, own, rim_0, rim_1, share):
     return pl.pallas_call(
         finish_kernel,
         out_shape=jax.ShapeDtypeStruct((NODES, F), jnp.bfloat16),
-        in_specs=[smem, hbm] + [vmem] * 3,
-        out_specs=vmem,
-        scratch_shapes=[pltpu.VMEM((NODES, F), jnp.float32), pltpu.SemaphoreType.DMA],
-        compiler_params=params,
+        in_specs=[anywhere] * 5,
+        out_specs=hbm,
+        scratch_shapes=[
+            pltpu.VMEM((NODES, F), jnp.float32),
+            pltpu.VMEM((2 * HALO, F), jnp.bfloat16),
+            pltpu.VMEM((HUB, F), jnp.float32),
+            pltpu.VMEM((NODES, F), jnp.bfloat16),
+            pltpu.SMEM((HUB,), jnp.int32),
+            pltpu.SemaphoreType.DMA((6,)),
+        ],
+        compiler_params=pltpu.CompilerParams(vmem_limit_bytes=16 * 2**20),
         cost_estimate=cost(3),
         name="finish",
-    )(hub_rows, own, from_above, from_below, share)
+    )(hub_rows, own, rim_0, rim_1, share)
 
 
 def swap(value, axis, flip):
@@ -504,10 +561,9 @@
     return lax.ppermute(value, axis, [(i, i ^ flip) for i in range(count)])
 
 
-def shifted(value, axis, by):
-    count = lax.axis_size(axis)
-    pairs = [(i, i + by) for i in range(count) if 0 <= i + by < count]
-    return lax.ppermute(value, axis, pairs)
+def swap_rims(first, second):
+    above = lax.ppermute(first, "z", [(0, 1), (1, 0), (2, 3), (3, 2)])
+    return above, lax.ppermute(second, "z", [(1, 2), (2, 1)])
 
 
 def halves(value, bit):
@@ -517,9 +573,11 @@
     return keep, give
 
 
-def halve(value, axis, flip, bit):
-    keep, give = halves(value, bit)
-    return keep, swap(give.astype(jnp.bfloat16), axis, flip)
+def halve(keep, got, axis, flip, bit):
+    mine, other_mine = halves(keep, bit)
+    theirs, other_theirs = halves(got, bit)
+    give = (other_mine.astype(jnp.float32) + other_theirs.astype(jnp.float32)).astype(jnp.bfloat16)
+    return plus(mine, theirs), swap(give, axis, flip)
 
 
 def plus(keep, got):
@@ -534,34 +592,31 @@
     x, y, core = lax.axis_index("x"), lax.axis_index("y"), lax.axis_index("core")
     counts = counts.reshape(ROWS, LANES)
 
-    h0 = pick_hubs(hub_rows, features)
+    h0, *rims = pick_hubs(hub_rows, features)
     h1 = swap(h0, "y", 1)
-    flat, perm, ends = plan(all_plan_kernel, (tiles, tile, line), 4, neighbors.T, counts)
-    all_lists = lists(perm, ends, flat)
-    h1, flat, features = tie(h1, flat, features)
+    flat, order = plan(all_plan_kernel, (tiles, ordered), 4, neighbors.T, counts)
+    all_lists = lists(order, flat)
+    h1, flat = tie(h1, flat)
     held = jnp.concatenate([h0, h1], axis=0)
     h2 = swap(held, "y", 3)
-    lower = shifted(features[NODES - HALO :], "z", 1)
-    upper = shifted(features[:HALO], "z", -1)
-    h2, flat = tie(h2, flat)
+    slots, order = plan(hub_plan_kernel, (tiles, ordered), 4, flat, counts)
+    hub_lists = lists(order, slots)
+    h2, flat, hub_lists, *rims = tie(h2, flat, hub_lists, *rims)
     held = jnp.concatenate([held, h2], axis=0)
     h3 = swap(held, "x", 1)
-    slots, perm, ends = plan(hub_plan_kernel, (tiles, tile, line), 4, flat, counts)
-    hub_lists = lists(perm, ends, slots)
-    h3, lower, upper, flat, *hub_lists = tie(h3, lower, upper, flat, *hub_lists)
+    rims = swap_rims(*rims)
+    h3, flat = tie(h3, flat)
     held = jnp.concatenate([held, h3], axis=0)
     h4 = swap(held, "x", 3)
-    slots, perm, ends, own_perm, own_ends = plan(
-        rim_plan_kernel, (tiles, tile, line, tile, line), 5, flat, counts
-    )
-    rim_lists = lists(perm, ends, slots)
-    own_lists = lists(own_perm, own_ends, slots)
-    h4, rim_lists, own_lists = tie(h4, rim_lists, own_lists)
+    slots, order, own_order = plan(rim_plan_kernel, (tiles, ordered, ordered), 5, flat, counts)
+    rim_lists = lists(order, slots)
+    own_lists = lists(own_order, slots)
+    h4, rim_lists, own_lists, *rims = tie(h4, rim_lists, own_lists, *rims)
     held = jnp.concatenate([held, h4], axis=0)
     h5 = swap(held, "core", 1)
 
     act, src, base, grads = forward(
-        all_lists, features, lower, upper, (h0, h1, h2, h3, h4, h5), counts,
+        all_lists, features, rims, (h0, h1, h2, h3, h4, h5), counts,
         w_self, w_neigh, out_bias.reshape(1, H), cotangent,
     )
 
@@ -572,32 +627,31 @@
     got = swap(give, "core", 1)
     other = swap(grads, "z", 3)
     got, src = tie(got, src)
-    keep, got = halve(plus(keep, got), "x", 3, x // 2)
-    (rim,) = scatter("rim", 2 * HALO, jnp.bfloat16, 8, 6, rim_lists, src)
-    keep, got, src, other, rim = tie(keep, got, src, other, rim)
+    keep, got = halve(keep, got, "x", 3, x // 2)
+    rims = scatter("rim", 2 * HALO, jnp.bfloat16, 8, 6, rim_lists, src)
+    keep, got, src, other, *rims = tie(keep, got, src, other, *rims)
 
     grads, give = halves(grads + other, core)
     other = swap(give, "core", 1)
-    keep, got = halve(plus(keep, got), "x", 1, x % 2)
+    keep, got = halve(keep, got, "x", 1, x % 2)
     other, src = tie(other, src)
     grads = grads + other
     other = swap(grads, "x", 3)
+    rims = swap_rims(*rims)
     (own,) = scatter("own", NODES, jnp.float32, 20, CHAINS, own_lists, src, base)
-    keep, got, other, rim, own = tie(keep, got, other, rim, own)
-
-    keep, got = halve(plus(keep, got), "y", 3, y // 2)
+    keep, got, other, own, *rims = tie(keep, got, other, own, *rims)
+
+    keep, got = halve(keep, got, "y", 3, y // 2)
     grads = grads + other
     other = swap(grads, "x", 1)
-    from_below = shifted(rim[:HALO], "z", -1)
-    from_above = shifted(rim[HALO:], "z", 1)
-    keep, got, other, from_below, from_above = tie(keep, got, other, from_below, from_above)
-    keep, got = halve(plus(keep, got), "y", 1, y % 2)
+    keep, got, other = tie(keep, got, other)
+    keep, got = halve(keep, got, "y", 1, y % 2)
     grads = grads + other
     other = swap(grads, "y", 3)
     keep, got, other = tie(keep, got, other)
     grads = grads + other
     other = swap(grads, "y", 1)
-    grad_features = finish(hub_rows, own, from_above, from_below, plus(keep, got))
+    grad_features = finish(hub_rows, own, *rims, plus(keep, got))
     other, grad_features = tie(other, grad_features)
     grads = grads + other
     other = swap(grads, "core", 1)

time: 143 us -> 144 us (level)
  local copies, waits for them, and re-layouts: 1.86 us -> 10.7 us
  Pallas kernels: 86.6 us -> 82.8 us
  waiting for transfers between devices: 13.6 us -> 10.8 us
  starting transfers between devices: 36 us -> 33.6 us
    unnamed x30 -> x38, local copies, waits for them, and re-layouts: 0.89 us -> 9.23 us
    ppermute x4, starting transfers between devices: 10.1 us -> 3.78 us  [the longest x2 2.05 us: swap_rims(): return (above, lax.ppermute(second, 'z', [(1, 2), (2, 1)]))]
    ppermute x18, starting transfers between devices: 25.9 us -> 29.8 us  [swap(): return lax.ppermute(value, axis, [(i, i ^ flip) for i in range(count)])]
    ppermute x4, waiting for transfers between devices: 2.58 us -> 0.01 us  [the longest x2 0.01 us: swap_rims(): return (above, lax.ppermute(second, 'z', [(1, 2), (2, 1)]))]
    pallas_call x3, Pallas kernels: 39.4 us -> 37.2 us  [scatter(): pl.pallas_call(functools.partial(scatter_kernel, kind), out_shape=(jax.Sh...]
    pallas_call x1, Pallas kernels: 4.28 us -> 2.27 us  [finish(): pl.pallas_call(finish_kernel, out_shape=jax.ShapeDtypeStruct((NODES, F),...]
    add x5 -> x1, other arithmetic: 1.89 us -> 0.01 us  [plus(): return keep.astype(jnp.float32) + got.astype(jnp.float32)]
  transfers between devices with their start and end apart: 22 -> 22, of which waited for: 7 -> 8; matrix products, arithmetic and copies ran while one was open for 2% -> 3% of each run, Pallas kernels for 38% -> 35%
where the time goes in v5:
time: 144 us; the launch traced here: 142 us
  Pallas kernels  82.8 us (58%)
  starting transfers between devices  33.6 us (23%)
  waiting for transfers between devices  10.8 us (8%)
  local copies, waits for them, and re-layouts  10.7 us (7%)
  other arithmetic  3.46 us (2%)
    pallas_call x3, Pallas kernels, scatter(): pl.pallas_call(functools.partial(scatter_kernel, kind), out_shape=(jax.Sh...  37.2 us
    pallas_call x1, Pallas kernels, forward(): pl.pallas_call(forward_kernel, out_shape=(jax.ShapeDtypeStruct((NODES, H)...  30.1 us
    ppermute x18, starting transfers between devices, swap(): return lax.ppermute(value, axis, [(i, i ^ flip) for i in range(count)])  29.8 us
    ppermute x18, waiting for transfers between devices, swap(): return lax.ppermute(value, axis, [(i, i ^ flip) for i in range(count)])  10.8 us
    pallas_call x3, Pallas kernels, plan(): pl.pallas_call(kernel, out_shape=outs, in_specs=[vmem] * len(inputs), out...  9.89 us
    unnamed x38, local copies, waits for them, and re-layouts  9.23 us
    pallas_call x1, Pallas kernels, pick_hubs(): pl.pallas_call(hub_kernel, out_shape=(jax.ShapeDtypeStruct((HUB, F), jnp....  3.36 us
  transfers between devices with their start and end apart: 22, of which 8 were waited for; matrix products, arithmetic and copies ran while one was open for 3% of the time, Pallas kernels for 35%

profile of v5, /device:TPU:1, one launch (start us, length us, event | category | flops | bytes accessed | tf_op | source)
XLA Modules:
  0.0 142.3 jit_solution(14186288831254822872)
XLA Ops:
  0.6 3.4 %pick_hubs.1 = (bf16[128,128]{1,0:T(8,128)(2,1)}, bf16[1024,128]{1,0:T(8,128)(2,1)}, bf16[1024,128]{1,0:T(8,128)(2,1)}) custom-call(s32[128]{0:T(128)} %hub_rows.3, bf16[4096,128]{1,0:T(8,128)(2,1)} %features.3), custom_call_target="tpu_custom_call" | custom-call | flops 2000000000 | tf_op jit(solution)/shard_map/pick_hubs/pallas_call | solution.py:82
  4.0 2.2 %collective-permute-start = (bf16[128,128]{1,0:T(8,128)(2,1)}, bf16[128,128]{1,0:T(8,128)(2,1)S(1)}, u32[]{:S(2)}, u32[]{:S(2)}) collective-permute-start(bf16[128,128]{1,0:T(8,128)(2,1)} %get-tuple-element.70.refs_0_), channel_id=1, source_target_pairs={{0,8},{8,0},{16,24},{24,16},{1,9},{9,1},{17,25},{25,17},{2,10},{10... | collective-permute-start | bytes 98312 | tf_op jit(solution)/shard_map/ppermute | solution.py:561
  6.2 2.7 %all_plan_kernel.1 = (s32[320,128]{1,0:T(8,128)}, s32[40,128]{1,0:T(8,128)}) custom-call(s32[10,4096]{1,0:T(8,128)} %bitcast.17, s32[32,128]{1,0:T(8,128)} %bitcast.10), custom_call_target="tpu_custom_call" | custom-call | flops 4000000000 | tf_op jit(solution)/shard_map/all_plan_kernel/pallas_call | solution.py:212
  9.6 2.0 %collective-permute-start.1 = (bf16[256,128]{1,0:T(8,128)(2,1)S(1)}, bf16[256,128]{1,0:T(8,128)(2,1)S(1)}, u32[]{:S(2)}, u32[]{:S(2)}) collective-permute-start(bf16[256,128]{1,0:T(8,128)(2,1)S(1)} %pad_maximum_fusion.2), channel_id=1, source_target_pairs={{0,24},{8,16},{16,8},{24,0},{1,25},{9,17},{17,9},{25,1},{2,26},{10... | collective-permute-start | bytes 196616 | tf_op jit(solution)/shard_map/ppermute | solution.py:561
  11.6 2.7 %hub_plan_kernel.1 = (s32[320,128]{1,0:T(8,128)}, s32[40,128]{1,0:T(8,128)}) custom-call(s32[320,128]{1,0:T(8,128)} %get-tuple-element.80.flat, s32[32,128]{1,0:T(8,128)} %bitcast.11), custom_call_target="tpu_custom_call" | custom-call | flops 4000000000 | tf_op jit(solution)/shard_map/hub_plan_kernel/pallas_call | solution.py:212
  14.3 1.3 collective-permute-start.2
  16.2 1.6 %collective-permute-start.4 = (bf16[1024,128]{1,0:T(8,128)(2,1)}, bf16[1024,128]{1,0:T(8,128)(2,1)S(1)}, u32[]{:S(2)}, u32[]{:S(2)}) collective-permute-start(bf16[1024,128]{1,0:T(8,128)(2,1)} %get-tuple-element.84), channel_id=1, source_target_pairs={{0,32},{32,0},{64,96},{96,64},{1,33},{33,1},{65,97},{97,65},{2,34}... | collective-permute-start | bytes 786440 | tf_op jit(solution)/shard_map/ppermute | solution.py:565
  17.8 1.4 collective-permute-start.5
  20.6 1.9 %collective-permute-start.3 = (bf16[1024,128]{1,0:T(8,128)(2,1)}, bf16[1024,128]{1,0:T(8,128)(2,1)S(1)}, u32[]{:S(2)}, u32[]{:S(2)}) collective-permute-start(bf16[1024,128]{1,0:T(8,128)(2,1)} %pad_maximum_fusion), channel_id=1, source_target_pairs={{0,6},{2,4},{4,2},{6,0},{1,7},{3,5},{5,3},{7,1},{8,14},{10,12},{12... | collective-permute-start | bytes 786440 | tf_op jit(solution)/shard_map/ppermute | solution.py:561
  22.5 4.4 %rim_plan_kernel.1 = (s32[320,128]{1,0:T(8,128)}, s32[40,128]{1,0:T(8,128)}, s32[40,128]{1,0:T(8,128)}) custom-call(s32[320,128]{1,0:T(8,128)} %get-tuple-element.80.flat, s32[32,128]{1,0:T(8,128)} %bitcast.12), custom_call_target="tpu_custom_call" | custom-call | flops 5000000000 | tf_op jit(solution)/shard_map/rim_plan_kernel/pallas_call | solution.py:212
  28.4 3.2 %collective-permute-start.6 = (bf16[2048,128]{1,0:T(8,128)(2,1)}, bf16[2048,128]{1,0:T(8,128)(2,1)S(1)}, u32[]{:S(2)}, u32[]{:S(2)}) collective-permute-start(bf16[2048,128]{1,0:T(8,128)(2,1)} %constant_dynamic-update-slice_fusion), channel_id=1, source_target_pairs={{0,1},{1,0},{2,3},{3,2},{4,5},{5,4},{6,7},{7,6},{8,9},{9,8},{10,11... | collective-permute-start | bytes 1572872 | tf_op jit(solution)/shard_map/ppermute | solution.py:561
  31.6 1.7 %collective-permute-done.6.refs_5_ = bf16[2048,128]{1,0:T(8,128)(2,1)S(1)} collective-permute-done((bf16[2048,128]{1,0:T(8,128)(2,1)}, bf16[2048,128]{1,0:T(8,128)(2,1)S(1)}, u32[]{:S(2)}, u32[]{:S(2)}) %collective-permute-start.6) | collective-permute-done | bytes 524320 | tf_op jit(solution)/shard_map/ppermute | solution.py:561
  37.3 30.1 %forward.1 = (bf16[4096,256]{1,0:T(8,128)(2,1)}, f32[4096,128]{1,0:T(8,128)S(1)}, f32[4096,128]{1,0:T(8,128)S(1)}, f32[272,256]{1,0:T(8,128)S(1)}) custom-call(s32[5120]{0:T(1024)S(1)} %bitcast.16, s32[40960]{0:T(1024)S(1)} %bitcast.15, bf16[4096,128]{1,0:T(8,128)(2,1)S(1)} %copy-done.2, bf16[1024,128]{1,0:T(8,128)(2,1)S(1)} %copy-done.4, ...), custom_call_target="tpu_custom_call" | custom-call | flops 30000001024 | tf_op jit(solution)/shard_map/forward/pallas_call | solution.py:390
  67.4 1.3 copy-done.13
  68.8 1.3 copy-done.14
  70.1 3.7 %collective-permute-start.7 = (f32[272,256]{1,0:T(8,128)S(1)}, f32[272,256]{1,0:T(8,128)S(1)}, u32[]{:S(2)}, u32[]{:S(2)}) collective-permute-start(f32[272,256]{1,0:T(8,128)S(1)} %get-tuple-element.90), channel_id=1, source_target_pairs={{0,32},{32,0},{64,96},{96,64},{1,33},{33,1},{65,97},{97,65},{2,34}... | collective-permute-start | bytes 835592 | tf_op jit(solution)/shard_map/ppermute | solution.py:561
  73.8 9.1 %hub_scatter.1 = (bf16[2048,128]{1,0:T(8,128)(2,1)}, bf16[2048,128]{1,0:T(8,128)(2,1)}) custom-call(s32[5120]{0:T(1024)} %bitcast.23, s32[40960]{0:T(1024)} %bitcast.20, f32[4096,128]{1,0:T(8,128)} %copy-done.13), custom_call_target="tpu_custom_call" | custom-call | flops 8000000000 | tf_op jit(solution)/shard_map/hub_scatter/pallas_call | solution.py:486
  84.3 1.2 collective-permute-done.8
  85.4 1.2 add_convert_fusion
  86.6 2.0 %collective-permute-start.9 = (bf16[1024,128]{1,0:T(8,128)(2,1)S(1)}, bf16[1024,128]{1,0:T(8,128)(2,1)S(1)}, u32[]{:S(2)}, u32[]{:S(2)}) collective-permute-start(bf16[1024,128]{1,0:T(8,128)(2,1)S(1)} %get-tuple-element.131), channel_id=1, source_target_pairs={{0,6},{2,4},{4,2},{6,0},{1,7},{3,5},{5,3},{7,1},{8,14},{10,12},{12... | collective-permute-start | bytes 786440 | tf_op jit(solution)/shard_map/ppermute | solution.py:561
  88.5 8.4 %rim_scatter.1 = (bf16[1024,128]{1,0:T(8,128)(2,1)}, bf16[1024,128]{1,0:T(8,128)(2,1)}) custom-call(s32[5120]{0:T(1024)} %bitcast.22, s32[40960]{0:T(1024)} %bitcast.18, f32[4096,128]{1,0:T(8,128)} %copy-done.13), custom_call_target="tpu_custom_call" | custom-call | flops 8000000000 | tf_op jit(solution)/shard_map/rim_scatter/pallas_call | solution.py:486
  98.9 1.2 collective-permute-start.13
  100.1 19.6 %own_scatter.1.own = f32[4096,128]{1,0:T(8,128)} custom-call(s32[5120]{0:T(1024)} %bitcast.21, s32[40960]{0:T(1024)} %bitcast.19, f32[4096,128]{1,0:T(8,128)} %copy-done.13, f32[4096,128]{1,0:T(8,128)} %copy-done.14), custom_call_target="tpu_custom_call" | custom-call | flops 20000000000 | tf_op jit(solution)/shard_map/own_scatter/pallas_call | solution.py:486
  119.8 1.0 collective-permute-start.17
  120.9 2.2 %collective-permute-start.16 = (bf16[256,128]{1,0:T(8,128)(2,1)S(1)}, bf16[256,128]{1,0:T(8,128)(2,1)S(1)}, u32[]{:S(2)}, u32[]{:S(2)}) collective-permute-start(bf16[256,128]{1,0:T(8,128)(2,1)S(1)} %get-tuple-element.135), channel_id=1, source_target_pairs={{0,24},{8,16},{16,8},{24,0},{1,25},{9,17},{17,9},{25,1},{2,26},{10... | collective-permute-start | bytes 196616 | tf_op jit(solution)/shard_map/ppermute | solution.py:561
  123.1 2.2 %collective-permute-done.16 = bf16[256,128]{1,0:T(8,128)(2,1)S(1)} collective-permute-done((bf16[256,128]{1,0:T(8,128)(2,1)S(1)}, bf16[256,128]{1,0:T(8,128)(2,1)S(1)}, u32[]{:S(2)}, u32[]{:S(2)}) %collective-permute-start.16) | collective-permute-done | bytes 65568 | tf_op jit(solution)/shard_map/ppermute | solution.py:561
  125.3 2.2 %collective-permute-start.19 = (f32[136,256]{1,0:T(8,128)S(1)}, f32[136,256]{1,0:T(8,128)S(1)}, u32[]{:S(2)}, u32[]{:S(2)}) collective-permute-start(f32[136,256]{1,0:T(8,128)S(1)} %add.114), channel_id=1, source_target_pairs={{0,24},{8,16},{16,8},{24,0},{1,25},{9,17},{17,9},{25,1},{2,26},{10... | collective-permute-start | bytes 417800 | tf_op jit(solution)/shard_map/ppermute | solution.py:561
  127.6 2.8 %collective-permute-done.18 = bf16[128,128]{1,0:T(8,128)(2,1)S(1)} collective-permute-done((bf16[128,128]{1,0:T(8,128)(2,1)S(1)}, bf16[128,128]{1,0:T(8,128)(2,1)S(1)}, u32[]{:S(2)}, u32[]{:S(2)}) %collective-permute-start.18) | collective-permute-done | bytes 32800 | tf_op jit(solution)/shard_map/ppermute | solution.py:561
  130.8 2.3 %finish.1 = bf16[4096,128]{1,0:T(8,128)(2,1)} custom-call(s32[128]{0:T(128)S(1)} %copy-done.9, f32[4096,128]{1,0:T(8,128)S(1)} %copy-done.12, bf16[1024,128]{1,0:T(8,128)(2,1)S(1)} %collective-permute-done.14.rim_0, bf16[1024,128]{1,0:T(8,128)(2,1)S(1)} %collective-permute-done.15.rim_1, f32[128,128]{1,0:T(8,128)S(1)} %convert_add_fusion.3.share), custom_call_target="tpu_custom_call" | custom-call | flops 3000000000 | tf_op jit(solution)/shard_map/finish/pallas_call | solution.py:540
  133.1 1.6 %collective-permute-done.20 = f32[136,256]{1,0:T(8,128)S(1)} collective-permute-done((f32[136,256]{1,0:T(8,128)S(1)}, f32[136,256]{1,0:T(8,128)S(1)}, u32[]{:S(2)}, u32[]{:S(2)}) %collective-permute-start.20) | collective-permute-done | bytes 139296 | tf_op jit(solution)/shard_map/ppermute | solution.py:561
  134.7 4.6 %collective-permute-start.21 = (f32[136,256]{1,0:T(8,128)S(1)}, f32[136,256]{1,0:T(8,128)S(1)}, u32[]{:S(2)}, u32[]{:S(2)}) collective-permute-start(f32[136,256]{1,0:T(8,128)S(1)} %add.122), channel_id=1, source_target_pairs={{0,1},{1,0},{2,3},{3,2},{4,5},{5,4},{6,7},{7,6},{8,9},{9,8},{10,11... | collective-permute-start | bytes 417800 | tf_op jit(solution)/shard_map/ppermute | solution.py:561
  139.3 1.0 collective-permute-done.21
  (80 shorter events, 13.8 us)
Async XLA Ops:
  4.0 5.6 %collective-permute-start = (bf16[128,128]{1,0:T(8,128)(2,1)}, bf16[128,128]{1,0:T(8,128)(2,1)S(1)}, u32[]{:S(2)}, u32[]{:S(2)}) collective-permute-start(bf16[128,128]{1,0:T(8,128)(2,1)} %get-tuple-element.70.refs_0_), channel_id=1, source_target_pairs={{0,8},{8,0},{16,24},{24,16},{1,9},{9,1},{17,25},{25,17},{2,10},{10... | collective-permute-start | bytes 98312 | tf_op jit(solution)/shard_map/ppermute | solution.py:561
  6.2 2.7 %copy-start = (bf16[128,128]{1,0:T(8,128)(2,1)S(1)}, bf16[128,128]{1,0:T(8,128)(2,1)}, u32[]{:S(2)}) copy-start(bf16[128,128]{1,0:T(8,128)(2,1)} %get-tuple-element.70.refs_0_) | copy-start | bytes 98308
  9.6 4.7 %collective-permute-start.1 = (bf16[256,128]{1,0:T(8,128)(2,1)S(1)}, bf16[256,128]{1,0:T(8,128)(2,1)S(1)}, u32[]{:S(2)}, u32[]{:S(2)}) collective-permute-start(bf16[256,128]{1,0:T(8,128)(2,1)S(1)} %pad_maximum_fusion.2), channel_id=1, source_target_pairs={{0,24},{8,16},{16,8},{24,0},{1,25},{9,17},{17,9},{25,1},{2,26},{10... | collective-permute-start | bytes 196616 | tf_op jit(solution)/shard_map/ppermute | solution.py:561
  14.3 5.6 %collective-permute-start.2 = (bf16[512,128]{1,0:T(8,128)(2,1)S(1)}, bf16[512,128]{1,0:T(8,128)(2,1)S(1)}, u32[]{:S(2)}, u32[]{:S(2)}) collective-permute-start(bf16[512,128]{1,0:T(8,128)(2,1)S(1)} %pad_maximum_fusion.1), channel_id=1, source_target_pairs={{0,2},{2,0},{4,6},{6,4},{1,3},{3,1},{5,7},{7,5},{8,10},{10,8},{12,... | collective-permute-start | bytes 393224 | tf_op jit(solution)/shard_map/ppermute | solution.py:561
  16.2 11.4 %collective-permute-start.4 = (bf16[1024,128]{1,0:T(8,128)(2,1)}, bf16[1024,128]{1,0:T(8,128)(2,1)S(1)}, u32[]{:S(2)}, u32[]{:S(2)}) collective-permute-start(bf16[1024,128]{1,0:T(8,128)(2,1)} %get-tuple-element.84), channel_id=1, source_target_pairs={{0,32},{32,0},{64,96},{96,64},{1,33},{33,1},{65,97},{97,65},{2,34}... | collective-permute-start | bytes 786440 | tf_op jit(solution)/shard_map/ppermute | solution.py:565
  17.8 9.8 %collective-permute-start.5 = (bf16[1024,128]{1,0:T(8,128)(2,1)}, bf16[1024,128]{1,0:T(8,128)(2,1)}, u32[]{:S(2)}, u32[]{:S(2)}) collective-permute-start(bf16[1024,128]{1,0:T(8,128)(2,1)} %get-tuple-element.85), channel_id=1, source_target_pairs={{32,64},{64,32},{33,65},{65,33},{34,66},{66,34},{35,67},{67,35},{3... | collective-permute-start | bytes 786440 | tf_op jit(solution)/shard_map/ppermute | solution.py:566
  20.6 12.7 %copy-start.1 = (bf16[4096,256]{1,0:T(8,128)(2,1)S(1)}, bf16[4096,256]{1,0:T(8,128)(2,1)}, u32[]{:S(2)}) copy-start(bf16[4096,256]{1,0:T(8,128)(2,1)} %refs_10_.1) | copy-start | bytes 6291460
  20.6 12.7 %copy-start.2 = (bf16[4096,128]{1,0:T(8,128)(2,1)S(1)}, bf16[4096,128]{1,0:T(8,128)(2,1)}, u32[]{:S(2)}) copy-start(bf16[4096,128]{1,0:T(8,128)(2,1)} %features.3) | copy-start | bytes 3145732
  20.6 12.7 %copy-start.5 = (bf16[128,256]{1,0:T(8,128)(2,1)S(1)}, bf16[128,256]{1,0:T(8,128)(2,1)}, u32[]{:S(2)}) copy-start(bf16[128,256]{1,0:T(8,128)(2,1)} %refs_7_.1) | copy-start | bytes 196612
  20.6 12.7 %copy-start.6 = (bf16[128,256]{1,0:T(8,128)(2,1)S(1)}, bf16[128,256]{1,0:T(8,128)(2,1)}, u32[]{:S(2)}) copy-start(bf16[128,256]{1,0:T(8,128)(2,1)} %refs_8_.1) | copy-start | bytes 196612
  20.6 7.0 %collective-permute-start.3 = (bf16[1024,128]{1,0:T(8,128)(2,1)}, bf16[1024,128]{1,0:T(8,128)(2,1)S(1)}, u32[]{:S(2)}, u32[]{:S(2)}) collective-permute-start(bf16[1024,128]{1,0:T(8,128)(2,1)} %pad_maximum_fusion), channel_id=1, source_target_pairs={{0,6},{2,4},{4,2},{6,0},{1,7},{3,5},{5,3},{7,1},{8,14},{10,12},{12... | collective-permute-start | bytes 786440 | tf_op jit(solution)/shard_map/ppermute | solution.py:561
  27.6 5.7 %copy-start.3 = (bf16[1024,128]{1,0:T(8,128)(2,1)}, bf16[1024,128]{1,0:T(8,128)(2,1)S(1)}, u32[]{:S(2)}) copy-start(bf16[1024,128]{1,0:T(8,128)(2,1)S(1)} %collective-permute-done.4.rim_up) | copy-start | bytes 786436
  28.4 4.9 %collective-permute-start.6 = (bf16[2048,128]{1,0:T(8,128)(2,1)}, bf16[2048,128]{1,0:T(8,128)(2,1)S(1)}, u32[]{:S(2)}, u32[]{:S(2)}) collective-permute-start(bf16[2048,128]{1,0:T(8,128)(2,1)} %constant_dynamic-update-slice_fusion), channel_id=1, source_target_pairs={{0,1},{1,0},{2,3},{3,2},{4,5},{5,4},{6,7},{7,6},{8,9},{9,8},{10,11... | collective-permute-start | bytes 1572872 | tf_op jit(solution)/shard_map/ppermute | solution.py:561
  67.4 1.3 copy-start.13
  68.8 1.3 copy-start.14
  70.1 12.9 %collective-permute-start.7 = (f32[272,256]{1,0:T(8,128)S(1)}, f32[272,256]{1,0:T(8,128)S(1)}, u32[]{:S(2)}, u32[]{:S(2)}) collective-permute-start(f32[272,256]{1,0:T(8,128)S(1)} %get-tuple-element.90), channel_id=1, source_target_pairs={{0,32},{32,0},{64,96},{96,64},{1,33},{33,1},{65,97},{97,65},{2,34}... | collective-permute-start | bytes 835592 | tf_op jit(solution)/shard_map/ppermute | solution.py:561
  83.0 2.4 %collective-permute-start.8 = (bf16[2048,128]{1,0:T(8,128)(2,1)}, bf16[2048,128]{1,0:T(8,128)(2,1)S(1)}, u32[]{:S(2)}, u32[]{:S(2)}) collective-permute-start(bf16[2048,128]{1,0:T(8,128)(2,1)} %get-tuple-element.98), channel_id=1, source_target_pairs={{0,1},{1,0},{2,3},{3,2},{4,5},{5,4},{6,7},{7,6},{8,9},{9,8},{10,11... | collective-permute-start | bytes 1572872 | tf_op jit(solution)/shard_map/ppermute | solution.py:561
  83.7 13.3 %collective-permute-start.10 = (f32[272,256]{1,0:T(8,128)S(1)}, f32[272,256]{1,0:T(8,128)S(1)}, u32[]{:S(2)}, u32[]{:S(2)}) collective-permute-start(f32[272,256]{1,0:T(8,128)S(1)} %add.95), channel_id=1, source_target_pairs={{0,96},{32,64},{64,32},{96,0},{1,97},{33,65},{65,33},{97,1},{2,98}... | collective-permute-start | bytes 835592 | tf_op jit(solution)/shard_map/ppermute | solution.py:561
  86.6 10.4 %collective-permute-start.9 = (bf16[1024,128]{1,0:T(8,128)(2,1)S(1)}, bf16[1024,128]{1,0:T(8,128)(2,1)S(1)}, u32[]{:S(2)}, u32[]{:S(2)}) collective-permute-start(bf16[1024,128]{1,0:T(8,128)(2,1)S(1)} %get-tuple-element.131), channel_id=1, source_target_pairs={{0,6},{2,4},{4,2},{6,0},{1,7},{3,5},{5,3},{7,1},{8,14},{10,12},{12... | collective-permute-start | bytes 786440 | tf_op jit(solution)/shard_map/ppermute | solution.py:561
  97.1 1.8 %collective-permute-start.11 = (f32[136,256]{1,0:T(8,128)S(1)}, f32[136,256]{1,0:T(8,128)S(1)}, u32[]{:S(2)}, u32[]{:S(2)}) collective-permute-start(f32[136,256]{1,0:T(8,128)S(1)} %constant_dynamic-slice_fusion), channel_id=1, source_target_pairs={{0,1},{1,0},{2,3},{3,2},{4,5},{5,4},{6,7},{7,6},{8,9},{9,8},{10,11... | collective-permute-start | bytes 417800 | tf_op jit(solution)/shard_map/ppermute | solution.py:561
  97.9 21.8 %collective-permute-start.12 = (bf16[512,128]{1,0:T(8,128)(2,1)S(1)}, bf16[512,128]{1,0:T(8,128)(2,1)S(1)}, u32[]{:S(2)}, u32[]{:S(2)}) collective-permute-start(bf16[512,128]{1,0:T(8,128)(2,1)S(1)} %get-tuple-element.133), channel_id=1, source_target_pairs={{0,2},{2,0},{4,6},{6,4},{1,3},{3,1},{5,7},{7,5},{8,10},{10,8},{12,... | collective-permute-start | bytes 393224 | tf_op jit(solution)/shard_map/ppermute | solution.py:561
  98.0 21.7 %collective-permute-start.14 = (bf16[1024,128]{1,0:T(8,128)(2,1)S(1)}, bf16[1024,128]{1,0:T(8,128)(2,1)S(1)}, u32[]{:S(2)}, u32[]{:S(2)}) collective-permute-start(bf16[1024,128]{1,0:T(8,128)(2,1)S(1)} %copy-done.16), channel_id=1, source_target_pairs={{0,32},{32,0},{64,96},{96,64},{1,33},{33,1},{65,97},{97,65},{2,34}... | collective-permute-start | bytes 786440 | tf_op jit(solution)/shard_map/ppermute | solution.py:565
  98.1 21.6 %collective-permute-start.15 = (bf16[1024,128]{1,0:T(8,128)(2,1)S(1)}, bf16[1024,128]{1,0:T(8,128)(2,1)S(1)}, u32[]{:S(2)}, u32[]{:S(2)}) collective-permute-start(bf16[1024,128]{1,0:T(8,128)(2,1)S(1)} %copy-done.15), channel_id=1, source_target_pairs={{32,64},{64,32},{33,65},{65,33},{34,66},{66,34},{35,67},{67,35},{3... | collective-permute-start | bytes 786440 | tf_op jit(solution)/shard_map/ppermute | solution.py:566
  98.9 20.9 %collective-permute-start.13 = (f32[136,256]{1,0:T(8,128)S(1)}, f32[136,256]{1,0:T(8,128)S(1)}, u32[]{:S(2)}, u32[]{:S(2)}) collective-permute-start(f32[136,256]{1,0:T(8,128)S(1)} %dynamic-slice_add_fusion), channel_id=1, source_target_pairs={{0,6},{2,4},{4,2},{6,0},{1,7},{3,5},{5,3},{7,1},{8,14},{10,12},{12... | collective-permute-start | bytes 417800 | tf_op jit(solution)/shard_map/ppermute | solution.py:561
  119.7 11.0 %copy-start.9 = (s32[128]{0:T(128)S(1)}, s32[128]{0:T(128)}, u32[]{:S(2)}) copy-start(s32[128]{0:T(128)} %hub_rows.3) | copy-start | bytes 1540
  119.8 11.0 %copy-start.12 = (f32[4096,128]{1,0:T(8,128)S(1)}, f32[4096,128]{1,0:T(8,128)}, u32[]{:S(2)}) copy-start(f32[4096,128]{1,0:T(8,128)} %own_scatter.1.own) | copy-start | bytes 6291460
  119.8 5.5 %collective-permute-start.17 = (f32[136,256]{1,0:T(8,128)S(1)}, f32[136,256]{1,0:T(8,128)S(1)}, u32[]{:S(2)}, u32[]{:S(2)}) collective-permute-start(f32[136,256]{1,0:T(8,128)S(1)} %add.109), channel_id=1, source_target_pairs={{0,2},{2,0},{4,6},{6,4},{1,3},{3,1},{5,7},{7,5},{8,10},{10,8},{12,... | collective-permute-start | bytes 417800 | tf_op jit(solution)/shard_map/ppermute | solution.py:561
  120.9 4.4 %collective-permute-start.16 = (bf16[256,128]{1,0:T(8,128)(2,1)S(1)}, bf16[256,128]{1,0:T(8,128)(2,1)S(1)}, u32[]{:S(2)}, u32[]{:S(2)}) collective-permute-start(bf16[256,128]{1,0:T(8,128)(2,1)S(1)} %get-tuple-element.135), channel_id=1, source_target_pairs={{0,24},{8,16},{16,8},{24,0},{1,25},{9,17},{17,9},{25,1},{2,26},{10... | collective-permute-start | bytes 196616 | tf_op jit(solution)/shard_map/ppermute | solution.py:561
  125.3 5.2 %collective-permute-start.19 = (f32[136,256]{1,0:T(8,128)S(1)}, f32[136,256]{1,0:T(8,128)S(1)}, u32[]{:S(2)}, u32[]{:S(2)}) collective-permute-start(f32[136,256]{1,0:T(8,128)S(1)} %add.114), channel_id=1, source_target_pairs={{0,24},{8,16},{16,8},{24,0},{1,25},{9,17},{17,9},{25,1},{2,26},{10... | collective-permute-start | bytes 417800 | tf_op jit(solution)/shard_map/ppermute | solution.py:561
  127.5 2.8 %collective-permute-start.18 = (bf16[128,128]{1,0:T(8,128)(2,1)S(1)}, bf16[128,128]{1,0:T(8,128)(2,1)S(1)}, u32[]{:S(2)}, u32[]{:S(2)}) collective-permute-start(bf16[128,128]{1,0:T(8,128)(2,1)S(1)} %get-tuple-element.137), channel_id=1, source_target_pairs={{0,8},{8,0},{16,24},{24,16},{1,9},{9,1},{17,25},{25,17},{2,10},{10... | collective-permute-start | bytes 98312 | tf_op jit(solution)/shard_map/ppermute | solution.py:561
  130.6 4.1 %collective-permute-start.20 = (f32[136,256]{1,0:T(8,128)S(1)}, f32[136,256]{1,0:T(8,128)S(1)}, u32[]{:S(2)}, u32[]{:S(2)}) collective-permute-start(f32[136,256]{1,0:T(8,128)S(1)} %add.120), channel_id=1, source_target_pairs={{0,8},{8,0},{16,24},{24,16},{1,9},{9,1},{17,25},{25,17},{2,10},{10... | collective-permute-start | bytes 417800 | tf_op jit(solution)/shard_map/ppermute | solution.py:561
  134.7 5.6 %collective-permute-start.21 = (f32[136,256]{1,0:T(8,128)S(1)}, f32[136,256]{1,0:T(8,128)S(1)}, u32[]{:S(2)}, u32[]{:S(2)}) collective-permute-start(f32[136,256]{1,0:T(8,128)S(1)} %add.122), channel_id=1, source_target_pairs={{0,1},{1,0},{2,3},{3,2},{4,5},{5,4},{6,7},{7,6},{8,9},{9,8},{10,11... | collective-permute-start | bytes 417800 | tf_op jit(solution)/shard_map/ppermute | solution.py:561
  (7 other events, 6.2 us)

commit v6 on v5

--- a/solution.py
+++ b/solution.py
@@ -36,6 +36,10 @@
     return 16 if count <= 3 else 8
 
 
+def wide_group_of(count):
+    return 32 if count == 1 else 16
+
+
 def cost(us):
     return pl.CostEstimate(flops=int(us * 1e9), bytes_accessed=0, transcendentals=0)
 
@@ -44,29 +48,15 @@
     return (lax.axis_index("z") & 1) ^ (1 - half)
 
 
-def hub_kernel(hub_rows, features, out, *refs):
-    rims, (here, wide, rows, sems) = refs[:2], refs[2:]
-    part = NODES // 4
-    copies = []
-    for k in range(4):
-        cut = pl.ds(k * part, part)
-        copies.append(pltpu.make_async_copy(features.at[cut], here.at[cut], sems.at[k]))
-        copies[k].start()
-    for k in range(4):
-        copies[k].wait()
-
-        @pl.loop(0, part // 512)
-        def _(i, k=k):
-            cut = pl.ds(k * part + i * 512, 512)
-            wide[cut, :] = here[cut, :].astype(jnp.float32)
-
-    sends = []
-    for half in range(2):
-        at = pl.multiple_of(faces_up(half) * (NODES - HALO), HALO)
-        sends.append(
-            pltpu.make_async_copy(here.at[pl.ds(at, HALO)], rims[half], sems.at[4 + half])
-        )
-        sends[half].start()
+def faces_up(half):
+    return (lax.axis_index("z") & 1) ^ (1 - half)
+
+
+def hub_kernel(hub_rows, features, out, wide, rows):
+    @pl.loop(0, NODES // 512)
+    def _(i):
+        cut = pl.ds(i * 512, 512)
+        wide[cut, :] = features[cut, :].astype(jnp.float32)
 
     @pl.loop(0, HUB // 16)
     def _(i):
@@ -74,23 +64,15 @@
             rows[pl.ds(i * 16 + u, 1), :] = wide[pl.ds(hub_rows[i * 16 + u], 1), :]
 
     out[...] = rows[...].astype(jnp.bfloat16)
-    for send in sends:
-        send.wait()
 
 
 def pick_hubs(hub_rows, features):
     return pl.pallas_call(
         hub_kernel,
-        out_shape=(jax.ShapeDtypeStruct((HUB, F), jnp.bfloat16),)
-        + (jax.ShapeDtypeStruct((HALO, F), jnp.bfloat16),) * 2,
-        in_specs=[smem, hbm],
-        out_specs=(vmem, hbm, hbm),
-        scratch_shapes=[
-            pltpu.VMEM((NODES, F), jnp.bfloat16),
-            pltpu.VMEM((NODES, F), jnp.float32),
-            pltpu.VMEM((HUB, F), jnp.float32),
-            pltpu.SemaphoreType.DMA((6,)),
-        ],
+        out_shape=jax.ShapeDtypeStruct((HUB, F), jnp.bfloat16),
+        in_specs=[smem, vmem],
+        out_specs=vmem,
+        scratch_shapes=[pltpu.VMEM((NODES, F), jnp.float32), pltpu.VMEM((HUB, F), jnp.float32)],
         compiler_params=params,
         cost_estimate=cost(2),
         name="pick_hubs",
@@ -244,7 +226,7 @@
         for copy in self.copies:
             copy.start()
 
-    def visit(self, act):
+    def visit(self, act, group_of):
         slots, copies = self.slots, self.copies[1:]
         self.copies[0].wait()
         for count in range(1, FANOUT + 1):
@@ -273,7 +255,7 @@
         ref[pl.ds(at + i * step, step), :] = jnp.zeros((step, F), jnp.float32)
 
 
-BLOCK = 512
+BLOCK = 1024
 HUB_PIECES = (1, 1, 2, 4, 8, 16)
 
 
@@ -306,6 +288,8 @@
         copy.start()
     late.append(cot_copy)
     grads[...] = jnp.zeros_like(grads)
+    self_at = pl.multiple_of(lax.axis_index("core") * HALF, 8)
+    neigh_at = pl.multiple_of((1 - lax.axis_index("core")) * HALF, 8)
 
     def widen(source, start, at, rows):
         step = 256
@@ -342,7 +326,7 @@
                 total = total + table[pl.ds(slots[s][n], 1), :]
             sums[pl.ds(n, 1), :] = total
 
-    todo.visit(gather)
+    todo.visit(gather, wide_group_of)
     for copy in late:
         copy.wait()
 
@@ -369,9 +353,9 @@
         products = lax.dot_general(
             both, dz, (((0,), (0,)), ((), ())), preferred_element_type=jnp.float32
         )
-        grads[0:F, :] += products[:F]
-        grads[HALF : HALF + F, :] += products[F:]
-        grads[F:HALF, :] += jnp.sum(
+        grads[pl.ds(self_at, F), :] += products[:F]
+        grads[pl.ds(neigh_at, F), :] += products[F:]
+        grads[pl.ds(self_at + F, 8), :] += jnp.sum(
             dz.astype(jnp.float32).reshape(BLOCK // 8, 8, H), axis=0
         )
         back = lax.dot_general(
@@ -395,7 +379,7 @@
             jax.ShapeDtypeStruct((NODES, F), jnp.float32),
             jax.ShapeDtypeStruct((2 * HALF, H), jnp.float32),
         ),
-        in_specs=list_specs + [anywhere] * (3 + len(hubs)) + [hbm] * 5,
+        in_specs=list_specs + [hbm] * (3 + len(hubs)) + [hbm] * 5,
         out_specs=(hbm, hbm, hbm, vmem),
         scratch_shapes=[
             pltpu.VMEM((EXTENT, F), jnp.float32),
@@ -413,7 +397,7 @@
         ]
         + list_scratch
         + [pltpu.SemaphoreType.DMA((14,)), pltpu.SemaphoreType.DMA((3,))],
-        compiler_params=pltpu.CompilerParams(vmem_limit_bytes=40 * 2**20),
+        compiler_params=params,
         cost_estimate=cost(30),
         name="forward",
     )(*lists, features, *rims, *hubs, counts, w_self, w_neigh, bias, cot)
@@ -457,7 +441,7 @@
                 at = pl.ds(slots[s][n], 1)
                 chain[at, :] = chain[at, :] + row
 
-    todo.visit(scatter)
+    todo.visit(scatter, group_of)
 
     part = rows // len(outs)
     for half, out in enumerate(outs):
@@ -465,8 +449,10 @@
         @pl.loop(0, part // HUB)
         def _(i, half=half, out=out):
             if kind == "hub":
-                core = lax.axis_index("core") ^ half
-                taken = (((i & 3) * 4) + (i >> 2)) * 2 + core
+                flip_x, flip_y = (i >> 2) ^ (i >> 3), (i & 3) ^ ((i >> 1) & 1)
+                owner_y = lax.axis_index("y") ^ flip_y
+                owner_x = lax.axis_index("x") ^ flip_x
+                taken = owner_y * 8 + owner_x * 2 + (lax.axis_index("core") ^ half)
             elif kind == "rim":
                 taken = i + faces_up(half) * (HALO // HUB)
             else:
@@ -556,6 +542,27 @@
     )(hub_rows, own, rim_0, rim_1, share)
 
 
+def hand_out_kernel(mine, other, grad_self, grad_neigh, grad_bias):
+    first = lax.axis_index("core") == 0
+    grad_self[...] = jnp.where(first, mine[0:F, :], other[0:F, :])
+    grad_neigh[...] = jnp.where(first, other[0:F, :], mine[0:F, :])
+    bias = jnp.where(first, mine[F:HALF, :], other[F:HALF, :])
+    grad_bias[...] = jnp.sum(bias, axis=0, keepdims=True)
+
+
+def hand_out(mine, other):
+    return pl.pallas_call(
+        hand_out_kernel,
+        out_shape=(jax.ShapeDtypeStruct((F, H), jnp.float32),) * 2
+        + (jax.ShapeDtypeStruct((1, H), jnp.float32),),
+        in_specs=[vmem] * 2,
+        out_specs=(vmem,) * 3,
+        compiler_params=pltpu.CompilerParams(vmem_limit_bytes=8 * 2**20),
+        cost_estimate=cost(1),
+        name="hand_out",
+    )(mine, other)
+
+
 def swap(value, axis, flip):
     count = lax.axis_size(axis)
     return lax.ppermute(value, axis, [(i, i ^ flip) for i in range(count)])
@@ -566,18 +573,14 @@
     return above, lax.ppermute(second, "z", [(1, 2), (2, 1)])
 
 
-def halves(value, bit):
+def halves(value):
     rows = value.shape[0] // 2
-    keep = lax.dynamic_slice_in_dim(value, bit * rows, rows, axis=0)
-    give = lax.dynamic_slice_in_dim(value, (1 - bit) * rows, rows, axis=0)
-    return keep, give
-
-
-def halve(keep, got, axis, flip, bit):
-    mine, other_mine = halves(keep, bit)
-    theirs, other_theirs = halves(got, bit)
-    give = (other_mine.astype(jnp.float32) + other_theirs.astype(jnp.float32)).astype(jnp.bfloat16)
-    return plus(mine, theirs), swap(give, axis, flip)
+    return value[:rows], value[rows:]
+
+
+def halve(keep, got, axis, flip):
+    mine, give = halves(plus(keep, got))
+    return mine, swap(give.astype(jnp.bfloat16), axis, flip)
 
 
 def plus(keep, got):
@@ -589,10 +592,9 @@
 
 
 def on_device(features, neighbors, counts, hub_rows, w_self, w_neigh, out_bias, cotangent):
-    x, y, core = lax.axis_index("x"), lax.axis_index("y"), lax.axis_index("core")
     counts = counts.reshape(ROWS, LANES)
 
-    h0, *rims = pick_hubs(hub_rows, features)
+    h0 = pick_hubs(hub_rows, features)
     h1 = swap(h0, "y", 1)
     flat, order = plan(all_plan_kernel, (tiles, ordered), 4, neighbors.T, counts)
     all_lists = lists(order, flat)
@@ -601,10 +603,13 @@
     h2 = swap(held, "y", 3)
     slots, order = plan(hub_plan_kernel, (tiles, ordered), 4, flat, counts)
     hub_lists = lists(order, slots)
-    h2, flat, hub_lists, *rims = tie(h2, flat, hub_lists, *rims)
+    h2, flat, edges, *hub_lists = tie(h2, flat, features, *hub_lists)
     held = jnp.concatenate([held, h2], axis=0)
     h3 = swap(held, "x", 1)
-    rims = swap_rims(*rims)
+    rims = swap_rims(*(
+        lax.dynamic_slice_in_dim(edges, faces_up(half) * (NODES - HALO), HALO, axis=0)
+        for half in range(2)
+    ))
     h3, flat = tie(h3, flat)
     held = jnp.concatenate([held, h3], axis=0)
     h4 = swap(held, "x", 3)
@@ -627,13 +632,13 @@
     got = swap(give, "core", 1)
     other = swap(grads, "z", 3)
     got, src = tie(got, src)
-    keep, got = halve(keep, got, "x", 3, x // 2)
+    keep, got = halve(keep, got, "x", 3)
     rims = scatter("rim", 2 * HALO, jnp.bfloat16, 8, 6, rim_lists, src)
     keep, got, src, other, *rims = tie(keep, got, src, other, *rims)
 
-    grads, give = halves(grads + other, core)
+    grads, give = halves(grads + other)
     other = swap(give, "core", 1)
-    keep, got = halve(keep, got, "x", 1, x % 2)
+    keep, got = halve(keep, got, "x", 1)
     other, src = tie(other, src)
     grads = grads + other
     other = swap(grads, "x", 3)
@@ -641,11 +646,11 @@
     (own,) = scatter("own", NODES, jnp.float32, 20, CHAINS, own_lists, src, base)
     keep, got, other, own, *rims = tie(keep, got, other, own, *rims)
 
-    keep, got = halve(keep, got, "y", 3, y // 2)
+    keep, got = halve(keep, got, "y", 3)
     grads = grads + other
     other = swap(grads, "x", 1)
     keep, got, other = tie(keep, got, other)
-    keep, got = halve(keep, got, "y", 1, y % 2)
+    keep, got = halve(keep, got, "y", 1)
     grads = grads + other
     other = swap(grads, "y", 3)
     keep, got, other = tie(keep, got, other)
@@ -655,9 +660,8 @@
     other, grad_features = tie(other, grad_features)
     grads = grads + other
     other = swap(grads, "core", 1)
-    first = jnp.where(core == 0, grads, other)
-    second = jnp.where(core == 0, other, grads)
-    return act, grad_features, first[:F], second[:F], jnp.sum(first[F:], axis=0)
+    grad_self, grad_neigh, grad_bias = hand_out(grads, other)
+    return act, grad_features, grad_self, grad_neigh, grad_bias.reshape(H)
 
 
 def solution(mesh):

time: 144 us -> 131 us (0.910)
  local copies, waits for them, and re-layouts: 10.7 us -> 1.1 us
  other arithmetic: 3.46 us -> 1.48 us
    unnamed x38 -> x32, local copies, waits for them, and re-layouts: 9.23 us -> 0.89 us
    ppermute x18, starting transfers between devices: 29.8 us -> 31.3 us  [swap(): return lax.ppermute(value, axis, [(i, i ^ flip) for i in range(count)])]
    pallas_call x1 -> x2, Pallas kernels: 3.36 us -> 2.88 us  [the longest x1 2.16 us: pick_hubs(): pl.pallas_call(hub_kernel, out_shape=jax.ShapeDtypeStruct((HUB, F), jnp.b...]
  transfers between devices with their start and end apart: 22 -> 22, of which waited for: 8 -> 7; matrix products, arithmetic and copies ran while one was open for 3% -> 1% of each run, Pallas kernels for 35% -> 38%
where the time goes in v6:
time: 131 us; the launch traced here: 130 us
  Pallas kernels  81.6 us (62%)
  starting transfers between devices  34.5 us (26%)
  waiting for transfers between devices  10.1 us (8%)
  other arithmetic  1.48 us (1%)
    pallas_call x3, Pallas kernels, scatter(): pl.pallas_call(functools.partial(scatter_kernel, kind), out_shape=(jax.Sh...  37.7 us
    ppermute x18, starting transfers between devices, swap(): return lax.ppermute(value, axis, [(i, i ^ flip) for i in range(count)])  31.3 us
    pallas_call x1, Pallas kernels, forward(): pl.pallas_call(forward_kernel, out_shape=(jax.ShapeDtypeStruct((NODES, H)...  28.8 us
    ppermute x18, waiting for transfers between devices, swap(): return lax.ppermute(value, axis, [(i, i ^ flip) for i in range(count)])  10 us
    pallas_call x3, Pallas kernels, plan(): pl.pallas_call(kernel, out_shape=outs, in_specs=[vmem] * len(inputs), out...  9.89 us
  transfers between devices with their start and end apart: 22, of which 7 were waited for; matrix products, arithmetic and copies ran while one was open for 1% of the time, Pallas kernels for 38%

profile of v6, /device:TPU:1, one launch (start us, length us, event | category | flops | bytes accessed | tf_op | source)
XLA Modules:
  0.0 129.8 jit_solution(7423122467611754143)
XLA Ops:
  0.6 2.2 %pick_hubs.1.refs_0_ = bf16[128,128]{1,0:T(8,128)(2,1)} custom-call(s32[128]{0:T(128)} %hub_rows.3, bf16[4096,128]{1,0:T(8,128)(2,1)} %features.3), custom_call_target="tpu_custom_call" | custom-call | flops 2000000000 | tf_op jit(solution)/shard_map/pick_hubs/pallas_call | solution.py:70
  2.8 2.1 %collective-permute-start = (bf16[128,128]{1,0:T(8,128)(2,1)}, bf16[128,128]{1,0:T(8,128)(2,1)S(1)}, u32[]{:S(2)}, u32[]{:S(2)}) collective-permute-start(bf16[128,128]{1,0:T(8,128)(2,1)} %pick_hubs.1.refs_0_), channel_id=1, source_target_pairs={{0,8},{8,0},{16,24},{24,16},{1,9},{9,1},{17,25},{25,17},{2,10},{10... | collective-permute-start | bytes 98312 | tf_op jit(solution)/shard_map/ppermute | solution.py:568
  4.9 2.7 %all_plan_kernel.1 = (s32[320,128]{1,0:T(8,128)}, s32[40,128]{1,0:T(8,128)}) custom-call(s32[10,4096]{1,0:T(8,128)} %bitcast.11, s32[32,128]{1,0:T(8,128)} %bitcast.12), custom_call_target="tpu_custom_call" | custom-call | flops 4000000000 | tf_op jit(solution)/shard_map/all_plan_kernel/pallas_call | solution.py:194
  7.7 2.0 %collective-permute-start.1 = (bf16[256,128]{1,0:T(8,128)(2,1)S(1)}, bf16[256,128]{1,0:T(8,128)(2,1)S(1)}, u32[]{:S(2)}, u32[]{:S(2)}) collective-permute-start(bf16[256,128]{1,0:T(8,128)(2,1)S(1)} %pad_maximum_fusion.2), channel_id=1, source_target_pairs={{0,24},{8,16},{16,8},{24,0},{1,25},{9,17},{17,9},{25,1},{2,26},{10... | collective-permute-start | bytes 196616 | tf_op jit(solution)/shard_map/ppermute | solution.py:568
  9.7 2.7 %hub_plan_kernel.1 = (s32[320,128]{1,0:T(8,128)}, s32[40,128]{1,0:T(8,128)}) custom-call(s32[320,128]{1,0:T(8,128)} %get-tuple-element.76.flat, s32[32,128]{1,0:T(8,128)} %bitcast.13), custom_call_target="tpu_custom_call" | custom-call | flops 4000000000 | tf_op jit(solution)/shard_map/hub_plan_kernel/pallas_call | solution.py:194
  12.5 1.3 collective-permute-start.2
  13.8 1.7 %collective-permute-start.4 = (bf16[1024,128]{1,0:T(8,128)(2,1)S(1)}, bf16[1024,128]{1,0:T(8,128)(2,1)S(1)}, u32[]{:S(2)}, u32[]{:S(2)}) collective-permute-start(bf16[1024,128]{1,0:T(8,128)(2,1)S(1)} %get-tuple-element.130), channel_id=1, source_target_pairs={{0,32},{32,0},{64,96},{96,64},{1,33},{33,1},{65,97},{97,65},{2,34}... | collective-permute-start | bytes 786440 | tf_op jit(solution)/shard_map/ppermute | solution.py:572
  16.4 2.6 %collective-permute-start.3 = (bf16[1024,128]{1,0:T(8,128)(2,1)S(1)}, bf16[1024,128]{1,0:T(8,128)(2,1)S(1)}, u32[]{:S(2)}, u32[]{:S(2)}) collective-permute-start(bf16[1024,128]{1,0:T(8,128)(2,1)S(1)} %pad_maximum_fusion), channel_id=1, source_target_pairs={{0,6},{2,4},{4,2},{6,0},{1,7},{3,5},{5,3},{7,1},{8,14},{10,12},{12... | collective-permute-start | bytes 786440 | tf_op jit(solution)/shard_map/ppermute | solution.py:568
  19.0 4.4 %rim_plan_kernel.1 = (s32[320,128]{1,0:T(8,128)}, s32[40,128]{1,0:T(8,128)}, s32[40,128]{1,0:T(8,128)}) custom-call(s32[320,128]{1,0:T(8,128)} %get-tuple-element.76.flat, s32[32,128]{1,0:T(8,128)} %bitcast.14), custom_call_target="tpu_custom_call" | custom-call | flops 5000000000 | tf_op jit(solution)/shard_map/rim_plan_kernel/pallas_call | solution.py:194
  23.5 3.6 %collective-permute-start.6 = (bf16[2048,128]{1,0:T(8,128)(2,1)S(1)}, bf16[2048,128]{1,0:T(8,128)(2,1)S(1)}, u32[]{:S(2)}, u32[]{:S(2)}) collective-permute-start(bf16[2048,128]{1,0:T(8,128)(2,1)S(1)} %constant_dynamic-update-slice_fusion), channel_id=1, source_target_pairs={{0,1},{1,0},{2,3},{3,2},{4,5},{5,4},{6,7},{7,6},{8,9},{9,8},{10,11... | collective-permute-start | bytes 1572872 | tf_op jit(solution)/shard_map/ppermute | solution.py:568
  27.2 1.5 %collective-permute-done.6.refs_5_ = bf16[2048,128]{1,0:T(8,128)(2,1)S(1)} collective-permute-done((bf16[2048,128]{1,0:T(8,128)(2,1)S(1)}, bf16[2048,128]{1,0:T(8,128)(2,1)S(1)}, u32[]{:S(2)}, u32[]{:S(2)}) %collective-permute-start.6) | collective-permute-done | bytes 524320 | tf_op jit(solution)/shard_map/ppermute | solution.py:568
  28.7 0.8 copy-done.9
  29.5 28.8 %forward.1 = (bf16[4096,256]{1,0:T(8,128)(2,1)}, f32[4096,128]{1,0:T(8,128)}, f32[4096,128]{1,0:T(8,128)}, f32[272,256]{1,0:T(8,128)}) custom-call(s32[5120]{0:T(1024)} %bitcast.22, s32[40960]{0:T(1024)} %bitcast.19, bf16[4096,128]{1,0:T(8,128)(2,1)} %features.3, bf16[1024,128]{1,0:T(8,128)(2,1)} %copy-done.12, bf16[1024,128]{1,0:T(8,128)(2,1)} %copy-done.13, ...), custom_call_target="tpu_custom_call" | custom-call | flops 30000001024 | tf_op jit(solution)/shard_map/forward/pallas_call | solution.py:374
  58.3 3.5 %collective-permute-start.7 = (f32[272,256]{1,0:T(8,128)}, f32[272,256]{1,0:T(8,128)S(1)}, u32[]{:S(2)}, u32[]{:S(2)}) collective-permute-start(f32[272,256]{1,0:T(8,128)} %get-tuple-element.85), channel_id=1, source_target_pairs={{0,32},{32,0},{64,96},{96,64},{1,33},{33,1},{65,97},{97,65},{2,34}... | collective-permute-start | bytes 835592 | tf_op jit(solution)/shard_map/ppermute | solution.py:568
  61.8 9.3 %hub_scatter.1 = (bf16[2048,128]{1,0:T(8,128)(2,1)}, bf16[2048,128]{1,0:T(8,128)(2,1)}) custom-call(s32[5120]{0:T(1024)} %bitcast.23, s32[40960]{0:T(1024)} %bitcast.20, f32[4096,128]{1,0:T(8,128)} %get-tuple-element.108.src), custom_call_target="tpu_custom_call" | custom-call | flops 8000000000 | tf_op jit(solution)/shard_map/hub_scatter/pallas_call | solution.py:472
  71.7 0.8 collective-permute-start.10
  72.5 0.9 collective-permute-done.8
  73.4 1.1 convert_add_fusion
  74.6 2.0 %collective-permute-start.9 = (bf16[1024,128]{1,0:T(8,128)(2,1)S(1)}, bf16[1024,128]{1,0:T(8,128)(2,1)S(1)}, u32[]{:S(2)}, u32[]{:S(2)}) collective-permute-start(bf16[1024,128]{1,0:T(8,128)(2,1)S(1)} %slice.59), channel_id=1, source_target_pairs={{0,6},{2,4},{4,2},{6,0},{1,7},{3,5},{5,3},{7,1},{8,14},{10,12},{12... | collective-permute-start | bytes 786440 | tf_op jit(solution)/shard_map/ppermute | solution.py:568
  76.7 8.6 %rim_scatter.1 = (bf16[1024,128]{1,0:T(8,128)(2,1)}, bf16[1024,128]{1,0:T(8,128)(2,1)}) custom-call(s32[5120]{0:T(1024)} %bitcast.24, s32[40960]{0:T(1024)} %bitcast.17, f32[4096,128]{1,0:T(8,128)} %get-tuple-element.108.src), custom_call_target="tpu_custom_call" | custom-call | flops 8000000000 | tf_op jit(solution)/shard_map/rim_scatter/pallas_call | solution.py:472
  87.4 0.7 collective-permute-start.13
  88.1 19.8 %own_scatter.1.own = f32[4096,128]{1,0:T(8,128)} custom-call(s32[5120]{0:T(1024)} %bitcast.21, s32[40960]{0:T(1024)} %bitcast.18, f32[4096,128]{1,0:T(8,128)} %get-tuple-element.108.src, f32[4096,128]{1,0:T(8,128)} %get-tuple-element.109.refs_0_), custom_call_target="tpu_custom_call" | custom-call | flops 20000000000 | tf_op jit(solution)/shard_map/own_scatter/pallas_call | solution.py:472
  108.0 0.9 collective-permute-start.17
  108.9 2.4 %collective-permute-start.16 = (bf16[256,128]{1,0:T(8,128)(2,1)S(1)}, bf16[256,128]{1,0:T(8,128)(2,1)S(1)}, u32[]{:S(2)}, u32[]{:S(2)}) collective-permute-start(bf16[256,128]{1,0:T(8,128)(2,1)S(1)} %slice.61), channel_id=1, source_target_pairs={{0,24},{8,16},{16,8},{24,0},{1,25},{9,17},{17,9},{25,1},{2,26},{10... | collective-permute-start | bytes 196616 | tf_op jit(solution)/shard_map/ppermute | solution.py:568
  111.3 2.0 %collective-permute-done.16 = bf16[256,128]{1,0:T(8,128)(2,1)S(1)} collective-permute-done((bf16[256,128]{1,0:T(8,128)(2,1)S(1)}, bf16[256,128]{1,0:T(8,128)(2,1)S(1)}, u32[]{:S(2)}, u32[]{:S(2)}) %collective-permute-start.16) | collective-permute-done | bytes 65568 | tf_op jit(solution)/shard_map/ppermute | solution.py:568
  113.3 2.4 %collective-permute-start.19 = (f32[136,256]{1,0:T(8,128)S(1)}, f32[136,256]{1,0:T(8,128)S(1)}, u32[]{:S(2)}, u32[]{:S(2)}) collective-permute-start(f32[136,256]{1,0:T(8,128)S(1)} %add.51), channel_id=1, source_target_pairs={{0,24},{8,16},{16,8},{24,0},{1,25},{9,17},{17,9},{25,1},{2,26},{10... | collective-permute-start | bytes 417800 | tf_op jit(solution)/shard_map/ppermute | solution.py:568
  115.8 2.7 %collective-permute-done.18 = bf16[128,128]{1,0:T(8,128)(2,1)S(1)} collective-permute-done((bf16[128,128]{1,0:T(8,128)(2,1)S(1)}, bf16[128,128]{1,0:T(8,128)(2,1)S(1)}, u32[]{:S(2)}, u32[]{:S(2)}) %collective-permute-start.18) | collective-permute-done | bytes 32800 | tf_op jit(solution)/shard_map/ppermute | solution.py:568
  119.0 2.3 %finish.1 = bf16[4096,128]{1,0:T(8,128)(2,1)} custom-call(s32[128]{0:T(128)S(1)} %copy-done, f32[4096,128]{1,0:T(8,128)S(1)} %copy-done.1, bf16[1024,128]{1,0:T(8,128)(2,1)S(1)} %collective-permute-done.14.rim_0, bf16[1024,128]{1,0:T(8,128)(2,1)S(1)} %collective-permute-done.15.rim_1, f32[128,128]{1,0:T(8,128)S(1)} %convert_add_fusion.4.share), custom_call_target="tpu_custom_call" | custom-call | flops 3000000000 | tf_op jit(solution)/shard_map/finish/pallas_call | solution.py:526
  121.3 1.7 %collective-permute-done.20 = f32[136,256]{1,0:T(8,128)S(1)} collective-permute-done((f32[136,256]{1,0:T(8,128)S(1)}, f32[136,256]{1,0:T(8,128)S(1)}, u32[]{:S(2)}, u32[]{:S(2)}) %collective-permute-start.20) | collective-permute-done | bytes 139296 | tf_op jit(solution)/shard_map/ppermute | solution.py:568
  122.9 5.1 %collective-permute-start.21 = (f32[136,256]{1,0:T(8,128)S(1)}, f32[136,256]{1,0:T(8,128)S(1)}, u32[]{:S(2)}, u32[]{:S(2)}) collective-permute-start(f32[136,256]{1,0:T(8,128)S(1)} %add.55.mine), channel_id=1, source_target_pairs={{0,1},{1,0},{2,3},{3,2},{4,5},{5,4},{6,7},{7,6},{8,9},{9,8},{10,11... | collective-permute-start | bytes 417800 | tf_op jit(solution)/shard_map/ppermute | solution.py:568
  128.1 1.0 collective-permute-done.21.other
  129.1 0.7 hand_out.1
  (80 shorter events, 4.3 us)
Async XLA Ops:
  2.8 4.9 %collective-permute-start = (bf16[128,128]{1,0:T(8,128)(2,1)}, bf16[128,128]{1,0:T(8,128)(2,1)S(1)}, u32[]{:S(2)}, u32[]{:S(2)}) collective-permute-start(bf16[128,128]{1,0:T(8,128)(2,1)} %pick_hubs.1.refs_0_), channel_id=1, source_target_pairs={{0,8},{8,0},{16,24},{24,16},{1,9},{9,1},{17,25},{25,17},{2,10},{10... | collective-permute-start | bytes 98312 | tf_op jit(solution)/shard_map/ppermute | solution.py:568
  7.7 8.7 %copy-start.5 = (bf16[128,128]{1,0:T(8,128)(2,1)}, bf16[128,128]{1,0:T(8,128)(2,1)S(1)}, u32[]{:S(2)}) copy-start(bf16[128,128]{1,0:T(8,128)(2,1)S(1)} %collective-permute-done.refs_1_) | copy-start | bytes 98308
  7.7 6.1 %copy-start.7 = (bf16[4096,128]{1,0:T(8,128)(2,1)S(1)}, bf16[4096,128]{1,0:T(8,128)(2,1)}, u32[]{:S(2)}) copy-start(bf16[4096,128]{1,0:T(8,128)(2,1)} %features.3) | copy-start | bytes 3145732
  7.7 4.7 %collective-permute-start.1 = (bf16[256,128]{1,0:T(8,128)(2,1)S(1)}, bf16[256,128]{1,0:T(8,128)(2,1)S(1)}, u32[]{:S(2)}, u32[]{:S(2)}) collective-permute-start(bf16[256,128]{1,0:T(8,128)(2,1)S(1)} %pad_maximum_fusion.2), channel_id=1, source_target_pairs={{0,24},{8,16},{16,8},{24,0},{1,25},{9,17},{17,9},{25,1},{2,26},{10... | collective-permute-start | bytes 196616 | tf_op jit(solution)/shard_map/ppermute | solution.py:568
  12.4 10.9 %copy-start.2 = (bf16[256,128]{1,0:T(8,128)(2,1)}, bf16[256,128]{1,0:T(8,128)(2,1)S(1)}, u32[]{:S(2)}) copy-start(bf16[256,128]{1,0:T(8,128)(2,1)S(1)} %collective-permute-done.1.refs_2_) | copy-start | bytes 196612
  12.5 3.9 %collective-permute-start.2 = (bf16[512,128]{1,0:T(8,128)(2,1)S(1)}, bf16[512,128]{1,0:T(8,128)(2,1)S(1)}, u32[]{:S(2)}, u32[]{:S(2)}) collective-permute-start(bf16[512,128]{1,0:T(8,128)(2,1)S(1)} %pad_maximum_fusion.1), channel_id=1, source_target_pairs={{0,2},{2,0},{4,6},{6,4},{1,3},{3,1},{5,7},{7,5},{8,10},{10,8},{12,... | collective-permute-start | bytes 393224 | tf_op jit(solution)/shard_map/ppermute | solution.py:568
  13.8 9.6 %collective-permute-start.4 = (bf16[1024,128]{1,0:T(8,128)(2,1)S(1)}, bf16[1024,128]{1,0:T(8,128)(2,1)S(1)}, u32[]{:S(2)}, u32[]{:S(2)}) collective-permute-start(bf16[1024,128]{1,0:T(8,128)(2,1)S(1)} %get-tuple-element.130), channel_id=1, source_target_pairs={{0,32},{32,0},{64,96},{96,64},{1,33},{33,1},{65,97},{97,65},{2,34}... | collective-permute-start | bytes 786440 | tf_op jit(solution)/shard_map/ppermute | solution.py:572
  15.5 7.9 %collective-permute-start.5 = (bf16[1024,128]{1,0:T(8,128)(2,1)S(1)}, bf16[1024,128]{1,0:T(8,128)(2,1)S(1)}, u32[]{:S(2)}, u32[]{:S(2)}) collective-permute-start(bf16[1024,128]{1,0:T(8,128)(2,1)S(1)} %get-tuple-element.129), channel_id=1, source_target_pairs={{32,64},{64,32},{33,65},{65,33},{34,66},{66,34},{35,67},{67,35},{3... | collective-permute-start | bytes 786440 | tf_op jit(solution)/shard_map/ppermute | solution.py:573
  16.4 7.0 %copy-start.3 = (bf16[512,128]{1,0:T(8,128)(2,1)}, bf16[512,128]{1,0:T(8,128)(2,1)S(1)}, u32[]{:S(2)}) copy-start(bf16[512,128]{1,0:T(8,128)(2,1)S(1)} %collective-permute-done.2.refs_3_) | copy-start | bytes 393220
  16.4 7.1 %collective-permute-start.3 = (bf16[1024,128]{1,0:T(8,128)(2,1)S(1)}, bf16[1024,128]{1,0:T(8,128)(2,1)S(1)}, u32[]{:S(2)}, u32[]{:S(2)}) collective-permute-start(bf16[1024,128]{1,0:T(8,128)(2,1)S(1)} %pad_maximum_fusion), channel_id=1, source_target_pairs={{0,6},{2,4},{4,2},{6,0},{1,7},{3,5},{5,3},{7,1},{8,14},{10,12},{12... | collective-permute-start | bytes 786440 | tf_op jit(solution)/shard_map/ppermute | solution.py:568
  23.4 5.3 %copy-start.12 = (bf16[1024,128]{1,0:T(8,128)(2,1)}, bf16[1024,128]{1,0:T(8,128)(2,1)S(1)}, u32[]{:S(2)}) copy-start(bf16[1024,128]{1,0:T(8,128)(2,1)S(1)} %collective-permute-done.4.rim_up) | copy-start | bytes 786436
  23.4 5.3 %copy-start.13 = (bf16[1024,128]{1,0:T(8,128)(2,1)}, bf16[1024,128]{1,0:T(8,128)(2,1)S(1)}, u32[]{:S(2)}) copy-start(bf16[1024,128]{1,0:T(8,128)(2,1)S(1)} %collective-permute-done.5.rim_down) | copy-start | bytes 786436
  23.5 5.2 %copy-start.8 = (bf16[1024,128]{1,0:T(8,128)(2,1)}, bf16[1024,128]{1,0:T(8,128)(2,1)S(1)}, u32[]{:S(2)}) copy-start(bf16[1024,128]{1,0:T(8,128)(2,1)S(1)} %collective-permute-done.3.refs_4_) | copy-start | bytes 786436
  23.5 5.2 %collective-permute-start.6 = (bf16[2048,128]{1,0:T(8,128)(2,1)S(1)}, bf16[2048,128]{1,0:T(8,128)(2,1)S(1)}, u32[]{:S(2)}, u32[]{:S(2)}) collective-permute-start(bf16[2048,128]{1,0:T(8,128)(2,1)S(1)} %constant_dynamic-update-slice_fusion), channel_id=1, source_target_pairs={{0,1},{1,0},{2,3},{3,2},{4,5},{5,4},{6,7},{7,6},{8,9},{9,8},{10,11... | collective-permute-start | bytes 1572872 | tf_op jit(solution)/shard_map/ppermute | solution.py:568
  58.3 12.8 %collective-permute-start.7 = (f32[272,256]{1,0:T(8,128)}, f32[272,256]{1,0:T(8,128)S(1)}, u32[]{:S(2)}, u32[]{:S(2)}) collective-permute-start(f32[272,256]{1,0:T(8,128)} %get-tuple-element.85), channel_id=1, source_target_pairs={{0,32},{32,0},{64,96},{96,64},{1,33},{33,1},{65,97},{97,65},{2,34}... | collective-permute-start | bytes 835592 | tf_op jit(solution)/shard_map/ppermute | solution.py:568
  61.8 9.9 %copy-start.6 = (f32[272,256]{1,0:T(8,128)S(1)}, f32[272,256]{1,0:T(8,128)}, u32[]{:S(2)}) copy-start(f32[272,256]{1,0:T(8,128)} %get-tuple-element.85) | copy-start | bytes 835588
  71.2 2.3 %collective-permute-start.8 = (bf16[2048,128]{1,0:T(8,128)(2,1)}, bf16[2048,128]{1,0:T(8,128)(2,1)S(1)}, u32[]{:S(2)}, u32[]{:S(2)}) collective-permute-start(bf16[2048,128]{1,0:T(8,128)(2,1)} %get-tuple-element.93), channel_id=1, source_target_pairs={{0,1},{1,0},{2,3},{3,2},{4,5},{5,4},{6,7},{7,6},{8,9},{9,8},{10,11... | collective-permute-start | bytes 1572872 | tf_op jit(solution)/shard_map/ppermute | solution.py:568
  71.7 13.6 %collective-permute-start.10 = (f32[272,256]{1,0:T(8,128)S(1)}, f32[272,256]{1,0:T(8,128)S(1)}, u32[]{:S(2)}, u32[]{:S(2)}) collective-permute-start(f32[272,256]{1,0:T(8,128)S(1)} %add.44), channel_id=1, source_target_pairs={{0,96},{32,64},{64,32},{96,0},{1,97},{33,65},{65,33},{97,1},{2,98}... | collective-permute-start | bytes 835592 | tf_op jit(solution)/shard_map/ppermute | solution.py:568
  74.6 10.7 %collective-permute-start.9 = (bf16[1024,128]{1,0:T(8,128)(2,1)S(1)}, bf16[1024,128]{1,0:T(8,128)(2,1)S(1)}, u32[]{:S(2)}, u32[]{:S(2)}) collective-permute-start(bf16[1024,128]{1,0:T(8,128)(2,1)S(1)} %slice.59), channel_id=1, source_target_pairs={{0,6},{2,4},{4,2},{6,0},{1,7},{3,5},{5,3},{7,1},{8,14},{10,12},{12... | collective-permute-start | bytes 786440 | tf_op jit(solution)/shard_map/ppermute | solution.py:568
  85.4 1.9 %collective-permute-start.11 = (f32[136,256]{1,0:T(8,128)S(1)}, f32[136,256]{1,0:T(8,128)S(1)}, u32[]{:S(2)}, u32[]{:S(2)}) collective-permute-start(f32[136,256]{1,0:T(8,128)S(1)} %slice.47), channel_id=1, source_target_pairs={{0,1},{1,0},{2,3},{3,2},{4,5},{5,4},{6,7},{7,6},{8,9},{9,8},{10,11... | collective-permute-start | bytes 417800 | tf_op jit(solution)/shard_map/ppermute | solution.py:568
  86.2 21.7 %collective-permute-start.12 = (bf16[512,128]{1,0:T(8,128)(2,1)S(1)}, bf16[512,128]{1,0:T(8,128)(2,1)S(1)}, u32[]{:S(2)}, u32[]{:S(2)}) collective-permute-start(bf16[512,128]{1,0:T(8,128)(2,1)S(1)} %slice.60), channel_id=1, source_target_pairs={{0,2},{2,0},{4,6},{6,4},{1,3},{3,1},{5,7},{7,5},{8,10},{10,8},{12,... | collective-permute-start | bytes 393224 | tf_op jit(solution)/shard_map/ppermute | solution.py:568
  86.5 21.5 %collective-permute-start.14 = (bf16[1024,128]{1,0:T(8,128)(2,1)S(1)}, bf16[1024,128]{1,0:T(8,128)(2,1)S(1)}, u32[]{:S(2)}, u32[]{:S(2)}) collective-permute-start(bf16[1024,128]{1,0:T(8,128)(2,1)S(1)} %copy-done.11), channel_id=1, source_target_pairs={{0,32},{32,0},{64,96},{96,64},{1,33},{33,1},{65,97},{97,65},{2,34}... | collective-permute-start | bytes 786440 | tf_op jit(solution)/shard_map/ppermute | solution.py:572
  86.7 21.3 %collective-permute-start.15 = (bf16[1024,128]{1,0:T(8,128)(2,1)S(1)}, bf16[1024,128]{1,0:T(8,128)(2,1)S(1)}, u32[]{:S(2)}, u32[]{:S(2)}) collective-permute-start(bf16[1024,128]{1,0:T(8,128)(2,1)S(1)} %copy-done.10), channel_id=1, source_target_pairs={{32,64},{64,32},{33,65},{65,33},{34,66},{66,34},{35,67},{67,35},{3... | collective-permute-start | bytes 786440 | tf_op jit(solution)/shard_map/ppermute | solution.py:573
  87.4 20.6 %collective-permute-start.13 = (f32[136,256]{1,0:T(8,128)S(1)}, f32[136,256]{1,0:T(8,128)S(1)}, u32[]{:S(2)}, u32[]{:S(2)}) collective-permute-start(f32[136,256]{1,0:T(8,128)S(1)} %slice_add_fusion), channel_id=1, source_target_pairs={{0,6},{2,4},{4,2},{6,0},{1,7},{3,5},{5,3},{7,1},{8,14},{10,12},{12... | collective-permute-start | bytes 417800 | tf_op jit(solution)/shard_map/ppermute | solution.py:568
  107.9 11.1 %copy-start = (s32[128]{0:T(128)S(1)}, s32[128]{0:T(128)}, u32[]{:S(2)}) copy-start(s32[128]{0:T(128)} %hub_rows.3) | copy-start | bytes 1540
  107.9 11.1 %copy-start.1 = (f32[4096,128]{1,0:T(8,128)S(1)}, f32[4096,128]{1,0:T(8,128)}, u32[]{:S(2)}) copy-start(f32[4096,128]{1,0:T(8,128)} %own_scatter.1.own) | copy-start | bytes 6291460
  108.0 5.3 %collective-permute-start.17 = (f32[136,256]{1,0:T(8,128)S(1)}, f32[136,256]{1,0:T(8,128)S(1)}, u32[]{:S(2)}, u32[]{:S(2)}) collective-permute-start(f32[136,256]{1,0:T(8,128)S(1)} %add.49), channel_id=1, source_target_pairs={{0,2},{2,0},{4,6},{6,4},{1,3},{3,1},{5,7},{7,5},{8,10},{10,8},{12,... | collective-permute-start | bytes 417800 | tf_op jit(solution)/shard_map/ppermute | solution.py:568
  108.9 4.4 %collective-permute-start.16 = (bf16[256,128]{1,0:T(8,128)(2,1)S(1)}, bf16[256,128]{1,0:T(8,128)(2,1)S(1)}, u32[]{:S(2)}, u32[]{:S(2)}) collective-permute-start(bf16[256,128]{1,0:T(8,128)(2,1)S(1)} %slice.61), channel_id=1, source_target_pairs={{0,24},{8,16},{16,8},{24,0},{1,25},{9,17},{17,9},{25,1},{2,26},{10... | collective-permute-start | bytes 196616 | tf_op jit(solution)/shard_map/ppermute | solution.py:568
  113.3 5.2 %collective-permute-start.19 = (f32[136,256]{1,0:T(8,128)S(1)}, f32[136,256]{1,0:T(8,128)S(1)}, u32[]{:S(2)}, u32[]{:S(2)}) collective-permute-start(f32[136,256]{1,0:T(8,128)S(1)} %add.51), channel_id=1, source_target_pairs={{0,24},{8,16},{16,8},{24,0},{1,25},{9,17},{17,9},{25,1},{2,26},{10... | collective-permute-start | bytes 417800 | tf_op jit(solution)/shard_map/ppermute | solution.py:568
  115.7 2.8 %collective-permute-start.18 = (bf16[128,128]{1,0:T(8,128)(2,1)S(1)}, bf16[128,128]{1,0:T(8,128)(2,1)S(1)}, u32[]{:S(2)}, u32[]{:S(2)}) collective-permute-start(bf16[128,128]{1,0:T(8,128)(2,1)S(1)} %slice.62), channel_id=1, source_target_pairs={{0,8},{8,0},{16,24},{24,16},{1,9},{9,1},{17,25},{25,17},{2,10},{10... | collective-permute-start | bytes 98312 | tf_op jit(solution)/shard_map/ppermute | solution.py:568
  118.6 4.3 %collective-permute-start.20 = (f32[136,256]{1,0:T(8,128)S(1)}, f32[136,256]{1,0:T(8,128)S(1)}, u32[]{:S(2)}, u32[]{:S(2)}) collective-permute-start(f32[136,256]{1,0:T(8,128)S(1)} %add.53), channel_id=1, source_target_pairs={{0,8},{8,0},{16,24},{24,16},{1,9},{9,1},{17,25},{25,17},{2,10},{10... | collective-permute-start | bytes 417800 | tf_op jit(solution)/shard_map/ppermute | solution.py:568
  122.9 6.1 %collective-permute-start.21 = (f32[136,256]{1,0:T(8,128)S(1)}, f32[136,256]{1,0:T(8,128)S(1)}, u32[]{:S(2)}, u32[]{:S(2)}) collective-permute-start(f32[136,256]{1,0:T(8,128)S(1)} %add.55.mine), channel_id=1, source_target_pairs={{0,1},{1,0},{2,3},{3,2},{4,5},{5,4},{6,7},{7,6},{8,9},{9,8},{10,11... | collective-permute-start | bytes 417800 | tf_op jit(solution)/shard_map/ppermute | solution.py:568
  (4 other events, 6.2 us)

commit v7 on v6

--- a/solution.py
+++ b/solution.py
@@ -578,13 +578,16 @@
     return value[:rows], value[rows:]
 
 
-def halve(keep, got, axis, flip):
-    mine, give = halves(plus(keep, got))
-    return mine, swap(give.astype(jnp.bfloat16), axis, flip)
-
-
-def plus(keep, got):
-    return keep.astype(jnp.float32) + got.astype(jnp.float32)
+def give_half(parts, axis, flip):
+    rows = min(part.shape[0] for part in parts)
+    return swap(add_up(parts, rows // 2, rows).astype(jnp.bfloat16), axis, flip)
+
+
+def add_up(parts, start, stop):
+    total = parts[0][start:stop].astype(jnp.float32)
+    for part in parts[1:]:
+        total = total + part[start:stop].astype(jnp.float32)
+    return total
 
 
 def tie(*values):
@@ -629,37 +632,35 @@
     keep, give = scatter("hub", HUBS, jnp.bfloat16, 8, 6, hub_lists, src)
     keep, give, src, other = tie(keep, give, src, other)
     grads = grads + other
-    got = swap(give, "core", 1)
+    parts = [keep, swap(give, "core", 1)]
     other = swap(grads, "z", 3)
-    got, src = tie(got, src)
-    keep, got = halve(keep, got, "x", 3)
+    parts, src = tie(parts, src)
+    got = give_half(parts, "x", 3)
     rims = scatter("rim", 2 * HALO, jnp.bfloat16, 8, 6, rim_lists, src)
-    keep, got, src, other, *rims = tie(keep, got, src, other, *rims)
+    parts, src, other, rims = tie(parts + [got], src, other, rims)
 
     grads, give = halves(grads + other)
     other = swap(give, "core", 1)
-    keep, got = halve(keep, got, "x", 1)
+    got = give_half(parts, "x", 1)
     other, src = tie(other, src)
     grads = grads + other
-    other = swap(grads, "x", 3)
+    others = [swap(grads, "x", flip) for flip in (1, 3, 2)]
+    (own,) = scatter("own", NODES, jnp.float32, 20, CHAINS, own_lists, src, base)
+    parts, others, own, rims = tie(parts + [got], others, own, rims)
+
+    grads = (grads + others[0]) + (others[1] + others[2])
+    got = give_half(parts, "y", 3)
+    other = swap(grads, "y", 1)
     rims = swap_rims(*rims)
-    (own,) = scatter("own", NODES, jnp.float32, 20, CHAINS, own_lists, src, base)
-    keep, got, other, own, *rims = tie(keep, got, other, own, *rims)
-
-    keep, got = halve(keep, got, "y", 3)
-    grads = grads + other
-    other = swap(grads, "x", 1)
-    keep, got, other = tie(keep, got, other)
-    keep, got = halve(keep, got, "y", 1)
+    parts, other = tie(parts + [got], other)
+    got = give_half(parts, "y", 1)
     grads = grads + other
     other = swap(grads, "y", 3)
-    keep, got, other = tie(keep, got, other)
-    grads = grads + other
-    other = swap(grads, "y", 1)
-    grad_features = finish(hub_rows, own, *rims, plus(keep, got))
-    other, grad_features = tie(other, grad_features)
+    parts, other, rims = tie(parts + [got], other, rims)
     grads = grads + other
     other = swap(grads, "core", 1)
+    grad_features = finish(hub_rows, own, *rims, add_up(parts, 0, HUB))
+    other, grad_features = tie(other, grad_features)
     grad_self, grad_neigh, grad_bias = hand_out(grads, other)
     return act, grad_features, grad_self, grad_neigh, grad_bias.reshape(H)
 

time: 131 us -> 128 us (0.977)
  waiting for transfers between devices: 10.1 us -> 8.15 us
    ppermute x18 -> x19, waiting for transfers between devices: 10 us -> 8.14 us  [swap(): return lax.ppermute(value, axis, [(i, i ^ flip) for i in range(count)])]
    ppermute x18 -> x19, starting transfers between devices: 31.3 us -> 31 us  [swap(): return lax.ppermute(value, axis, [(i, i ^ flip) for i in range(count)])]
  transfers between devices with their start and end apart: 22 -> 23, of which waited for: 7 -> 7; matrix products, arithmetic and copies ran while one was open for 1% -> 1% of each run, Pallas kernels for 38% -> 39%
where the time goes in v7:
time: 128 us; the launch traced here: 127 us
  Pallas kernels  81.1 us (63%)
  starting transfers between devices  34.7 us (27%)
  waiting for transfers between devices  8.15 us (6%)
  other arithmetic  1.38 us (1%)
    pallas_call x3, Pallas kernels, scatter(): pl.pallas_call(functools.partial(scatter_kernel, kind), out_shape=(jax.Sh...  37.6 us
    ppermute x19, starting transfers between devices, swap(): return lax.ppermute(value, axis, [(i, i ^ flip) for i in range(count)])  31 us
    pallas_call x1, Pallas kernels, forward(): pl.pallas_call(forward_kernel, out_shape=(jax.ShapeDtypeStruct((NODES, H)...  28.4 us
    pallas_call x3, Pallas kernels, plan(): pl.pallas_call(kernel, out_shape=outs, in_specs=[vmem] * len(inputs), out...  9.89 us
    ppermute x19, waiting for transfers between devices, swap(): return lax.ppermute(value, axis, [(i, i ^ flip) for i in range(count)])  8.14 us
  transfers between devices with their start and end apart: 23, of which 7 were waited for; matrix products, arithmetic and copies ran while one was open for 1% of the time, Pallas kernels for 39%

profile of v7, /device:TPU:1, one launch (start us, length us, event | category | flops | bytes accessed | tf_op | source)
XLA Modules:
  0.0 127.2 jit_solution(10571743990086080954)
XLA Ops:
  0.6 2.2 %pick_hubs.1.refs_0_ = bf16[128,128]{1,0:T(8,128)(2,1)} custom-call(s32[128]{0:T(128)} %hub_rows.3, bf16[4096,128]{1,0:T(8,128)(2,1)} %features.3), custom_call_target="tpu_custom_call" | custom-call | flops 2000000000 | tf_op jit(solution)/shard_map/pick_hubs/pallas_call | solution.py:70
  2.8 2.1 %collective-permute-start = (bf16[128,128]{1,0:T(8,128)(2,1)}, bf16[128,128]{1,0:T(8,128)(2,1)S(1)}, u32[]{:S(2)}, u32[]{:S(2)}) collective-permute-start(bf16[128,128]{1,0:T(8,128)(2,1)} %pick_hubs.1.refs_0_), channel_id=1, source_target_pairs={{0,8},{8,0},{16,24},{24,16},{1,9},{9,1},{17,25},{25,17},{2,10},{10... | collective-permute-start | bytes 98312 | tf_op jit(solution)/shard_map/ppermute | solution.py:568
  4.9 2.8 %all_plan_kernel.1 = (s32[320,128]{1,0:T(8,128)}, s32[40,128]{1,0:T(8,128)}) custom-call(s32[10,4096]{1,0:T(8,128)} %bitcast.11, s32[32,128]{1,0:T(8,128)} %bitcast.12), custom_call_target="tpu_custom_call" | custom-call | flops 4000000000 | tf_op jit(solution)/shard_map/all_plan_kernel/pallas_call | solution.py:194
  7.7 2.0 %collective-permute-start.1 = (bf16[256,128]{1,0:T(8,128)(2,1)S(1)}, bf16[256,128]{1,0:T(8,128)(2,1)S(1)}, u32[]{:S(2)}, u32[]{:S(2)}) collective-permute-start(bf16[256,128]{1,0:T(8,128)(2,1)S(1)} %pad_maximum_fusion.2), channel_id=1, source_target_pairs={{0,24},{8,16},{16,8},{24,0},{1,25},{9,17},{17,9},{25,1},{2,26},{10... | collective-permute-start | bytes 196616 | tf_op jit(solution)/shard_map/ppermute | solution.py:568
  9.7 2.7 %hub_plan_kernel.1 = (s32[320,128]{1,0:T(8,128)}, s32[40,128]{1,0:T(8,128)}) custom-call(s32[320,128]{1,0:T(8,128)} %get-tuple-element.91.flat, s32[32,128]{1,0:T(8,128)} %bitcast.13), custom_call_target="tpu_custom_call" | custom-call | flops 4000000000 | tf_op jit(solution)/shard_map/hub_plan_kernel/pallas_call | solution.py:194
  12.5 1.3 %collective-permute-start.2 = (bf16[512,128]{1,0:T(8,128)(2,1)S(1)}, bf16[512,128]{1,0:T(8,128)(2,1)S(1)}, u32[]{:S(2)}, u32[]{:S(2)}) collective-permute-start(bf16[512,128]{1,0:T(8,128)(2,1)S(1)} %pad_maximum_fusion.1), channel_id=1, source_target_pairs={{0,2},{2,0},{4,6},{6,4},{1,3},{3,1},{5,7},{7,5},{8,10},{10,8},{12,... | collective-permute-start | bytes 393224 | tf_op jit(solution)/shard_map/ppermute | solution.py:568
  13.8 1.7 %collective-permute-start.4 = (bf16[1024,128]{1,0:T(8,128)(2,1)S(1)}, bf16[1024,128]{1,0:T(8,128)(2,1)S(1)}, u32[]{:S(2)}, u32[]{:S(2)}) collective-permute-start(bf16[1024,128]{1,0:T(8,128)(2,1)S(1)} %get-tuple-element.160), channel_id=1, source_target_pairs={{0,32},{32,0},{64,96},{96,64},{1,33},{33,1},{65,97},{97,65},{2,34}... | collective-permute-start | bytes 786440 | tf_op jit(solution)/shard_map/ppermute | solution.py:572
  16.4 2.6 %collective-permute-start.3 = (bf16[1024,128]{1,0:T(8,128)(2,1)S(1)}, bf16[1024,128]{1,0:T(8,128)(2,1)S(1)}, u32[]{:S(2)}, u32[]{:S(2)}) collective-permute-start(bf16[1024,128]{1,0:T(8,128)(2,1)S(1)} %pad_maximum_fusion), channel_id=1, source_target_pairs={{0,6},{2,4},{4,2},{6,0},{1,7},{3,5},{5,3},{7,1},{8,14},{10,12},{12... | collective-permute-start | bytes 786440 | tf_op jit(solution)/shard_map/ppermute | solution.py:568
  19.0 4.4 %rim_plan_kernel.1 = (s32[320,128]{1,0:T(8,128)}, s32[40,128]{1,0:T(8,128)}, s32[40,128]{1,0:T(8,128)}) custom-call(s32[320,128]{1,0:T(8,128)} %get-tuple-element.91.flat, s32[32,128]{1,0:T(8,128)} %bitcast.14), custom_call_target="tpu_custom_call" | custom-call | flops 5000000000 | tf_op jit(solution)/shard_map/rim_plan_kernel/pallas_call | solution.py:194
  23.5 3.6 %collective-permute-start.6 = (bf16[2048,128]{1,0:T(8,128)(2,1)S(1)}, bf16[2048,128]{1,0:T(8,128)(2,1)S(1)}, u32[]{:S(2)}, u32[]{:S(2)}) collective-permute-start(bf16[2048,128]{1,0:T(8,128)(2,1)S(1)} %constant_dynamic-update-slice_fusion), channel_id=1, source_target_pairs={{0,1},{1,0},{2,3},{3,2},{4,5},{5,4},{6,7},{7,6},{8,9},{9,8},{10,11... | collective-permute-start | bytes 1572872 | tf_op jit(solution)/shard_map/ppermute | solution.py:568
  27.2 1.5 %collective-permute-done.6.refs_5_ = bf16[2048,128]{1,0:T(8,128)(2,1)S(1)} collective-permute-done((bf16[2048,128]{1,0:T(8,128)(2,1)S(1)}, bf16[2048,128]{1,0:T(8,128)(2,1)S(1)}, u32[]{:S(2)}, u32[]{:S(2)}) %collective-permute-start.6) | collective-permute-done | bytes 524320 | tf_op jit(solution)/shard_map/ppermute | solution.py:568
  28.7 0.8 copy-done.10
  29.5 28.4 %forward.1 = (bf16[4096,256]{1,0:T(8,128)(2,1)}, f32[4096,128]{1,0:T(8,128)}, f32[4096,128]{1,0:T(8,128)}, f32[272,256]{1,0:T(8,128)}) custom-call(s32[5120]{0:T(1024)} %bitcast.22, s32[40960]{0:T(1024)} %bitcast.19, bf16[4096,128]{1,0:T(8,128)(2,1)} %features.3, bf16[1024,128]{1,0:T(8,128)(2,1)} %copy-done.13, bf16[1024,128]{1,0:T(8,128)(2,1)} %copy-done.14, ...), custom_call_target="tpu_custom_call" | custom-call | flops 30000001024 | tf_op jit(solution)/shard_map/forward/pallas_call | solution.py:374
  57.9 3.6 %collective-permute-start.7 = (f32[272,256]{1,0:T(8,128)}, f32[272,256]{1,0:T(8,128)S(1)}, u32[]{:S(2)}, u32[]{:S(2)}) collective-permute-start(f32[272,256]{1,0:T(8,128)} %get-tuple-element.100), channel_id=1, source_target_pairs={{0,32},{32,0},{64,96},{96,64},{1,33},{33,1},{65,97},{97,65},{2,34}... | collective-permute-start | bytes 835592 | tf_op jit(solution)/shard_map/ppermute | solution.py:568
  61.6 9.2 %hub_scatter.1 = (bf16[2048,128]{1,0:T(8,128)(2,1)}, bf16[2048,128]{1,0:T(8,128)(2,1)}) custom-call(s32[5120]{0:T(1024)} %bitcast.23, s32[40960]{0:T(1024)} %bitcast.20, f32[4096,128]{1,0:T(8,128)} %get-tuple-element.125.src), custom_call_target="tpu_custom_call" | custom-call | flops 8000000000 | tf_op jit(solution)/shard_map/hub_scatter/pallas_call | solution.py:472
  70.8 0.8 collective-permute-start.8
  72.2 1.2 collective-permute-done.8
  73.4 1.0 add_convert_fusion
  74.4 1.9 %collective-permute-start.9 = (bf16[1024,128]{1,0:T(8,128)(2,1)S(1)}, bf16[1024,128]{1,0:T(8,128)(2,1)S(1)}, u32[]{:S(2)}, u32[]{:S(2)}) collective-permute-start(bf16[1024,128]{1,0:T(8,128)(2,1)S(1)} %add_convert_fusion), channel_id=1, source_target_pairs={{0,6},{2,4},{4,2},{6,0},{1,7},{3,5},{5,3},{7,1},{8,14},{10,12},{12... | collective-permute-start | bytes 786440 | tf_op jit(solution)/shard_map/ppermute | solution.py:568
  76.3 8.4 %rim_scatter.1 = (bf16[1024,128]{1,0:T(8,128)(2,1)}, bf16[1024,128]{1,0:T(8,128)(2,1)}) custom-call(s32[5120]{0:T(1024)} %bitcast.24, s32[40960]{0:T(1024)} %bitcast.17, f32[4096,128]{1,0:T(8,128)} %get-tuple-element.125.src), custom_call_target="tpu_custom_call" | custom-call | flops 8000000000 | tf_op jit(solution)/shard_map/rim_scatter/pallas_call | solution.py:472
  86.4 0.9 collective-permute-start.13
  87.3 1.1 collective-permute-start.14
  88.4 1.3 %collective-permute-start.15 = (f32[136,256]{1,0:T(8,128)S(1)}, f32[136,256]{1,0:T(8,128)S(1)}, u32[]{:S(2)}, u32[]{:S(2)}) collective-permute-start(f32[136,256]{1,0:T(8,128)S(1)} %slice_add_fusion), channel_id=1, source_target_pairs={{0,4},{2,6},{4,0},{6,2},{1,5},{3,7},{5,1},{7,3},{8,12},{10,14},{12... | collective-permute-start | bytes 417800 | tf_op jit(solution)/shard_map/ppermute | solution.py:568
  89.8 19.9 %own_scatter.1.own = f32[4096,128]{1,0:T(8,128)} custom-call(s32[5120]{0:T(1024)} %bitcast.21, s32[40960]{0:T(1024)} %bitcast.18, f32[4096,128]{1,0:T(8,128)} %get-tuple-element.125.src, f32[4096,128]{1,0:T(8,128)} %get-tuple-element.126.refs_0_), custom_call_target="tpu_custom_call" | custom-call | flops 20000000000 | tf_op jit(solution)/shard_map/own_scatter/pallas_call | solution.py:472
  109.8 0.9 collective-permute-start.17
  110.7 1.8 %collective-permute-start.16 = (bf16[256,128]{1,0:T(8,128)(2,1)S(1)}, bf16[256,128]{1,0:T(8,128)(2,1)S(1)}, u32[]{:S(2)}, u32[]{:S(2)}) collective-permute-start(bf16[256,128]{1,0:T(8,128)(2,1)S(1)} %add_convert_fusion.2), channel_id=1, source_target_pairs={{0,24},{8,16},{16,8},{24,0},{1,25},{9,17},{17,9},{25,1},{2,26},{10... | collective-permute-start | bytes 196616 | tf_op jit(solution)/shard_map/ppermute | solution.py:568
  113.8 1.3 %collective-permute-done.16 = bf16[256,128]{1,0:T(8,128)(2,1)S(1)} collective-permute-done((bf16[256,128]{1,0:T(8,128)(2,1)S(1)}, bf16[256,128]{1,0:T(8,128)(2,1)S(1)}, u32[]{:S(2)}, u32[]{:S(2)}) %collective-permute-start.16) | collective-permute-done | bytes 65568 | tf_op jit(solution)/shard_map/ppermute | solution.py:568
  115.1 1.8 %collective-permute-start.19 = (f32[136,256]{1,0:T(8,128)S(1)}, f32[136,256]{1,0:T(8,128)S(1)}, u32[]{:S(2)}, u32[]{:S(2)}) collective-permute-start(f32[136,256]{1,0:T(8,128)S(1)} %add.89), channel_id=1, source_target_pairs={{0,24},{8,16},{16,8},{24,0},{1,25},{9,17},{17,9},{25,1},{2,26},{10... | collective-permute-start | bytes 417800 | tf_op jit(solution)/shard_map/ppermute | solution.py:568
  117.1 3.0 %collective-permute-done.18 = bf16[128,128]{1,0:T(8,128)(2,1)S(1)} collective-permute-done((bf16[128,128]{1,0:T(8,128)(2,1)S(1)}, bf16[128,128]{1,0:T(8,128)(2,1)S(1)}, u32[]{:S(2)}, u32[]{:S(2)}) %collective-permute-start.18) | collective-permute-done | bytes 32800 | tf_op jit(solution)/shard_map/ppermute | solution.py:568
  120.4 3.8 %collective-permute-start.22 = (f32[136,256]{1,0:T(8,128)S(1)}, f32[136,256]{1,0:T(8,128)S(1)}, u32[]{:S(2)}, u32[]{:S(2)}) collective-permute-start(f32[136,256]{1,0:T(8,128)S(1)} %add.94.mine), channel_id=1, source_target_pairs={{0,1},{1,0},{2,3},{3,2},{4,5},{5,4},{6,7},{7,6},{8,9},{9,8},{10,11... | collective-permute-start | bytes 417800 | tf_op jit(solution)/shard_map/ppermute | solution.py:568
  124.2 2.3 %finish.1 = bf16[4096,128]{1,0:T(8,128)(2,1)} custom-call(s32[128]{0:T(128)S(1)} %copy-done, f32[4096,128]{1,0:T(8,128)S(1)} %copy-done.1, bf16[1024,128]{1,0:T(8,128)(2,1)S(1)} %collective-permute-done.20.rim_0, bf16[1024,128]{1,0:T(8,128)(2,1)S(1)} %collective-permute-done.21.rim_1, f32[128,128]{1,0:T(8,128)S(1)} %convert_add_fusion.share), custom_call_target="tpu_custom_call" | custom-call | flops 3000000000 | tf_op jit(solution)/shard_map/finish/pallas_call | solution.py:526
  126.5 0.7 hand_out.1
  (75 shorter events, 5.0 us)
Async XLA Ops:
  2.8 4.9 %collective-permute-start = (bf16[128,128]{1,0:T(8,128)(2,1)}, bf16[128,128]{1,0:T(8,128)(2,1)S(1)}, u32[]{:S(2)}, u32[]{:S(2)}) collective-permute-start(bf16[128,128]{1,0:T(8,128)(2,1)} %pick_hubs.1.refs_0_), channel_id=1, source_target_pairs={{0,8},{8,0},{16,24},{24,16},{1,9},{9,1},{17,25},{25,17},{2,10},{10... | collective-permute-start | bytes 98312 | tf_op jit(solution)/shard_map/ppermute | solution.py:568
  7.7 8.7 %copy-start.6 = (bf16[128,128]{1,0:T(8,128)(2,1)}, bf16[128,128]{1,0:T(8,128)(2,1)S(1)}, u32[]{:S(2)}) copy-start(bf16[128,128]{1,0:T(8,128)(2,1)S(1)} %collective-permute-done.refs_1_) | copy-start | bytes 98308
  7.7 4.7 %collective-permute-start.1 = (bf16[256,128]{1,0:T(8,128)(2,1)S(1)}, bf16[256,128]{1,0:T(8,128)(2,1)S(1)}, u32[]{:S(2)}, u32[]{:S(2)}) collective-permute-start(bf16[256,128]{1,0:T(8,128)(2,1)S(1)} %pad_maximum_fusion.2), channel_id=1, source_target_pairs={{0,24},{8,16},{16,8},{24,0},{1,25},{9,17},{17,9},{25,1},{2,26},{10... | collective-permute-start | bytes 196616 | tf_op jit(solution)/shard_map/ppermute | solution.py:568
  12.4 10.9 %copy-start.2 = (bf16[256,128]{1,0:T(8,128)(2,1)}, bf16[256,128]{1,0:T(8,128)(2,1)S(1)}, u32[]{:S(2)}) copy-start(bf16[256,128]{1,0:T(8,128)(2,1)S(1)} %collective-permute-done.1.refs_2_) | copy-start | bytes 196612
  12.5 3.9 %collective-permute-start.2 = (bf16[512,128]{1,0:T(8,128)(2,1)S(1)}, bf16[512,128]{1,0:T(8,128)(2,1)S(1)}, u32[]{:S(2)}, u32[]{:S(2)}) collective-permute-start(bf16[512,128]{1,0:T(8,128)(2,1)S(1)} %pad_maximum_fusion.1), channel_id=1, source_target_pairs={{0,2},{2,0},{4,6},{6,4},{1,3},{3,1},{5,7},{7,5},{8,10},{10,8},{12,... | collective-permute-start | bytes 393224 | tf_op jit(solution)/shard_map/ppermute | solution.py:568
  13.8 9.6 %collective-permute-start.4 = (bf16[1024,128]{1,0:T(8,128)(2,1)S(1)}, bf16[1024,128]{1,0:T(8,128)(2,1)S(1)}, u32[]{:S(2)}, u32[]{:S(2)}) collective-permute-start(bf16[1024,128]{1,0:T(8,128)(2,1)S(1)} %get-tuple-element.160), channel_id=1, source_target_pairs={{0,32},{32,0},{64,96},{96,64},{1,33},{33,1},{65,97},{97,65},{2,34}... | collective-permute-start | bytes 786440 | tf_op jit(solution)/shard_map/ppermute | solution.py:572
  15.5 7.9 %collective-permute-start.5 = (bf16[1024,128]{1,0:T(8,128)(2,1)S(1)}, bf16[1024,128]{1,0:T(8,128)(2,1)S(1)}, u32[]{:S(2)}, u32[]{:S(2)}) collective-permute-start(bf16[1024,128]{1,0:T(8,128)(2,1)S(1)} %get-tuple-element.159), channel_id=1, source_target_pairs={{32,64},{64,32},{33,65},{65,33},{34,66},{66,34},{35,67},{67,35},{3... | collective-permute-start | bytes 786440 | tf_op jit(solution)/shard_map/ppermute | solution.py:573
  16.4 7.0 %copy-start.4 = (bf16[512,128]{1,0:T(8,128)(2,1)}, bf16[512,128]{1,0:T(8,128)(2,1)S(1)}, u32[]{:S(2)}) copy-start(bf16[512,128]{1,0:T(8,128)(2,1)S(1)} %collective-permute-done.2.refs_3_) | copy-start | bytes 393220
  16.4 7.0 %collective-permute-start.3 = (bf16[1024,128]{1,0:T(8,128)(2,1)S(1)}, bf16[1024,128]{1,0:T(8,128)(2,1)S(1)}, u32[]{:S(2)}, u32[]{:S(2)}) collective-permute-start(bf16[1024,128]{1,0:T(8,128)(2,1)S(1)} %pad_maximum_fusion), channel_id=1, source_target_pairs={{0,6},{2,4},{4,2},{6,0},{1,7},{3,5},{5,3},{7,1},{8,14},{10,12},{12... | collective-permute-start | bytes 786440 | tf_op jit(solution)/shard_map/ppermute | solution.py:568
  23.5 5.2 %collective-permute-start.6 = (bf16[2048,128]{1,0:T(8,128)(2,1)S(1)}, bf16[2048,128]{1,0:T(8,128)(2,1)S(1)}, u32[]{:S(2)}, u32[]{:S(2)}) collective-permute-start(bf16[2048,128]{1,0:T(8,128)(2,1)S(1)} %constant_dynamic-update-slice_fusion), channel_id=1, source_target_pairs={{0,1},{1,0},{2,3},{3,2},{4,5},{5,4},{6,7},{7,6},{8,9},{9,8},{10,11... | collective-permute-start | bytes 1572872 | tf_op jit(solution)/shard_map/ppermute | solution.py:568
  57.9 12.9 %collective-permute-start.7 = (f32[272,256]{1,0:T(8,128)}, f32[272,256]{1,0:T(8,128)S(1)}, u32[]{:S(2)}, u32[]{:S(2)}) collective-permute-start(f32[272,256]{1,0:T(8,128)} %get-tuple-element.100), channel_id=1, source_target_pairs={{0,32},{32,0},{64,96},{96,64},{1,33},{33,1},{65,97},{97,65},{2,34}... | collective-permute-start | bytes 835592 | tf_op jit(solution)/shard_map/ppermute | solution.py:568
  61.6 10.1 %copy-start.7 = (f32[272,256]{1,0:T(8,128)S(1)}, f32[272,256]{1,0:T(8,128)}, u32[]{:S(2)}) copy-start(f32[272,256]{1,0:T(8,128)} %get-tuple-element.100) | copy-start | bytes 835588
  70.8 2.6 %collective-permute-start.8 = (bf16[2048,128]{1,0:T(8,128)(2,1)}, bf16[2048,128]{1,0:T(8,128)(2,1)S(1)}, u32[]{:S(2)}, u32[]{:S(2)}) collective-permute-start(bf16[2048,128]{1,0:T(8,128)(2,1)} %get-tuple-element.108), channel_id=1, source_target_pairs={{0,1},{1,0},{2,3},{3,2},{4,5},{5,4},{6,7},{7,6},{8,9},{9,8},{10,11... | collective-permute-start | bytes 1572872 | tf_op jit(solution)/shard_map/ppermute | solution.py:568
  71.7 13.1 %collective-permute-start.10 = (f32[272,256]{1,0:T(8,128)S(1)}, f32[272,256]{1,0:T(8,128)S(1)}, u32[]{:S(2)}, u32[]{:S(2)}) collective-permute-start(f32[272,256]{1,0:T(8,128)S(1)} %add.77), channel_id=1, source_target_pairs={{0,96},{32,64},{64,32},{96,0},{1,97},{33,65},{65,33},{97,1},{2,98}... | collective-permute-start | bytes 835592 | tf_op jit(solution)/shard_map/ppermute | solution.py:568
  74.4 11.0 %copy-start.3 = (bf16[2048,128]{1,0:T(8,128)(2,1)S(1)}, bf16[2048,128]{1,0:T(8,128)(2,1)}, u32[]{:S(2)}) copy-start(bf16[2048,128]{1,0:T(8,128)(2,1)} %get-tuple-element.148) | copy-start | bytes 1572868
  74.4 10.4 %collective-permute-start.9 = (bf16[1024,128]{1,0:T(8,128)(2,1)S(1)}, bf16[1024,128]{1,0:T(8,128)(2,1)S(1)}, u32[]{:S(2)}, u32[]{:S(2)}) collective-permute-start(bf16[1024,128]{1,0:T(8,128)(2,1)S(1)} %add_convert_fusion), channel_id=1, source_target_pairs={{0,6},{2,4},{4,2},{6,0},{1,7},{3,5},{5,3},{7,1},{8,14},{10,12},{12... | collective-permute-start | bytes 786440 | tf_op jit(solution)/shard_map/ppermute | solution.py:568
  84.9 1.5 %collective-permute-start.11 = (f32[136,256]{1,0:T(8,128)S(1)}, f32[136,256]{1,0:T(8,128)S(1)}, u32[]{:S(2)}, u32[]{:S(2)}) collective-permute-start(f32[136,256]{1,0:T(8,128)S(1)} %slice.85), channel_id=1, source_target_pairs={{0,1},{1,0},{2,3},{3,2},{4,5},{5,4},{6,7},{7,6},{8,9},{9,8},{10,11... | collective-permute-start | bytes 417800 | tf_op jit(solution)/shard_map/ppermute | solution.py:568
  85.5 24.2 %collective-permute-start.12 = (bf16[512,128]{1,0:T(8,128)(2,1)S(1)}, bf16[512,128]{1,0:T(8,128)(2,1)S(1)}, u32[]{:S(2)}, u32[]{:S(2)}) collective-permute-start(bf16[512,128]{1,0:T(8,128)(2,1)S(1)} %add_convert_fusion.1), channel_id=1, source_target_pairs={{0,2},{2,0},{4,6},{6,4},{1,3},{3,1},{5,7},{7,5},{8,10},{10,8},{12,... | collective-permute-start | bytes 393224 | tf_op jit(solution)/shard_map/ppermute | solution.py:568
  86.4 23.3 %collective-permute-start.13 = (f32[136,256]{1,0:T(8,128)S(1)}, f32[136,256]{1,0:T(8,128)S(1)}, u32[]{:S(2)}, u32[]{:S(2)}) collective-permute-start(f32[136,256]{1,0:T(8,128)S(1)} %slice_add_fusion), channel_id=1, source_target_pairs={{0,2},{2,0},{4,6},{6,4},{1,3},{3,1},{5,7},{7,5},{8,10},{10,8},{12,... | collective-permute-start | bytes 417800 | tf_op jit(solution)/shard_map/ppermute | solution.py:568
  87.3 22.4 %collective-permute-start.14 = (f32[136,256]{1,0:T(8,128)S(1)}, f32[136,256]{1,0:T(8,128)S(1)}, u32[]{:S(2)}, u32[]{:S(2)}) collective-permute-start(f32[136,256]{1,0:T(8,128)S(1)} %slice_add_fusion), channel_id=1, source_target_pairs={{0,6},{2,4},{4,2},{6,0},{1,7},{3,5},{5,3},{7,1},{8,14},{10,12},{12... | collective-permute-start | bytes 417800 | tf_op jit(solution)/shard_map/ppermute | solution.py:568
  88.4 21.3 %collective-permute-start.15 = (f32[136,256]{1,0:T(8,128)S(1)}, f32[136,256]{1,0:T(8,128)S(1)}, u32[]{:S(2)}, u32[]{:S(2)}) collective-permute-start(f32[136,256]{1,0:T(8,128)S(1)} %slice_add_fusion), channel_id=1, source_target_pairs={{0,4},{2,6},{4,0},{6,2},{1,5},{3,7},{5,1},{7,3},{8,12},{10,14},{12... | collective-permute-start | bytes 417800 | tf_op jit(solution)/shard_map/ppermute | solution.py:568
  89.8 22.8 %copy-start.12 = (bf16[1024,128]{1,0:T(8,128)(2,1)S(1)}, bf16[1024,128]{1,0:T(8,128)(2,1)}, u32[]{:S(2)}) copy-start(bf16[1024,128]{1,0:T(8,128)(2,1)} %get-tuple-element.142) | copy-start | bytes 786436
  89.8 23.4 %copy-start.11 = (bf16[1024,128]{1,0:T(8,128)(2,1)S(1)}, bf16[1024,128]{1,0:T(8,128)(2,1)}, u32[]{:S(2)}) copy-start(bf16[1024,128]{1,0:T(8,128)(2,1)} %get-tuple-element.143) | copy-start | bytes 786436
  109.7 14.5 %copy-start = (s32[128]{0:T(128)S(1)}, s32[128]{0:T(128)}, u32[]{:S(2)}) copy-start(s32[128]{0:T(128)} %hub_rows.3) | copy-start | bytes 1540
  109.7 14.5 %copy-start.1 = (f32[4096,128]{1,0:T(8,128)S(1)}, f32[4096,128]{1,0:T(8,128)}, u32[]{:S(2)}) copy-start(f32[4096,128]{1,0:T(8,128)} %own_scatter.1.own) | copy-start | bytes 6291460
  109.8 5.3 %collective-permute-start.17 = (f32[136,256]{1,0:T(8,128)S(1)}, f32[136,256]{1,0:T(8,128)S(1)}, u32[]{:S(2)}, u32[]{:S(2)}) collective-permute-start(f32[136,256]{1,0:T(8,128)S(1)} %add_add_fusion), channel_id=1, source_target_pairs={{0,8},{8,0},{16,24},{24,16},{1,9},{9,1},{17,25},{25,17},{2,10},{10... | collective-permute-start | bytes 417800 | tf_op jit(solution)/shard_map/ppermute | solution.py:568
  110.7 4.4 %collective-permute-start.16 = (bf16[256,128]{1,0:T(8,128)(2,1)S(1)}, bf16[256,128]{1,0:T(8,128)(2,1)S(1)}, u32[]{:S(2)}, u32[]{:S(2)}) collective-permute-start(bf16[256,128]{1,0:T(8,128)(2,1)S(1)} %add_convert_fusion.2), channel_id=1, source_target_pairs={{0,24},{8,16},{16,8},{24,0},{1,25},{9,17},{17,9},{25,1},{2,26},{10... | collective-permute-start | bytes 196616 | tf_op jit(solution)/shard_map/ppermute | solution.py:568
  112.5 7.6 %collective-permute-start.20 = (bf16[1024,128]{1,0:T(8,128)(2,1)S(1)}, bf16[1024,128]{1,0:T(8,128)(2,1)S(1)}, u32[]{:S(2)}, u32[]{:S(2)}) collective-permute-start(bf16[1024,128]{1,0:T(8,128)(2,1)S(1)} %copy-done.12), channel_id=1, source_target_pairs={{0,32},{32,0},{64,96},{96,64},{1,33},{33,1},{65,97},{97,65},{2,34}... | collective-permute-start | bytes 786440 | tf_op jit(solution)/shard_map/ppermute | solution.py:572
  113.1 7.0 %collective-permute-start.21 = (bf16[1024,128]{1,0:T(8,128)(2,1)S(1)}, bf16[1024,128]{1,0:T(8,128)(2,1)S(1)}, u32[]{:S(2)}, u32[]{:S(2)}) collective-permute-start(bf16[1024,128]{1,0:T(8,128)(2,1)S(1)} %copy-done.11), channel_id=1, source_target_pairs={{32,64},{64,32},{33,65},{65,33},{34,66},{66,34},{35,67},{67,35},{3... | collective-permute-start | bytes 786440 | tf_op jit(solution)/shard_map/ppermute | solution.py:573
  115.1 5.2 %collective-permute-start.19 = (f32[136,256]{1,0:T(8,128)S(1)}, f32[136,256]{1,0:T(8,128)S(1)}, u32[]{:S(2)}, u32[]{:S(2)}) collective-permute-start(f32[136,256]{1,0:T(8,128)S(1)} %add.89), channel_id=1, source_target_pairs={{0,24},{8,16},{16,8},{24,0},{1,25},{9,17},{17,9},{25,1},{2,26},{10... | collective-permute-start | bytes 417800 | tf_op jit(solution)/shard_map/ppermute | solution.py:568
  117.0 3.1 %collective-permute-start.18 = (bf16[128,128]{1,0:T(8,128)(2,1)S(1)}, bf16[128,128]{1,0:T(8,128)(2,1)S(1)}, u32[]{:S(2)}, u32[]{:S(2)}) collective-permute-start(bf16[128,128]{1,0:T(8,128)(2,1)S(1)} %add_convert_fusion.3), channel_id=1, source_target_pairs={{0,8},{8,0},{16,24},{24,16},{1,9},{9,1},{17,25},{25,17},{2,10},{10... | collective-permute-start | bytes 98312 | tf_op jit(solution)/shard_map/ppermute | solution.py:568
  120.4 6.1 %collective-permute-start.22 = (f32[136,256]{1,0:T(8,128)S(1)}, f32[136,256]{1,0:T(8,128)S(1)}, u32[]{:S(2)}, u32[]{:S(2)}) collective-permute-start(f32[136,256]{1,0:T(8,128)S(1)} %add.94.mine), channel_id=1, source_target_pairs={{0,1},{1,0},{2,3},{3,2},{4,5},{5,4},{6,7},{7,6},{8,9},{9,8},{10,11... | collective-permute-start | bytes 417800 | tf_op jit(solution)/shard_map/ppermute | solution.py:568
  (6 other events, 25.4 us)

commit v8 on v7

--- a/solution.py
+++ b/solution.py
@@ -20,7 +20,6 @@
 HUB_AT = 2 * HALO + NODES
 EXTENT = HUB_AT + HUBS
 LANES = 128
-CHAINS = 8
 VMEM_BYTES = 60 * 2**20
 HALF = F + 8
 AXES = ("z", "y", "x", "core")
@@ -255,12 +254,13 @@
         ref[pl.ds(at + i * step, step), :] = jnp.zeros((step, F), jnp.float32)
 
 
-BLOCK = 1024
-HUB_PIECES = (1, 1, 2, 4, 8, 16)
+BLOCK = 2048
+HUB_PIECES = (1, 1, 2, 4, 8, 8, 8)
+PIECES = len(HUB_PIECES)
 
 
 def forward_kernel(order, slots, features, rim_up, rim_down, *refs):
-    pieces, refs = refs[:6], refs[6:]
+    pieces, refs = refs[:PIECES], refs[PIECES:]
     small, cotangent, (act, src, base, grads) = refs[:4], refs[4], refs[5:9]
     table, sums, features_at, rims_at, hubs_at, cot_at, act_at, src_at, base_at = refs[9:18]
     small_at, lists_at, (sem_in, sem_out) = refs[18:21], refs[21:-2], refs[-2:]
@@ -280,10 +280,10 @@
     for copy in copies:
         copy.start()
     todo = Lists(False, order, slots, *lists_at)
-    cot_copy = pltpu.make_async_copy(cotangent, cot_at, sem_in.at[9])
+    cot_copy = pltpu.make_async_copy(cotangent, cot_at, sem_in.at[3 + PIECES])
     cot_copy.start()
     to = (counts, weights.at[pl.ds(0, F)], weights.at[pl.ds(F, F)], bias)
-    late = [pltpu.make_async_copy(small[k], to[k], sem_in.at[10 + k]) for k in range(4)]
+    late = [pltpu.make_async_copy(small[k], to[k], sem_in.at[4 + PIECES + k]) for k in range(4)]
     for copy in late:
         copy.start()
     late.append(cot_copy)
@@ -307,7 +307,7 @@
         widen(rims_at, half * HALO, pl.multiple_of(faces_up(half) * UPPER, HALO), HALO)
     y, x, core = lax.axis_index("y"), lax.axis_index("x"), lax.axis_index("core")
     position = 0
-    for k in range(6):
+    for k in range(PIECES):
         copies[3 + k].wait()
         for _ in range(HUB_PIECES[k]):
             b = [(position >> k) & 1 for k in range(5)]
@@ -396,7 +396,7 @@
             pltpu.VMEM((1, H), jnp.float32),
         ]
         + list_scratch
-        + [pltpu.SemaphoreType.DMA((14,)), pltpu.SemaphoreType.DMA((3,))],
+        + [pltpu.SemaphoreType.DMA((8 + PIECES,)), pltpu.SemaphoreType.DMA((3,))],
         compiler_params=params,
         cost_estimate=cost(30),
         name="forward",
@@ -619,12 +619,12 @@
     slots, order, own_order = plan(rim_plan_kernel, (tiles, ordered, ordered), 5, flat, counts)
     rim_lists = lists(order, slots)
     own_lists = lists(own_order, slots)
-    h4, rim_lists, own_lists, *rims = tie(h4, rim_lists, own_lists, *rims)
-    held = jnp.concatenate([held, h4], axis=0)
     h5 = swap(held, "core", 1)
+    h4, h5, rim_lists, own_lists, *rims = tie(h4, h5, rim_lists, own_lists, *rims)
+    h6 = swap(h4, "core", 1)
 
     act, src, base, grads = forward(
-        all_lists, features, rims, (h0, h1, h2, h3, h4, h5), counts,
+        all_lists, features, rims, (h0, h1, h2, h3, h4, h5, h6), counts,
         w_self, w_neigh, out_bias.reshape(1, H), cotangent,
     )
 
@@ -645,7 +645,7 @@
     other, src = tie(other, src)
     grads = grads + other
     others = [swap(grads, "x", flip) for flip in (1, 3, 2)]
-    (own,) = scatter("own", NODES, jnp.float32, 20, CHAINS, own_lists, src, base)
+    (own,) = scatter("own", NODES, jnp.float32, 20, 12, own_lists, src, base)
     parts, others, own, rims = tie(parts + [got], others, own, rims)
 
     grads = (grads + others[0]) + (others[1] + others[2])

time: 128 us -> 127 us (level)
    ppermute x19 -> x20, starting transfers between devices: 31 us -> 30.4 us  [swap(): return lax.ppermute(value, axis, [(i, i ^ flip) for i in range(count)])]
    ppermute x19 -> x20, waiting for transfers between devices: 8.14 us -> 8.01 us  [swap(): return lax.ppermute(value, axis, [(i, i ^ flip) for i in range(count)])]
  transfers between devices with their start and end apart: 23 -> 24, of which waited for: 7 -> 6; matrix products, arithmetic and copies ran while one was open for 1% -> 1% of each run, Pallas kernels for 39% -> 40%
where the time goes in v8:
time: 127 us; the launch traced here: 126 us
  Pallas kernels  80.9 us (64%)
  starting transfers between devices  34 us (27%)
  waiting for transfers between devices  8.02 us (6%)
  other arithmetic  1.38 us (1%)
    pallas_call x3, Pallas kernels, scatter(): pl.pallas_call(functools.partial(scatter_kernel, kind), out_shape=(jax.Sh...  37.7 us
    ppermute x20, starting transfers between devices, swap(): return lax.ppermute(value, axis, [(i, i ^ flip) for i in range(count)])  30.4 us
    pallas_call x1, Pallas kernels, forward(): pl.pallas_call(forward_kernel, out_shape=(jax.ShapeDtypeStruct((NODES, H)...  28.1 us
    pallas_call x3, Pallas kernels, plan(): pl.pallas_call(kernel, out_shape=outs, in_specs=[vmem] * len(inputs), out...  9.91 us
    ppermute x20, waiting for transfers between devices, swap(): return lax.ppermute(value, axis, [(i, i ^ flip) for i in range(count)])  8.01 us
  transfers between devices with their start and end apart: 24, of which 6 were waited for; matrix products, arithmetic and copies ran while one was open for 1% of the time, Pallas kernels for 40%

profile of v8, /device:TPU:1, one launch (start us, length us, event | category | flops | bytes accessed | tf_op | source)
XLA Modules:
  0.0 126.1 jit_solution(8412474595117739552)
XLA Ops:
  0.6 2.2 %pick_hubs.1.refs_0_ = bf16[128,128]{1,0:T(8,128)(2,1)} custom-call(s32[128]{0:T(128)} %hub_rows.3, bf16[4096,128]{1,0:T(8,128)(2,1)} %features.3), custom_call_target="tpu_custom_call" | custom-call | flops 2000000000 | tf_op jit(solution)/shard_map/pick_hubs/pallas_call | solution.py:69
  2.8 2.1 %collective-permute-start = (bf16[128,128]{1,0:T(8,128)(2,1)}, bf16[128,128]{1,0:T(8,128)(2,1)S(1)}, u32[]{:S(2)}, u32[]{:S(2)}) collective-permute-start(bf16[128,128]{1,0:T(8,128)(2,1)} %pick_hubs.1.refs_0_), channel_id=1, source_target_pairs={{0,8},{8,0},{16,24},{24,16},{1,9},{9,1},{17,25},{25,17},{2,10},{10... | collective-permute-start | bytes 98312 | tf_op jit(solution)/shard_map/ppermute | solution.py:568
  4.9 2.8 %all_plan_kernel.1 = (s32[320,128]{1,0:T(8,128)}, s32[40,128]{1,0:T(8,128)}) custom-call(s32[10,4096]{1,0:T(8,128)} %bitcast.11, s32[32,128]{1,0:T(8,128)} %bitcast.12), custom_call_target="tpu_custom_call" | custom-call | flops 4000000000 | tf_op jit(solution)/shard_map/all_plan_kernel/pallas_call | solution.py:193
  7.7 2.0 %collective-permute-start.1 = (bf16[256,128]{1,0:T(8,128)(2,1)S(1)}, bf16[256,128]{1,0:T(8,128)(2,1)S(1)}, u32[]{:S(2)}, u32[]{:S(2)}) collective-permute-start(bf16[256,128]{1,0:T(8,128)(2,1)S(1)} %pad_maximum_fusion.2), channel_id=1, source_target_pairs={{0,24},{8,16},{16,8},{24,0},{1,25},{9,17},{17,9},{25,1},{2,26},{10... | collective-permute-start | bytes 196616 | tf_op jit(solution)/shard_map/ppermute | solution.py:568
  9.7 2.7 %hub_plan_kernel.1 = (s32[320,128]{1,0:T(8,128)}, s32[40,128]{1,0:T(8,128)}) custom-call(s32[320,128]{1,0:T(8,128)} %get-tuple-element.92.flat, s32[32,128]{1,0:T(8,128)} %bitcast.13), custom_call_target="tpu_custom_call" | custom-call | flops 4000000000 | tf_op jit(solution)/shard_map/hub_plan_kernel/pallas_call | solution.py:193
  12.4 1.3 %collective-permute-start.2 = (bf16[512,128]{1,0:T(8,128)(2,1)S(1)}, bf16[512,128]{1,0:T(8,128)(2,1)S(1)}, u32[]{:S(2)}, u32[]{:S(2)}) collective-permute-start(bf16[512,128]{1,0:T(8,128)(2,1)S(1)} %pad_maximum_fusion.1), channel_id=1, source_target_pairs={{0,2},{2,0},{4,6},{6,4},{1,3},{3,1},{5,7},{7,5},{8,10},{10,8},{12,... | collective-permute-start | bytes 393224 | tf_op jit(solution)/shard_map/ppermute | solution.py:568
  13.8 1.7 %collective-permute-start.5 = (bf16[1024,128]{1,0:T(8,128)(2,1)S(1)}, bf16[1024,128]{1,0:T(8,128)(2,1)S(1)}, u32[]{:S(2)}, u32[]{:S(2)}) collective-permute-start(bf16[1024,128]{1,0:T(8,128)(2,1)S(1)} %get-tuple-element.162), channel_id=1, source_target_pairs={{0,32},{32,0},{64,96},{96,64},{1,33},{33,1},{65,97},{97,65},{2,34}... | collective-permute-start | bytes 786440 | tf_op jit(solution)/shard_map/ppermute | solution.py:572
  16.4 2.6 %collective-permute-start.3 = (bf16[1024,128]{1,0:T(8,128)(2,1)S(1)}, bf16[1024,128]{1,0:T(8,128)(2,1)S(1)}, u32[]{:S(2)}, u32[]{:S(2)}) collective-permute-start(bf16[1024,128]{1,0:T(8,128)(2,1)S(1)} %pad_maximum_fusion), channel_id=1, source_target_pairs={{0,6},{2,4},{4,2},{6,0},{1,7},{3,5},{5,3},{7,1},{8,14},{10,12},{12... | collective-permute-start | bytes 786440 | tf_op jit(solution)/shard_map/ppermute | solution.py:568
  18.9 3.3 %collective-permute-start.4 = (bf16[1024,128]{1,0:T(8,128)(2,1)S(1)}, bf16[1024,128]{1,0:T(8,128)(2,1)S(1)}, u32[]{:S(2)}, u32[]{:S(2)}) collective-permute-start(bf16[1024,128]{1,0:T(8,128)(2,1)S(1)} %pad_maximum_fusion), channel_id=1, source_target_pairs={{0,1},{1,0},{2,3},{3,2},{4,5},{5,4},{6,7},{7,6},{8,9},{9,8},{10,11... | collective-permute-start | bytes 786440 | tf_op jit(solution)/shard_map/ppermute | solution.py:568
  22.2 4.4 %rim_plan_kernel.1 = (s32[320,128]{1,0:T(8,128)}, s32[40,128]{1,0:T(8,128)}, s32[40,128]{1,0:T(8,128)}) custom-call(s32[320,128]{1,0:T(8,128)} %get-tuple-element.92.flat, s32[32,128]{1,0:T(8,128)} %bitcast.14), custom_call_target="tpu_custom_call" | custom-call | flops 5000000000 | tf_op jit(solution)/shard_map/rim_plan_kernel/pallas_call | solution.py:193
  27.1 1.2 collective-permute-done.7.refs_6_
  28.3 0.7 copy-done.15
  29.0 28.1 %forward.1 = (bf16[4096,256]{1,0:T(8,128)(2,1)}, f32[4096,128]{1,0:T(8,128)}, f32[4096,128]{1,0:T(8,128)}, f32[272,256]{1,0:T(8,128)}) custom-call(s32[5120]{0:T(1024)} %bitcast.23, s32[40960]{0:T(1024)} %bitcast.20, bf16[4096,128]{1,0:T(8,128)(2,1)} %features.3, bf16[1024,128]{1,0:T(8,128)(2,1)} %copy-done.11, bf16[1024,128]{1,0:T(8,128)(2,1)} %copy-done.12, ...), custom_call_target="tpu_custom_call" | custom-call | flops 30000001024 | tf_op jit(solution)/shard_map/forward/pallas_call | solution.py:374
  57.2 3.8 %collective-permute-start.8 = (f32[272,256]{1,0:T(8,128)}, f32[272,256]{1,0:T(8,128)S(1)}, u32[]{:S(2)}, u32[]{:S(2)}) collective-permute-start(f32[272,256]{1,0:T(8,128)} %get-tuple-element.102), channel_id=1, source_target_pairs={{0,32},{32,0},{64,96},{96,64},{1,33},{33,1},{65,97},{97,65},{2,34}... | collective-permute-start | bytes 835592 | tf_op jit(solution)/shard_map/ppermute | solution.py:568
  61.0 9.0 %hub_scatter.1 = (bf16[2048,128]{1,0:T(8,128)(2,1)}, bf16[2048,128]{1,0:T(8,128)(2,1)}) custom-call(s32[5120]{0:T(1024)} %bitcast.21, s32[40960]{0:T(1024)} %bitcast.17, f32[4096,128]{1,0:T(8,128)} %get-tuple-element.127.src), custom_call_target="tpu_custom_call" | custom-call | flops 8000000000 | tf_op jit(solution)/shard_map/hub_scatter/pallas_call | solution.py:472
  70.0 1.2 collective-permute-start.9
  71.4 1.6 %collective-permute-done.9 = bf16[2048,128]{1,0:T(8,128)(2,1)S(1)} collective-permute-done((bf16[2048,128]{1,0:T(8,128)(2,1)}, bf16[2048,128]{1,0:T(8,128)(2,1)S(1)}, u32[]{:S(2)}, u32[]{:S(2)}) %collective-permute-start.9) | collective-permute-done | bytes 524320 | tf_op jit(solution)/shard_map/ppermute | solution.py:568
  73.0 1.0 add_convert_fusion
  74.0 1.5 %collective-permute-start.10 = (bf16[1024,128]{1,0:T(8,128)(2,1)S(1)}, bf16[1024,128]{1,0:T(8,128)(2,1)S(1)}, u32[]{:S(2)}, u32[]{:S(2)}) collective-permute-start(bf16[1024,128]{1,0:T(8,128)(2,1)S(1)} %add_convert_fusion), channel_id=1, source_target_pairs={{0,6},{2,4},{4,2},{6,0},{1,7},{3,5},{5,3},{7,1},{8,14},{10,12},{12... | collective-permute-start | bytes 786440 | tf_op jit(solution)/shard_map/ppermute | solution.py:568
  75.5 8.7 %rim_scatter.1 = (bf16[1024,128]{1,0:T(8,128)(2,1)}, bf16[1024,128]{1,0:T(8,128)(2,1)}) custom-call(s32[5120]{0:T(1024)} %bitcast.24, s32[40960]{0:T(1024)} %bitcast.18, f32[4096,128]{1,0:T(8,128)} %get-tuple-element.127.src), custom_call_target="tpu_custom_call" | custom-call | flops 8000000000 | tf_op jit(solution)/shard_map/rim_scatter/pallas_call | solution.py:472
  84.3 0.8 collective-permute-start.12
  85.2 0.8 collective-permute-done.12
  86.8 1.3 %collective-permute-start.15 = (f32[136,256]{1,0:T(8,128)S(1)}, f32[136,256]{1,0:T(8,128)S(1)}, u32[]{:S(2)}, u32[]{:S(2)}) collective-permute-start(f32[136,256]{1,0:T(8,128)S(1)} %slice_add_fusion), channel_id=1, source_target_pairs={{0,6},{2,4},{4,2},{6,0},{1,7},{3,5},{5,3},{7,1},{8,14},{10,12},{12... | collective-permute-start | bytes 417800 | tf_op jit(solution)/shard_map/ppermute | solution.py:568
  88.1 1.3 %collective-permute-start.16 = (f32[136,256]{1,0:T(8,128)S(1)}, f32[136,256]{1,0:T(8,128)S(1)}, u32[]{:S(2)}, u32[]{:S(2)}) collective-permute-start(f32[136,256]{1,0:T(8,128)S(1)} %slice_add_fusion), channel_id=1, source_target_pairs={{0,4},{2,6},{4,0},{6,2},{1,5},{3,7},{5,1},{7,3},{8,12},{10,14},{12... | collective-permute-start | bytes 417800 | tf_op jit(solution)/shard_map/ppermute | solution.py:568
  89.4 20.0 %own_scatter.1.own = f32[4096,128]{1,0:T(8,128)} custom-call(s32[5120]{0:T(1024)} %bitcast.22, s32[40960]{0:T(1024)} %bitcast.19, f32[4096,128]{1,0:T(8,128)} %get-tuple-element.127.src, f32[4096,128]{1,0:T(8,128)} %get-tuple-element.128.refs_0_), custom_call_target="tpu_custom_call" | custom-call | flops 20000000000 | tf_op jit(solution)/shard_map/own_scatter/pallas_call | solution.py:472
  109.6 2.1 %collective-permute-start.17 = (bf16[256,128]{1,0:T(8,128)(2,1)S(1)}, bf16[256,128]{1,0:T(8,128)(2,1)S(1)}, u32[]{:S(2)}, u32[]{:S(2)}) collective-permute-start(bf16[256,128]{1,0:T(8,128)(2,1)S(1)} %add_convert_fusion.2), channel_id=1, source_target_pairs={{0,24},{8,16},{16,8},{24,0},{1,25},{9,17},{17,9},{25,1},{2,26},{10... | collective-permute-start | bytes 196616 | tf_op jit(solution)/shard_map/ppermute | solution.py:568
  113.0 1.1 collective-permute-done.17
  114.1 2.1 %collective-permute-start.20 = (f32[136,256]{1,0:T(8,128)S(1)}, f32[136,256]{1,0:T(8,128)S(1)}, u32[]{:S(2)}, u32[]{:S(2)}) collective-permute-start(f32[136,256]{1,0:T(8,128)S(1)} %add.89), channel_id=1, source_target_pairs={{0,24},{8,16},{16,8},{24,0},{1,25},{9,17},{17,9},{25,1},{2,26},{10... | collective-permute-start | bytes 417800 | tf_op jit(solution)/shard_map/ppermute | solution.py:568
  116.3 3.0 %collective-permute-done.19 = bf16[128,128]{1,0:T(8,128)(2,1)S(1)} collective-permute-done((bf16[128,128]{1,0:T(8,128)(2,1)S(1)}, bf16[128,128]{1,0:T(8,128)(2,1)S(1)}, u32[]{:S(2)}, u32[]{:S(2)}) %collective-permute-start.19) | collective-permute-done | bytes 32800 | tf_op jit(solution)/shard_map/ppermute | solution.py:568
  119.4 3.6 %collective-permute-start.23 = (f32[136,256]{1,0:T(8,128)S(1)}, f32[136,256]{1,0:T(8,128)S(1)}, u32[]{:S(2)}, u32[]{:S(2)}) collective-permute-start(f32[136,256]{1,0:T(8,128)S(1)} %add.94.mine), channel_id=1, source_target_pairs={{0,1},{1,0},{2,3},{3,2},{4,5},{5,4},{6,7},{7,6},{8,9},{9,8},{10,11... | collective-permute-start | bytes 417800 | tf_op jit(solution)/shard_map/ppermute | solution.py:568
  123.1 2.3 %finish.1 = bf16[4096,128]{1,0:T(8,128)(2,1)} custom-call(s32[128]{0:T(128)S(1)} %copy-done, f32[4096,128]{1,0:T(8,128)S(1)} %copy-done.1, bf16[1024,128]{1,0:T(8,128)(2,1)S(1)} %collective-permute-done.21.rim_0, bf16[1024,128]{1,0:T(8,128)(2,1)S(1)} %collective-permute-done.22.rim_1, f32[128,128]{1,0:T(8,128)S(1)} %convert_add_fusion.share), custom_call_target="tpu_custom_call" | custom-call | flops 3000000000 | tf_op jit(solution)/shard_map/finish/pallas_call | solution.py:526
  125.4 0.7 hand_out.1
  (74 shorter events, 4.0 us)
Async XLA Ops:
  2.8 4.9 %collective-permute-start = (bf16[128,128]{1,0:T(8,128)(2,1)}, bf16[128,128]{1,0:T(8,128)(2,1)S(1)}, u32[]{:S(2)}, u32[]{:S(2)}) collective-permute-start(bf16[128,128]{1,0:T(8,128)(2,1)} %pick_hubs.1.refs_0_), channel_id=1, source_target_pairs={{0,8},{8,0},{16,24},{24,16},{1,9},{9,1},{17,25},{25,17},{2,10},{10... | collective-permute-start | bytes 98312 | tf_op jit(solution)/shard_map/ppermute | solution.py:568
  7.7 4.7 %collective-permute-start.1 = (bf16[256,128]{1,0:T(8,128)(2,1)S(1)}, bf16[256,128]{1,0:T(8,128)(2,1)S(1)}, u32[]{:S(2)}, u32[]{:S(2)}) collective-permute-start(bf16[256,128]{1,0:T(8,128)(2,1)S(1)} %pad_maximum_fusion.2), channel_id=1, source_target_pairs={{0,24},{8,16},{16,8},{24,0},{1,25},{9,17},{17,9},{25,1},{2,26},{10... | collective-permute-start | bytes 196616 | tf_op jit(solution)/shard_map/ppermute | solution.py:568
  12.4 14.2 %copy-start.7 = (bf16[256,128]{1,0:T(8,128)(2,1)}, bf16[256,128]{1,0:T(8,128)(2,1)S(1)}, u32[]{:S(2)}) copy-start(bf16[256,128]{1,0:T(8,128)(2,1)S(1)} %collective-permute-done.1.refs_2_) | copy-start | bytes 196612
  12.4 3.9 %collective-permute-start.2 = (bf16[512,128]{1,0:T(8,128)(2,1)S(1)}, bf16[512,128]{1,0:T(8,128)(2,1)S(1)}, u32[]{:S(2)}, u32[]{:S(2)}) collective-permute-start(bf16[512,128]{1,0:T(8,128)(2,1)S(1)} %pad_maximum_fusion.1), channel_id=1, source_target_pairs={{0,2},{2,0},{4,6},{6,4},{1,3},{3,1},{5,7},{7,5},{8,10},{10,8},{12,... | collective-permute-start | bytes 393224 | tf_op jit(solution)/shard_map/ppermute | solution.py:568
  13.8 12.9 %collective-permute-start.5 = (bf16[1024,128]{1,0:T(8,128)(2,1)S(1)}, bf16[1024,128]{1,0:T(8,128)(2,1)S(1)}, u32[]{:S(2)}, u32[]{:S(2)}) collective-permute-start(bf16[1024,128]{1,0:T(8,128)(2,1)S(1)} %get-tuple-element.162), channel_id=1, source_target_pairs={{0,32},{32,0},{64,96},{96,64},{1,33},{33,1},{65,97},{97,65},{2,34}... | collective-permute-start | bytes 786440 | tf_op jit(solution)/shard_map/ppermute | solution.py:572
  15.5 11.2 %collective-permute-start.6 = (bf16[1024,128]{1,0:T(8,128)(2,1)S(1)}, bf16[1024,128]{1,0:T(8,128)(2,1)S(1)}, u32[]{:S(2)}, u32[]{:S(2)}) collective-permute-start(bf16[1024,128]{1,0:T(8,128)(2,1)S(1)} %get-tuple-element.161), channel_id=1, source_target_pairs={{32,64},{64,32},{33,65},{65,33},{34,66},{66,34},{35,67},{67,35},{3... | collective-permute-start | bytes 786440 | tf_op jit(solution)/shard_map/ppermute | solution.py:573
  16.3 10.3 %copy-start.8 = (bf16[512,128]{1,0:T(8,128)(2,1)}, bf16[512,128]{1,0:T(8,128)(2,1)S(1)}, u32[]{:S(2)}) copy-start(bf16[512,128]{1,0:T(8,128)(2,1)S(1)} %collective-permute-done.2.refs_3_) | copy-start | bytes 393220
  16.4 10.3 %collective-permute-start.3 = (bf16[1024,128]{1,0:T(8,128)(2,1)S(1)}, bf16[1024,128]{1,0:T(8,128)(2,1)S(1)}, u32[]{:S(2)}, u32[]{:S(2)}) collective-permute-start(bf16[1024,128]{1,0:T(8,128)(2,1)S(1)} %pad_maximum_fusion), channel_id=1, source_target_pairs={{0,6},{2,4},{4,2},{6,0},{1,7},{3,5},{5,3},{7,1},{8,14},{10,12},{12... | collective-permute-start | bytes 786440 | tf_op jit(solution)/shard_map/ppermute | solution.py:568
  18.9 7.8 %collective-permute-start.4 = (bf16[1024,128]{1,0:T(8,128)(2,1)S(1)}, bf16[1024,128]{1,0:T(8,128)(2,1)S(1)}, u32[]{:S(2)}, u32[]{:S(2)}) collective-permute-start(bf16[1024,128]{1,0:T(8,128)(2,1)S(1)} %pad_maximum_fusion), channel_id=1, source_target_pairs={{0,1},{1,0},{2,3},{3,2},{4,5},{5,4},{6,7},{7,6},{8,9},{9,8},{10,11... | collective-permute-start | bytes 786440 | tf_op jit(solution)/shard_map/ppermute | solution.py:568
  26.7 1.6 %collective-permute-start.7 = (bf16[1024,128]{1,0:T(8,128)(2,1)S(1)}, bf16[1024,128]{1,0:T(8,128)(2,1)S(1)}, u32[]{:S(2)}, u32[]{:S(2)}) collective-permute-start(bf16[1024,128]{1,0:T(8,128)(2,1)S(1)} %collective-permute-done.3.refs_4_), channel_id=1, source_target_pairs={{0,1},{1,0},{2,3},{3,2},{4,5},{5,4},{6,7},{7,6},{8,9},{9,8},{10,11... | collective-permute-start | bytes 786440 | tf_op jit(solution)/shard_map/ppermute | solution.py:568
  57.2 12.8 %collective-permute-start.8 = (f32[272,256]{1,0:T(8,128)}, f32[272,256]{1,0:T(8,128)S(1)}, u32[]{:S(2)}, u32[]{:S(2)}) collective-permute-start(f32[272,256]{1,0:T(8,128)} %get-tuple-element.102), channel_id=1, source_target_pairs={{0,32},{32,0},{64,96},{96,64},{1,33},{33,1},{65,97},{97,65},{2,34}... | collective-permute-start | bytes 835592 | tf_op jit(solution)/shard_map/ppermute | solution.py:568
  61.0 10.2 %copy-start.5 = (f32[272,256]{1,0:T(8,128)S(1)}, f32[272,256]{1,0:T(8,128)}, u32[]{:S(2)}) copy-start(f32[272,256]{1,0:T(8,128)} %get-tuple-element.102) | copy-start | bytes 835588
  70.0 2.9 %collective-permute-start.9 = (bf16[2048,128]{1,0:T(8,128)(2,1)}, bf16[2048,128]{1,0:T(8,128)(2,1)S(1)}, u32[]{:S(2)}, u32[]{:S(2)}) collective-permute-start(bf16[2048,128]{1,0:T(8,128)(2,1)} %get-tuple-element.110), channel_id=1, source_target_pairs={{0,1},{1,0},{2,3},{3,2},{4,5},{5,4},{6,7},{7,6},{8,9},{9,8},{10,11... | collective-permute-start | bytes 1572872 | tf_op jit(solution)/shard_map/ppermute | solution.py:568
  71.3 13.0 %collective-permute-start.11 = (f32[272,256]{1,0:T(8,128)S(1)}, f32[272,256]{1,0:T(8,128)S(1)}, u32[]{:S(2)}, u32[]{:S(2)}) collective-permute-start(f32[272,256]{1,0:T(8,128)S(1)} %add.77), channel_id=1, source_target_pairs={{0,96},{32,64},{64,32},{96,0},{1,97},{33,65},{65,33},{97,1},{2,98}... | collective-permute-start | bytes 835592 | tf_op jit(solution)/shard_map/ppermute | solution.py:568
  74.0 11.1 %copy-start.2 = (bf16[2048,128]{1,0:T(8,128)(2,1)S(1)}, bf16[2048,128]{1,0:T(8,128)(2,1)}, u32[]{:S(2)}) copy-start(bf16[2048,128]{1,0:T(8,128)(2,1)} %get-tuple-element.150) | copy-start | bytes 1572868
  74.0 10.2 %collective-permute-start.10 = (bf16[1024,128]{1,0:T(8,128)(2,1)S(1)}, bf16[1024,128]{1,0:T(8,128)(2,1)S(1)}, u32[]{:S(2)}, u32[]{:S(2)}) collective-permute-start(bf16[1024,128]{1,0:T(8,128)(2,1)S(1)} %add_convert_fusion), channel_id=1, source_target_pairs={{0,6},{2,4},{4,2},{6,0},{1,7},{3,5},{5,3},{7,1},{8,14},{10,12},{12... | collective-permute-start | bytes 786440 | tf_op jit(solution)/shard_map/ppermute | solution.py:568
  84.3 1.8 %collective-permute-start.12 = (f32[136,256]{1,0:T(8,128)S(1)}, f32[136,256]{1,0:T(8,128)S(1)}, u32[]{:S(2)}, u32[]{:S(2)}) collective-permute-start(f32[136,256]{1,0:T(8,128)S(1)} %slice.85), channel_id=1, source_target_pairs={{0,1},{1,0},{2,3},{3,2},{4,5},{5,4},{6,7},{7,6},{8,9},{9,8},{10,11... | collective-permute-start | bytes 417800 | tf_op jit(solution)/shard_map/ppermute | solution.py:568
  85.1 24.3 %collective-permute-start.13 = (bf16[512,128]{1,0:T(8,128)(2,1)S(1)}, bf16[512,128]{1,0:T(8,128)(2,1)S(1)}, u32[]{:S(2)}, u32[]{:S(2)}) collective-permute-start(bf16[512,128]{1,0:T(8,128)(2,1)S(1)} %add_convert_fusion.1), channel_id=1, source_target_pairs={{0,2},{2,0},{4,6},{6,4},{1,3},{3,1},{5,7},{7,5},{8,10},{10,8},{12,... | collective-permute-start | bytes 393224 | tf_op jit(solution)/shard_map/ppermute | solution.py:568
  86.1 23.3 %collective-permute-start.14 = (f32[136,256]{1,0:T(8,128)S(1)}, f32[136,256]{1,0:T(8,128)S(1)}, u32[]{:S(2)}, u32[]{:S(2)}) collective-permute-start(f32[136,256]{1,0:T(8,128)S(1)} %slice_add_fusion), channel_id=1, source_target_pairs={{0,2},{2,0},{4,6},{6,4},{1,3},{3,1},{5,7},{7,5},{8,10},{10,8},{12,... | collective-permute-start | bytes 417800 | tf_op jit(solution)/shard_map/ppermute | solution.py:568
  86.8 22.7 %collective-permute-start.15 = (f32[136,256]{1,0:T(8,128)S(1)}, f32[136,256]{1,0:T(8,128)S(1)}, u32[]{:S(2)}, u32[]{:S(2)}) collective-permute-start(f32[136,256]{1,0:T(8,128)S(1)} %slice_add_fusion), channel_id=1, source_target_pairs={{0,6},{2,4},{4,2},{6,0},{1,7},{3,5},{5,3},{7,1},{8,14},{10,12},{12... | collective-permute-start | bytes 417800 | tf_op jit(solution)/shard_map/ppermute | solution.py:568
  88.1 21.3 %collective-permute-start.16 = (f32[136,256]{1,0:T(8,128)S(1)}, f32[136,256]{1,0:T(8,128)S(1)}, u32[]{:S(2)}, u32[]{:S(2)}) collective-permute-start(f32[136,256]{1,0:T(8,128)S(1)} %slice_add_fusion), channel_id=1, source_target_pairs={{0,4},{2,6},{4,0},{6,2},{1,5},{3,7},{5,1},{7,3},{8,12},{10,14},{12... | collective-permute-start | bytes 417800 | tf_op jit(solution)/shard_map/ppermute | solution.py:568
  89.4 22.3 %copy-start.10 = (bf16[1024,128]{1,0:T(8,128)(2,1)S(1)}, bf16[1024,128]{1,0:T(8,128)(2,1)}, u32[]{:S(2)}) copy-start(bf16[1024,128]{1,0:T(8,128)(2,1)} %get-tuple-element.144) | copy-start | bytes 786436
  89.4 22.9 %copy-start.9 = (bf16[1024,128]{1,0:T(8,128)(2,1)S(1)}, bf16[1024,128]{1,0:T(8,128)(2,1)}, u32[]{:S(2)}) copy-start(bf16[1024,128]{1,0:T(8,128)(2,1)} %get-tuple-element.145) | copy-start | bytes 786436
  109.4 13.7 %copy-start = (s32[128]{0:T(128)S(1)}, s32[128]{0:T(128)}, u32[]{:S(2)}) copy-start(s32[128]{0:T(128)} %hub_rows.3) | copy-start | bytes 1540
  109.4 13.7 %copy-start.1 = (f32[4096,128]{1,0:T(8,128)S(1)}, f32[4096,128]{1,0:T(8,128)}, u32[]{:S(2)}) copy-start(f32[4096,128]{1,0:T(8,128)} %own_scatter.1.own) | copy-start | bytes 6291460
  109.5 4.5 %collective-permute-start.18 = (f32[136,256]{1,0:T(8,128)S(1)}, f32[136,256]{1,0:T(8,128)S(1)}, u32[]{:S(2)}, u32[]{:S(2)}) collective-permute-start(f32[136,256]{1,0:T(8,128)S(1)} %add_add_fusion), channel_id=1, source_target_pairs={{0,8},{8,0},{16,24},{24,16},{1,9},{9,1},{17,25},{25,17},{2,10},{10... | collective-permute-start | bytes 417800 | tf_op jit(solution)/shard_map/ppermute | solution.py:568
  109.6 4.4 %collective-permute-start.17 = (bf16[256,128]{1,0:T(8,128)(2,1)S(1)}, bf16[256,128]{1,0:T(8,128)(2,1)S(1)}, u32[]{:S(2)}, u32[]{:S(2)}) collective-permute-start(bf16[256,128]{1,0:T(8,128)(2,1)S(1)} %add_convert_fusion.2), channel_id=1, source_target_pairs={{0,24},{8,16},{16,8},{24,0},{1,25},{9,17},{17,9},{25,1},{2,26},{10... | collective-permute-start | bytes 196616 | tf_op jit(solution)/shard_map/ppermute | solution.py:568
  111.8 7.6 %collective-permute-start.21 = (bf16[1024,128]{1,0:T(8,128)(2,1)S(1)}, bf16[1024,128]{1,0:T(8,128)(2,1)S(1)}, u32[]{:S(2)}, u32[]{:S(2)}) collective-permute-start(bf16[1024,128]{1,0:T(8,128)(2,1)S(1)} %copy-done.10), channel_id=1, source_target_pairs={{0,32},{32,0},{64,96},{96,64},{1,33},{33,1},{65,97},{97,65},{2,34}... | collective-permute-start | bytes 786440 | tf_op jit(solution)/shard_map/ppermute | solution.py:572
  112.3 7.1 %collective-permute-start.22 = (bf16[1024,128]{1,0:T(8,128)(2,1)S(1)}, bf16[1024,128]{1,0:T(8,128)(2,1)S(1)}, u32[]{:S(2)}, u32[]{:S(2)}) collective-permute-start(bf16[1024,128]{1,0:T(8,128)(2,1)S(1)} %copy-done.9), channel_id=1, source_target_pairs={{32,64},{64,32},{33,65},{65,33},{34,66},{66,34},{35,67},{67,35},{3... | collective-permute-start | bytes 786440 | tf_op jit(solution)/shard_map/ppermute | solution.py:573
  114.1 5.3 %collective-permute-start.20 = (f32[136,256]{1,0:T(8,128)S(1)}, f32[136,256]{1,0:T(8,128)S(1)}, u32[]{:S(2)}, u32[]{:S(2)}) collective-permute-start(f32[136,256]{1,0:T(8,128)S(1)} %add.89), channel_id=1, source_target_pairs={{0,24},{8,16},{16,8},{24,0},{1,25},{9,17},{17,9},{25,1},{2,26},{10... | collective-permute-start | bytes 417800 | tf_op jit(solution)/shard_map/ppermute | solution.py:568
  116.2 3.1 %collective-permute-start.19 = (bf16[128,128]{1,0:T(8,128)(2,1)S(1)}, bf16[128,128]{1,0:T(8,128)(2,1)S(1)}, u32[]{:S(2)}, u32[]{:S(2)}) collective-permute-start(bf16[128,128]{1,0:T(8,128)(2,1)S(1)} %add_convert_fusion.3), channel_id=1, source_target_pairs={{0,8},{8,0},{16,24},{24,16},{1,9},{9,1},{17,25},{25,17},{2,10},{10... | collective-permute-start | bytes 98312 | tf_op jit(solution)/shard_map/ppermute | solution.py:568
  119.4 6.0 %collective-permute-start.23 = (f32[136,256]{1,0:T(8,128)S(1)}, f32[136,256]{1,0:T(8,128)S(1)}, u32[]{:S(2)}, u32[]{:S(2)}) collective-permute-start(f32[136,256]{1,0:T(8,128)S(1)} %add.94.mine), channel_id=1, source_target_pairs={{0,1},{1,0},{2,3},{3,2},{4,5},{5,4},{6,7},{7,6},{8,9},{9,8},{10,11... | collective-permute-start | bytes 417800 | tf_op jit(solution)/shard_map/ppermute | solution.py:568
  (8 other events, 24.9 us)

commit v9 on v8

--- a/solution.py
+++ b/solution.py
@@ -413,7 +413,7 @@
 def scatter_kernel(kind, order, slots, src, *refs):
     if kind == "own":
         base, refs = refs[0], refs[1:]
-    parts = 1 if kind == "own" else 2
+    parts = {"own": 1, "rim": 2, "hub": 4}[kind]
     outs, refs = refs[:parts], refs[parts:]
     lists_at, (src_at, out_at, sems), chains = refs[: FANOUT + 2], refs[FANOUT + 2 : FANOUT + 5], refs[
         FANOUT + 5 :
@@ -449,10 +449,11 @@
         @pl.loop(0, part // HUB)
         def _(i, half=half, out=out):
             if kind == "hub":
-                flip_x, flip_y = (i >> 2) ^ (i >> 3), (i & 3) ^ ((i >> 1) & 1)
+                j = i + (half & 1) * (COLS // 4)
+                flip_x, flip_y = (j >> 2) ^ (j >> 3), (j & 3) ^ ((j >> 1) & 1)
                 owner_y = lax.axis_index("y") ^ flip_y
                 owner_x = lax.axis_index("x") ^ flip_x
-                taken = owner_y * 8 + owner_x * 2 + (lax.axis_index("core") ^ half)
+                taken = owner_y * 8 + owner_x * 2 + (lax.axis_index("core") ^ (half >> 1))
             elif kind == "rim":
                 taken = i + faces_up(half) * (HALO // HUB)
             else:
@@ -468,7 +469,7 @@
 
 
 def scatter(kind, rows, dtype, us, chains, lists, *inputs):
-    parts = 1 if kind == "own" else 2
+    parts = {"own": 1, "rim": 2, "hub": 4}[kind]
     return pl.pallas_call(
         functools.partial(scatter_kernel, kind),
         out_shape=(jax.ShapeDtypeStruct((rows // parts, F), dtype),) * parts,
@@ -478,7 +479,7 @@
         + [
             pltpu.VMEM((NODES, F), jnp.float32),
             pltpu.VMEM((rows, F), dtype),
-            pltpu.SemaphoreType.DMA((4,)),
+            pltpu.SemaphoreType.DMA((6,)),
         ]
         + [pltpu.VMEM((rows, F), jnp.float32)] * chains,
         compiler_params=params,
@@ -629,13 +630,14 @@
     )
 
     other = swap(grads, "z", 1)
-    keep, give = scatter("hub", HUBS, jnp.bfloat16, 8, 6, hub_lists, src)
-    keep, give, src, other = tie(keep, give, src, other)
+    keep, keep_far, give, give_far = scatter("hub", HUBS, jnp.bfloat16, 8, 6, hub_lists, src)
+    keep, keep_far, give, give_far, src, other = tie(keep, keep_far, give, give_far, src, other)
     grads = grads + other
+    far = [keep_far, swap(give_far, "core", 1)]
+    other = swap(grads, "z", 3)
+    far, src, give = tie(far, src, give)
+    got = swap(add_up(far, 0, far[0].shape[0]).astype(jnp.bfloat16), "x", 3)
     parts = [keep, swap(give, "core", 1)]
-    other = swap(grads, "z", 3)
-    parts, src = tie(parts, src)
-    got = give_half(parts, "x", 3)
     rims = scatter("rim", 2 * HALO, jnp.bfloat16, 8, 6, rim_lists, src)
     parts, src, other, rims = tie(parts + [got], src, other, rims)
 

time: 127 us -> 126 us (level)
    ppermute x20 -> x21, starting transfers between devices: 30.4 us -> 31.2 us  [swap(): return lax.ppermute(value, axis, [(i, i ^ flip) for i in range(count)])]
    ppermute x20 -> x21, waiting for transfers between devices: 8.01 us -> 7.63 us  [swap(): return lax.ppermute(value, axis, [(i, i ^ flip) for i in range(count)])]
  transfers between devices with their start and end apart: 24 -> 25, of which waited for: 6 -> 6; matrix products, arithmetic and copies ran while one was open for 1% -> 1% of each run, Pallas kernels for 40% -> 40%
where the time goes in v9:
time: 126 us
  Pallas kernels  81.1 us (64%)
  starting transfers between devices  34.3 us (27%)
  waiting for transfers between devices  7.64 us (6%)
  other arithmetic  1.38 us (1%)
    pallas_call x3, Pallas kernels, scatter(): pl.pallas_call(functools.partial(scatter_kernel, kind), out_shape=(jax.Sh...  37.9 us
    ppermute x21, starting transfers between devices, swap(): return lax.ppermute(value, axis, [(i, i ^ flip) for i in range(count)])  31.2 us
    pallas_call x1, Pallas kernels, forward(): pl.pallas_call(forward_kernel, out_shape=(jax.ShapeDtypeStruct((NODES, H)...  28.1 us
    pallas_call x3, Pallas kernels, plan(): pl.pallas_call(kernel, out_shape=outs, in_specs=[vmem] * len(inputs), out...  9.91 us
    ppermute x21, waiting for transfers between devices, swap(): return lax.ppermute(value, axis, [(i, i ^ flip) for i in range(count)])  7.63 us
  transfers between devices with their start and end apart: 25, of which 6 were waited for; matrix products, arithmetic and copies ran while one was open for 1% of the time, Pallas kernels for 40%

profile of v9, /device:TPU:1, one launch (start us, length us, event | category | flops | bytes accessed | tf_op | source)
XLA Modules:
  0.0 126.2 jit_solution(17416845502567073630)
XLA Ops:
  0.6 2.2 %pick_hubs.1.refs_0_ = bf16[128,128]{1,0:T(8,128)(2,1)} custom-call(s32[128]{0:T(128)} %hub_rows.3, bf16[4096,128]{1,0:T(8,128)(2,1)} %features.3), custom_call_target="tpu_custom_call" | custom-call | flops 2000000000 | tf_op jit(solution)/shard_map/pick_hubs/pallas_call | solution.py:69
  2.8 2.1 %collective-permute-start = (bf16[128,128]{1,0:T(8,128)(2,1)}, bf16[128,128]{1,0:T(8,128)(2,1)S(1)}, u32[]{:S(2)}, u32[]{:S(2)}) collective-permute-start(bf16[128,128]{1,0:T(8,128)(2,1)} %pick_hubs.1.refs_0_), channel_id=1, source_target_pairs={{0,8},{8,0},{16,24},{24,16},{1,9},{9,1},{17,25},{25,17},{2,10},{10... | collective-permute-start | bytes 98312 | tf_op jit(solution)/shard_map/ppermute | solution.py:569
  4.9 2.8 %all_plan_kernel.1 = (s32[320,128]{1,0:T(8,128)}, s32[40,128]{1,0:T(8,128)}) custom-call(s32[10,4096]{1,0:T(8,128)} %bitcast.11, s32[32,128]{1,0:T(8,128)} %bitcast.12), custom_call_target="tpu_custom_call" | custom-call | flops 4000000000 | tf_op jit(solution)/shard_map/all_plan_kernel/pallas_call | solution.py:193
  7.7 2.0 %collective-permute-start.1 = (bf16[256,128]{1,0:T(8,128)(2,1)S(1)}, bf16[256,128]{1,0:T(8,128)(2,1)S(1)}, u32[]{:S(2)}, u32[]{:S(2)}) collective-permute-start(bf16[256,128]{1,0:T(8,128)(2,1)S(1)} %pad_maximum_fusion.2), channel_id=1, source_target_pairs={{0,24},{8,16},{16,8},{24,0},{1,25},{9,17},{17,9},{25,1},{2,26},{10... | collective-permute-start | bytes 196616 | tf_op jit(solution)/shard_map/ppermute | solution.py:569
  9.7 2.7 %hub_plan_kernel.1 = (s32[320,128]{1,0:T(8,128)}, s32[40,128]{1,0:T(8,128)}) custom-call(s32[320,128]{1,0:T(8,128)} %get-tuple-element.97.flat, s32[32,128]{1,0:T(8,128)} %bitcast.13), custom_call_target="tpu_custom_call" | custom-call | flops 4000000000 | tf_op jit(solution)/shard_map/hub_plan_kernel/pallas_call | solution.py:193
  12.4 1.3 %collective-permute-start.2 = (bf16[512,128]{1,0:T(8,128)(2,1)S(1)}, bf16[512,128]{1,0:T(8,128)(2,1)S(1)}, u32[]{:S(2)}, u32[]{:S(2)}) collective-permute-start(bf16[512,128]{1,0:T(8,128)(2,1)S(1)} %pad_maximum_fusion.1), channel_id=1, source_target_pairs={{0,2},{2,0},{4,6},{6,4},{1,3},{3,1},{5,7},{7,5},{8,10},{10,8},{12,... | collective-permute-start | bytes 393224 | tf_op jit(solution)/shard_map/ppermute | solution.py:569
  13.8 1.7 %collective-permute-start.5 = (bf16[1024,128]{1,0:T(8,128)(2,1)S(1)}, bf16[1024,128]{1,0:T(8,128)(2,1)S(1)}, u32[]{:S(2)}, u32[]{:S(2)}) collective-permute-start(bf16[1024,128]{1,0:T(8,128)(2,1)S(1)} %get-tuple-element.172), channel_id=1, source_target_pairs={{0,32},{32,0},{64,96},{96,64},{1,33},{33,1},{65,97},{97,65},{2,34}... | collective-permute-start | bytes 786440 | tf_op jit(solution)/shard_map/ppermute | solution.py:573
  15.5 0.7 collective-permute-start.6
  16.4 2.6 %collective-permute-start.3 = (bf16[1024,128]{1,0:T(8,128)(2,1)S(1)}, bf16[1024,128]{1,0:T(8,128)(2,1)S(1)}, u32[]{:S(2)}, u32[]{:S(2)}) collective-permute-start(bf16[1024,128]{1,0:T(8,128)(2,1)S(1)} %pad_maximum_fusion), channel_id=1, source_target_pairs={{0,6},{2,4},{4,2},{6,0},{1,7},{3,5},{5,3},{7,1},{8,14},{10,12},{12... | collective-permute-start | bytes 786440 | tf_op jit(solution)/shard_map/ppermute | solution.py:569
  18.9 3.3 %collective-permute-start.4 = (bf16[1024,128]{1,0:T(8,128)(2,1)S(1)}, bf16[1024,128]{1,0:T(8,128)(2,1)S(1)}, u32[]{:S(2)}, u32[]{:S(2)}) collective-permute-start(bf16[1024,128]{1,0:T(8,128)(2,1)S(1)} %pad_maximum_fusion), channel_id=1, source_target_pairs={{0,1},{1,0},{2,3},{3,2},{4,5},{5,4},{6,7},{7,6},{8,9},{9,8},{10,11... | collective-permute-start | bytes 786440 | tf_op jit(solution)/shard_map/ppermute | solution.py:569
  22.2 4.4 %rim_plan_kernel.1 = (s32[320,128]{1,0:T(8,128)}, s32[40,128]{1,0:T(8,128)}, s32[40,128]{1,0:T(8,128)}) custom-call(s32[320,128]{1,0:T(8,128)} %get-tuple-element.97.flat, s32[32,128]{1,0:T(8,128)} %bitcast.14), custom_call_target="tpu_custom_call" | custom-call | flops 5000000000 | tf_op jit(solution)/shard_map/rim_plan_kernel/pallas_call | solution.py:193
  27.1 1.2 collective-permute-done.7.refs_6_
  28.4 0.7 copy-done.15
  29.1 28.1 %forward.1 = (bf16[4096,256]{1,0:T(8,128)(2,1)}, f32[4096,128]{1,0:T(8,128)}, f32[4096,128]{1,0:T(8,128)}, f32[272,256]{1,0:T(8,128)}) custom-call(s32[5120]{0:T(1024)} %bitcast.23, s32[40960]{0:T(1024)} %bitcast.20, bf16[4096,128]{1,0:T(8,128)(2,1)} %features.3, bf16[1024,128]{1,0:T(8,128)(2,1)} %copy-done.11, bf16[1024,128]{1,0:T(8,128)(2,1)} %copy-done.12, ...), custom_call_target="tpu_custom_call" | custom-call | flops 30000001024 | tf_op jit(solution)/shard_map/forward/pallas_call | solution.py:374
  57.1 3.6 %collective-permute-start.8 = (f32[272,256]{1,0:T(8,128)}, f32[272,256]{1,0:T(8,128)S(1)}, u32[]{:S(2)}, u32[]{:S(2)}) collective-permute-start(f32[272,256]{1,0:T(8,128)} %get-tuple-element.107), channel_id=1, source_target_pairs={{0,32},{32,0},{64,96},{96,64},{1,33},{33,1},{65,97},{97,65},{2,34}... | collective-permute-start | bytes 835592 | tf_op jit(solution)/shard_map/ppermute | solution.py:569
  60.7 9.5 %hub_scatter.1 = (bf16[1024,128]{1,0:T(8,128)(2,1)}, bf16[1024,128]{1,0:T(8,128)(2,1)}, bf16[1024,128]{1,0:T(8,128)(2,1)}, bf16[1024,128]{1,0:T(8,128)(2,1)}) custom-call(s32[5120]{0:T(1024)} %bitcast.22, s32[40960]{0:T(1024)} %bitcast.19, f32[4096,128]{1,0:T(8,128)} %get-tuple-element.137.src), custom_call_target="tpu_custom_call" | custom-call | flops 8000000000 | tf_op jit(solution)/shard_map/hub_scatter/pallas_call | solution.py:473
  71.3 0.8 collective-permute-done.9
  72.1 1.0 add_convert_fusion
  73.2 1.9 %collective-permute-start.11 = (bf16[1024,128]{1,0:T(8,128)(2,1)S(1)}, bf16[1024,128]{1,0:T(8,128)(2,1)S(1)}, u32[]{:S(2)}, u32[]{:S(2)}) collective-permute-start(bf16[1024,128]{1,0:T(8,128)(2,1)S(1)} %add_convert_fusion), channel_id=1, source_target_pairs={{0,6},{2,4},{4,2},{6,0},{1,7},{3,5},{5,3},{7,1},{8,14},{10,12},{12... | collective-permute-start | bytes 786440 | tf_op jit(solution)/shard_map/ppermute | solution.py:569
  75.7 8.5 %rim_scatter.1 = (bf16[1024,128]{1,0:T(8,128)(2,1)}, bf16[1024,128]{1,0:T(8,128)(2,1)}) custom-call(s32[5120]{0:T(1024)} %bitcast.24, s32[40960]{0:T(1024)} %bitcast.17, f32[4096,128]{1,0:T(8,128)} %get-tuple-element.137.src), custom_call_target="tpu_custom_call" | custom-call | flops 8000000000 | tf_op jit(solution)/shard_map/rim_scatter/pallas_call | solution.py:473
  84.6 1.2 collective-permute-done.13
  86.2 1.1 collective-permute-start.16
  87.3 1.8 %collective-permute-start.17 = (f32[136,256]{1,0:T(8,128)S(1)}, f32[136,256]{1,0:T(8,128)S(1)}, u32[]{:S(2)}, u32[]{:S(2)}) collective-permute-start(f32[136,256]{1,0:T(8,128)S(1)} %slice_add_fusion), channel_id=1, source_target_pairs={{0,4},{2,6},{4,0},{6,2},{1,5},{3,7},{5,1},{7,3},{8,12},{10,14},{12... | collective-permute-start | bytes 417800 | tf_op jit(solution)/shard_map/ppermute | solution.py:569
  89.2 19.9 %own_scatter.1.own = f32[4096,128]{1,0:T(8,128)} custom-call(s32[5120]{0:T(1024)} %bitcast.21, s32[40960]{0:T(1024)} %bitcast.18, f32[4096,128]{1,0:T(8,128)} %get-tuple-element.137.src, f32[4096,128]{1,0:T(8,128)} %get-tuple-element.138.refs_0_), custom_call_target="tpu_custom_call" | custom-call | flops 20000000000 | tf_op jit(solution)/shard_map/own_scatter/pallas_call | solution.py:473
  109.6 2.5 %collective-permute-start.18 = (bf16[256,128]{1,0:T(8,128)(2,1)S(1)}, bf16[256,128]{1,0:T(8,128)(2,1)S(1)}, u32[]{:S(2)}, u32[]{:S(2)}) collective-permute-start(bf16[256,128]{1,0:T(8,128)(2,1)S(1)} %add_convert_fusion.2), channel_id=1, source_target_pairs={{0,24},{8,16},{16,8},{24,0},{1,25},{9,17},{17,9},{25,1},{2,26},{10... | collective-permute-start | bytes 196616 | tf_op jit(solution)/shard_map/ppermute | solution.py:569
  112.2 0.7 collective-permute-start.23
  112.8 1.2 collective-permute-done.18
  114.0 2.5 %collective-permute-start.21 = (f32[136,256]{1,0:T(8,128)S(1)}, f32[136,256]{1,0:T(8,128)S(1)}, u32[]{:S(2)}, u32[]{:S(2)}) collective-permute-start(f32[136,256]{1,0:T(8,128)S(1)} %add.89), channel_id=1, source_target_pairs={{0,24},{8,16},{16,8},{24,0},{1,25},{9,17},{17,9},{25,1},{2,26},{10... | collective-permute-start | bytes 417800 | tf_op jit(solution)/shard_map/ppermute | solution.py:569
  116.7 3.0 %collective-permute-done.20 = bf16[128,128]{1,0:T(8,128)(2,1)S(1)} collective-permute-done((bf16[128,128]{1,0:T(8,128)(2,1)S(1)}, bf16[128,128]{1,0:T(8,128)(2,1)S(1)}, u32[]{:S(2)}, u32[]{:S(2)}) %collective-permute-start.20) | collective-permute-done | bytes 32800 | tf_op jit(solution)/shard_map/ppermute | solution.py:569
  119.7 3.4 %collective-permute-start.24 = (f32[136,256]{1,0:T(8,128)S(1)}, f32[136,256]{1,0:T(8,128)S(1)}, u32[]{:S(2)}, u32[]{:S(2)}) collective-permute-start(f32[136,256]{1,0:T(8,128)S(1)} %add.94.mine), channel_id=1, source_target_pairs={{0,1},{1,0},{2,3},{3,2},{4,5},{5,4},{6,7},{7,6},{8,9},{9,8},{10,11... | collective-permute-start | bytes 417800 | tf_op jit(solution)/shard_map/ppermute | solution.py:569
  123.2 2.3 %finish.1 = bf16[4096,128]{1,0:T(8,128)(2,1)} custom-call(s32[128]{0:T(128)S(1)} %copy-done, f32[4096,128]{1,0:T(8,128)S(1)} %copy-done.1, bf16[1024,128]{1,0:T(8,128)(2,1)S(1)} %collective-permute-done.22.rim_0, bf16[1024,128]{1,0:T(8,128)(2,1)S(1)} %collective-permute-done.23.rim_1, f32[128,128]{1,0:T(8,128)S(1)} %convert_add_fusion.share), custom_call_target="tpu_custom_call" | custom-call | flops 3000000000 | tf_op jit(solution)/shard_map/finish/pallas_call | solution.py:527
  125.5 0.7 hand_out.1
  (76 shorter events, 3.8 us)
Async XLA Ops:
  2.8 4.9 %collective-permute-start = (bf16[128,128]{1,0:T(8,128)(2,1)}, bf16[128,128]{1,0:T(8,128)(2,1)S(1)}, u32[]{:S(2)}, u32[]{:S(2)}) collective-permute-start(bf16[128,128]{1,0:T(8,128)(2,1)} %pick_hubs.1.refs_0_), channel_id=1, source_target_pairs={{0,8},{8,0},{16,24},{24,16},{1,9},{9,1},{17,25},{25,17},{2,10},{10... | collective-permute-start | bytes 98312 | tf_op jit(solution)/shard_map/ppermute | solution.py:569
  7.7 4.7 %collective-permute-start.1 = (bf16[256,128]{1,0:T(8,128)(2,1)S(1)}, bf16[256,128]{1,0:T(8,128)(2,1)S(1)}, u32[]{:S(2)}, u32[]{:S(2)}) collective-permute-start(bf16[256,128]{1,0:T(8,128)(2,1)S(1)} %pad_maximum_fusion.2), channel_id=1, source_target_pairs={{0,24},{8,16},{16,8},{24,0},{1,25},{9,17},{17,9},{25,1},{2,26},{10... | collective-permute-start | bytes 196616 | tf_op jit(solution)/shard_map/ppermute | solution.py:569
  12.4 14.2 %copy-start.7 = (bf16[256,128]{1,0:T(8,128)(2,1)}, bf16[256,128]{1,0:T(8,128)(2,1)S(1)}, u32[]{:S(2)}) copy-start(bf16[256,128]{1,0:T(8,128)(2,1)S(1)} %collective-permute-done.1.refs_2_) | copy-start | bytes 196612
  12.4 3.9 %collective-permute-start.2 = (bf16[512,128]{1,0:T(8,128)(2,1)S(1)}, bf16[512,128]{1,0:T(8,128)(2,1)S(1)}, u32[]{:S(2)}, u32[]{:S(2)}) collective-permute-start(bf16[512,128]{1,0:T(8,128)(2,1)S(1)} %pad_maximum_fusion.1), channel_id=1, source_target_pairs={{0,2},{2,0},{4,6},{6,4},{1,3},{3,1},{5,7},{7,5},{8,10},{10,8},{12,... | collective-permute-start | bytes 393224 | tf_op jit(solution)/shard_map/ppermute | solution.py:569
  13.8 12.9 %collective-permute-start.5 = (bf16[1024,128]{1,0:T(8,128)(2,1)S(1)}, bf16[1024,128]{1,0:T(8,128)(2,1)S(1)}, u32[]{:S(2)}, u32[]{:S(2)}) collective-permute-start(bf16[1024,128]{1,0:T(8,128)(2,1)S(1)} %get-tuple-element.172), channel_id=1, source_target_pairs={{0,32},{32,0},{64,96},{96,64},{1,33},{33,1},{65,97},{97,65},{2,34}... | collective-permute-start | bytes 786440 | tf_op jit(solution)/shard_map/ppermute | solution.py:573
  15.5 11.2 %collective-permute-start.6 = (bf16[1024,128]{1,0:T(8,128)(2,1)S(1)}, bf16[1024,128]{1,0:T(8,128)(2,1)S(1)}, u32[]{:S(2)}, u32[]{:S(2)}) collective-permute-start(bf16[1024,128]{1,0:T(8,128)(2,1)S(1)} %get-tuple-element.171), channel_id=1, source_target_pairs={{32,64},{64,32},{33,65},{65,33},{34,66},{66,34},{35,67},{67,35},{3... | collective-permute-start | bytes 786440 | tf_op jit(solution)/shard_map/ppermute | solution.py:574
  16.3 10.3 %copy-start.8 = (bf16[512,128]{1,0:T(8,128)(2,1)}, bf16[512,128]{1,0:T(8,128)(2,1)S(1)}, u32[]{:S(2)}) copy-start(bf16[512,128]{1,0:T(8,128)(2,1)S(1)} %collective-permute-done.2.refs_3_) | copy-start | bytes 393220
  16.4 10.3 %collective-permute-start.3 = (bf16[1024,128]{1,0:T(8,128)(2,1)S(1)}, bf16[1024,128]{1,0:T(8,128)(2,1)S(1)}, u32[]{:S(2)}, u32[]{:S(2)}) collective-permute-start(bf16[1024,128]{1,0:T(8,128)(2,1)S(1)} %pad_maximum_fusion), channel_id=1, source_target_pairs={{0,6},{2,4},{4,2},{6,0},{1,7},{3,5},{5,3},{7,1},{8,14},{10,12},{12... | collective-permute-start | bytes 786440 | tf_op jit(solution)/shard_map/ppermute | solution.py:569
  18.9 7.8 %collective-permute-start.4 = (bf16[1024,128]{1,0:T(8,128)(2,1)S(1)}, bf16[1024,128]{1,0:T(8,128)(2,1)S(1)}, u32[]{:S(2)}, u32[]{:S(2)}) collective-permute-start(bf16[1024,128]{1,0:T(8,128)(2,1)S(1)} %pad_maximum_fusion), channel_id=1, source_target_pairs={{0,1},{1,0},{2,3},{3,2},{4,5},{5,4},{6,7},{7,6},{8,9},{9,8},{10,11... | collective-permute-start | bytes 786440 | tf_op jit(solution)/shard_map/ppermute | solution.py:569
  26.7 1.6 %collective-permute-start.7 = (bf16[1024,128]{1,0:T(8,128)(2,1)S(1)}, bf16[1024,128]{1,0:T(8,128)(2,1)S(1)}, u32[]{:S(2)}, u32[]{:S(2)}) collective-permute-start(bf16[1024,128]{1,0:T(8,128)(2,1)S(1)} %collective-permute-done.3.refs_4_), channel_id=1, source_target_pairs={{0,1},{1,0},{2,3},{3,2},{4,5},{5,4},{6,7},{7,6},{8,9},{9,8},{10,11... | collective-permute-start | bytes 786440 | tf_op jit(solution)/shard_map/ppermute | solution.py:569
  57.1 13.1 %collective-permute-start.8 = (f32[272,256]{1,0:T(8,128)}, f32[272,256]{1,0:T(8,128)S(1)}, u32[]{:S(2)}, u32[]{:S(2)}) collective-permute-start(f32[272,256]{1,0:T(8,128)} %get-tuple-element.107), channel_id=1, source_target_pairs={{0,32},{32,0},{64,96},{96,64},{1,33},{33,1},{65,97},{97,65},{2,34}... | collective-permute-start | bytes 835592 | tf_op jit(solution)/shard_map/ppermute | solution.py:569
  70.2 1.9 %collective-permute-start.9 = (bf16[1024,128]{1,0:T(8,128)(2,1)}, bf16[1024,128]{1,0:T(8,128)(2,1)S(1)}, u32[]{:S(2)}, u32[]{:S(2)}) collective-permute-start(bf16[1024,128]{1,0:T(8,128)(2,1)} %get-tuple-element.118), channel_id=1, source_target_pairs={{0,1},{1,0},{2,3},{3,2},{4,5},{5,4},{6,7},{7,6},{8,9},{9,8},{10,11... | collective-permute-start | bytes 786440 | tf_op jit(solution)/shard_map/ppermute | solution.py:569
  70.8 13.5 %collective-permute-start.12 = (f32[272,256]{1,0:T(8,128)S(1)}, f32[272,256]{1,0:T(8,128)S(1)}, u32[]{:S(2)}, u32[]{:S(2)}) collective-permute-start(f32[272,256]{1,0:T(8,128)S(1)} %add.77), channel_id=1, source_target_pairs={{0,96},{32,64},{64,32},{96,0},{1,97},{33,65},{65,33},{97,1},{2,98}... | collective-permute-start | bytes 835592 | tf_op jit(solution)/shard_map/ppermute | solution.py:569
  73.2 11.3 %copy-start.6 = (bf16[1024,128]{1,0:T(8,128)(2,1)S(1)}, bf16[1024,128]{1,0:T(8,128)(2,1)}, u32[]{:S(2)}) copy-start(bf16[1024,128]{1,0:T(8,128)(2,1)} %get-tuple-element.160) | copy-start | bytes 786436
  73.2 11.1 %collective-permute-start.11 = (bf16[1024,128]{1,0:T(8,128)(2,1)S(1)}, bf16[1024,128]{1,0:T(8,128)(2,1)S(1)}, u32[]{:S(2)}, u32[]{:S(2)}) collective-permute-start(bf16[1024,128]{1,0:T(8,128)(2,1)S(1)} %add_convert_fusion), channel_id=1, source_target_pairs={{0,6},{2,4},{4,2},{6,0},{1,7},{3,5},{5,3},{7,1},{8,14},{10,12},{12... | collective-permute-start | bytes 786440 | tf_op jit(solution)/shard_map/ppermute | solution.py:569
  75.1 9.2 %collective-permute-start.10 = (bf16[1024,128]{1,0:T(8,128)(2,1)}, bf16[1024,128]{1,0:T(8,128)(2,1)S(1)}, u32[]{:S(2)}, u32[]{:S(2)}) collective-permute-start(bf16[1024,128]{1,0:T(8,128)(2,1)} %get-tuple-element.121), channel_id=1, source_target_pairs={{0,1},{1,0},{2,3},{3,2},{4,5},{5,4},{6,7},{7,6},{8,9},{9,8},{10,11... | collective-permute-start | bytes 786440 | tf_op jit(solution)/shard_map/ppermute | solution.py:569
  84.4 1.4 %collective-permute-start.13 = (f32[136,256]{1,0:T(8,128)S(1)}, f32[136,256]{1,0:T(8,128)S(1)}, u32[]{:S(2)}, u32[]{:S(2)}) collective-permute-start(f32[136,256]{1,0:T(8,128)S(1)} %slice.77), channel_id=1, source_target_pairs={{0,1},{1,0},{2,3},{3,2},{4,5},{5,4},{6,7},{7,6},{8,9},{9,8},{10,11... | collective-permute-start | bytes 417800 | tf_op jit(solution)/shard_map/ppermute | solution.py:569
  84.5 24.6 %collective-permute-start.14 = (bf16[512,128]{1,0:T(8,128)(2,1)S(1)}, bf16[512,128]{1,0:T(8,128)(2,1)S(1)}, u32[]{:S(2)}, u32[]{:S(2)}) collective-permute-start(bf16[512,128]{1,0:T(8,128)(2,1)S(1)} %add_convert_fusion.1), channel_id=1, source_target_pairs={{0,2},{2,0},{4,6},{6,4},{1,3},{3,1},{5,7},{7,5},{8,10},{10,8},{12,... | collective-permute-start | bytes 393224 | tf_op jit(solution)/shard_map/ppermute | solution.py:569
  85.8 23.3 %collective-permute-start.15 = (f32[136,256]{1,0:T(8,128)S(1)}, f32[136,256]{1,0:T(8,128)S(1)}, u32[]{:S(2)}, u32[]{:S(2)}) collective-permute-start(f32[136,256]{1,0:T(8,128)S(1)} %slice_add_fusion), channel_id=1, source_target_pairs={{0,2},{2,0},{4,6},{6,4},{1,3},{3,1},{5,7},{7,5},{8,10},{10,8},{12,... | collective-permute-start | bytes 417800 | tf_op jit(solution)/shard_map/ppermute | solution.py:569
  86.2 22.9 %collective-permute-start.16 = (f32[136,256]{1,0:T(8,128)S(1)}, f32[136,256]{1,0:T(8,128)S(1)}, u32[]{:S(2)}, u32[]{:S(2)}) collective-permute-start(f32[136,256]{1,0:T(8,128)S(1)} %slice_add_fusion), channel_id=1, source_target_pairs={{0,6},{2,4},{4,2},{6,0},{1,7},{3,5},{5,3},{7,1},{8,14},{10,12},{12... | collective-permute-start | bytes 417800 | tf_op jit(solution)/shard_map/ppermute | solution.py:569
  87.3 21.8 %collective-permute-start.17 = (f32[136,256]{1,0:T(8,128)S(1)}, f32[136,256]{1,0:T(8,128)S(1)}, u32[]{:S(2)}, u32[]{:S(2)}) collective-permute-start(f32[136,256]{1,0:T(8,128)S(1)} %slice_add_fusion), channel_id=1, source_target_pairs={{0,4},{2,6},{4,0},{6,2},{1,5},{3,7},{5,1},{7,3},{8,12},{10,14},{12... | collective-permute-start | bytes 417800 | tf_op jit(solution)/shard_map/ppermute | solution.py:569
  89.2 22.9 %copy-start.10 = (bf16[1024,128]{1,0:T(8,128)(2,1)S(1)}, bf16[1024,128]{1,0:T(8,128)(2,1)}, u32[]{:S(2)}) copy-start(bf16[1024,128]{1,0:T(8,128)(2,1)} %get-tuple-element.154) | copy-start | bytes 786436
  89.2 23.0 %copy-start.9 = (bf16[1024,128]{1,0:T(8,128)(2,1)S(1)}, bf16[1024,128]{1,0:T(8,128)(2,1)}, u32[]{:S(2)}) copy-start(bf16[1024,128]{1,0:T(8,128)(2,1)} %get-tuple-element.155) | copy-start | bytes 786436
  109.1 14.1 %copy-start = (s32[128]{0:T(128)S(1)}, s32[128]{0:T(128)}, u32[]{:S(2)}) copy-start(s32[128]{0:T(128)} %hub_rows.3) | copy-start | bytes 1540
  109.1 14.1 %copy-start.1 = (f32[4096,128]{1,0:T(8,128)S(1)}, f32[4096,128]{1,0:T(8,128)}, u32[]{:S(2)}) copy-start(f32[4096,128]{1,0:T(8,128)} %own_scatter.1.own) | copy-start | bytes 6291460
  109.2 4.8 %collective-permute-start.19 = (f32[136,256]{1,0:T(8,128)S(1)}, f32[136,256]{1,0:T(8,128)S(1)}, u32[]{:S(2)}, u32[]{:S(2)}) collective-permute-start(f32[136,256]{1,0:T(8,128)S(1)} %add_add_fusion), channel_id=1, source_target_pairs={{0,8},{8,0},{16,24},{24,16},{1,9},{9,1},{17,25},{25,17},{2,10},{10... | collective-permute-start | bytes 417800 | tf_op jit(solution)/shard_map/ppermute | solution.py:569
  109.6 4.4 %collective-permute-start.18 = (bf16[256,128]{1,0:T(8,128)(2,1)S(1)}, bf16[256,128]{1,0:T(8,128)(2,1)S(1)}, u32[]{:S(2)}, u32[]{:S(2)}) collective-permute-start(bf16[256,128]{1,0:T(8,128)(2,1)S(1)} %add_convert_fusion.2), channel_id=1, source_target_pairs={{0,24},{8,16},{16,8},{24,0},{1,25},{9,17},{17,9},{25,1},{2,26},{10... | collective-permute-start | bytes 196616 | tf_op jit(solution)/shard_map/ppermute | solution.py:569
  112.1 7.6 %collective-permute-start.22 = (bf16[1024,128]{1,0:T(8,128)(2,1)S(1)}, bf16[1024,128]{1,0:T(8,128)(2,1)S(1)}, u32[]{:S(2)}, u32[]{:S(2)}) collective-permute-start(bf16[1024,128]{1,0:T(8,128)(2,1)S(1)} %copy-done.10), channel_id=1, source_target_pairs={{0,32},{32,0},{64,96},{96,64},{1,33},{33,1},{65,97},{97,65},{2,34}... | collective-permute-start | bytes 786440 | tf_op jit(solution)/shard_map/ppermute | solution.py:573
  112.2 7.5 %collective-permute-start.23 = (bf16[1024,128]{1,0:T(8,128)(2,1)S(1)}, bf16[1024,128]{1,0:T(8,128)(2,1)S(1)}, u32[]{:S(2)}, u32[]{:S(2)}) collective-permute-start(bf16[1024,128]{1,0:T(8,128)(2,1)S(1)} %copy-done.9), channel_id=1, source_target_pairs={{32,64},{64,32},{33,65},{65,33},{34,66},{66,34},{35,67},{67,35},{3... | collective-permute-start | bytes 786440 | tf_op jit(solution)/shard_map/ppermute | solution.py:574
  114.0 5.7 %collective-permute-start.21 = (f32[136,256]{1,0:T(8,128)S(1)}, f32[136,256]{1,0:T(8,128)S(1)}, u32[]{:S(2)}, u32[]{:S(2)}) collective-permute-start(f32[136,256]{1,0:T(8,128)S(1)} %add.89), channel_id=1, source_target_pairs={{0,24},{8,16},{16,8},{24,0},{1,25},{9,17},{17,9},{25,1},{2,26},{10... | collective-permute-start | bytes 417800 | tf_op jit(solution)/shard_map/ppermute | solution.py:569
  116.6 3.1 %collective-permute-start.20 = (bf16[128,128]{1,0:T(8,128)(2,1)S(1)}, bf16[128,128]{1,0:T(8,128)(2,1)S(1)}, u32[]{:S(2)}, u32[]{:S(2)}) collective-permute-start(bf16[128,128]{1,0:T(8,128)(2,1)S(1)} %add_convert_fusion.3), channel_id=1, source_target_pairs={{0,8},{8,0},{16,24},{24,16},{1,9},{9,1},{17,25},{25,17},{2,10},{10... | collective-permute-start | bytes 98312 | tf_op jit(solution)/shard_map/ppermute | solution.py:569
  119.7 5.7 %collective-permute-start.24 = (f32[136,256]{1,0:T(8,128)S(1)}, f32[136,256]{1,0:T(8,128)S(1)}, u32[]{:S(2)}, u32[]{:S(2)}) collective-permute-start(f32[136,256]{1,0:T(8,128)S(1)} %add.94.mine), channel_id=1, source_target_pairs={{0,1},{1,0},{2,3},{3,2},{4,5},{5,4},{6,7},{7,6},{8,9},{9,8},{10,11... | collective-permute-start | bytes 417800 | tf_op jit(solution)/shard_map/ppermute | solution.py:569
  (9 other events, 34.9 us)
